TPU v7x, 32 devices: a whole 2x2x4 slice. The times are simulated.
32 devices in a mesh: seq: 16 (over z, x, core), tp: 2 (over y).
Axes of the slice: x: 2, y: 2, z: 4, core: 2. Of those that a mesh axis runs over, the one named last changes fastest.
Arguments:
- stream_x: bfloat16 [2048, 4096], P('seq', 'tp'), may hold values from -6 to 6
- norm_gain: float32 [4096], replicated, may hold values from 0.1 to 1.9
- w_qkv: bfloat16 [4096, 6144], P('seq', 'tp'), may hold values from -0.09375 to 0.09375
- cache_kv: bfloat16 [2, 1024, 1024], P(None, 'seq', 'tp'), may hold values from -400 to 400
- recomp_hidden: bfloat16 [128, 4096], P('seq', 'tp'), may hold values from -6 to 6
- recomp_index: int32 [128], P('seq'), may hold values from 0 to 1023, as said below
- prefix_len: int32 [1], replicated, may hold values from 512 to 1024
Outputs:
- attended: bfloat16 [2048, 4096], P('seq', 'tp')
Inputs may be any that keep to these rules, and one draw needn't show every extreme that they name: `recomp_index`: the entries held by index s of seq name distinct cache rows of s * 64 to s * 64 + 63.
All inputs are finite; a program needn't handle non-finite values.
Results may differ from a plain program's by a relative error of at most 0.015.
The roundings to bfloat16 on the way count: a program that leaves them out, or rounds other values in their place, can miss the bound.
Values may be sent and summed in bfloat16 or wider, within the bound.
No kernel may reach another device: no remote copies, remote signals or barrier semaphores. Data moves between devices by JAX's collectives and lax.ppermute only.
A program may use at most 64 MiB of HBM per device.

v0:
```python
import math

import jax
import jax.numpy as jnp
from jax import lax
from jax.sharding import PartitionSpec as P

HEADS = 32
KVH = 8
HD = 128


def normed(rows, gain):
    values = rows.astype(jnp.float32)
    spread = jnp.mean(values * values, axis=-1, keepdims=True)
    return (values * lax.rsqrt(spread + 1e-05) * gain).astype(jnp.bfloat16)


def rotate(values, places):
    half = values.shape[-1] // 2
    freq = jnp.exp(-math.log(1000000.0) * jnp.arange(half, dtype=jnp.float32) * 2.0 / (2 * half))
    angle = places[:, None] * freq[None, :]
    shape = (angle.shape[0],) + (1,) * (values.ndim - 2) + (half,)
    cosine = jnp.cos(angle).reshape(shape)
    sine = jnp.sin(angle).reshape(shape)
    first = values[..., :half]
    second = values[..., half:]
    return jnp.concatenate([first * cosine - second * sine, first * sine + second * cosine], -1)


def add_rows(left, piece):
    return jnp.dot(left, piece, preferred_element_type=jnp.float32)


def per_device(stream_x, norm_gain, w_qkv, cache_kv, recomp_hidden, recomp_index, prefix_len):
    whole_x, whole_h = (
        lax.all_gather(stream_x, "tp", axis=1, tiled=True),
        lax.all_gather(recomp_hidden, "tp", axis=1, tiled=True),
    )
    normed_x = normed(whole_x, norm_gain)
    normed_h = normed(whole_h, norm_gain)
    tok_rows = normed_x.shape[0]
    redo_rows = normed_h.shape[0]
    group = HEADS // KVH
    local = w_qkv.shape[1] // ((group + 2) * HD)
    cache_rows = cache_kv.shape[1]
    seq_at = lax.axis_index("seq")
    stacked = jnp.concatenate([normed_x, normed_h], 0)
    full = add_rows(stacked, lax.all_gather(w_qkv, "seq", axis=0, tiled=True))
    full = full.reshape(tok_rows + redo_rows, local, group + 2, HD)
    query_raw = full[:tok_rows, :, :group]
    kv_part = full[:, :, group:]
    begin = prefix_len[0]
    token_ids = seq_at * tok_rows + jnp.arange(tok_rows, dtype=jnp.int32)
    places = (token_ids + begin).astype(jnp.float32)
    query = rotate(query_raw, places).astype(jnp.bfloat16)
    new_keys = rotate(kv_part[:tok_rows, :, 0], places).astype(jnp.bfloat16)
    new_values = kv_part[:tok_rows, :, 1].astype(jnp.bfloat16)
    redo_keys = rotate(kv_part[tok_rows:, :, 0], recomp_index.astype(jnp.float32)).astype(
        jnp.bfloat16
    )
    redo_values = kv_part[tok_rows:, :, 1].astype(jnp.bfloat16)
    rows_here = recomp_index - seq_at * cache_rows
    keys_c = cache_kv[0].at[rows_here].set(redo_keys.reshape(redo_rows, local * HD))
    values_c = cache_kv[1].at[rows_here].set(redo_values.reshape(redo_rows, local * HD))
    held = jnp.stack(
        [
            jnp.concatenate([new_keys.reshape(tok_rows, local * HD), keys_c], 0),
            jnp.concatenate([new_values.reshape(tok_rows, local * HD), values_c], 0),
        ]
    )
    span = tok_rows + cache_rows
    scale = 1.0 / math.sqrt(HD)

    def attend_one(carry, piece, start):
        top_old, total, accum = carry
        count = piece.shape[1]
        rows = start + jnp.arange(count, dtype=jnp.int32)
        owner = rows // span
        within = rows % span
        is_stream = within < tok_rows
        stream_pos = owner * tok_rows + within
        cache_pos = owner * cache_rows + within - tok_rows
        allowed = jnp.where(
            is_stream[None, :],
            stream_pos[None, :] <= token_ids[:, None],
            (cache_pos < begin)[None, :],
        )
        key_rows = piece[0].reshape(count, local, HD)
        value_rows = piece[1].reshape(count, local, HD)
        score = (
            jnp.einsum("tkgd,nkd->kgtn", query, key_rows, preferred_element_type=jnp.float32)
            * scale
        )
        score = jnp.where(allowed[None, None], score, -1e30)
        top_new = jnp.maximum(top_old, jnp.max(score, -1))
        weights = jnp.where(allowed[None, None], jnp.exp(score - top_new[..., None]), 0.0)
        keep = jnp.exp(top_old - top_new)
        total = total * keep + jnp.sum(weights, -1)
        accum = accum * keep[..., None] + jnp.einsum(
            "kgtn,nkd->kgtd",
            weights.astype(jnp.bfloat16),
            value_rows,
            preferred_element_type=jnp.float32,
        )
        return (top_new, total, accum)

    init = (
        jnp.full((local, group, tok_rows), -1e30, jnp.float32),
        jnp.zeros((local, group, tok_rows), jnp.float32),
        jnp.zeros((local, group, tok_rows, HD), jnp.float32),
    )
    carry = init
    piece = lax.all_gather(held, "seq", axis=1, tiled=True)
    count = piece.shape[1]
    shards = count // span
    pieces = jnp.transpose(piece.reshape(2, shards, span, piece.shape[2]), (1, 0, 2, 3))

    def step(state, item):
        index, single = item
        return (attend_one(state, single, index * span), None)

    carry, unused = lax.scan(step, carry, (jnp.arange(shards, dtype=jnp.int32), pieces))
    top_all, total, accum = carry
    mixed = accum / total[..., None]
    return (
        jnp.transpose(mixed, (2, 0, 1, 3))
        .reshape(tok_rows, local * group * HD)
        .astype(jnp.bfloat16)
    )


def solution(mesh):
    placed = (
        P("seq", "tp"),
        P(),
        P("seq", "tp"),
        P(None, "seq", "tp"),
        P("seq", "tp"),
        P("seq"),
        P(),
    )
    return jax.shard_map(
        per_device, mesh=mesh, in_specs=placed, out_specs=P("seq", "tp"), check_vma=False
    )
```

profile of v0, /device:TPU:0, one launch (start us, length us, event | category | flops | bytes accessed | tf_op | source)
XLA Modules:
  0.0 424.2 jit_solution(11230327723489907048)
XLA Ops:
  8.7 5.5 %all_gather.13 = bf16[8,4096]{1,0:T(8,128)(2,1)S(1)} all-gather(bf16[8,2048]{1,0:T(8,128)(2,1)S(1)} %copy-done.7), channel_id=1, replica_groups=mesh['seq'=16,'tp'=2] {'tp'}, dimensions={1}, use_global_device_ids=true | all-gather | bytes 98304 | tf_op jit(solution)/shard_map/all_gather | solution.py:38
  15.6 17.3 %all-gather.4.cloned.1.call-done = bf16[128,4096]{1,0:T(8,128)(2,1)} async-done(((bf16[128,2048]{1,0:T(8,128)(2,1)}), bf16[128,4096]{1,0:T(8,128)(2,1)}) %all-gather.4.cloned.1.call-update) | async-done | bytes 1048592 | tf_op jit(solution)/shard_map/all_gather | solution.py:37
  33.0 1.6 fusion.14
  34.9 128.3 %all-gather.6.cloned.1.call-done = bf16[4096,3072]{1,0:T(8,128)(2,1)} async-done(((bf16[256,3072]{1,0:T(8,128)(2,1)}), bf16[4096,3072]{1,0:T(8,128)(2,1)}) %all-gather.6.cloned.1.call-update) | async-done | bytes 25165840 | tf_op jit(solution)/shard_map/all_gather | solution.py:49
  163.2 13.0 %fusion.17 = f32[136,3072]{1,0:T(8,128)} fusion(bf16[4096,3072]{1,0:T(8,128)(2,1)} %all-gather.6.cloned.1.call-done, bf16[8,4096]{1,0:T(8,128)(2,1)S(1)} %fusion.24, bf16[128,4096]{1,0:T(8,128)(2,1)S(1)} %fusion.16), kind=kOutput, calls=%fused_computation.35 | convolution fusion | flops 3424780288 | bytes 27951104 | tf_op jit(solution)/shard_map/dot_general | solution.py:32
  176.2 2.1 reshape.289
  180.1 2.1 scatter_custom_fusion
  186.0 1.1 copy.39
  188.8 60.3 %all-gather.8.cloned.1.call-done = bf16[2,3072,512]{2,0,1:T(2,128)(2,1)} async-done(((bf16[2,192,512]{2,0,1:T(2,128)(2,1)}), bf16[2,3072,512]{2,0,1:T(2,128)(2,1)}) %all-gather.8.cloned.1.call-update) | async-done | bytes 6291472 | tf_op jit(solution)/shard_map/all_gather | solution.py:114
  249.1 6.4 %copy.40 = bf16[2,3072,512]{2,1,0:T(8,128)(2,1)} copy(bf16[2,3072,512]{2,0,1:T(2,128)(2,1)} %all-gather.8.cloned.1.call-done) | data formatting | bytes 12582912 | tf_op jit(solution)/shard_map/all_gather | solution.py:114
  255.6 159.5 %while.17 = (s32[]{:T(128)}, f32[4,4,128]{2,1,0:T(4,128)}, f32[4,4,128]{2,1,0:T(4,128)}, f32[4,4,128,128]{3,2,1,0:T(8,128)S(1)}, s32[16]{0:T(128)S(1)}, /*index=...) while((s32[]{:T(128)}, f32[4,4,128]{2,1,0:T(4,128)}, ...), condition=%wide.region_7.8_spmd.clone, body=%wide.region_4.7_spmd.clone.sunk | while | flops 205717824 | bytes 10424377 | solution.py:123
  259.4 1.1 fusion.48
  260.6 1.0 fusion.49
  262.3 1.9 convolution_add_fusion.2
  268.7 1.1 fusion.48
  270.6 1.0 fusion.49
  272.3 1.9 convolution_add_fusion.2
  277.5 1.0 dynamic-slice_bitcast_fusion.2
  278.7 1.1 fusion.48
  280.6 1.0 fusion.49
  282.3 1.9 convolution_add_fusion.2
  288.7 1.1 fusion.48
  290.6 1.0 fusion.49
  292.3 1.9 convolution_add_fusion.2
  297.6 1.0 dynamic-slice_bitcast_fusion.2
  298.7 1.1 fusion.48
  300.6 1.0 fusion.49
  302.3 1.9 convolution_add_fusion.2
  308.7 1.1 fusion.48
  310.6 1.0 fusion.49
  312.3 1.9 convolution_add_fusion.2
  317.6 1.0 dynamic-slice_bitcast_fusion.2
  318.7 1.1 fusion.48
  320.6 1.0 fusion.49
  322.4 1.9 convolution_add_fusion.2
  328.7 1.1 fusion.48
  330.6 1.0 fusion.49
  332.4 1.9 convolution_add_fusion.2
  338.7 1.1 fusion.48
  340.6 1.0 fusion.49
  342.4 1.9 convolution_add_fusion.2
  348.7 1.1 fusion.48
  350.7 1.0 fusion.49
  352.4 1.9 convolution_add_fusion.2
  358.8 1.1 fusion.48
  360.7 1.0 fusion.49
  362.4 1.9 convolution_add_fusion.2
  368.8 1.1 fusion.48
  370.7 1.0 fusion.49
  372.4 1.9 convolution_add_fusion.2
  378.8 1.1 fusion.48
  380.7 1.0 fusion.49
  382.4 1.9 convolution_add_fusion.2
  388.8 1.1 fusion.48
  390.7 1.0 fusion.49
  392.4 1.9 convolution_add_fusion.2
  398.8 1.1 fusion.48
  400.7 1.0 fusion.49
  402.5 1.9 convolution_add_fusion.2
  408.8 1.1 fusion.48
  410.7 1.0 fusion.49
  412.5 1.9 convolution_add_fusion.2
  415.0 1.0 fusion.21
  416.5 1.2 convert_element_type.70
  (402 shorter events, 89.5 us)
Async XLA Ops:
  6.5 2.2 copy-start.7
  6.5 7.9 %copy-start.8 = (s32[8]{0:T(128)S(1)}, s32[8]{0:T(128)}, u32[]{:S(2)}) copy-start(s32[8]{0:T(128)} %param.14) | copy-start | bytes 100
  6.5 8.3 %copy-start.5 = (bf16[2,64,512]{2,1,0:T(8,128)(2,1)S(1)}, bf16[2,64,512]{2,1,0:T(8,128)(2,1)}, u32[]{:S(2)}) copy-start(bf16[2,64,512]{2,1,0:T(8,128)(2,1)} %param.12) | copy-start | bytes 393220
  6.5 9.0 %copy-start.6 = (f32[4096]{0:T(1024)S(1)}, f32[4096]{0:T(1024)}, u32[]{:S(2)}) copy-start(f32[4096]{0:T(1024)} %param.10) | copy-start | bytes 49156
  6.5 26.4 %all-gather.4.cloned.1.call-start = ((), (), s32[]{:S(2)}) async-start(), calls=%async_computation | async-start | bytes 1572864 | tf_op jit(solution)/shard_map/all_gather | solution.py:37
  7.3 155.9 %all-gather.6.cloned.1.call-start = ((), (), s32[]{:S(2)}) async-start(), calls=%async_computation.1 | async-start | bytes 26738688 | tf_op jit(solution)/shard_map/all_gather | solution.py:49
  8.0 241.1 %all-gather.8.cloned.1.call-start = ((), (), s32[]{:S(2)}) async-start(), calls=%async_computation.2 | async-start | bytes 6684672 | tf_op jit(solution)/shard_map/all_gather | solution.py:114
  178.9 4.2 copy-start.4
  255.6 2.7 copy-start.9
  262.3 2.6 copy-start.10
  264.8 2.7 copy-start.9
  269.8 1.8 copy-start.1
  269.8 1.8 copy-start.2
  272.3 2.6 copy-start.10
  274.8 2.7 copy-start.9
  279.8 1.8 copy-start.1
  279.8 1.8 copy-start.2
  282.3 2.6 copy-start.10
  284.9 2.7 copy-start.9
  289.8 1.8 copy-start.1
  289.8 1.8 copy-start.2
  292.3 2.6 copy-start.10
  294.9 2.7 copy-start.9
  299.8 1.8 copy-start.1
  299.8 1.8 copy-start.2
  302.3 2.6 copy-start.10
  304.9 2.7 copy-start.9
  309.8 1.8 copy-start.1
  309.8 1.8 copy-start.2
  312.3 2.6 copy-start.10
  314.9 2.7 copy-start.9
  319.8 1.8 copy-start.1
  319.9 1.8 copy-start.2
  322.3 2.6 copy-start.10
  324.9 2.7 copy-start.9
  329.9 1.8 copy-start.1
  332.4 2.6 copy-start.10
  334.9 2.7 copy-start.9
  339.9 1.8 copy-start.1
  339.9 1.8 copy-start.2
  342.4 2.6 copy-start.10
  344.9 2.7 copy-start.9
  349.9 1.8 copy-start.1
  349.9 1.8 copy-start.2
  352.4 2.6 copy-start.10
  354.9 2.7 copy-start.9
  359.9 1.8 copy-start.1
  359.9 1.8 copy-start.2
  362.4 2.6 copy-start.10
  365.0 2.7 copy-start.9
  369.9 1.8 copy-start.1
  372.4 2.6 copy-start.10
  375.0 2.7 copy-start.9
  379.9 1.8 copy-start.1
  382.4 2.6 copy-start.10
  385.0 2.7 copy-start.9
  389.9 1.8 copy-start.1
  392.4 2.6 copy-start.10
  395.0 2.7 copy-start.9
  399.9 1.8 copy-start.1
  402.4 2.6 copy-start.10
  405.0 2.7 copy-start.9
  410.0 1.8 copy-start.1
  412.5 2.6 copy-start.10
  (25 other events, 24.1 us)
Sparse Core Ops, SparseCore 0:
  8.9 23.9 all-gather.3
  34.6 128.5 all-gather.5
  187.2 61.8 all-gather.7
where the time goes:
time: 429 us; the launch traced here: 424 us
  waiting for transfers between devices  207 us (48%)
  local copies, waits for them, and re-layouts  64.6 us (15%)
  matrix products  62.3 us (15%)
  other arithmetic  58.3 us (14%)
  between operations  14 us (3%)
  loops' own time  12.1 us (3%)
  blocking collectives  5.51 us (1%)
    all_gather x1, waiting for transfers between devices, per_device(): full = add_rows(stacked, lax.all_gather(w_qkv, 'seq', axis=0, tiled=True))  128 us
    all_gather x1, waiting for transfers between devices, per_device(): piece = lax.all_gather(held, 'seq', axis=1, tiled=True)  60.3 us
    dot_general x16, matrix products, attend_one(): jnp.einsum('kgtn,nkd->kgtd', weights.astype(jnp.bfloat16), value_rows, pr...  31.1 us
    dynamic_slice x32, local copies, waits for them, and re-layouts, per_device(): lax.scan(step, carry, (jnp.arange(shards, dtype=jnp.int32), pieces))  25.7 us
    while x176, local copies, waits for them, and re-layouts  19.2 us
    dot_general x16, matrix products, attend_one(): jnp.einsum('tkgd,nkd->kgtn', query, key_rows, preferred_element_type=jnp....  18.1 us
    all_gather x1, waiting for transfers between devices, per_device(): lax.all_gather(stream_x, 'tp', axis=1, tiled=True)  17.3 us
    reduce_sum x16, other arithmetic, attend_one(): total = total * keep + jnp.sum(weights, -1)  16.4 us
  transfers between devices with their start and end apart: 3, of which 3 were waited for; matrix products, arithmetic and copies ran while one was open for 1% of the time, Pallas kernels for 0%

commit v1 on v0

v1 whole, which is shorter than its diff:
```python
import functools
import math

import jax
import jax.numpy as jnp
from jax import lax
from jax.experimental import pallas as pl
from jax.experimental.pallas import tpu as pltpu
from jax.sharding import PartitionSpec as P

HEADS = 32
KVH = 8
HD = 128
GROUP = HEADS // KVH
WIDTH = (GROUP + 2) * HD
FEATS = 256
FAR = -1e30
VMEM = pl.BlockSpec(memory_space=pltpu.VMEM)
SMEM = pl.BlockSpec(memory_space=pltpu.SMEM)


def swap(value, axis, size, mask):
    return lax.ppermute(value, axis, [(i, i ^ mask) for i in range(size)])


def norm_kernel(count, *refs):
    parts, gains, outs = refs[:count], refs[count : 2 * count], refs[2 * count :]
    values = [part[...].astype(jnp.float32) for part in parts]
    total = sum(jnp.sum(v * v, axis=-1, keepdims=True) for v in values)
    width = sum(v.shape[1] for v in values)
    factor = lax.rsqrt(total / width + 1e-05)
    for value, gain, out in zip(values, gains, outs):
        rows = (value * factor * gain[...]).astype(jnp.bfloat16)
        for block in range(out.shape[0]):
            out[block] = rows[:, block * FEATS : (block + 1) * FEATS]


def norm(parts, gains):
    rows = parts[0].shape[0]
    return pl.pallas_call(
        functools.partial(norm_kernel, len(parts)),
        out_shape=[
            jax.ShapeDtypeStruct((p.shape[1] // FEATS, rows, FEATS), jnp.bfloat16) for p in parts
        ],
        in_specs=[VMEM] * (2 * len(parts)),
        out_specs=[VMEM] * len(parts),
        compiler_params=pltpu.CompilerParams(vmem_limit_bytes=24 * 2**20),
        name="norm",
    )(*parts, *[g.reshape(1, -1) for g in gains])


def project_kernel(n_x, n_w, tok, *refs):
    x_ids, w_ids = refs[0], refs[1]
    x_parts = refs[2 : 2 + n_x]
    w_parts = refs[2 + n_x : 2 + n_x + n_w]
    cosine, sine, cache, pick, q_out, kv_out, held = refs[2 + n_x + n_w :]
    tile = pl.program_id(0)

    @pl.when(tile == 0)
    def _():
        at = 0
        for part in x_parts:
            for block in range(part.shape[0]):
                held[x_ids[at]] = part[block]
                at += 1

    total = None
    at = 0
    for part in w_parts:
        for block in range(part.shape[0]):
            term = jnp.dot(held[w_ids[at]], part[block], preferred_element_type=jnp.float32)
            total = term if total is None else total + term
            at += 1
    cos_rows, sin_rows = cosine[...], sine[...]

    def rotated(value):
        return value * cos_rows + pltpu.roll(value, HD // 2, 1) * sin_rows

    @pl.when(tile > 0)
    def _():
        for head in range(2):
            turned = rotated(total[:, head * HD : (head + 1) * HD])
            q_out[head] = turned[:tok].astype(jnp.bfloat16)

    @pl.when(tile == 0)
    def _():
        rows = jnp.concatenate([rotated(total[:, :HD]), total[:, HD:]], 1).astype(jnp.bfloat16)
        rows = rows.astype(jnp.float32)
        kv_out[:tok] = rows[:tok].astype(jnp.bfloat16)
        chosen = pick[...]
        fresh = jnp.dot(chosen, rows[tok:], preferred_element_type=jnp.float32, precision=lax.Precision.HIGHEST)
        hit = jnp.sum(chosen, axis=1, keepdims=True) > 0.5
        kept = cache[...].astype(jnp.float32)
        kv_out[tok:] = jnp.where(hit, fresh, kept).astype(jnp.bfloat16)


def project(x_parts, x_ids, w_parts, w_ids, cosine, sine, cache, pick, tok):
    rows = x_parts[0].shape[1]
    blocks = sum(p.shape[0] for p in x_parts)
    span = tok + cache.shape[0]
    full = lambda a: pl.BlockSpec(a.shape, lambda t, n=a.ndim: (0,) * n)
    tiles = WIDTH // FEATS
    w_spec = lambda a: pl.BlockSpec(
        (a.shape[0], FEATS, FEATS), lambda t: (0, 0, lax.rem(t + tiles - 1, tiles))
    )
    return pl.pallas_call(
        functools.partial(project_kernel, len(x_parts), len(w_parts), tok),
        grid=(tiles,),
        out_shape=[
            jax.ShapeDtypeStruct((GROUP, tok, HD), jnp.bfloat16),
            jax.ShapeDtypeStruct((span, 2 * HD), jnp.bfloat16),
        ],
        in_specs=[SMEM, SMEM]
        + [full(a) for a in x_parts]
        + [w_spec(a) for a in w_parts]
        + [full(a) for a in (cosine, sine, cache, pick)],
        out_specs=[
            pl.BlockSpec((2, tok, HD), lambda t: (jnp.maximum(t - 1, 0), 0, 0)),
            pl.BlockSpec((span, 2 * HD), lambda t: (0, 0)),
        ],
        scratch_shapes=[pltpu.VMEM((blocks, rows, FEATS), jnp.bfloat16)],
        compiler_params=pltpu.CompilerParams(vmem_limit_bytes=40 * 2**20),
        cost_estimate=pl.CostEstimate(
            flops=2 * rows * blocks * FEATS * WIDTH,
            bytes_accessed=2 * blocks * FEATS * (WIDTH + rows),
            transcendentals=0,
        ),
        name="project",
    )(x_ids, w_ids, *x_parts, *w_parts, cosine, sine, cache, pick)


def attend_kernel(n_kv, tok, *refs):
    begin_ref, q_ids, kv_ids = refs[:3]
    q_ref = refs[3]
    kv_refs = refs[4 : 4 + n_kv]
    out, top, total, accum = refs[4 + n_kv :]
    begin = begin_ref[0]
    q_id = q_ids[pl.program_id(0)]
    query = q_ref[0].reshape(GROUP * tok, HD)
    scale = math.log2(math.e) / math.sqrt(HD)
    places = [(ref, i) for ref in kv_refs for i in range(ref.shape[0])]
    cache_rows = kv_refs[0].shape[1] - tok
    top[...] = jnp.full(top.shape, FAR, jnp.float32)
    total[...] = jnp.zeros(total.shape, jnp.float32)
    accum[...] = jnp.zeros(accum.shape, jnp.float32)

    def take(keys, values, allowed):
        score = lax.dot_general(
            query, keys, (((1,), (1,)), ((), ())), preferred_element_type=jnp.float32
        )
        score = score * scale
        if allowed is not None:
            score = jnp.where(allowed(score.shape), score, FAR)
        old = top[...]
        new = jnp.maximum(old, jnp.max(score, axis=1, keepdims=True))
        weights = jnp.exp2(score - new)
        keep = jnp.exp2(old - new)
        top[...] = new
        total[...] = total[...] * keep + jnp.sum(weights, axis=1, keepdims=True)
        accum[...] = accum[...] * keep + jnp.dot(
            weights.astype(jnp.bfloat16), values, preferred_element_type=jnp.float32
        )

    at = 0
    while at < len(places):
        group = places[at : at + 4]
        ids = [kv_ids[at + i] for i in range(len(group))]
        at += len(group)
        least = functools.reduce(jnp.minimum, ids)
        most = functools.reduce(jnp.maximum, ids)

        def rows(first, last, group=group):
            keys = jnp.concatenate([ref[i, first:last, :HD] for ref, i in group], 0)
            values = jnp.concatenate([ref[i, first:last, HD:] for ref, i in group], 0)
            return keys, values

        def starts(shape, step, ids=ids):
            column = lax.broadcasted_iota(jnp.int32, shape, 1)
            which = column // step
            first = jnp.zeros(shape, jnp.int32)
            for i, one in enumerate(ids):
                first = jnp.where(which == i, one * step, first)
            return first + column % step

        def causal(shape, starts=starts):
            row = lax.broadcasted_iota(jnp.int32, shape, 0)
            return starts(shape, tok) <= q_id * tok + row % tok

        def prefix(shape, starts=starts):
            return starts(shape, cache_rows) < begin

        @pl.when((most + 1) * cache_rows <= begin)
        def _(rows=rows):
            take(*rows(tok, tok + cache_rows), None)

        @pl.when(((most + 1) * cache_rows > begin) & (least * cache_rows < begin))
        def _(rows=rows, prefix=prefix):
            take(*rows(tok, tok + cache_rows), prefix)

        @pl.when(most < q_id)
        def _(rows=rows):
            take(*rows(0, tok), None)

        @pl.when((most >= q_id) & (least <= q_id))
        def _(rows=rows, causal=causal):
            take(*rows(0, tok), causal)

    mixed = (accum[...] / total[...]).astype(jnp.bfloat16)
    for head in range(GROUP):
        out[0, :, head * HD : (head + 1) * HD] = mixed[head * tok : (head + 1) * tok]


def attend(begin, query, q_ids, kv_parts, kv_ids, tok):
    slots = query.shape[0]
    full = lambda a: pl.BlockSpec(a.shape, lambda t, n=a.ndim: (0,) * n)
    n_rows = sum(a.shape[0] for a in kv_parts) * kv_parts[0].shape[1]
    return pl.pallas_call(
        functools.partial(attend_kernel, len(kv_parts), tok),
        grid=(slots,),
        out_shape=jax.ShapeDtypeStruct((slots, tok, GROUP * HD), jnp.bfloat16),
        in_specs=[SMEM, SMEM, SMEM, pl.BlockSpec((1, GROUP, tok, HD), lambda t: (t, 0, 0, 0))]
        + [full(a) for a in kv_parts],
        out_specs=pl.BlockSpec((1, tok, GROUP * HD), lambda t: (t, 0, 0)),
        scratch_shapes=[
            pltpu.VMEM((GROUP * tok, 1), jnp.float32),
            pltpu.VMEM((GROUP * tok, 1), jnp.float32),
            pltpu.VMEM((GROUP * tok, HD), jnp.float32),
        ],
        compiler_params=pltpu.CompilerParams(vmem_limit_bytes=40 * 2**20),
        cost_estimate=pl.CostEstimate(
            flops=4 * slots * GROUP * tok * n_rows * HD,
            bytes_accessed=4 * n_rows * HD,
            transcendentals=slots * GROUP * tok * n_rows,
        ),
        name="attend",
    )(begin, q_ids, kv_ids, query, *kv_parts)


def per_device(
    seq, tp, stream_x, norm_gain, w_qkv, cache_kv, recomp_hidden, recomp_index, prefix_len
):
    tok, redo = stream_x.shape[0], recomp_hidden.shape[0]
    cache_rows = cache_kv.shape[1]
    heads = w_qkv.shape[1] // WIDTH
    near = seq // heads
    at, side = lax.axis_index("seq"), lax.axis_index("tp")
    plane, inner = at // near, at % near
    begin = prefix_len[0]
    squared = near == 4 and heads == 4 and tp == 2

    def across(value, k):
        return swap(value, "seq", seq, k * near) if k else value

    w_mine = [
        across(lax.dynamic_slice_in_dim(w_qkv, (plane ^ k) * WIDTH, WIDTH, 1), k)
        for k in range(heads)
    ]
    caches = []
    for k in range(heads):
        part = lax.dynamic_slice_in_dim(cache_kv, (plane ^ k) * HD, HD, 2)
        caches.append(across(jnp.concatenate([part[0], part[1]], 1), k))
    index_all = lax.all_gather(recomp_index, "seq", axis=0, tiled=True)

    raw = jnp.concatenate([stream_x, recomp_hidden], 0)
    rows = tok + redo
    part_blocks = raw.shape[1] // FEATS
    block_ids = jnp.arange(part_blocks, dtype=jnp.int32)
    if tp == 2:
        other = swap(raw, "tp", tp, 1)
        wide = raw.shape[1]
        gains = [
            lax.dynamic_slice_in_dim(norm_gain, side * wide, wide),
            lax.dynamic_slice_in_dim(norm_gain, (1 - side) * wide, wide),
        ]
        own, opposite = norm([raw, other], gains)
        x_ids = jnp.concatenate([side * part_blocks + block_ids, (1 - side) * part_blocks + block_ids])
    else:
        whole = lax.all_gather(raw, "tp", axis=1, tiled=True)
        (own,) = norm([whole], [norm_gain])
        opposite = None
        x_ids = jnp.arange(own.shape[0], dtype=jnp.int32)
    if heads == 4:
        middle = [(i * near + j, (3 - i) * near + j) for i in (1, 2) for j in range(near)]
        outward = [(i * near + j, (i * 3 - 3) * near + j) for i in (1, 2) for j in range(near)]
        is_mid = (plane == 1) | (plane == 2)
        first = across(own, 1)
        mid_own = lax.ppermute(own, "seq", middle)
        mid_first = lax.ppermute(first, "seq", middle)
        out_own = lax.ppermute(mid_own, "seq", outward)
        out_first = lax.ppermute(mid_first, "seq", outward)
        chunks = [own, first, jnp.where(is_mid, mid_first, out_own), jnp.where(is_mid, mid_own, out_first)]
    else:
        chunks = [across(own, k) for k in range(heads)]
    if opposite is None:
        x_slots = [[chunk] for chunk in chunks]
    else:
        x_slots = [[own, opposite]] + [[chunk, swap(chunk, "tp", tp, 1)] for chunk in chunks[1:]]

    if squared:
        w_parts, w_ids = [], []
        for pair in (0, 2):
            mine = jnp.stack(w_mine[pair : pair + 2])
            line = swap(mine, "seq", seq, 2)
            both = jnp.concatenate([mine, line], 0)
            far = swap(both, "seq", seq, 1)
            w_parts += [both, far]
            for flip in (0, 1):
                for turn in (0, 2):
                    w_ids += [(plane ^ k) * near + (inner ^ turn ^ flip) for k in (pair, pair + 1)]
        w_ids = jnp.stack(w_ids).astype(jnp.int32)
    else:
        groups = [[i * near + j for j in range(near)] for i in range(heads)]
        gathered = [
            lax.all_gather(w, "seq", axis=0, tiled=True, axis_index_groups=groups) for w in w_mine
        ]
        per = gathered[0].shape[0] // FEATS
        w_parts = [g.reshape(per, FEATS, WIDTH) for g in gathered]
        w_ids = jnp.concatenate(
            [(plane ^ k) * per + jnp.arange(per, dtype=jnp.int32) for k in range(heads)]
        )

    half = HD // 2
    freq = jnp.exp(-math.log(1000000.0) * jnp.arange(half, dtype=jnp.float32) * 2.0 / (2 * half))
    queries, kv_new, q_ids = [], [], []
    for k in range(heads):
        source = (plane ^ k) * near + inner
        q_ids.append(source)
        rows_at = lax.dynamic_slice_in_dim(index_all, source * redo, redo)
        token_ids = source * tok + jnp.arange(tok, dtype=jnp.int32)
        places = jnp.concatenate([token_ids + begin, rows_at]).astype(jnp.float32)
        angle = places[:, None] * freq[None, :]
        cosine, sine = jnp.cos(angle), jnp.sin(angle)
        cosine = jnp.concatenate([cosine, cosine], 1)
        sine = jnp.concatenate([-sine, sine], 1)
        here = source * cache_rows + jnp.arange(cache_rows, dtype=jnp.int32)
        pick = (here[:, None] == rows_at[None, :]).astype(jnp.float32)
        q_one, kv_one = project(
            x_slots[k], x_ids, w_parts, w_ids, cosine, sine, caches[k], pick, tok
        )
        queries.append(q_one)
        kv_new.append(kv_one)
    q_ids = jnp.stack(q_ids).astype(jnp.int32)

    if squared:
        kv_parts, kv_ids = [], []
        for pair in (0, 2):
            mine = jnp.stack(kv_new[pair : pair + 2])
            line = swap(mine, "seq", seq, 2)
            both = jnp.concatenate([mine, line], 0)
            far = swap(both, "seq", seq, 1)
            parts = [both[0:1], both[2:3], far[0:1], far[2:3], both[1:2], both[3:4], far[1:2], far[3:4]]
            kv_parts += [jnp.concatenate(parts, 0)]
            for k in (pair, pair + 1):
                kv_ids += [(plane ^ k) * near + (inner ^ turn) for turn in (0, 2, 1, 3)]
        kv_ids = jnp.stack(kv_ids).astype(jnp.int32)
    else:
        kv_parts = [
            lax.all_gather(kv, "seq", axis=0, tiled=False, axis_index_groups=groups)
            for kv in kv_new
        ]
        kv_ids = jnp.concatenate(
            [(plane ^ k) * near + jnp.arange(near, dtype=jnp.int32) for k in range(heads)]
        )

    mixed = attend(prefix_len, jnp.stack(queries), q_ids, kv_parts, kv_ids, tok)
    back = jnp.stack([across(mixed[k], k) for k in range(heads)])
    columns = [lax.dynamic_index_in_dim(back, plane ^ h, 0, keepdims=False) for h in range(heads)]
    return jnp.concatenate(columns, 1)


def solution(mesh):
    placed = (
        P("seq", "tp"),
        P(),
        P("seq", "tp"),
        P(None, "seq", "tp"),
        P("seq", "tp"),
        P("seq"),
        P(),
    )
    return jax.shard_map(
        functools.partial(per_device, mesh.shape["seq"], mesh.shape["tp"]),
        mesh=mesh,
        in_specs=placed,
        out_specs=P("seq", "tp"),
        check_vma=False,
    )
```

time: 429 us -> 206 us (0.48); the launches traced: 424 us -> 208 us
  waiting for transfers between devices: 207 us -> 66.3 us
  matrix products: 62.3 us -> 0 us
  local copies, waits for them, and re-layouts: 64.6 us -> 7.4 us
  Pallas kernels: 0 us -> 52.8 us
  other arithmetic: 58.3 us -> 19.8 us
  starting transfers between devices: 0.11 us -> 27.4 us
  blocking collectives: 5.51 us -> 31.9 us
  loops' own time: 12.1 us -> 0 us
  between operations: 14 us -> 2.07 us
    all_gather x3 -> x0, waiting for transfers between devices: 206 us -> none  [the longest x1 128 us: per_device(): full = add_rows(stacked, lax.all_gather(w_qkv, 'seq', axis=0, tiled=True))]
    ppermute x0 -> x26, waiting for transfers between devices: none -> 66.3 us  [the longest x22 44 us: swap(): return lax.ppermute(value, axis, [(i, i ^ mask) for i in range(size)])]
    dot_general x33 -> x0, matrix products: 62.3 us -> none  [the longest x16 31.1 us: attend_one(): jnp.einsum('kgtn,nkd->kgtd', weights.astype(jnp.bfloat16), value_rows, pr...]
    pallas_call x0 -> x6, Pallas kernels: none -> 52.8 us  [the longest x1 34.6 us: attend(): pl.pallas_call(functools.partial(attend_kernel, len(kv_parts), tok), grid...]
    unnamed x0 -> x1, blocking collectives: none -> 31.9 us
    ppermute x0 -> x26, starting transfers between devices: none -> 27.4 us  [the longest x22 21.8 us: swap(): return lax.ppermute(value, axis, [(i, i ^ mask) for i in range(size)])]
    dynamic_slice x32 -> x3, local copies, waits for them, and re-layouts: 25.7 us -> 2.46 us  [the longest x1 2.36 us: per_device(): lax.dynamic_slice_in_dim(w_qkv, (plane ^ k) * WIDTH, WIDTH, 1)]
    while x176 -> x0, local copies, waits for them, and re-layouts: 19.2 us -> none
  transfers between devices with their start and end apart: 3 -> 26, of which waited for: 3 -> 9; matrix products, arithmetic and copies ran while one was open for 1% -> 11% of each run, Pallas kernels for 0% -> 9%
where the time goes in v1:
time: 206 us; the launch traced here: 208 us
  waiting for transfers between devices  66.3 us (32%)
  Pallas kernels  52.8 us (26%)
  blocking collectives  31.9 us (15%)
  starting transfers between devices  27.4 us (13%)
  other arithmetic  19.8 us (10%)
  local copies, waits for them, and re-layouts  7.4 us (4%)
  between operations  2.07 us (1%)
    ppermute x22, waiting for transfers between devices, swap(): return lax.ppermute(value, axis, [(i, i ^ mask) for i in range(size)])  44 us
    pallas_call x1, Pallas kernels, attend(): pl.pallas_call(functools.partial(attend_kernel, len(kv_parts), tok), grid...  34.6 us
    unnamed x1, blocking collectives  31.9 us
    ppermute x22, starting transfers between devices, swap(): return lax.ppermute(value, axis, [(i, i ^ mask) for i in range(size)])  21.8 us
    pallas_call x4, Pallas kernels, project(): pl.pallas_call(functools.partial(project_kernel, len(x_parts), len(w_part...  16.9 us
    ppermute x1, waiting for transfers between devices, per_device(): out_own = lax.ppermute(mid_own, 'seq', outward)  12.4 us
    ppermute x1, waiting for transfers between devices, per_device(): out_first = lax.ppermute(mid_first, 'seq', outward)  9.92 us
  transfers between devices with their start and end apart: 26, of which 9 were waited for; matrix products, arithmetic and copies ran while one was open for 11% of the time, Pallas kernels for 9%

profile of v1, /device:TPU:0, one launch (start us, length us, event | category | flops | bytes accessed | tf_op | source)
XLA Modules:
  0.0 207.7 jit_solution(15903264860389000410)
XLA Ops:
  0.0 1.1 constant_dynamic-update-slice_fusion.1
  1.1 0.8 constant_dynamic-update-slice_fusion.refs_0_
  1.8 3.0 %collective-permute-start = (bf16[136,2048]{1,0:T(8,128)(2,1)S(1)}, bf16[136,2048]{1,0:T(8,128)(2,1)S(1)}, u32[]{:S(2)}, u32[]{:S(2)}) collective-permute-start(bf16[136,2048]{1,0:T(8,128)(2,1)S(1)} %constant_dynamic-update-slice_fusion.refs_0_), channel_id=1, source_target_pairs={{0,1},{1,0},{2,3},{3,2},{4,5},{5,4},{6,7},{7,6},{8,9},{9,8},{10,11... | collective-permute-start | bytes 1671176 | tf_op jit(solution)/shard_map/ppermute | solution.py:23
  4.8 2.4 %constant_dynamic-slice_fusion.1 = (bf16[256,768]{1,0:T(8,128)(2,1)S(1)}, bf16[256,768]{1,0:T(8,128)(2,1)}, bf16[1,256,768]{2,1,0:T(8,128)(2,1)S(1)}, bf16[256,768]{1,0:T(8,128)(2,1)}) fusion(bf16[256,3072]{1,0:T(8,128)(2,1)} %param.9, s32[]{:T(128)S(6)} %select_n.84, s32[]{:T(128)S(6)} %select_n.83, s32[]{:T(128)S(6)} %select_n.82, s32[]{:T(128)S(6)} %select_n.85), kind=kLoop, calls=%fused_computation.76 | loop fusion | bytes 3145744 | tf_op jit(solution)/shard_map/dynamic_slice | solution.py:255
  7.2 1.6 collective-permute-start.1
  8.8 2.5 %collective-permute-start.5 = (bf16[256,768]{1,0:T(8,128)(2,1)}, bf16[256,768]{1,0:T(8,128)(2,1)S(1)}, u32[]{:S(2)}, u32[]{:S(2)}) collective-permute-start(bf16[256,768]{1,0:T(8,128)(2,1)} %get-tuple-element.28), channel_id=1, source_target_pairs={{0,24},{2,26},{4,28},{6,30},{8,16},{10,18},{12,20},{14,22},{16,8},... | collective-permute-start | bytes 1179656 | tf_op jit(solution)/shard_map/ppermute | solution.py:23
  11.2 0.1 collective-permute-start.4
  12.0 0.7 dynamic-slice
  13.4 0.2 dynamic-update-slice
  13.6 31.9 %all-reduce = s32[128]{0:T(128)S(1)} all-reduce(s32[128]{0:T(128)S(1)} %dynamic-update-slice), channel_id=1, replica_groups=mesh['seq'=16,'tp'=2] {'seq'}, use_global_device_ids=true, to_apply=%add | all-reduce | flops 128 | bytes 1024
  45.7 1.7 fusion
  47.8 0.9 dynamic-slice_bitcast_fusion.12
  48.6 0.6 pad_maximum_fusion.22
  49.2 0.6 pad_maximum_fusion.21
  49.9 0.6 pad_maximum_fusion.20
  50.5 0.5 iota_add_fusion.4
  51.1 1.0 pad_maximum_fusion.18.refs_9_
  52.2 1.0 pad_maximum_fusion.2
  53.2 1.5 collective-permute-start.2
  54.7 1.1 pad_maximum_fusion.3
  55.8 0.5 collective-permute-start.6
  56.3 0.7 pad_maximum_fusion.16.refs_9_
  57.0 0.7 pad_maximum_fusion.14.refs_9_
  57.8 0.7 compare_convert_fusion.refs_11_
  58.4 1.2 norm.1
  59.7 0.8 copy-done
  60.5 1.6 collective-permute-start.12
  62.1 11.8 %collective-permute-done.2 = bf16[2,256,768]{2,1,0:T(8,128)(2,1)} collective-permute-done((bf16[2,256,768]{2,1,0:T(8,128)(2,1)}, bf16[2,256,768]{2,1,0:T(8,128)(2,1)}, u32[]{:S(2)}, u32[]{:S(2)}) %collective-permute-start.2) | collective-permute-done | bytes 786464 | tf_op jit(solution)/shard_map/ppermute | solution.py:23
  74.0 1.3 pad_maximum_fusion.refs_4_
  75.4 13.1 %collective-permute-done.6 = bf16[2,256,768]{2,1,0:T(8,128)(2,1)} collective-permute-done((bf16[2,256,768]{2,1,0:T(8,128)(2,1)}, bf16[2,256,768]{2,1,0:T(8,128)(2,1)}, u32[]{:S(2)}, u32[]{:S(2)}) %collective-permute-start.6) | collective-permute-done | bytes 786464 | tf_op jit(solution)/shard_map/ppermute | solution.py:23
  88.5 1.3 pad_maximum_fusion.1.refs_6_
  89.9 1.6 pad_maximum_fusion.12.refs_9_
  91.5 1.5 collective-permute-start.11
  93.0 0.7 compare_convert_fusion.1.refs_11_
  93.7 1.3 collective-permute-start.13
  95.0 0.7 pad_add_fusion.1.refs_0_
  95.7 0.7 compare_convert_fusion.2.refs_11_
  96.4 1.3 collective-permute-start.16
  97.7 0.7 compare_convert_fusion.3.refs_11_
  98.3 0.5 collective-permute-start.9
  98.9 12.4 %collective-permute-done.13 = bf16[8,136,256]{2,1,0:T(8,128)(2,1)S(1)} collective-permute-done((bf16[8,136,256]{2,1,0:T(8,128)(2,1)}, bf16[8,136,256]{2,1,0:T(8,128)(2,1)S(1)}, u32[]{:S(2)}, u32[]{:S(2)}) %collective-permute-start.13) | collective-permute-done | bytes 557088 | tf_op jit(solution)/shard_map/ppermute | solution.py:289
  111.2 0.9 broadcast_select_fusion.1.refs_2_
  112.1 0.5 collective-permute-start.14
  112.7 0.1 stack.165.refs_2_
  112.8 0.1 stack.170.refs_1_
  112.9 9.9 %collective-permute-done.16 = bf16[8,136,256]{2,1,0:T(8,128)(2,1)} collective-permute-done((bf16[8,136,256]{2,1,0:T(8,128)(2,1)}, bf16[8,136,256]{2,1,0:T(8,128)(2,1)}, u32[]{:S(2)}, u32[]{:S(2)}) %collective-permute-start.16) | collective-permute-done | bytes 557088 | tf_op jit(solution)/shard_map/ppermute | solution.py:290
  122.8 1.1 broadcast_select_fusion.refs_2_
  124.0 3.0 %collective-permute-done.10.refs_10_ = bf16[64,256]{1,0:T(8,128)(2,1)S(1)} collective-permute-done((bf16[64,256]{1,0:T(8,128)(2,1)}, bf16[64,256]{1,0:T(8,128)(2,1)S(1)}, u32[]{:S(2)}, u32[]{:S(2)}) %collective-permute-start.10) | collective-permute-done | bytes 32800 | tf_op jit(solution)/shard_map/ppermute | solution.py:23
  127.0 2.3 %collective-permute-start.18 = (bf16[64,256]{1,0:T(8,128)(2,1)S(1)}, bf16[64,256]{1,0:T(8,128)(2,1)S(1)}, u32[]{:S(2)}, u32[]{:S(2)}) collective-permute-start(bf16[64,256]{1,0:T(8,128)(2,1)S(1)} %copy-done.17), channel_id=1, source_target_pairs={{0,24},{2,26},{4,28},{6,30},{8,16},{10,18},{12,20},{14,22},{16,8},... | collective-permute-start | bytes 98312 | tf_op jit(solution)/shard_map/ppermute | solution.py:23
  129.3 0.6 collective-permute-start.17
  129.9 4.4 %project.5 = (bf16[4,128,128]{2,1,0:T(8,128)(2,1)S(1)}, bf16[192,256]{1,0:T(8,128)(2,1)S(1)}) custom-call(s32[16]{0:T(128)S(1)} %pad_add_fusion.1.refs_0_, s32[16]{0:T(128)S(1)} %stack.170.refs_1_, bf16[8,136,256]{2,1,0:T(8,128)(2,1)} %collective-permute-done.8.refs_2_, bf16[8,136,256]{2,1,0:T(8,128)(2,1)} %collective-permute-done.9.refs_3_, ...), custom_call_target="tpu_custom_call" | custom-call | flops 855638016 | bytes 7405568 | tf_op jit(solution)/shard_map/project/pallas_call | solution.py:106
  134.4 4.2 %project.4 = (bf16[4,128,128]{2,1,0:T(8,128)(2,1)S(1)}, bf16[192,256]{1,0:T(8,128)(2,1)S(1)}) custom-call(s32[16]{0:T(128)S(1)} %pad_add_fusion.1.refs_0_, s32[16]{0:T(128)S(1)} %stack.170.refs_1_, bf16[8,136,256]{2,1,0:T(8,128)(2,1)} %get-tuple-element.15.refs_2_, bf16[8,136,256]{2,1,0:T(8,128)(2,1)S(1)} %copy-done.1, ...), custom_call_target="tpu_custom_call" | custom-call | flops 855638016 | bytes 7405568 | tf_op jit(solution)/shard_map/project/pallas_call | solution.py:106
  138.6 1.5 collective-permute-start.19
  140.2 4.4 %project.6 = (bf16[4,128,128]{2,1,0:T(8,128)(2,1)S(1)}, bf16[192,256]{1,0:T(8,128)(2,1)S(1)}) custom-call(s32[16]{0:T(128)S(1)} %pad_add_fusion.1.refs_0_, s32[16]{0:T(128)S(1)} %stack.170.refs_1_, bf16[8,136,256]{2,1,0:T(8,128)(2,1)} %broadcast_select_fusion.1.refs_2_, bf16[8,136,256]{2,1,0:T(8,128)(2,1)} %collective-permute-done.14.refs_3_, ...), custom_call_target="tpu_custom_call" | custom-call | flops 855638016 | bytes 7405568 | tf_op jit(solution)/shard_map/project/pallas_call | solution.py:106
  144.6 4.0 %project.7 = (bf16[4,128,128]{2,1,0:T(8,128)(2,1)S(1)}, bf16[192,256]{1,0:T(8,128)(2,1)S(1)}) custom-call(s32[16]{0:T(128)S(1)} %pad_add_fusion.1.refs_0_, s32[16]{0:T(128)S(1)} %stack.170.refs_1_, bf16[8,136,256]{2,1,0:T(8,128)(2,1)S(1)} %broadcast_select_fusion.refs_2_, bf16[8,136,256]{2,1,0:T(8,128)(2,1)S(1)} %collective-permute-done.17.refs_3_, ...), custom_call_target="tpu_custom_call" | custom-call | flops 855638016 | bytes 7405568 | tf_op jit(solution)/shard_map/project/pallas_call | solution.py:106
  148.6 0.6 collective-permute-start.21
  149.5 4.9 %collective-permute-done.21 = bf16[2,192,256]{2,1,0:T(8,128)(2,1)S(1)} collective-permute-done((bf16[2,192,256]{2,1,0:T(8,128)(2,1)S(1)}, bf16[2,192,256]{2,1,0:T(8,128)(2,1)S(1)}, u32[]{:S(2)}, u32[]{:S(2)}) %collective-permute-start.21) | collective-permute-done | bytes 196640 | tf_op jit(solution)/shard_map/ppermute | solution.py:23
  154.6 1.6 collective-permute-done.22
  156.3 34.6 %attend.1 = bf16[4,128,512]{2,1,0:T(8,128)(2,1)S(1)} custom-call(s32[1]{0:T(128)} %copy.28.refs_0_, s32[4]{0:T(128)S(1)} %pad_add_fusion.refs_1_, s32[16]{0:T(128)S(1)} %stack.165.refs_2_, bf16[4,4,128,128]{3,2,1,0:T(8,128)(2,1)S(1)} %pad_maximum_fusion.4.refs_3_, bf16[8,192,256]{2,1,0:T(8,128)(2,1)S(1)} %slice_dynamic-update-slice_fusion.6.refs_4_, ...), custom_call_target="tpu_custom_call" | custom-call | flops 3221225472 | bytes 1572864 | tf_op jit(solution)/shard_map/attend/pallas_call | solution.py:217
  190.9 1.5 collective-permute-start.25
  192.4 4.8 %collective-permute-start.24 = (bf16[128,512]{1,0:T(8,128)(2,1)S(1)}, bf16[128,512]{1,0:T(8,128)(2,1)S(1)}, u32[]{:S(2)}, u32[]{:S(2)}) collective-permute-start(bf16[128,512]{1,0:T(8,128)(2,1)S(1)} %get-tuple-element.35), channel_id=1, source_target_pairs={{0,16},{2,18},{4,20},{6,22},{8,24},{10,26},{12,28},{14,30},{16,0},... | collective-permute-start | bytes 393224 | tf_op jit(solution)/shard_map/ppermute | solution.py:23
  197.2 1.2 collective-permute-done.25
  198.4 8.4 %collective-permute-done.24 = bf16[128,512]{1,0:T(8,128)(2,1)S(1)} collective-permute-done((bf16[128,512]{1,0:T(8,128)(2,1)S(1)}, bf16[128,512]{1,0:T(8,128)(2,1)S(1)}, u32[]{:S(2)}, u32[]{:S(2)}) %collective-permute-start.24) | collective-permute-done | bytes 131104 | tf_op jit(solution)/shard_map/ppermute | solution.py:23
  206.9 0.8 pad_maximum_fusion.6
  (116 shorter events, 1.5 us)
Async XLA Ops:
  1.8 56.6 %collective-permute-start = (bf16[136,2048]{1,0:T(8,128)(2,1)S(1)}, bf16[136,2048]{1,0:T(8,128)(2,1)S(1)}, u32[]{:S(2)}, u32[]{:S(2)}) collective-permute-start(bf16[136,2048]{1,0:T(8,128)(2,1)S(1)} %constant_dynamic-update-slice_fusion.refs_0_), channel_id=1, source_target_pairs={{0,1},{1,0},{2,3},{3,2},{4,5},{5,4},{6,7},{7,6},{8,9},{9,8},{10,11... | collective-permute-start | bytes 1671176 | tf_op jit(solution)/shard_map/ppermute | solution.py:23
  4.8 7.2 %copy-start.23 = (u32[32]{0:T(128)S(1)}, u32[32]{0:T(128)}, u32[]{:S(2)}) copy-start(u32[32]{0:T(128)} %constant.75) | copy-start | bytes 388
  4.8 8.6 %copy-start.22 = (s32[8]{0:T(128)S(1)}, s32[8]{0:T(128)}, u32[]{:S(2)}) copy-start(s32[8]{0:T(128)} %param.12) | copy-start | bytes 100
  7.2 43.3 %copy-start.19 = (f32[4096]{0:T(1024)S(1)}, f32[4096]{0:T(1024)}, u32[]{:S(2)}) copy-start(f32[4096]{0:T(1024)} %param.8) | copy-start | bytes 49156
  7.2 45.0 %collective-permute-start.1 = (bf16[256,768]{1,0:T(8,128)(2,1)}, bf16[256,768]{1,0:T(8,128)(2,1)S(1)}, u32[]{:S(2)}, u32[]{:S(2)}) collective-permute-start(bf16[256,768]{1,0:T(8,128)(2,1)} %get-tuple-element.26), channel_id=1, source_target_pairs={{0,8},{2,10},{4,12},{6,14},{8,0},{10,2},{12,4},{14,6},{16,24},{18,... | collective-permute-start | bytes 1179656 | tf_op jit(solution)/shard_map/ppermute | solution.py:23
  8.8 45.9 %collective-permute-start.5 = (bf16[256,768]{1,0:T(8,128)(2,1)}, bf16[256,768]{1,0:T(8,128)(2,1)S(1)}, u32[]{:S(2)}, u32[]{:S(2)}) collective-permute-start(bf16[256,768]{1,0:T(8,128)(2,1)} %get-tuple-element.28), channel_id=1, source_target_pairs={{0,24},{2,26},{4,28},{6,30},{8,16},{10,18},{12,20},{14,22},{16,8},... | collective-permute-start | bytes 1179656 | tf_op jit(solution)/shard_map/ppermute | solution.py:23
  11.2 43.5 %collective-permute-start.4 = (bf16[256,768]{1,0:T(8,128)(2,1)S(1)}, bf16[256,768]{1,0:T(8,128)(2,1)S(1)}, u32[]{:S(2)}, u32[]{:S(2)}) collective-permute-start(bf16[256,768]{1,0:T(8,128)(2,1)S(1)} %get-tuple-element.25), channel_id=1, source_target_pairs={{0,16},{2,18},{4,20},{6,22},{8,24},{10,26},{12,28},{14,30},{16,0},... | collective-permute-start | bytes 1179656 | tf_op jit(solution)/shard_map/ppermute | solution.py:23
  45.7 2.1 copy-start.20
  52.1 4.2 %copy-start.15 = (f32[136,64]{1,0:T(8,128)S(1)}, f32[136,64]{1,0:T(8,128)}, u32[]{:S(2)}) copy-start(f32[136,64]{1,0:T(8,128)} %get-tuple-element.62) | copy-start | bytes 104452
  52.2 4.2 %copy-start.16 = (f32[136,64]{1,0:T(8,128)S(1)}, f32[136,64]{1,0:T(8,128)}, u32[]{:S(2)}) copy-start(f32[136,64]{1,0:T(8,128)} %get-tuple-element.64) | copy-start | bytes 104452
  52.2 4.9 %copy-start.13 = (f32[136,64]{1,0:T(8,128)S(1)}, f32[136,64]{1,0:T(8,128)}, u32[]{:S(2)}) copy-start(f32[136,64]{1,0:T(8,128)} %get-tuple-element.65) | copy-start | bytes 104452
  52.2 4.9 %copy-start.14 = (f32[136,64]{1,0:T(8,128)S(1)}, f32[136,64]{1,0:T(8,128)}, u32[]{:S(2)}) copy-start(f32[136,64]{1,0:T(8,128)} %get-tuple-element.67) | copy-start | bytes 104452
  52.2 5.6 %copy-start.21 = (s32[8]{0:T(128)S(1)}, s32[8]{0:T(128)}, u32[]{:S(2)}) copy-start(s32[8]{0:T(128)} %copy-done.20) | copy-start | bytes 100
  53.2 20.8 %collective-permute-start.2 = (bf16[2,256,768]{2,1,0:T(8,128)(2,1)}, bf16[2,256,768]{2,1,0:T(8,128)(2,1)}, u32[]{:S(2)}, u32[]{:S(2)}) collective-permute-start(bf16[2,256,768]{2,1,0:T(8,128)(2,1)} %pad_maximum_fusion.2), channel_id=1, source_target_pairs={{0,4},{2,6},{4,0},{6,2},{8,12},{10,14},{12,8},{14,10},{16,20},{18,... | collective-permute-start | bytes 2359304 | tf_op jit(solution)/shard_map/ppermute | solution.py:23
  54.7 5.0 %copy-start.9 = (bf16[256,768]{1,0:T(8,128)(2,1)}, bf16[256,768]{1,0:T(8,128)(2,1)S(1)}, u32[]{:S(2)}) copy-start(bf16[256,768]{1,0:T(8,128)(2,1)S(1)} %collective-permute-done.5) | copy-start | bytes 1179652
  54.7 5.0 %copy-start.11 = (bf16[256,768]{1,0:T(8,128)(2,1)}, bf16[256,768]{1,0:T(8,128)(2,1)S(1)}, u32[]{:S(2)}) copy-start(bf16[256,768]{1,0:T(8,128)(2,1)S(1)} %collective-permute-done.4) | copy-start | bytes 1179652
  55.8 32.7 %collective-permute-start.6 = (bf16[2,256,768]{2,1,0:T(8,128)(2,1)}, bf16[2,256,768]{2,1,0:T(8,128)(2,1)}, u32[]{:S(2)}, u32[]{:S(2)}) collective-permute-start(bf16[2,256,768]{2,1,0:T(8,128)(2,1)} %pad_maximum_fusion.3), channel_id=1, source_target_pairs={{0,4},{2,6},{4,0},{6,2},{8,12},{10,14},{12,8},{14,10},{16,20},{18,... | collective-permute-start | bytes 2359304 | tf_op jit(solution)/shard_map/ppermute | solution.py:23
  59.7 0.8 copy-start
  60.5 31.0 %collective-permute-start.8 = (bf16[8,136,256]{2,1,0:T(8,128)(2,1)}, bf16[8,136,256]{2,1,0:T(8,128)(2,1)}, u32[]{:S(2)}, u32[]{:S(2)}) collective-permute-start(bf16[8,136,256]{2,1,0:T(8,128)(2,1)} %get-tuple-element.15.refs_2_), channel_id=1, source_target_pairs={{0,8},{2,10},{4,12},{6,14},{8,0},{10,2},{12,4},{14,6},{16,24},{18,... | collective-permute-start | bytes 1671176 | tf_op jit(solution)/shard_map/ppermute | solution.py:23
  60.5 27.9 %copy-start.10 = (bf16[256,768]{1,0:T(8,128)(2,1)S(1)}, bf16[256,768]{1,0:T(8,128)(2,1)}, u32[]{:S(2)}) copy-start(bf16[256,768]{1,0:T(8,128)(2,1)} %copy-done.9) | copy-start | bytes 1179652
  60.5 27.9 %copy-start.12 = (bf16[256,768]{1,0:T(8,128)(2,1)S(1)}, bf16[256,768]{1,0:T(8,128)(2,1)}, u32[]{:S(2)}) copy-start(bf16[256,768]{1,0:T(8,128)(2,1)} %copy-done.11) | copy-start | bytes 1179652
  60.5 33.2 %collective-permute-start.12 = (bf16[8,136,256]{2,1,0:T(8,128)(2,1)}, bf16[8,136,256]{2,1,0:T(8,128)(2,1)}, u32[]{:S(2)}, u32[]{:S(2)}) collective-permute-start(bf16[8,136,256]{2,1,0:T(8,128)(2,1)} %get-tuple-element.15.refs_2_), channel_id=1, source_target_pairs={{8,16},{10,18},{12,20},{14,22},{16,8},{18,10},{20,12},{22,14},{9,1... | collective-permute-start | bytes 1671176 | tf_op jit(solution)/shard_map/ppermute | solution.py:287
  75.3 54.1 %collective-permute-start.3 = (bf16[4,256,768]{2,1,0:T(8,128)(2,1)S(1)}, bf16[4,256,768]{2,1,0:T(8,128)(2,1)}, u32[]{:S(2)}, u32[]{:S(2)}) collective-permute-start(bf16[4,256,768]{2,1,0:T(8,128)(2,1)S(1)} %pad_maximum_fusion.refs_4_), channel_id=1, source_target_pairs={{0,2},{2,0},{4,6},{6,4},{8,10},{10,8},{12,14},{14,12},{16,18},{18,... | collective-permute-start | bytes 4718600 | tf_op jit(solution)/shard_map/ppermute | solution.py:23
  89.8 40.2 %collective-permute-start.7 = (bf16[4,256,768]{2,1,0:T(8,128)(2,1)S(1)}, bf16[4,256,768]{2,1,0:T(8,128)(2,1)}, u32[]{:S(2)}, u32[]{:S(2)}) collective-permute-start(bf16[4,256,768]{2,1,0:T(8,128)(2,1)S(1)} %pad_maximum_fusion.1.refs_6_), channel_id=1, source_target_pairs={{0,2},{2,0},{4,6},{6,4},{8,10},{10,8},{12,14},{14,12},{16,18},{18,... | collective-permute-start | bytes 4718600 | tf_op jit(solution)/shard_map/ppermute | solution.py:23
  91.5 4.9 %collective-permute-start.11 = (bf16[8,136,256]{2,1,0:T(8,128)(2,1)}, bf16[8,136,256]{2,1,0:T(8,128)(2,1)}, u32[]{:S(2)}, u32[]{:S(2)}) collective-permute-start(bf16[8,136,256]{2,1,0:T(8,128)(2,1)} %collective-permute-done.8.refs_2_), channel_id=1, source_target_pairs={{8,16},{10,18},{12,20},{14,22},{16,8},{18,10},{20,12},{22,14},{9,1... | collective-permute-start | bytes 1671176 | tf_op jit(solution)/shard_map/ppermute | solution.py:288
  93.7 17.5 %collective-permute-start.13 = (bf16[8,136,256]{2,1,0:T(8,128)(2,1)}, bf16[8,136,256]{2,1,0:T(8,128)(2,1)S(1)}, u32[]{:S(2)}, u32[]{:S(2)}) collective-permute-start(bf16[8,136,256]{2,1,0:T(8,128)(2,1)} %collective-permute-done.12), channel_id=1, source_target_pairs={{8,0},{10,2},{12,4},{14,6},{16,24},{18,26},{20,28},{22,30},{9,1},{... | collective-permute-start | bytes 1671176 | tf_op jit(solution)/shard_map/ppermute | solution.py:289
  96.4 26.5 %collective-permute-start.16 = (bf16[8,136,256]{2,1,0:T(8,128)(2,1)}, bf16[8,136,256]{2,1,0:T(8,128)(2,1)}, u32[]{:S(2)}, u32[]{:S(2)}) collective-permute-start(bf16[8,136,256]{2,1,0:T(8,128)(2,1)} %collective-permute-done.11), channel_id=1, source_target_pairs={{8,0},{10,2},{12,4},{14,6},{16,24},{18,26},{20,28},{22,30},{9,1},{... | collective-permute-start | bytes 1671176 | tf_op jit(solution)/shard_map/ppermute | solution.py:290
  98.3 31.0 %collective-permute-start.9 = (bf16[8,136,256]{2,1,0:T(8,128)(2,1)}, bf16[8,136,256]{2,1,0:T(8,128)(2,1)}, u32[]{:S(2)}, u32[]{:S(2)}) collective-permute-start(bf16[8,136,256]{2,1,0:T(8,128)(2,1)} %collective-permute-done.8.refs_2_), channel_id=1, source_target_pairs={{0,1},{1,0},{2,3},{3,2},{4,5},{5,4},{6,7},{7,6},{8,9},{9,8},{10,11... | collective-permute-start | bytes 1671176 | tf_op jit(solution)/shard_map/ppermute | solution.py:23
  112.1 28.0 %collective-permute-start.14 = (bf16[8,136,256]{2,1,0:T(8,128)(2,1)}, bf16[8,136,256]{2,1,0:T(8,128)(2,1)}, u32[]{:S(2)}, u32[]{:S(2)}) collective-permute-start(bf16[8,136,256]{2,1,0:T(8,128)(2,1)} %broadcast_select_fusion.1.refs_2_), channel_id=1, source_target_pairs={{0,1},{1,0},{2,3},{3,2},{4,5},{5,4},{6,7},{7,6},{8,9},{9,8},{10,11... | collective-permute-start | bytes 1671176 | tf_op jit(solution)/shard_map/ppermute | solution.py:23
  112.9 14.1 %copy-start.17 = (bf16[64,256]{1,0:T(8,128)(2,1)S(1)}, bf16[64,256]{1,0:T(8,128)(2,1)}, u32[]{:S(2)}) copy-start(bf16[64,256]{1,0:T(8,128)(2,1)} %pad_maximum_fusion.22) | copy-start | bytes 98308
  112.9 16.4 %copy-start.18 = (bf16[64,256]{1,0:T(8,128)(2,1)S(1)}, bf16[64,256]{1,0:T(8,128)(2,1)}, u32[]{:S(2)}) copy-start(bf16[64,256]{1,0:T(8,128)(2,1)} %pad_maximum_fusion.21) | copy-start | bytes 98308
  112.9 17.0 %copy-start.3 = (f32[136,128]{1,0:T(8,128)S(1)}, f32[136,128]{1,0:T(8,128)}, u32[]{:S(2)}) copy-start(f32[136,128]{1,0:T(8,128)} %pad_maximum_fusion.14.refs_9_) | copy-start | bytes 208900
  112.9 17.0 %copy-start.8 = (f32[64,8]{1,0:T(8,128)S(1)}, f32[64,8]{1,0:T(8,128)}, u32[]{:S(2)}) copy-start(f32[64,8]{1,0:T(8,128)} %compare_convert_fusion.2.refs_11_) | copy-start | bytes 6148
  122.8 4.1 %collective-permute-start.10 = (bf16[64,256]{1,0:T(8,128)(2,1)}, bf16[64,256]{1,0:T(8,128)(2,1)S(1)}, u32[]{:S(2)}, u32[]{:S(2)}) collective-permute-start(bf16[64,256]{1,0:T(8,128)(2,1)} %pad_maximum_fusion.20), channel_id=1, source_target_pairs={{0,8},{2,10},{4,12},{6,14},{8,0},{10,2},{12,4},{14,6},{16,24},{18,... | collective-permute-start | bytes 98312 | tf_op jit(solution)/shard_map/ppermute | solution.py:23
  124.0 10.3 %copy-start.1 = (bf16[8,136,256]{2,1,0:T(8,128)(2,1)S(1)}, bf16[8,136,256]{2,1,0:T(8,128)(2,1)}, u32[]{:S(2)}) copy-start(bf16[8,136,256]{2,1,0:T(8,128)(2,1)} %copy-done) | copy-start | bytes 1671172
  124.0 10.3 %copy-start.4 = (f32[136,128]{1,0:T(8,128)S(1)}, f32[136,128]{1,0:T(8,128)}, u32[]{:S(2)}) copy-start(f32[136,128]{1,0:T(8,128)} %pad_maximum_fusion.12.refs_9_) | copy-start | bytes 208900
  124.0 10.3 %copy-start.7 = (f32[64,8]{1,0:T(8,128)S(1)}, f32[64,8]{1,0:T(8,128)}, u32[]{:S(2)}) copy-start(f32[64,8]{1,0:T(8,128)} %compare_convert_fusion.3.refs_11_) | copy-start | bytes 6148
  127.0 17.6 %collective-permute-start.18 = (bf16[64,256]{1,0:T(8,128)(2,1)S(1)}, bf16[64,256]{1,0:T(8,128)(2,1)S(1)}, u32[]{:S(2)}, u32[]{:S(2)}) collective-permute-start(bf16[64,256]{1,0:T(8,128)(2,1)S(1)} %copy-done.17), channel_id=1, source_target_pairs={{0,24},{2,26},{4,28},{6,30},{8,16},{10,18},{12,20},{14,22},{16,8},... | collective-permute-start | bytes 98312 | tf_op jit(solution)/shard_map/ppermute | solution.py:23
  129.3 10.8 %collective-permute-start.15 = (bf16[64,256]{1,0:T(8,128)(2,1)S(1)}, bf16[64,256]{1,0:T(8,128)(2,1)S(1)}, u32[]{:S(2)}, u32[]{:S(2)}) collective-permute-start(bf16[64,256]{1,0:T(8,128)(2,1)S(1)} %copy-done.18), channel_id=1, source_target_pairs={{0,16},{2,18},{4,20},{6,22},{8,24},{10,26},{12,28},{14,30},{16,0},... | collective-permute-start | bytes 98312 | tf_op jit(solution)/shard_map/ppermute | solution.py:23
  129.3 15.2 %collective-permute-start.17 = (bf16[8,136,256]{2,1,0:T(8,128)(2,1)S(1)}, bf16[8,136,256]{2,1,0:T(8,128)(2,1)S(1)}, u32[]{:S(2)}, u32[]{:S(2)}) collective-permute-start(bf16[8,136,256]{2,1,0:T(8,128)(2,1)S(1)} %broadcast_select_fusion.refs_2_), channel_id=1, source_target_pairs={{0,1},{1,0},{2,3},{3,2},{4,5},{5,4},{6,7},{7,6},{8,9},{9,8},{10,11... | collective-permute-start | bytes 1671176 | tf_op jit(solution)/shard_map/ppermute | solution.py:23
  134.3 5.8 %copy-start.2 = (f32[136,128]{1,0:T(8,128)S(1)}, f32[136,128]{1,0:T(8,128)}, u32[]{:S(2)}) copy-start(f32[136,128]{1,0:T(8,128)} %pad_maximum_fusion.16.refs_9_) | copy-start | bytes 208900
  134.3 5.8 %copy-start.6 = (f32[64,8]{1,0:T(8,128)S(1)}, f32[64,8]{1,0:T(8,128)}, u32[]{:S(2)}) copy-start(f32[64,8]{1,0:T(8,128)} %compare_convert_fusion.1.refs_11_) | copy-start | bytes 6148
  138.6 6.0 %copy-start.5 = (f32[64,8]{1,0:T(8,128)S(1)}, f32[64,8]{1,0:T(8,128)}, u32[]{:S(2)}) copy-start(f32[64,8]{1,0:T(8,128)} %compare_convert_fusion.refs_11_) | copy-start | bytes 6148
  138.6 10.7 %collective-permute-start.19 = (bf16[2,192,256]{2,1,0:T(8,128)(2,1)S(1)}, bf16[2,192,256]{2,1,0:T(8,128)(2,1)S(1)}, u32[]{:S(2)}, u32[]{:S(2)}) collective-permute-start(bf16[2,192,256]{2,1,0:T(8,128)(2,1)S(1)} %pad_maximum_fusion.9), channel_id=1, source_target_pairs={{0,4},{2,6},{4,0},{6,2},{8,12},{10,14},{12,8},{14,10},{16,20},{18,... | collective-permute-start | bytes 589832 | tf_op jit(solution)/shard_map/ppermute | solution.py:23
  148.6 5.7 %collective-permute-start.21 = (bf16[2,192,256]{2,1,0:T(8,128)(2,1)S(1)}, bf16[2,192,256]{2,1,0:T(8,128)(2,1)S(1)}, u32[]{:S(2)}, u32[]{:S(2)}) collective-permute-start(bf16[2,192,256]{2,1,0:T(8,128)(2,1)S(1)} %pad_maximum_fusion.10), channel_id=1, source_target_pairs={{0,4},{2,6},{4,0},{6,2},{8,12},{10,14},{12,8},{14,10},{16,20},{18,... | collective-permute-start | bytes 589832 | tf_op jit(solution)/shard_map/ppermute | solution.py:23
  149.4 5.1 %collective-permute-start.20 = (bf16[4,192,256]{2,1,0:T(8,128)(2,1)S(1)}, bf16[4,192,256]{2,1,0:T(8,128)(2,1)S(1)}, u32[]{:S(2)}, u32[]{:S(2)}) collective-permute-start(bf16[4,192,256]{2,1,0:T(8,128)(2,1)S(1)} %pad_maximum_fusion.7), channel_id=1, source_target_pairs={{0,2},{2,0},{4,6},{6,4},{8,10},{10,8},{12,14},{14,12},{16,18},{18,... | collective-permute-start | bytes 1179656 | tf_op jit(solution)/shard_map/ppermute | solution.py:23
  154.4 1.8 collective-permute-start.22
  190.9 7.4 %collective-permute-start.25 = (bf16[128,512]{1,0:T(8,128)(2,1)S(1)}, bf16[128,512]{1,0:T(8,128)(2,1)S(1)}, u32[]{:S(2)}, u32[]{:S(2)}) collective-permute-start(bf16[128,512]{1,0:T(8,128)(2,1)S(1)} %get-tuple-element.34), channel_id=1, source_target_pairs={{0,24},{2,26},{4,28},{6,30},{8,16},{10,18},{12,20},{14,22},{16,8},... | collective-permute-start | bytes 393224 | tf_op jit(solution)/shard_map/ppermute | solution.py:23
  192.4 14.4 %collective-permute-start.24 = (bf16[128,512]{1,0:T(8,128)(2,1)S(1)}, bf16[128,512]{1,0:T(8,128)(2,1)S(1)}, u32[]{:S(2)}, u32[]{:S(2)}) collective-permute-start(bf16[128,512]{1,0:T(8,128)(2,1)S(1)} %get-tuple-element.35), channel_id=1, source_target_pairs={{0,16},{2,18},{4,20},{6,22},{8,24},{10,26},{12,28},{14,30},{16,0},... | collective-permute-start | bytes 393224 | tf_op jit(solution)/shard_map/ppermute | solution.py:23
  197.2 9.6 %collective-permute-start.23 = (bf16[128,512]{1,0:T(8,128)(2,1)S(1)}, bf16[128,512]{1,0:T(8,128)(2,1)S(1)}, u32[]{:S(2)}, u32[]{:S(2)}) collective-permute-start(bf16[128,512]{1,0:T(8,128)(2,1)S(1)} %get-tuple-element.36), channel_id=1, source_target_pairs={{0,8},{2,10},{4,12},{6,14},{8,0},{10,2},{12,4},{14,6},{16,24},{18,... | collective-permute-start | bytes 393224 | tf_op jit(solution)/shard_map/ppermute | solution.py:23

commit v2 on v1

v2 whole, which is shorter than its diff:
```python
import functools
import math

import jax
import jax.numpy as jnp
from jax import lax
from jax.experimental import pallas as pl
from jax.experimental.pallas import tpu as pltpu
from jax.sharding import PartitionSpec as P

HEADS = 32
KVH = 8
HD = 128
GROUP = HEADS // KVH
WIDTH = (GROUP + 2) * HD
FEATS = 256
FAR = -1e30
VMEM = pl.BlockSpec(memory_space=pltpu.VMEM)
SMEM = pl.BlockSpec(memory_space=pltpu.SMEM)


def swap(value, axis, size, mask):
    return lax.ppermute(value, axis, [(i, i ^ mask) for i in range(size)])


def norm_kernel(count, *refs):
    parts, gains, outs = refs[:count], refs[count : 2 * count], refs[2 * count :]
    values = [part[...].astype(jnp.float32) for part in parts]
    total = sum(jnp.sum(v * v, axis=-1, keepdims=True) for v in values)
    width = sum(v.shape[1] for v in values)
    factor = lax.rsqrt(total / width + 1e-05)
    for value, gain, out in zip(values, gains, outs):
        rows = (value * factor * gain[...]).astype(jnp.bfloat16)
        for block in range(out.shape[0]):
            out[block] = rows[:, block * FEATS : (block + 1) * FEATS]


def norm(parts, gains):
    rows = parts[0].shape[0]
    return pl.pallas_call(
        functools.partial(norm_kernel, len(parts)),
        out_shape=[
            jax.ShapeDtypeStruct((p.shape[1] // FEATS, rows, FEATS), jnp.bfloat16) for p in parts
        ],
        in_specs=[VMEM] * (2 * len(parts)),
        out_specs=[VMEM] * len(parts),
        compiler_params=pltpu.CompilerParams(vmem_limit_bytes=24 * 2**20),
        name="norm",
    )(*parts, *[g.reshape(1, -1) for g in gains])


def project_kernel(n_x, n_w, tok, redo, *refs):
    x_ids, w_ids = refs[0], refs[1]
    x_parts = refs[2 : 2 + n_x]
    w_parts = refs[2 + n_x : 2 + n_x + n_w]
    cosine, sine, cache, q_out, kv_out, held = refs[2 + n_x + n_w :]
    tile = pl.program_id(0)
    span = kv_out.shape[0]
    cache_rows = span - tok

    @pl.when(tile == 0)
    def _():
        at = 0
        for part in x_parts:
            for block in range(part.shape[0]):
                held[x_ids[at]] = part[block]
                at += 1

    total = None
    at = 0
    for part in w_parts:
        for block in range(part.shape[0]):
            term = jnp.dot(held[w_ids[at]], part[block], preferred_element_type=jnp.float32)
            total = term if total is None else total + term
            at += 1

    def rotated(value, first, last):
        turned = pltpu.roll(value, HD // 2, 1)
        return value * cosine[0, first:last] + turned * sine[0, first:last]

    @pl.when(tile > 0)
    def _():
        for head in range(2):
            value = total[:tok, head * HD : (head + 1) * HD]
            q_out[head] = rotated(value, 0, tok).astype(jnp.bfloat16)

    @pl.when(tile == 0)
    def _():
        keys = rotated(total[:tok, :HD], 0, tok)
        kv_out[:tok] = jnp.concatenate([keys, total[:tok, HD:]], 1).astype(jnp.bfloat16)
        offsets = cache[cache_rows : cache_rows + 1, :redo].astype(jnp.float32)
        row = lax.broadcasted_iota(jnp.int32, (cache_rows, redo), 0).astype(jnp.float32)
        chosen = (row == offsets).astype(jnp.float32)
        fresh = jnp.dot(
            chosen,
            total[tok : tok + redo],
            preferred_element_type=jnp.float32,
            precision=lax.Precision.HIGHEST,
        )
        fresh = jnp.concatenate([rotated(fresh[:, :HD], tok, span), fresh[:, HD:]], 1)
        hit = jnp.sum(chosen, axis=1, keepdims=True) > 0.5
        kept = cache[:cache_rows].astype(jnp.float32)
        kv_out[tok:] = jnp.where(hit, fresh, kept).astype(jnp.bfloat16)


def project(slot, x_parts, x_ids, w_parts, w_ids, cosine, sine, cache, tok, redo):
    rows = x_parts[0].shape[1]
    blocks = sum(p.shape[0] for p in x_parts)
    span = cosine.shape[1]
    full = lambda a: pl.BlockSpec(a.shape, lambda t, n=a.ndim: (0,) * n)
    tiles = WIDTH // FEATS
    w_spec = lambda a: pl.BlockSpec(
        (a.shape[0], FEATS, FEATS), lambda t: (0, 0, lax.rem(t + tiles - 1, tiles))
    )
    table = pl.BlockSpec((1, span, HD), lambda t: (slot, 0, 0))
    return pl.pallas_call(
        functools.partial(project_kernel, len(x_parts), len(w_parts), tok, redo),
        grid=(tiles,),
        out_shape=[
            jax.ShapeDtypeStruct((GROUP, tok, HD), jnp.bfloat16),
            jax.ShapeDtypeStruct((span, 2 * HD), jnp.bfloat16),
        ],
        in_specs=[SMEM, SMEM]
        + [full(a) for a in x_parts]
        + [w_spec(a) for a in w_parts]
        + [table, table, full(cache)],
        out_specs=[
            pl.BlockSpec((2, tok, HD), lambda t: (jnp.maximum(t - 1, 0), 0, 0)),
            pl.BlockSpec((span, 2 * HD), lambda t: (0, 0)),
        ],
        scratch_shapes=[pltpu.VMEM((blocks, rows, FEATS), jnp.bfloat16)],
        compiler_params=pltpu.CompilerParams(vmem_limit_bytes=40 * 2**20),
        cost_estimate=pl.CostEstimate(
            flops=2 * rows * blocks * FEATS * WIDTH,
            bytes_accessed=2 * blocks * FEATS * (WIDTH + rows),
            transcendentals=0,
        ),
        name="project",
    )(x_ids, w_ids, *x_parts, *w_parts, cosine, sine, cache)


def attend_kernel(slot, tok, places, *refs):
    begin_ref, q_ids, kv_ids, q_ref = refs[:4]
    kv_refs = refs[4:-5]
    out, scores, top, total, accum = refs[-5:]
    begin = begin_ref[0]
    q_id = q_ids[slot]
    heads = GROUP * tok
    scale = math.log2(math.e) / math.sqrt(HD)
    span = kv_refs[0].shape[1]
    cache_rows = span - tok
    top[...] = jnp.full(top.shape, FAR, jnp.float32)
    total[...] = jnp.zeros(total.shape, jnp.float32)
    accum[...] = jnp.zeros(accum.shape, jnp.float32)

    def score(column, keys, allowed):
        value = lax.dot_general(
            q_ref[...].reshape(heads, HD),
            keys,
            (((1,), (1,)), ((), ())),
            preferred_element_type=jnp.float32,
        )
        if allowed is not None:
            value = jnp.where(allowed(value.shape), value, FAR)
        scores[:, column : column + value.shape[1]] = value
        most = top[...]
        for lane in range(0, value.shape[1], HD):
            most = jnp.maximum(most, value[:, lane : lane + HD])
        top[...] = most

    def mix(column, values):
        weights = []
        some = total[...]
        most = top[...]
        for lane in range(0, values.shape[0], HD):
            part = scores[:, column + lane : column + lane + HD]
            weight = jnp.exp2(part * scale - most)
            some = some + weight
            weights.append(weight.astype(jnp.bfloat16))
        total[...] = some
        accum[...] += jnp.dot(
            jnp.concatenate(weights, 1), values, preferred_element_type=jnp.float32
        )

    pending = []
    for at in range(0, len(places), 4):
        group = places[at : at + 4]
        ids = [kv_ids[at + i] for i in range(len(group))]
        least = functools.reduce(jnp.minimum, ids)
        most = functools.reduce(jnp.maximum, ids)
        base = at * span

        def rows(first, last, half, group=group):
            return jnp.concatenate(
                [kv_refs[n][i, first:last, half * HD : (half + 1) * HD] for n, i in group], 0
            )

        def starts(shape, step, ids=ids):
            column = lax.broadcasted_iota(jnp.int32, shape, 1)
            which = column // step
            first = jnp.zeros(shape, jnp.int32)
            for i, one in enumerate(ids):
                first = jnp.where(which == i, one * step, first)
            return first + column % step

        def causal(shape, starts=starts):
            row = lax.broadcasted_iota(jnp.int32, shape, 0)
            return starts(shape, tok) <= q_id * tok + row % tok

        def prefix(shape, starts=starts):
            return starts(shape, cache_rows) < begin

        shift = len(group) * tok

        @pl.when((most + 1) * cache_rows <= begin)
        def _(rows=rows, base=base):
            score(base + shift, rows(tok, span, 0), None)

        @pl.when(((most + 1) * cache_rows > begin) & (least * cache_rows < begin))
        def _(rows=rows, prefix=prefix, base=base):
            score(base + shift, rows(tok, span, 0), prefix)

        @pl.when(most < q_id)
        def _(rows=rows, base=base):
            score(base, rows(0, tok, 0), None)

        @pl.when((most >= q_id) & (least <= q_id))
        def _(rows=rows, causal=causal, base=base):
            score(base, rows(0, tok, 0), causal)

        pending.append((least * cache_rows < begin, least <= q_id, rows, base, shift))

    peak = jnp.max(top[...], axis=1, keepdims=True) * scale
    top[...] = jnp.broadcast_to(peak, top.shape)
    for cached, streamed, rows, base, shift in pending:

        @pl.when(cached)
        def _(rows=rows, base=base, shift=shift):
            mix(base + shift, rows(tok, span, 1))

        @pl.when(streamed)
        def _(rows=rows, base=base):
            mix(base, rows(0, tok, 1))

    mixed = (accum[...] / jnp.sum(total[...], axis=1, keepdims=True)).astype(jnp.bfloat16)
    for head in range(GROUP):
        out[:, head * HD : (head + 1) * HD] = mixed[head * tok : (head + 1) * tok]


def attend(slot, begin, query, q_ids, kv_parts, places, kv_ids, tok):
    span = kv_parts[0].shape[1]
    n_rows = len(places) * span
    heads = GROUP * tok
    return pl.pallas_call(
        functools.partial(attend_kernel, slot, tok, places),
        out_shape=jax.ShapeDtypeStruct((tok, GROUP * HD), jnp.bfloat16),
        in_specs=[SMEM, SMEM, SMEM] + [VMEM] * (1 + len(kv_parts)),
        out_specs=VMEM,
        scratch_shapes=[
            pltpu.VMEM((heads, n_rows), jnp.float32),
            pltpu.VMEM((heads, HD), jnp.float32),
            pltpu.VMEM((heads, HD), jnp.float32),
            pltpu.VMEM((heads, HD), jnp.float32),
        ],
        compiler_params=pltpu.CompilerParams(vmem_limit_bytes=50 * 2**20),
        cost_estimate=pl.CostEstimate(
            flops=4 * heads * n_rows * HD,
            bytes_accessed=4 * n_rows * HD,
            transcendentals=heads * n_rows,
        ),
        name="attend",
    )(begin, q_ids, kv_ids, query, *kv_parts)


def per_device(
    seq, tp, stream_x, norm_gain, w_qkv, cache_kv, recomp_hidden, recomp_index, prefix_len
):
    tok, redo = stream_x.shape[0], recomp_hidden.shape[0]
    cache_rows = cache_kv.shape[1]
    heads = w_qkv.shape[1] // WIDTH
    near = seq // heads
    at, side = lax.axis_index("seq"), lax.axis_index("tp")
    plane, inner = at // near, at % near
    begin = prefix_len[0]
    squared = near == 4 and heads == 4 and tp == 2

    def across(value, k):
        return swap(value, "seq", seq, k * near) if k else value

    w_mine = [
        across(lax.dynamic_slice_in_dim(w_qkv, (plane ^ k) * WIDTH, WIDTH, 1), k)
        for k in range(heads)
    ]
    offsets = (recomp_index - at * cache_rows).astype(jnp.bfloat16)
    offsets = jnp.pad(offsets[None, :], ((0, 15), (0, 2 * HD - redo)))
    caches = []
    for k in range(heads):
        part = lax.dynamic_slice_in_dim(cache_kv, (plane ^ k) * HD, HD, 2)
        part = jnp.concatenate([part[0], part[1]], 1)
        caches.append(across(jnp.concatenate([part, offsets], 0), k))

    raw = jnp.concatenate([stream_x, recomp_hidden], 0)
    rows = tok + redo
    part_blocks = raw.shape[1] // FEATS
    block_ids = jnp.arange(part_blocks, dtype=jnp.int32)
    if tp == 2:
        other = swap(raw, "tp", tp, 1)
        wide = raw.shape[1]
        gains = [
            lax.dynamic_slice_in_dim(norm_gain, side * wide, wide),
            lax.dynamic_slice_in_dim(norm_gain, (1 - side) * wide, wide),
        ]
        own, opposite = norm([raw, other], gains)
        x_ids = jnp.concatenate([side * part_blocks + block_ids, (1 - side) * part_blocks + block_ids])
    else:
        whole = lax.all_gather(raw, "tp", axis=1, tiled=True)
        (own,) = norm([whole], [norm_gain])
        opposite = None
        x_ids = jnp.arange(own.shape[0], dtype=jnp.int32)
    if heads == 4:
        beyond = across(own, 2)
        chunks = [own, across(own, 1), beyond, across(beyond, 1)]
    else:
        chunks = [across(own, k) for k in range(heads)]
    if opposite is None:
        x_slots = [[chunk] for chunk in chunks]
    else:
        x_slots = [[own, opposite]] + [[chunk, swap(chunk, "tp", tp, 1)] for chunk in chunks[1:]]

    if squared:
        w_parts, w_ids = [], []
        line = [swap(w, "seq", seq, 2) for w in w_mine]
        for pair in (0, 2):
            both = jnp.stack(w_mine[pair : pair + 2] + line[pair : pair + 2])
            far = swap(both, "seq", seq, 1)
            w_parts += [both, far]
            for flip in (0, 1):
                for turn in (0, 2):
                    w_ids += [(plane ^ k) * near + (inner ^ turn ^ flip) for k in (pair, pair + 1)]
        w_ids = jnp.stack(w_ids).astype(jnp.int32)
    else:
        groups = [[i * near + j for j in range(near)] for i in range(heads)]
        gathered = [
            lax.all_gather(w, "seq", axis=0, tiled=True, axis_index_groups=groups) for w in w_mine
        ]
        per = gathered[0].shape[0] // FEATS
        w_parts = [g.reshape(per, FEATS, WIDTH) for g in gathered]
        w_ids = jnp.concatenate(
            [(plane ^ k) * per + jnp.arange(per, dtype=jnp.int32) for k in range(heads)]
        )

    half = HD // 2
    freq = jnp.exp(-math.log(1000000.0) * jnp.arange(half, dtype=jnp.float32) * 2.0 / (2 * half))
    q_ids = jnp.stack([(plane ^ k) * near + inner for k in range(heads)]).astype(jnp.int32)
    token_ids = q_ids[:, None] * tok + jnp.arange(tok, dtype=jnp.int32) + begin
    row_ids = q_ids[:, None] * cache_rows + jnp.arange(cache_rows, dtype=jnp.int32)
    angle = jnp.concatenate([token_ids, row_ids], 1).astype(jnp.float32)[..., None] * freq
    cosine, sine = jnp.cos(angle), jnp.sin(angle)
    cosine = jnp.concatenate([cosine, cosine], -1)
    sine = jnp.concatenate([-sine, sine], -1)
    queries, kv_new = [], []
    for k in range(heads):
        q_one, kv_one = project(
            k, x_slots[k], x_ids, w_parts, w_ids, cosine, sine, caches[k], tok, redo
        )
        queries.append(q_one)
        kv_new.append(kv_one)

    if squared:
        kv_parts, places = [], []
        for slots in ((0, 1, 2), (3,)):
            mine = jnp.stack([kv_new[k] for k in slots])
            line = swap(mine, "seq", seq, 2)
            first = len(kv_parts)
            kv_parts += [mine, line, swap(mine, "seq", seq, 1), swap(line, "seq", seq, 1)]
            places += [(first + n, i) for i in range(len(slots)) for n in range(4)]
        turns = (0, 2, 1, 3)
        kv_ids = jnp.stack([(plane ^ k) * near + (inner ^ turn) for k in range(4) for turn in turns])
        kv_ids = kv_ids.astype(jnp.int32)
    else:
        kv_parts = [
            lax.all_gather(kv, "seq", axis=0, tiled=False, axis_index_groups=groups)
            for kv in kv_new
        ]
        places = [(k, i) for k in range(heads) for i in range(near)]
        kv_ids = jnp.concatenate(
            [(plane ^ k) * near + jnp.arange(near, dtype=jnp.int32) for k in range(heads)]
        )

    back = [None] * heads
    for k in reversed(range(heads)):
        mixed = attend(k, prefix_len, queries[k], q_ids, kv_parts, places, kv_ids, tok)
        back[k] = across(mixed, k)
    back = jnp.stack(back)
    columns = [lax.dynamic_index_in_dim(back, plane ^ h, 0, keepdims=False) for h in range(heads)]
    return jnp.concatenate(columns, 1)


def solution(mesh):
    placed = (
        P("seq", "tp"),
        P(),
        P("seq", "tp"),
        P(None, "seq", "tp"),
        P("seq", "tp"),
        P("seq"),
        P(),
    )
    return jax.shard_map(
        functools.partial(per_device, mesh.shape["seq"], mesh.shape["tp"]),
        mesh=mesh,
        in_specs=placed,
        out_specs=P("seq", "tp"),
        check_vma=False,
    )
```

time: 206 us -> 176 us (0.85); the launches traced: 208 us -> 176 us
  blocking collectives: 31.9 us -> 0 us
  waiting for transfers between devices: 66.3 us -> 87.5 us
  Pallas kernels: 52.8 us -> 37 us
  other arithmetic: 19.8 us -> 6.65 us
  starting transfers between devices: 27.4 us -> 35.6 us
    ppermute x22 -> x28, waiting for transfers between devices: 44 us -> 87.5 us  [swap(): return lax.ppermute(value, axis, [(i, i ^ mask) for i in range(size)])]
    unnamed x1 -> x0, blocking collectives: 31.9 us -> none
    ppermute x4 -> x0, waiting for transfers between devices: 22.3 us -> none  [the longest x1 12.4 us: per_device(): out_own = lax.ppermute(mid_own, 'seq', outward)]
    pallas_call x1 -> x4, Pallas kernels: 34.6 us -> 18.4 us  [attend(): pl.pallas_call(functools.partial(attend_kernel, slot, tok, places), out_s...]
    ppermute x22 -> x28, starting transfers between devices: 21.8 us -> 35.6 us  [swap(): return lax.ppermute(value, axis, [(i, i ^ mask) for i in range(size)])]
    concatenate x16 -> x2, other arithmetic: 8.92 us -> 0.94 us  [the longest x1 0.67 us: per_device(): caches.append(across(jnp.concatenate([part, offsets], 0), k))]
    ppermute x4 -> x0, starting transfers between devices: 5.67 us -> none  [the longest x1 1.6 us: per_device(): mid_own = lax.ppermute(own, 'seq', middle)]
    convert_element_type x6 -> x1, other arithmetic: 2.76 us -> 0.01 us  [per_device(): jnp.concatenate([token_ids, row_ids], 1).astype(jnp.float32)[..., None]]
  transfers between devices with their start and end apart: 26 -> 28, of which waited for: 9 -> 12; matrix products, arithmetic and copies ran while one was open for 11% -> 4% of each run, Pallas kernels for 9% -> 19%
where the time goes in v2:
time: 176 us
  waiting for transfers between devices  87.5 us (50%)
  Pallas kernels  37 us (21%)
  starting transfers between devices  35.6 us (20%)
  local copies, waits for them, and re-layouts  7.87 us (4%)
  other arithmetic  6.65 us (4%)
    ppermute x28, waiting for transfers between devices, swap(): return lax.ppermute(value, axis, [(i, i ^ mask) for i in range(size)])  87.5 us
    ppermute x28, starting transfers between devices, swap(): return lax.ppermute(value, axis, [(i, i ^ mask) for i in range(size)])  35.6 us
    pallas_call x4, Pallas kernels, attend(): pl.pallas_call(functools.partial(attend_kernel, slot, tok, places), out_s...  18.4 us
    pallas_call x4, Pallas kernels, project(): pl.pallas_call(functools.partial(project_kernel, len(x_parts), len(w_part...  16.9 us
    unnamed x49, local copies, waits for them, and re-layouts  5.49 us
  transfers between devices with their start and end apart: 28, of which 12 were waited for; matrix products, arithmetic and copies ran while one was open for 4% of the time, Pallas kernels for 19%

profile of v2, /device:TPU:0, one launch (start us, length us, event | category | flops | bytes accessed | tf_op | source)
XLA Modules:
  0.0 175.6 jit_solution(12382105924894971428)
XLA Ops:
  0.0 1.5 constant_dynamic-slice_fusion.1
  1.6 4.1 %collective-permute-start.5 = (bf16[256,768]{1,0:T(8,128)(2,1)S(1)}, bf16[256,768]{1,0:T(8,128)(2,1)S(1)}, u32[]{:S(2)}, u32[]{:S(2)}) collective-permute-start(bf16[256,768]{1,0:T(8,128)(2,1)S(1)} %get-tuple-element.27), channel_id=1, source_target_pairs={{0,16},{2,18},{4,20},{6,22},{8,24},{10,26},{12,28},{14,30},{16,0},... | collective-permute-start | bytes 1179656 | tf_op jit(solution)/shard_map/ppermute | solution.py:23
  5.7 1.3 collective-permute-start.6
  7.0 0.2 collective-permute-start.1
  7.2 1.5 collective-permute-start.2
  8.7 0.9 constant_dynamic-update-slice_fusion.1
  9.6 0.6 constant_dynamic-update-slice_fusion.refs_0_
  10.2 1.5 collective-permute-start
  11.8 20.7 %collective-permute-done.5 = bf16[256,768]{1,0:T(8,128)(2,1)S(1)} collective-permute-done((bf16[256,768]{1,0:T(8,128)(2,1)S(1)}, bf16[256,768]{1,0:T(8,128)(2,1)S(1)}, u32[]{:S(2)}, u32[]{:S(2)}) %collective-permute-start.5) | collective-permute-done | bytes 393248 | tf_op jit(solution)/shard_map/ppermute | solution.py:23
  32.5 1.8 %collective-permute-start.7 = (bf16[256,768]{1,0:T(8,128)(2,1)S(1)}, bf16[256,768]{1,0:T(8,128)(2,1)S(1)}, u32[]{:S(2)}, u32[]{:S(2)}) collective-permute-start(bf16[256,768]{1,0:T(8,128)(2,1)S(1)} %collective-permute-done.5), channel_id=1, source_target_pairs={{0,4},{2,6},{4,0},{6,2},{8,12},{10,14},{12,8},{14,10},{16,20},{18,... | collective-permute-start | bytes 1179656 | tf_op jit(solution)/shard_map/ppermute | solution.py:23
  34.3 0.2 collective-permute-start.8
  34.6 1.9 %collective-permute-start.3 = (bf16[256,768]{1,0:T(8,128)(2,1)S(1)}, bf16[256,768]{1,0:T(8,128)(2,1)}, u32[]{:S(2)}, u32[]{:S(2)}) collective-permute-start(bf16[256,768]{1,0:T(8,128)(2,1)S(1)} %collective-permute-done.1), channel_id=1, source_target_pairs={{0,4},{2,6},{4,0},{6,2},{8,12},{10,14},{12,8},{14,10},{16,20},{18,... | collective-permute-start | bytes 1179656 | tf_op jit(solution)/shard_map/ppermute | solution.py:23
  36.5 0.1 broadcast_multiply_fusion.1
  37.2 7.4 %collective-permute-done.7 = bf16[256,768]{1,0:T(8,128)(2,1)S(1)} collective-permute-done((bf16[256,768]{1,0:T(8,128)(2,1)S(1)}, bf16[256,768]{1,0:T(8,128)(2,1)S(1)}, u32[]{:S(2)}, u32[]{:S(2)}) %collective-permute-start.7) | collective-permute-done | bytes 393248 | tf_op jit(solution)/shard_map/ppermute | solution.py:23
  44.6 8.4 %collective-permute-done.8 = bf16[256,768]{1,0:T(8,128)(2,1)S(1)} collective-permute-done((bf16[256,768]{1,0:T(8,128)(2,1)S(1)}, bf16[256,768]{1,0:T(8,128)(2,1)S(1)}, u32[]{:S(2)}, u32[]{:S(2)}) %collective-permute-start.8) | collective-permute-done | bytes 393248 | tf_op jit(solution)/shard_map/ppermute | solution.py:23
  53.0 0.7 copy-done.18
  53.7 1.4 pad_maximum_fusion.1.refs_6_
  55.2 0.1 collective-permute-start.9
  55.3 3.7 %collective-permute-done.3 = bf16[256,768]{1,0:T(8,128)(2,1)} collective-permute-done((bf16[256,768]{1,0:T(8,128)(2,1)S(1)}, bf16[256,768]{1,0:T(8,128)(2,1)}, u32[]{:S(2)}, u32[]{:S(2)}) %collective-permute-start.3) | collective-permute-done | bytes 393248 | tf_op jit(solution)/shard_map/ppermute | solution.py:23
  58.9 1.6 pad_maximum_fusion.refs_4_
  60.7 1.7 norm.1
  62.4 0.8 copy-done.2
  63.2 3.4 %collective-permute-start.13 = (bf16[8,136,256]{2,1,0:T(8,128)(2,1)S(1)}, bf16[8,136,256]{2,1,0:T(8,128)(2,1)}, u32[]{:S(2)}, u32[]{:S(2)}) collective-permute-start(bf16[8,136,256]{2,1,0:T(8,128)(2,1)S(1)} %get-tuple-element.15.refs_2_), channel_id=1, source_target_pairs={{0,16},{2,18},{4,20},{6,22},{8,24},{10,26},{12,28},{14,30},{16,0},... | collective-permute-start | bytes 1671176 | tf_op jit(solution)/shard_map/ppermute | solution.py:23
  66.6 1.5 collective-permute-start.10
  68.1 0.8 copy-done
  68.9 0.7 fusion.4
  69.5 22.5 %collective-permute-done.13.refs_2_ = bf16[8,136,256]{2,1,0:T(8,128)(2,1)} collective-permute-done((bf16[8,136,256]{2,1,0:T(8,128)(2,1)S(1)}, bf16[8,136,256]{2,1,0:T(8,128)(2,1)}, u32[]{:S(2)}, u32[]{:S(2)}) %collective-permute-start.13) | collective-permute-done | bytes 557088 | tf_op jit(solution)/shard_map/ppermute | solution.py:23
  92.0 0.5 collective-permute-start.19
  92.5 1.5 collective-permute-start.14
  94.1 0.5 collective-permute-start.11
  94.6 0.1 pad_add_fusion.1.refs_0_
  94.7 0.1 stack.167.refs_1_
  94.8 1.4 fusion
  96.2 0.3 pad_maximum_fusion.4
  96.5 10.2 %collective-permute-done.19.refs_2_ = bf16[8,136,256]{2,1,0:T(8,128)(2,1)} collective-permute-done((bf16[8,136,256]{2,1,0:T(8,128)(2,1)}, bf16[8,136,256]{2,1,0:T(8,128)(2,1)}, u32[]{:S(2)}, u32[]{:S(2)}) %collective-permute-start.19) | collective-permute-done | bytes 557088 | tf_op jit(solution)/shard_map/ppermute | solution.py:23
  106.7 0.7 collective-permute-start.12
  107.4 3.5 %collective-permute-start.15 = (bf16[80,256]{1,0:T(8,128)(2,1)}, bf16[80,256]{1,0:T(8,128)(2,1)S(1)}, u32[]{:S(2)}, u32[]{:S(2)}) collective-permute-start(bf16[80,256]{1,0:T(8,128)(2,1)} %get-tuple-element.50), channel_id=1, source_target_pairs={{0,16},{2,18},{4,20},{6,22},{8,24},{10,26},{12,28},{14,30},{16,0},... | collective-permute-start | bytes 122888 | tf_op jit(solution)/shard_map/ppermute | solution.py:23
  110.9 1.5 collective-permute-start.20
  112.4 4.0 %project.4 = (bf16[4,128,128]{2,1,0:T(8,128)(2,1)S(1)}, bf16[192,256]{1,0:T(8,128)(2,1)S(1)}) custom-call(s32[16]{0:T(128)S(1)} %pad_add_fusion.1.refs_0_, s32[16]{0:T(128)S(1)} %stack.167.refs_1_, bf16[8,136,256]{2,1,0:T(8,128)(2,1)S(1)} %copy-done.1, bf16[8,136,256]{2,1,0:T(8,128)(2,1)S(1)} %copy-done.3, bf16[4,256,768]{2,1,0:T(8,128)(2,1)S(1)} %pad_maximum_fusion.refs_4_, ...), custom_call_target="tpu_custom_call" | custom-call | flops 855638016 | bytes 7405568 | tf_op jit(solution)/shard_map/project/pallas_call | solution.py:116
  116.4 3.9 %collective-permute-done.11.refs_3_ = bf16[8,136,256]{2,1,0:T(8,128)(2,1)} collective-permute-done((bf16[8,136,256]{2,1,0:T(8,128)(2,1)}, bf16[8,136,256]{2,1,0:T(8,128)(2,1)}, u32[]{:S(2)}, u32[]{:S(2)}) %collective-permute-start.11) | collective-permute-done | bytes 557088 | tf_op jit(solution)/shard_map/ppermute | solution.py:23
  120.3 4.3 %project.5 = (bf16[4,128,128]{2,1,0:T(8,128)(2,1)S(1)}, bf16[192,256]{1,0:T(8,128)(2,1)S(1)}) custom-call(s32[16]{0:T(128)S(1)} %pad_add_fusion.1.refs_0_, s32[16]{0:T(128)S(1)} %stack.167.refs_1_, bf16[8,136,256]{2,1,0:T(8,128)(2,1)} %collective-permute-done.10.refs_2_, bf16[8,136,256]{2,1,0:T(8,128)(2,1)} %collective-permute-done.11.refs_3_, ...), custom_call_target="tpu_custom_call" | custom-call | flops 855638016 | bytes 7405568 | tf_op jit(solution)/shard_map/project/pallas_call | solution.py:116
  124.7 0.6 copy-done.6
  125.4 4.4 %project.6 = (bf16[4,128,128]{2,1,0:T(8,128)(2,1)S(1)}, bf16[192,256]{1,0:T(8,128)(2,1)S(1)}) custom-call(s32[16]{0:T(128)S(1)} %pad_add_fusion.1.refs_0_, s32[16]{0:T(128)S(1)} %stack.167.refs_1_, bf16[8,136,256]{2,1,0:T(8,128)(2,1)} %collective-permute-done.13.refs_2_, bf16[8,136,256]{2,1,0:T(8,128)(2,1)} %collective-permute-done.14.refs_3_, ...), custom_call_target="tpu_custom_call" | custom-call | flops 855638016 | bytes 7405568 | tf_op jit(solution)/shard_map/project/pallas_call | solution.py:116
  129.8 1.5 collective-permute-start.16
  131.3 2.9 %collective-permute-start.21 = (bf16[80,256]{1,0:T(8,128)(2,1)S(1)}, bf16[80,256]{1,0:T(8,128)(2,1)S(1)}, u32[]{:S(2)}, u32[]{:S(2)}) collective-permute-start(bf16[80,256]{1,0:T(8,128)(2,1)S(1)} %copy-done.20), channel_id=1, source_target_pairs={{0,24},{2,26},{4,28},{6,30},{8,16},{10,18},{12,20},{14,22},{16,8},... | collective-permute-start | bytes 122888 | tf_op jit(solution)/shard_map/ppermute | solution.py:23
  134.3 2.4 %collective-permute-done.16.refs_5_ = bf16[3,192,256]{2,1,0:T(8,128)(2,1)} collective-permute-done((bf16[3,192,256]{2,1,0:T(8,128)(2,1)S(1)}, bf16[3,192,256]{2,1,0:T(8,128)(2,1)}, u32[]{:S(2)}, u32[]{:S(2)}) %collective-permute-start.16) | collective-permute-done | bytes 294944 | tf_op jit(solution)/shard_map/ppermute | solution.py:23
  136.7 0.6 collective-permute-done.21.refs_10_
  137.3 4.2 %project.7 = (bf16[4,128,128]{2,1,0:T(8,128)(2,1)S(1)}, bf16[192,256]{1,0:T(8,128)(2,1)S(1)}) custom-call(s32[16]{0:T(128)S(1)} %pad_add_fusion.1.refs_0_, s32[16]{0:T(128)S(1)} %stack.167.refs_1_, bf16[8,136,256]{2,1,0:T(8,128)(2,1)} %collective-permute-done.19.refs_2_, bf16[8,136,256]{2,1,0:T(8,128)(2,1)S(1)} %collective-permute-done.20.refs_3_, ...), custom_call_target="tpu_custom_call" | custom-call | flops 855638016 | bytes 7405568 | tf_op jit(solution)/shard_map/project/pallas_call | solution.py:116
  141.5 0.6 copy-done.10
  142.1 0.9 collective-permute-start.22
  143.1 0.2 collective-permute-start.23
  143.3 3.5 %collective-permute-done.22.refs_9_ = bf16[1,192,256]{2,1,0:T(8,128)(2,1)S(1)} collective-permute-done((bf16[1,192,256]{2,1,0:T(8,128)(2,1)S(1)}, bf16[1,192,256]{2,1,0:T(8,128)(2,1)S(1)}, u32[]{:S(2)}, u32[]{:S(2)}) %collective-permute-start.22) | collective-permute-done | bytes 98336 | tf_op jit(solution)/shard_map/ppermute | solution.py:23
  146.8 0.1 stack.162.refs_2_
  146.9 1.2 collective-permute-done.24.refs_11_
  148.1 0.9 copy-done.7
  149.0 4.4 %attend.5 = bf16[128,512]{1,0:T(8,128)(2,1)S(1)} custom-call(s32[1]{0:T(128)} %copy.9.refs_0_, s32[4]{0:T(128)S(1)} %get-tuple-element.26.refs_1_, s32[16]{0:T(128)S(1)} %stack.162.refs_2_, bf16[4,128,128]{2,1,0:T(8,128)(2,1)S(1)} %copy-done.7, bf16[3,192,256]{2,1,0:T(8,128)(2,1)S(1)} %pad_maximum_fusion.6.refs_4_, ...), custom_call_target="tpu_custom_call" | custom-call | flops 805306368 | bytes 1572864 | tf_op jit(solution)/shard_map/attend/pallas_call | solution.py:254
  153.4 1.0 collective-permute-start.25
  154.4 4.8 %attend.6 = bf16[128,512]{1,0:T(8,128)(2,1)S(1)} custom-call(s32[1]{0:T(128)} %copy.9.refs_0_, s32[4]{0:T(128)S(1)} %get-tuple-element.26.refs_1_, s32[16]{0:T(128)S(1)} %stack.162.refs_2_, bf16[4,128,128]{2,1,0:T(8,128)(2,1)S(1)} %copy-done.9, bf16[3,192,256]{2,1,0:T(8,128)(2,1)S(1)} %pad_maximum_fusion.6.refs_4_, ...), custom_call_target="tpu_custom_call" | custom-call | flops 805306368 | bytes 1572864 | tf_op jit(solution)/shard_map/attend/pallas_call | solution.py:254
  159.2 2.8 %collective-permute-start.26 = (bf16[128,512]{1,0:T(8,128)(2,1)S(1)}, bf16[128,512]{1,0:T(8,128)(2,1)S(1)}, u32[]{:S(2)}, u32[]{:S(2)}) collective-permute-start(bf16[128,512]{1,0:T(8,128)(2,1)S(1)} %attend.6), channel_id=1, source_target_pairs={{0,16},{2,18},{4,20},{6,22},{8,24},{10,26},{12,28},{14,30},{16,0},... | collective-permute-start | bytes 393224 | tf_op jit(solution)/shard_map/ppermute | solution.py:23
  162.0 5.4 %attend.7 = bf16[128,512]{1,0:T(8,128)(2,1)S(1)} custom-call(s32[1]{0:T(128)} %copy.9.refs_0_, s32[4]{0:T(128)S(1)} %get-tuple-element.26.refs_1_, s32[16]{0:T(128)S(1)} %stack.162.refs_2_, bf16[4,128,128]{2,1,0:T(8,128)(2,1)S(1)} %copy-done.11, bf16[3,192,256]{2,1,0:T(8,128)(2,1)S(1)} %pad_maximum_fusion.6.refs_4_, ...), custom_call_target="tpu_custom_call" | custom-call | flops 805306368 | bytes 1572864 | tf_op jit(solution)/shard_map/attend/pallas_call | solution.py:254
  167.4 0.4 collective-permute-start.27
  167.8 3.8 %attend.4 = bf16[128,512]{1,0:T(8,128)(2,1)S(1)} custom-call(s32[1]{0:T(128)} %copy.9.refs_0_, s32[4]{0:T(128)S(1)} %get-tuple-element.26.refs_1_, s32[16]{0:T(128)S(1)} %stack.162.refs_2_, bf16[4,128,128]{2,1,0:T(8,128)(2,1)S(1)} %copy-done.5, bf16[3,192,256]{2,1,0:T(8,128)(2,1)S(1)} %pad_maximum_fusion.6.refs_4_, ...), custom_call_target="tpu_custom_call" | custom-call | flops 805306368 | bytes 1572864 | tf_op jit(solution)/shard_map/attend/pallas_call | solution.py:254
  171.6 3.1 %collective-permute-done.27 = bf16[128,512]{1,0:T(8,128)(2,1)S(1)} collective-permute-done((bf16[128,512]{1,0:T(8,128)(2,1)S(1)}, bf16[128,512]{1,0:T(8,128)(2,1)S(1)}, u32[]{:S(2)}, u32[]{:S(2)}) %collective-permute-start.27) | collective-permute-done | bytes 131104 | tf_op jit(solution)/shard_map/ppermute | solution.py:23
  174.8 0.8 pad_maximum_fusion.3
  (74 shorter events, 0.6 us)
Async XLA Ops:
  0.0 8.7 %copy-start.13 = (bf16[128,2048]{1,0:T(8,128)(2,1)S(1)}, bf16[128,2048]{1,0:T(8,128)(2,1)}, u32[]{:S(2)}) copy-start(bf16[128,2048]{1,0:T(8,128)(2,1)} %param.7) | copy-start | bytes 1572868
  0.0 9.6 %copy-start.21 = (bf16[8,2048]{1,0:T(8,128)(2,1)S(1)}, bf16[8,2048]{1,0:T(8,128)(2,1)}, u32[]{:S(2)}) copy-start(bf16[8,2048]{1,0:T(8,128)(2,1)} %param.11) | copy-start | bytes 98308
  0.0 11.7 %copy-start.19 = (bf16[2,64,512]{2,1,0:T(8,128)(2,1)S(1)}, bf16[2,64,512]{2,1,0:T(8,128)(2,1)}, u32[]{:S(2)}) copy-start(bf16[2,64,512]{2,1,0:T(8,128)(2,1)} %param.10) | copy-start | bytes 393220
  0.0 34.5 %copy-start.22 = (f32[4096]{0:T(1024)S(1)}, f32[4096]{0:T(1024)}, u32[]{:S(2)}) copy-start(f32[4096]{0:T(1024)} %param.8) | copy-start | bytes 49156
  1.5 53.6 %copy-start.12 = (bf16[256,768]{1,0:T(8,128)(2,1)}, bf16[256,768]{1,0:T(8,128)(2,1)S(1)}, u32[]{:S(2)}) copy-start(bf16[256,768]{1,0:T(8,128)(2,1)S(1)} %get-tuple-element.29) | copy-start | bytes 1179652
  1.6 31.0 %collective-permute-start.5 = (bf16[256,768]{1,0:T(8,128)(2,1)S(1)}, bf16[256,768]{1,0:T(8,128)(2,1)S(1)}, u32[]{:S(2)}, u32[]{:S(2)}) collective-permute-start(bf16[256,768]{1,0:T(8,128)(2,1)S(1)} %get-tuple-element.27), channel_id=1, source_target_pairs={{0,16},{2,18},{4,20},{6,22},{8,24},{10,26},{12,28},{14,30},{16,0},... | collective-permute-start | bytes 1179656 | tf_op jit(solution)/shard_map/ppermute | solution.py:23
  5.7 28.7 %collective-permute-start.6 = (bf16[256,768]{1,0:T(8,128)(2,1)S(1)}, bf16[256,768]{1,0:T(8,128)(2,1)S(1)}, u32[]{:S(2)}, u32[]{:S(2)}) collective-permute-start(bf16[256,768]{1,0:T(8,128)(2,1)S(1)} %get-tuple-element.30), channel_id=1, source_target_pairs={{0,24},{2,26},{4,28},{6,30},{8,16},{10,18},{12,20},{14,22},{16,8},... | collective-permute-start | bytes 1179656 | tf_op jit(solution)/shard_map/ppermute | solution.py:23
  7.0 27.5 %collective-permute-start.1 = (bf16[256,768]{1,0:T(8,128)(2,1)S(1)}, bf16[256,768]{1,0:T(8,128)(2,1)S(1)}, u32[]{:S(2)}, u32[]{:S(2)}) collective-permute-start(bf16[256,768]{1,0:T(8,128)(2,1)S(1)} %get-tuple-element.28), channel_id=1, source_target_pairs={{0,8},{2,10},{4,12},{6,14},{8,0},{10,2},{12,4},{14,6},{16,24},{18,... | collective-permute-start | bytes 1179656 | tf_op jit(solution)/shard_map/ppermute | solution.py:23
  7.2 48.0 %collective-permute-start.2 = (bf16[256,768]{1,0:T(8,128)(2,1)S(1)}, bf16[256,768]{1,0:T(8,128)(2,1)S(1)}, u32[]{:S(2)}, u32[]{:S(2)}) collective-permute-start(bf16[256,768]{1,0:T(8,128)(2,1)S(1)} %get-tuple-element.29), channel_id=1, source_target_pairs={{0,4},{2,6},{4,0},{6,2},{8,12},{10,14},{12,8},{14,10},{16,20},{18,... | collective-permute-start | bytes 1179656 | tf_op jit(solution)/shard_map/ppermute | solution.py:23
  10.2 50.5 %collective-permute-start = (bf16[136,2048]{1,0:T(8,128)(2,1)}, bf16[136,2048]{1,0:T(8,128)(2,1)}, u32[]{:S(2)}, u32[]{:S(2)}) collective-permute-start(bf16[136,2048]{1,0:T(8,128)(2,1)} %constant_dynamic-update-slice_fusion.refs_0_), channel_id=1, source_target_pairs={{0,1},{1,0},{2,3},{3,2},{4,5},{5,4},{6,7},{7,6},{8,9},{9,8},{10,11... | collective-permute-start | bytes 1671176 | tf_op jit(solution)/shard_map/ppermute | solution.py:23
  32.5 12.1 %collective-permute-start.7 = (bf16[256,768]{1,0:T(8,128)(2,1)S(1)}, bf16[256,768]{1,0:T(8,128)(2,1)S(1)}, u32[]{:S(2)}, u32[]{:S(2)}) collective-permute-start(bf16[256,768]{1,0:T(8,128)(2,1)S(1)} %collective-permute-done.5), channel_id=1, source_target_pairs={{0,4},{2,6},{4,0},{6,2},{8,12},{10,14},{12,8},{14,10},{16,20},{18,... | collective-permute-start | bytes 1179656 | tf_op jit(solution)/shard_map/ppermute | solution.py:23
  34.3 18.6 %copy-start.16 = (bf16[256,768]{1,0:T(8,128)(2,1)}, bf16[256,768]{1,0:T(8,128)(2,1)S(1)}, u32[]{:S(2)}) copy-start(bf16[256,768]{1,0:T(8,128)(2,1)S(1)} %collective-permute-done.6) | copy-start | bytes 1179652
  34.3 18.6 %collective-permute-start.8 = (bf16[256,768]{1,0:T(8,128)(2,1)S(1)}, bf16[256,768]{1,0:T(8,128)(2,1)S(1)}, u32[]{:S(2)}, u32[]{:S(2)}) collective-permute-start(bf16[256,768]{1,0:T(8,128)(2,1)S(1)} %collective-permute-done.6), channel_id=1, source_target_pairs={{0,4},{2,6},{4,0},{6,2},{8,12},{10,14},{12,8},{14,10},{16,20},{18,... | collective-permute-start | bytes 1179656 | tf_op jit(solution)/shard_map/ppermute | solution.py:23
  34.5 20.6 %copy-start.14 = (bf16[256,768]{1,0:T(8,128)(2,1)}, bf16[256,768]{1,0:T(8,128)(2,1)S(1)}, u32[]{:S(2)}) copy-start(bf16[256,768]{1,0:T(8,128)(2,1)S(1)} %collective-permute-done.1) | copy-start | bytes 1179652
  34.6 24.4 %collective-permute-start.3 = (bf16[256,768]{1,0:T(8,128)(2,1)S(1)}, bf16[256,768]{1,0:T(8,128)(2,1)}, u32[]{:S(2)}, u32[]{:S(2)}) collective-permute-start(bf16[256,768]{1,0:T(8,128)(2,1)S(1)} %collective-permute-done.1), channel_id=1, source_target_pairs={{0,4},{2,6},{4,0},{6,2},{8,12},{10,14},{12,8},{14,10},{16,20},{18,... | collective-permute-start | bytes 1179656 | tf_op jit(solution)/shard_map/ppermute | solution.py:23
  44.6 8.4 %copy-start.17 = (bf16[256,768]{1,0:T(8,128)(2,1)}, bf16[256,768]{1,0:T(8,128)(2,1)S(1)}, u32[]{:S(2)}) copy-start(bf16[256,768]{1,0:T(8,128)(2,1)S(1)} %collective-permute-done.7) | copy-start | bytes 1179652
  53.0 0.7 copy-start.18
  55.2 52.2 %collective-permute-start.9 = (bf16[4,256,768]{2,1,0:T(8,128)(2,1)S(1)}, bf16[4,256,768]{2,1,0:T(8,128)(2,1)}, u32[]{:S(2)}, u32[]{:S(2)}) collective-permute-start(bf16[4,256,768]{2,1,0:T(8,128)(2,1)S(1)} %pad_maximum_fusion.1.refs_6_), channel_id=1, source_target_pairs={{0,2},{2,0},{4,6},{6,4},{8,10},{10,8},{12,14},{14,12},{16,18},{18,... | collective-permute-start | bytes 4718600 | tf_op jit(solution)/shard_map/ppermute | solution.py:23
  55.3 3.7 %copy-start.15 = (bf16[256,768]{1,0:T(8,128)(2,1)}, bf16[256,768]{1,0:T(8,128)(2,1)S(1)}, u32[]{:S(2)}) copy-start(bf16[256,768]{1,0:T(8,128)(2,1)S(1)} %collective-permute-done.2) | copy-start | bytes 1179652
  58.9 9.9 %copy-start.23 = (s32[8]{0:T(128)S(1)}, s32[8]{0:T(128)}, u32[]{:S(2)}) copy-start(s32[8]{0:T(128)} %param.12) | copy-start | bytes 100
  60.5 50.4 %collective-permute-start.4 = (bf16[4,256,768]{2,1,0:T(8,128)(2,1)S(1)}, bf16[4,256,768]{2,1,0:T(8,128)(2,1)}, u32[]{:S(2)}, u32[]{:S(2)}) collective-permute-start(bf16[4,256,768]{2,1,0:T(8,128)(2,1)S(1)} %pad_maximum_fusion.refs_4_), channel_id=1, source_target_pairs={{0,2},{2,0},{4,6},{6,4},{8,10},{10,8},{12,14},{14,12},{16,18},{18,... | collective-permute-start | bytes 4718600 | tf_op jit(solution)/shard_map/ppermute | solution.py:23
  62.4 0.8 copy-start.2
  63.2 28.8 %collective-permute-start.13 = (bf16[8,136,256]{2,1,0:T(8,128)(2,1)S(1)}, bf16[8,136,256]{2,1,0:T(8,128)(2,1)}, u32[]{:S(2)}, u32[]{:S(2)}) collective-permute-start(bf16[8,136,256]{2,1,0:T(8,128)(2,1)S(1)} %get-tuple-element.15.refs_2_), channel_id=1, source_target_pairs={{0,16},{2,18},{4,20},{6,22},{8,24},{10,26},{12,28},{14,30},{16,0},... | collective-permute-start | bytes 1671176 | tf_op jit(solution)/shard_map/ppermute | solution.py:23
  66.6 27.5 %collective-permute-start.10 = (bf16[8,136,256]{2,1,0:T(8,128)(2,1)S(1)}, bf16[8,136,256]{2,1,0:T(8,128)(2,1)}, u32[]{:S(2)}, u32[]{:S(2)}) collective-permute-start(bf16[8,136,256]{2,1,0:T(8,128)(2,1)S(1)} %get-tuple-element.15.refs_2_), channel_id=1, source_target_pairs={{0,8},{2,10},{4,12},{6,14},{8,0},{10,2},{12,4},{14,6},{16,24},{18,... | collective-permute-start | bytes 1671176 | tf_op jit(solution)/shard_map/ppermute | solution.py:23
  68.1 0.8 copy-start
  92.0 14.7 %collective-permute-start.19 = (bf16[8,136,256]{2,1,0:T(8,128)(2,1)}, bf16[8,136,256]{2,1,0:T(8,128)(2,1)}, u32[]{:S(2)}, u32[]{:S(2)}) collective-permute-start(bf16[8,136,256]{2,1,0:T(8,128)(2,1)} %collective-permute-done.13.refs_2_), channel_id=1, source_target_pairs={{0,8},{2,10},{4,12},{6,14},{8,0},{10,2},{12,4},{14,6},{16,24},{18,... | collective-permute-start | bytes 1671176 | tf_op jit(solution)/shard_map/ppermute | solution.py:23
  92.5 32.8 %collective-permute-start.14 = (bf16[8,136,256]{2,1,0:T(8,128)(2,1)}, bf16[8,136,256]{2,1,0:T(8,128)(2,1)}, u32[]{:S(2)}, u32[]{:S(2)}) collective-permute-start(bf16[8,136,256]{2,1,0:T(8,128)(2,1)} %collective-permute-done.13.refs_2_), channel_id=1, source_target_pairs={{0,1},{1,0},{2,3},{3,2},{4,5},{5,4},{6,7},{7,6},{8,9},{9,8},{10,11... | collective-permute-start | bytes 1671176 | tf_op jit(solution)/shard_map/ppermute | solution.py:23
  94.1 26.3 %collective-permute-start.11 = (bf16[8,136,256]{2,1,0:T(8,128)(2,1)}, bf16[8,136,256]{2,1,0:T(8,128)(2,1)}, u32[]{:S(2)}, u32[]{:S(2)}) collective-permute-start(bf16[8,136,256]{2,1,0:T(8,128)(2,1)} %collective-permute-done.10.refs_2_), channel_id=1, source_target_pairs={{0,1},{1,0},{2,3},{3,2},{4,5},{5,4},{6,7},{7,6},{8,9},{9,8},{10,11... | collective-permute-start | bytes 1671176 | tf_op jit(solution)/shard_map/ppermute | solution.py:23
  94.8 17.7 %copy-start.1 = (bf16[8,136,256]{2,1,0:T(8,128)(2,1)S(1)}, bf16[8,136,256]{2,1,0:T(8,128)(2,1)}, u32[]{:S(2)}) copy-start(bf16[8,136,256]{2,1,0:T(8,128)(2,1)} %copy-done) | copy-start | bytes 1671172
  94.8 17.7 %copy-start.3 = (bf16[8,136,256]{2,1,0:T(8,128)(2,1)S(1)}, bf16[8,136,256]{2,1,0:T(8,128)(2,1)}, u32[]{:S(2)}) copy-start(bf16[8,136,256]{2,1,0:T(8,128)(2,1)} %copy-done.2) | copy-start | bytes 1671172
  106.7 9.7 %collective-permute-start.12 = (bf16[80,256]{1,0:T(8,128)(2,1)}, bf16[80,256]{1,0:T(8,128)(2,1)S(1)}, u32[]{:S(2)}, u32[]{:S(2)}) collective-permute-start(bf16[80,256]{1,0:T(8,128)(2,1)} %get-tuple-element.49), channel_id=1, source_target_pairs={{0,8},{2,10},{4,12},{6,14},{8,0},{10,2},{12,4},{14,6},{16,24},{18,... | collective-permute-start | bytes 122888 | tf_op jit(solution)/shard_map/ppermute | solution.py:23
  107.4 18.0 %collective-permute-start.15 = (bf16[80,256]{1,0:T(8,128)(2,1)}, bf16[80,256]{1,0:T(8,128)(2,1)S(1)}, u32[]{:S(2)}, u32[]{:S(2)}) collective-permute-start(bf16[80,256]{1,0:T(8,128)(2,1)} %get-tuple-element.50), channel_id=1, source_target_pairs={{0,16},{2,18},{4,20},{6,22},{8,24},{10,26},{12,28},{14,30},{16,0},... | collective-permute-start | bytes 122888 | tf_op jit(solution)/shard_map/ppermute | solution.py:23
  110.9 26.4 %collective-permute-start.20 = (bf16[8,136,256]{2,1,0:T(8,128)(2,1)}, bf16[8,136,256]{2,1,0:T(8,128)(2,1)S(1)}, u32[]{:S(2)}, u32[]{:S(2)}) collective-permute-start(bf16[8,136,256]{2,1,0:T(8,128)(2,1)} %collective-permute-done.19.refs_2_), channel_id=1, source_target_pairs={{0,1},{1,0},{2,3},{3,2},{4,5},{5,4},{6,7},{7,6},{8,9},{9,8},{10,11... | collective-permute-start | bytes 1671176 | tf_op jit(solution)/shard_map/ppermute | solution.py:23
  116.4 8.3 %copy-start.4 = (bf16[4,128,128]{2,1,0:T(8,128)(2,1)}, bf16[4,128,128]{2,1,0:T(8,128)(2,1)S(1)}, u32[]{:S(2)}) copy-start(bf16[4,128,128]{2,1,0:T(8,128)(2,1)S(1)} %get-tuple-element.17.refs_3_) | copy-start | bytes 393220
  124.7 0.7 copy-start.6
  125.4 6.0 %copy-start.20 = (bf16[80,256]{1,0:T(8,128)(2,1)S(1)}, bf16[80,256]{1,0:T(8,128)(2,1)}, u32[]{:S(2)}) copy-start(bf16[80,256]{1,0:T(8,128)(2,1)} %get-tuple-element.51) | copy-start | bytes 122884
  129.7 7.5 %copy-start.8 = (bf16[4,128,128]{2,1,0:T(8,128)(2,1)}, bf16[4,128,128]{2,1,0:T(8,128)(2,1)S(1)}, u32[]{:S(2)}) copy-start(bf16[4,128,128]{2,1,0:T(8,128)(2,1)S(1)} %get-tuple-element.23.refs_3_) | copy-start | bytes 393220
  129.8 6.9 %collective-permute-start.16 = (bf16[3,192,256]{2,1,0:T(8,128)(2,1)S(1)}, bf16[3,192,256]{2,1,0:T(8,128)(2,1)}, u32[]{:S(2)}, u32[]{:S(2)}) collective-permute-start(bf16[3,192,256]{2,1,0:T(8,128)(2,1)S(1)} %pad_maximum_fusion.6.refs_4_), channel_id=1, source_target_pairs={{0,4},{2,6},{4,0},{6,2},{8,12},{10,14},{12,8},{14,10},{16,20},{18,... | collective-permute-start | bytes 884744 | tf_op jit(solution)/shard_map/ppermute | solution.py:23
  131.3 5.9 %collective-permute-start.21 = (bf16[80,256]{1,0:T(8,128)(2,1)S(1)}, bf16[80,256]{1,0:T(8,128)(2,1)S(1)}, u32[]{:S(2)}, u32[]{:S(2)}) collective-permute-start(bf16[80,256]{1,0:T(8,128)(2,1)S(1)} %copy-done.20), channel_id=1, source_target_pairs={{0,24},{2,26},{4,28},{6,30},{8,16},{10,18},{12,20},{14,22},{16,8},... | collective-permute-start | bytes 122888 | tf_op jit(solution)/shard_map/ppermute | solution.py:23
  134.3 13.8 %collective-permute-start.17 = (bf16[3,192,256]{2,1,0:T(8,128)(2,1)S(1)}, bf16[3,192,256]{2,1,0:T(8,128)(2,1)}, u32[]{:S(2)}, u32[]{:S(2)}) collective-permute-start(bf16[3,192,256]{2,1,0:T(8,128)(2,1)S(1)} %pad_maximum_fusion.6.refs_4_), channel_id=1, source_target_pairs={{0,2},{2,0},{4,6},{6,4},{8,10},{10,8},{12,14},{14,12},{16,18},{18,... | collective-permute-start | bytes 884744 | tf_op jit(solution)/shard_map/ppermute | solution.py:23
  136.7 11.4 %collective-permute-start.18 = (bf16[3,192,256]{2,1,0:T(8,128)(2,1)}, bf16[3,192,256]{2,1,0:T(8,128)(2,1)}, u32[]{:S(2)}, u32[]{:S(2)}) collective-permute-start(bf16[3,192,256]{2,1,0:T(8,128)(2,1)} %collective-permute-done.16.refs_5_), channel_id=1, source_target_pairs={{0,2},{2,0},{4,6},{6,4},{8,10},{10,8},{12,14},{14,12},{16,18},{18,... | collective-permute-start | bytes 884744 | tf_op jit(solution)/shard_map/ppermute | solution.py:23
  141.5 0.7 copy-start.10
  142.1 4.7 %collective-permute-start.22 = (bf16[1,192,256]{2,1,0:T(8,128)(2,1)S(1)}, bf16[1,192,256]{2,1,0:T(8,128)(2,1)S(1)}, u32[]{:S(2)}, u32[]{:S(2)}) collective-permute-start(bf16[1,192,256]{2,1,0:T(8,128)(2,1)S(1)} %bitcast.72), channel_id=1, source_target_pairs={{0,4},{2,6},{4,0},{6,2},{8,12},{10,14},{12,8},{14,10},{16,20},{18,... | collective-permute-start | bytes 294920 | tf_op jit(solution)/shard_map/ppermute | solution.py:23
  143.1 3.8 %collective-permute-start.23 = (bf16[1,192,256]{2,1,0:T(8,128)(2,1)S(1)}, bf16[1,192,256]{2,1,0:T(8,128)(2,1)S(1)}, u32[]{:S(2)}, u32[]{:S(2)}) collective-permute-start(bf16[1,192,256]{2,1,0:T(8,128)(2,1)S(1)} %bitcast.73), channel_id=1, source_target_pairs={{0,2},{2,0},{4,6},{6,4},{8,10},{10,8},{12,14},{14,12},{16,18},{18,... | collective-permute-start | bytes 294920 | tf_op jit(solution)/shard_map/ppermute | solution.py:23
  146.8 1.3 collective-permute-start.24
  148.1 0.9 copy-start.7
  149.0 5.4 %copy-start.9 = (bf16[4,128,128]{2,1,0:T(8,128)(2,1)S(1)}, bf16[4,128,128]{2,1,0:T(8,128)(2,1)}, u32[]{:S(2)}) copy-start(bf16[4,128,128]{2,1,0:T(8,128)(2,1)} %copy-done.8) | copy-start | bytes 393220
  153.4 8.6 %copy-start.11 = (bf16[4,128,128]{2,1,0:T(8,128)(2,1)S(1)}, bf16[4,128,128]{2,1,0:T(8,128)(2,1)}, u32[]{:S(2)}) copy-start(bf16[4,128,128]{2,1,0:T(8,128)(2,1)} %copy-done.10) | copy-start | bytes 393220
  153.4 18.2 %collective-permute-start.25 = (bf16[128,512]{1,0:T(8,128)(2,1)S(1)}, bf16[128,512]{1,0:T(8,128)(2,1)S(1)}, u32[]{:S(2)}, u32[]{:S(2)}) collective-permute-start(bf16[128,512]{1,0:T(8,128)(2,1)S(1)} %attend.5), channel_id=1, source_target_pairs={{0,8},{2,10},{4,12},{6,14},{8,0},{10,2},{12,4},{14,6},{16,24},{18,... | collective-permute-start | bytes 393224 | tf_op jit(solution)/shard_map/ppermute | solution.py:23
  159.2 8.6 %copy-start.5 = (bf16[4,128,128]{2,1,0:T(8,128)(2,1)S(1)}, bf16[4,128,128]{2,1,0:T(8,128)(2,1)}, u32[]{:S(2)}) copy-start(bf16[4,128,128]{2,1,0:T(8,128)(2,1)} %copy-done.4) | copy-start | bytes 393220
  159.2 12.4 %collective-permute-start.26 = (bf16[128,512]{1,0:T(8,128)(2,1)S(1)}, bf16[128,512]{1,0:T(8,128)(2,1)S(1)}, u32[]{:S(2)}, u32[]{:S(2)}) collective-permute-start(bf16[128,512]{1,0:T(8,128)(2,1)S(1)} %attend.6), channel_id=1, source_target_pairs={{0,16},{2,18},{4,20},{6,22},{8,24},{10,26},{12,28},{14,30},{16,0},... | collective-permute-start | bytes 393224 | tf_op jit(solution)/shard_map/ppermute | solution.py:23
  167.4 7.2 %collective-permute-start.27 = (bf16[128,512]{1,0:T(8,128)(2,1)S(1)}, bf16[128,512]{1,0:T(8,128)(2,1)S(1)}, u32[]{:S(2)}, u32[]{:S(2)}) collective-permute-start(bf16[128,512]{1,0:T(8,128)(2,1)S(1)} %attend.7), channel_id=1, source_target_pairs={{0,24},{2,26},{4,28},{6,30},{8,16},{10,18},{12,20},{14,22},{16,8},... | collective-permute-start | bytes 393224 | tf_op jit(solution)/shard_map/ppermute | solution.py:23

commit v3 on v2

v3 whole, which is shorter than its diff:
```python
import functools
import math

import jax
import jax.numpy as jnp
from jax import lax
from jax.experimental import pallas as pl
from jax.experimental.pallas import tpu as pltpu
from jax.sharding import PartitionSpec as P

HEADS = 32
KVH = 8
HD = 128
GROUP = HEADS // KVH
WIDTH = (GROUP + 2) * HD
FEATS = 256
FAR = -1e30
VMEM = pl.BlockSpec(memory_space=pltpu.VMEM)
SMEM = pl.BlockSpec(memory_space=pltpu.SMEM)


def swap(value, axis, size, mask, name="move"):
    with jax.named_scope(name):
        return lax.ppermute(value, axis, [(i, i ^ mask) for i in range(size)])


def after(value, *earlier):
    return lax.optimization_barrier((value,) + earlier)[0]


def squares_kernel(stream, hidden, out):
    tok = stream.shape[0]
    for ref, first in ((stream, 0), (hidden, tok)):
        value = ref[...].astype(jnp.float32)
        total = jnp.sum(value * value, axis=-1, keepdims=True)
        out[first : first + value.shape[0]] = jnp.broadcast_to(total, (value.shape[0], HD))


def squares(stream, hidden):
    return pl.pallas_call(
        squares_kernel,
        out_shape=jax.ShapeDtypeStruct((stream.shape[0] + hidden.shape[0], HD), jnp.float32),
        in_specs=[VMEM] * 2,
        out_specs=VMEM,
        compiler_params=pltpu.CompilerParams(vmem_limit_bytes=8 * 2**20),
        name="squares",
    )(stream, hidden)


def norm_kernel(width, count, stream, hidden, gain, *refs):
    sums, out = refs[:count], refs[count]
    tok = stream.shape[0]
    factor = lax.rsqrt(sum(s[:, :1] for s in sums) / width + 1e-05)
    for ref, first in ((stream, 0), (hidden, tok)):
        last = first + ref.shape[0]
        for block in range(out.shape[0]):
            lanes = slice(block * FEATS, (block + 1) * FEATS)
            value = ref[:, lanes].astype(jnp.float32)
            value = value * factor[first:last] * gain[:, lanes]
            out[block, first:last] = value.astype(jnp.bfloat16)


def norm(stream, hidden, gain, sums, width):
    blocks = stream.shape[1] // FEATS
    rows = stream.shape[0] + hidden.shape[0]
    return pl.pallas_call(
        functools.partial(norm_kernel, width, len(sums)),
        out_shape=jax.ShapeDtypeStruct((blocks, rows, FEATS), jnp.bfloat16),
        in_specs=[VMEM] * (3 + len(sums)),
        out_specs=VMEM,
        compiler_params=pltpu.CompilerParams(vmem_limit_bytes=12 * 2**20),
        name="norm",
    )(stream, hidden, gain.reshape(1, -1), *sums)


def unpack_kernel(plain, packed, fold, *refs):
    sources, outs = refs[: plain + packed], refs[plain + packed :]
    depth = outs[0].shape[1]
    for i, source in enumerate(sources):
        outs[0][i] = source[:depth]
        if i >= plain:
            extra = source.shape[0] - depth
            for j in range(fold):
                lanes = slice(j * 2 * HD, (j + 1) * 2 * HD)
                outs[1 + i - plain][j * extra : (j + 1) * extra] = source[depth:, lanes]


def unpack(plain, packed, depth, fold):
    extra = packed[0].shape[0] - depth
    count = len(plain) + len(packed)
    return pl.pallas_call(
        functools.partial(unpack_kernel, len(plain), len(packed), fold),
        out_shape=[jax.ShapeDtypeStruct((count, depth, WIDTH), jnp.bfloat16)]
        + [jax.ShapeDtypeStruct((fold * extra, 2 * HD), jnp.bfloat16)] * len(packed),
        in_specs=[VMEM] * count,
        out_specs=[VMEM] * (1 + len(packed)),
        compiler_params=pltpu.CompilerParams(vmem_limit_bytes=8 * 2**20),
        cost_estimate=pl.CostEstimate(flops=2 * 10**10, bytes_accessed=10**7, transcendentals=0),
        name="unpack",
    )(*plain, *packed)


def project_kernel(kind, first_slot, tok, redo, pitch, n_x, n_w, *refs):
    x_ids, w_ids = refs[:2]
    x_refs, refs = refs[2 : 2 + sum(n_x)], refs[2 + sum(n_x) :]
    w_refs, refs = refs[:n_w], refs[n_w:]
    chunks = len(n_x)
    cosine, sine, *refs = refs
    caches, (out, held) = refs[:-2], refs[-2:]
    span = cosine.shape[1]
    cache_rows = span - tok

    @pl.when(pl.program_id(0) == 0)
    def _():
        first = 0
        for chunk, count in enumerate(n_x):
            at = 0
            for part in x_refs[first : first + count]:
                for block in range(part.shape[0]):
                    held[x_ids[at], chunk * pitch : chunk * pitch + tok + redo] = part[block]
                    at += 1
            first += count

    total = None
    at = 0
    for part in w_refs:
        for block in range(part.shape[0]):
            term = jnp.dot(held[w_ids[at]], part[block], preferred_element_type=jnp.float32)
            total = term if total is None else total + term
            at += 1

    def rotated(value, chunk, first, last):
        turned = pltpu.roll(value, HD // 2, 1)
        slot = first_slot + chunk
        return value * cosine[slot, first:last] + turned * sine[slot, first:last]

    for chunk in range(chunks):
        mine = total[chunk * pitch : chunk * pitch + tok + redo]
        if kind == "queries":
            for head in range(2):
                value = mine[:tok, head * HD : (head + 1) * HD]
                out[chunk, head] = rotated(value, chunk, 0, tok).astype(jnp.bfloat16)
            continue
        keys = rotated(mine[:tok, :HD], chunk, 0, tok)
        out[chunk, :tok] = jnp.concatenate([keys, mine[:tok, HD:]], 1).astype(jnp.bfloat16)
        cache = caches[chunk]
        offsets = cache[cache_rows : cache_rows + 1, :redo].astype(jnp.float32)
        row = lax.broadcasted_iota(jnp.int32, (cache_rows, redo), 0).astype(jnp.float32)
        chosen = (row == offsets).astype(jnp.float32)
        fresh = jnp.dot(
            chosen,
            mine[tok:],
            preferred_element_type=jnp.float32,
            precision=lax.Precision.HIGHEST,
        )
        turned = rotated(fresh[:, :HD], chunk, tok, span)
        fresh = jnp.concatenate([turned, fresh[:, HD:]], 1)
        hit = jnp.sum(chosen, axis=1, keepdims=True) > 0.5
        kept = cache[:cache_rows].astype(jnp.float32)
        out[chunk, tok:] = jnp.where(hit, fresh, kept).astype(jnp.bfloat16)


def project(kind, first_slot, x_chunks, x_ids, w_parts, w_ids, cosine, sine, caches, tok, redo):
    chunks = len(x_chunks)
    blocks = sum(p.shape[0] for p in x_chunks[0])
    span = cosine.shape[1]
    pitch = -(-(tok + redo) // 16) * 16
    full = lambda a: pl.BlockSpec(a.shape, lambda t, n=a.ndim: (0,) * n)
    tiles, first = (2, 0) if kind == "queries" else (1, 2)
    w_spec = lambda a: pl.BlockSpec((a.shape[0], FEATS, FEATS), lambda t: (0, 0, first + t))
    if kind == "queries":
        out_shape = jax.ShapeDtypeStruct((chunks, GROUP, tok, HD), jnp.bfloat16)
        out_spec = pl.BlockSpec((chunks, 2, tok, HD), lambda t: (0, t, 0, 0))
        caches = []
    else:
        out_shape = jax.ShapeDtypeStruct((chunks, span, 2 * HD), jnp.bfloat16)
        out_spec = full(out_shape)
    x_parts = [p for chunk in x_chunks for p in chunk]
    n_x = [len(chunk) for chunk in x_chunks]
    return pl.pallas_call(
        functools.partial(project_kernel, kind, first_slot, tok, redo, pitch, n_x, len(w_parts)),
        grid=(tiles,),
        out_shape=out_shape,
        in_specs=[SMEM, SMEM]
        + [full(a) for a in x_parts]
        + [w_spec(a) for a in w_parts]
        + [full(a) for a in (cosine, sine, *caches)],
        out_specs=out_spec,
        scratch_shapes=[pltpu.VMEM((blocks, chunks * pitch, FEATS), jnp.bfloat16)],
        compiler_params=pltpu.CompilerParams(vmem_limit_bytes=56 * 2**20),
        cost_estimate=pl.CostEstimate(
            flops=2 * chunks * pitch * blocks * FEATS * FEATS * tiles,
            bytes_accessed=2 * blocks * FEATS * (FEATS * tiles + chunks * pitch),
            transcendentals=0,
        ),
        name=kind,
    )(x_ids, w_ids, *x_parts, *w_parts, cosine, sine, *caches)


def attend_kernel(slot, tok, places, *refs):
    begin_ref, q_ids, kv_ids, q_ref = refs[:4]
    kv_refs = refs[4:-5]
    out, scores, top, total, accum = refs[-5:]
    begin = begin_ref[0]
    q_id = q_ids[slot]
    heads = GROUP * tok
    scale = math.log2(math.e) / math.sqrt(HD)
    span = kv_refs[0].shape[1]
    cache_rows = span - tok
    top[...] = jnp.full(top.shape, FAR, jnp.float32)
    total[...] = jnp.zeros(total.shape, jnp.float32)
    accum[...] = jnp.zeros(accum.shape, jnp.float32)

    def score(column, keys, allowed):
        value = lax.dot_general(
            q_ref[0].reshape(heads, HD),
            keys,
            (((1,), (1,)), ((), ())),
            preferred_element_type=jnp.float32,
        )
        if allowed is not None:
            value = jnp.where(allowed(value.shape), value, FAR)
        scores[:, column : column + value.shape[1]] = value
        most = top[...]
        for lane in range(0, value.shape[1], HD):
            most = jnp.maximum(most, value[:, lane : lane + HD])
        top[...] = most

    def mix(column, values):
        weights = []
        some = total[...]
        most = top[...]
        for lane in range(0, values.shape[0], HD):
            part = scores[:, column + lane : column + lane + HD]
            weight = jnp.exp2(part * scale - most)
            some = some + weight
            weights.append(weight.astype(jnp.bfloat16))
        total[...] = some
        accum[...] += jnp.dot(
            jnp.concatenate(weights, 1), values, preferred_element_type=jnp.float32
        )

    pending = []
    for at in range(0, len(places), 4):
        group = places[at : at + 4]
        ids = [kv_ids[at + i] for i in range(len(group))]
        least = functools.reduce(jnp.minimum, ids)
        most = functools.reduce(jnp.maximum, ids)
        base = at * span

        def rows(first, last, half, group=group):
            return jnp.concatenate(
                [kv_refs[n][i, first:last, half * HD : (half + 1) * HD] for n, i in group], 0
            )

        def starts(shape, step, ids=ids):
            column = lax.broadcasted_iota(jnp.int32, shape, 1)
            which = column // step
            first = jnp.zeros(shape, jnp.int32)
            for i, one in enumerate(ids):
                first = jnp.where(which == i, one * step, first)
            return first + column % step

        def causal(shape, starts=starts):
            row = lax.broadcasted_iota(jnp.int32, shape, 0)
            return starts(shape, tok) <= q_id * tok + row % tok

        def prefix(shape, starts=starts):
            return starts(shape, cache_rows) < begin

        shift = len(group) * tok

        @pl.when((most + 1) * cache_rows <= begin)
        def _(rows=rows, base=base):
            score(base + shift, rows(tok, span, 0), None)

        @pl.when(((most + 1) * cache_rows > begin) & (least * cache_rows < begin))
        def _(rows=rows, prefix=prefix, base=base):
            score(base + shift, rows(tok, span, 0), prefix)

        @pl.when(most < q_id)
        def _(rows=rows, base=base):
            score(base, rows(0, tok, 0), None)

        @pl.when((most >= q_id) & (least <= q_id))
        def _(rows=rows, causal=causal, base=base):
            score(base, rows(0, tok, 0), causal)

        pending.append((least * cache_rows < begin, least <= q_id, rows, base, shift))

    peak = jnp.max(top[...], axis=1, keepdims=True) * scale
    top[...] = jnp.broadcast_to(peak, top.shape)
    for cached, streamed, rows, base, shift in pending:

        @pl.when(cached)
        def _(rows=rows, base=base, shift=shift):
            mix(base + shift, rows(tok, span, 1))

        @pl.when(streamed)
        def _(rows=rows, base=base):
            mix(base, rows(0, tok, 1))

    mixed = (accum[...] / jnp.sum(total[...], axis=1, keepdims=True)).astype(jnp.bfloat16)
    for head in range(GROUP):
        out[:, head * HD : (head + 1) * HD] = mixed[head * tok : (head + 1) * tok]


def attend(slot, begin, queries, index, q_ids, kv_parts, places, kv_ids, tok):
    span = kv_parts[0].shape[1]
    n_rows = len(places) * span
    heads = GROUP * tok
    return pl.pallas_call(
        functools.partial(attend_kernel, slot, tok, places),
        out_shape=jax.ShapeDtypeStruct((tok, GROUP * HD), jnp.bfloat16),
        grid=(1,),
        in_specs=[SMEM, SMEM, SMEM, pl.BlockSpec((1, GROUP, tok, HD), lambda t: (index, 0, 0, 0))]
        + [VMEM] * len(kv_parts),
        out_specs=VMEM,
        scratch_shapes=[
            pltpu.VMEM((heads, n_rows), jnp.float32),
            pltpu.VMEM((heads, HD), jnp.float32),
            pltpu.VMEM((heads, HD), jnp.float32),
            pltpu.VMEM((heads, HD), jnp.float32),
        ],
        compiler_params=pltpu.CompilerParams(vmem_limit_bytes=8 * 2**20 + 5 * heads * n_rows),
        cost_estimate=pl.CostEstimate(
            flops=4 * heads * n_rows * HD,
            bytes_accessed=4 * n_rows * HD,
            transcendentals=heads * n_rows,
        ),
        name="attend",
    )(begin, q_ids, kv_ids, queries, *kv_parts)


def per_device(
    seq, tp, stream_x, norm_gain, w_qkv, cache_kv, recomp_hidden, recomp_index, prefix_len
):
    tok, redo = stream_x.shape[0], recomp_hidden.shape[0]
    cache_rows = cache_kv.shape[1]
    heads = w_qkv.shape[1] // WIDTH
    crew = seq // heads
    at, side = lax.axis_index("seq"), lax.axis_index("tp")
    plane, inner = at // crew, at % crew
    begin = prefix_len[0]
    squared = crew == 4 and heads == 4 and tp == 2

    def across(value, k, name="planes"):
        return swap(value, "seq", seq, k * crew, f"{name}_{k}") if k else value

    w_cut = [lax.dynamic_slice_in_dim(w_qkv, (plane ^ k) * WIDTH, WIDTH, 1) for k in range(heads)]
    stream_x, w_cut = lax.optimization_barrier((stream_x, w_cut))
    sums = squares(stream_x, recomp_hidden)
    wide = stream_x.shape[1]
    width = wide * tp
    gain = lax.dynamic_slice_in_dim(norm_gain, side * wide, wide)
    sums = [sums, swap(sums, "tp", tp, 1, "side_sums")] if squared else [lax.psum(sums, "tp")]
    own = norm(stream_x, recomp_hidden, gain, sums, width)

    offsets = (recomp_index - at * cache_rows).astype(jnp.bfloat16)
    fold = WIDTH // (2 * HD)
    extra = -(-(cache_rows + 1) // (16 * fold)) * 16
    offsets = jnp.pad(offsets[None, :], ((0, fold * extra - cache_rows - 1), (0, 2 * HD - redo)))
    caches = []
    for k in range(heads):
        part = lax.dynamic_slice_in_dim(cache_kv, (plane ^ k) * HD, HD, 2)
        part = jnp.concatenate([part[0], part[1]], 1)
        caches.append(jnp.concatenate([part, offsets], 0))

    def folded(cache):
        return jnp.concatenate([cache[i * extra : (i + 1) * extra] for i in range(fold)], 1)

    half = HD // 2
    freq = jnp.exp(-math.log(1000000.0) * jnp.arange(half, dtype=jnp.float32) * 2.0 / (2 * half))
    q_ids = jnp.stack([(plane ^ k) * crew + inner for k in range(heads)]).astype(jnp.int32)
    token_ids = q_ids[:, None] * tok + jnp.arange(tok, dtype=jnp.int32) + begin
    row_ids = q_ids[:, None] * cache_rows + jnp.arange(cache_rows, dtype=jnp.int32)
    angle = jnp.concatenate([token_ids, row_ids], 1).astype(jnp.float32)[..., None] * freq
    cosine, sine = jnp.cos(angle), jnp.sin(angle)
    cosine = jnp.concatenate([cosine, cosine], -1)
    sine = jnp.concatenate([-sine, sine], -1)

    count = wide // FEATS
    groups = [[i * crew + j for j in range(crew)] for i in range(heads)]
    if squared:

        def sides(value, name):
            return swap(value, "tp", tp, 1, f"side_{name}")

        def line(value, name):
            return swap(value, "seq", seq, 2, f"line_{name}")

        def core(value, name):
            return swap(value, "seq", seq, 1, f"core_{name}")

        depth = w_qkv.shape[0]
        w_sent = [jnp.concatenate([w, folded(c)], 0) for w, c in zip(w_cut, caches)]
        w_own = w_cut[0][None]
        w_1, w_2 = across(w_sent[1], 1, "w"), across(w_sent[2], 2, "w")
        far, next_x = across(own, 2, "x_far"), across(own, 1, "x_next")
        own_side, w_line = sides(own, "own"), line(w_own, "w0")
        w_mid, *cache_mid = unpack([], [w_1, w_2], depth, fold)
        own, own_side, next_x, far, w_mid, cache_mid, w_3, w_line, cosine, sine = (
            lax.optimization_barrier(
                (own, own_side, next_x, far, w_mid, cache_mid, w_sent[3], w_line, cosine, sine)
            )
        )
        w_3 = across(w_3, 3, "w")
        last = across(far, 1, "x_last")
        next_side, far_side = sides(next_x, "next"), sides(far, "far")
        w_mid_line = line(w_mid, "w12")
        w_last, cache_last = unpack([], [w_3], depth, fold)
        w_last_line = line(w_last, "w3")
        last, next_side, far_side, w_last, w_mid, w_mid_line, w_last_line, w_line = (
            lax.optimization_barrier(
                (last, next_side, far_side, w_last, w_mid, w_mid_line, w_last_line, w_line)
            )
        )
        caches = [caches[0], *cache_mid, cache_last]
        last_side = sides(last, "last")
        w_parts = [w_own, w_mid, w_last, w_line, w_mid_line, w_last_line]
        w_parts += [core(w, "w") for w in w_parts]
        x_chunks = [[own, own_side], [next_x, next_side], [far, far_side], [last, last_side]]
        ids = jnp.arange(count, dtype=jnp.int32)
        x_ids = jnp.concatenate([side * count + ids, (1 - side) * count + ids])
        w_ids = [
            (plane ^ k) * crew + (inner ^ turn) for turn in (0, 2, 1, 3) for k in range(heads)
        ]
        w_ids = jnp.stack(w_ids).astype(jnp.int32)
    else:
        caches = [across(c, k) for k, c in enumerate(caches)]
        members = [
            [(i * crew + j) * tp + t for i in range(heads) for t in range(tp)] for j in range(crew)
        ]
        x_all = lax.all_gather(own, ("seq", "tp"), axis=0, tiled=True, axis_index_groups=members)
        x_chunks = [
            [lax.dynamic_slice_in_dim(x_all, (plane ^ k) * count * tp, count * tp)]
            for k in range(heads)
        ]
        x_ids = jnp.arange(count * tp, dtype=jnp.int32)
        gathered = [
            lax.all_gather(across(w, k), "seq", axis=0, tiled=True, axis_index_groups=groups)
            for k, w in enumerate(w_cut)
        ]
        per = gathered[0].shape[0] // FEATS
        w_parts = [g.reshape(per, FEATS, WIDTH) for g in gathered]
        w_ids = jnp.concatenate(
            [(plane ^ k) * per + jnp.arange(per, dtype=jnp.int32) for k in range(heads)]
        )

    def projected(kind, slots):
        chunks = [x_chunks[k] for k in slots]
        some = [caches[k] for k in slots]
        return project(kind, slots[0], chunks, x_ids, w_parts, w_ids, cosine, sine, some, tok, redo)

    calls = ((0, 1, 2), (3,)) if squared else (tuple(range(heads)),)
    kv_new = [projected("keys_values", slots) for slots in calls]
    queries = [projected("queries", slots) for slots in calls]

    if squared:
        kv_parts, places = [], []
        for mine, some in zip(kv_new, queries):
            far = swap(mine, "seq", seq, 2, "kv_line")
            far, some = lax.optimization_barrier((far, some))
            places += [(len(kv_parts) + n, i) for i in range(mine.shape[0]) for n in range(4)]
            kv_parts += [mine, far, core(mine, "kv"), core(far, "kv_line")]
        turns = (0, 2, 1, 3)
        kv_ids = jnp.stack([(plane ^ k) * crew + (inner ^ turn) for k in range(4) for turn in turns])
        kv_ids = kv_ids.astype(jnp.int32)
    else:
        kv_parts = [
            lax.all_gather(kv_new[0][k : k + 1], "seq", axis=0, tiled=True, axis_index_groups=groups)
            for k in range(heads)
        ]
        places = [(k, i) for k in range(heads) for i in range(crew)]
        kv_ids = jnp.concatenate(
            [(plane ^ k) * crew + jnp.arange(crew, dtype=jnp.int32) for k in range(heads)]
        )

    back = [None] * heads
    for k in reversed(range(heads)):
        some, index = (queries[k // 3], k % 3) if squared else (queries[0], k)
        mixed = attend(k, prefix_len, some, index, q_ids, kv_parts, places, kv_ids, tok)
        back[k] = across(mixed, k, "mixed")
    back = jnp.stack(back)
    columns = [lax.dynamic_index_in_dim(back, plane ^ h, 0, keepdims=False) for h in range(heads)]
    return jnp.concatenate(columns, 1)


def solution(mesh):
    placed = (
        P("seq", "tp"),
        P(),
        P("seq", "tp"),
        P(None, "seq", "tp"),
        P("seq", "tp"),
        P("seq"),
        P(),
    )
    return jax.shard_map(
        functools.partial(per_device, mesh.shape["seq"], mesh.shape["tp"]),
        mesh=mesh,
        in_specs=placed,
        out_specs=P("seq", "tp"),
        check_vma=False,
    )
```

time: 176 us -> 142 us (0.81)
  waiting for transfers between devices: 87.5 us -> 69.5 us
  starting transfers between devices: 35.6 us -> 23 us
  local copies, waits for them, and re-layouts: 7.87 us -> 5.64 us
    ppermute x28 -> x29, waiting for transfers between devices: 87.5 us -> 69.5 us  [swap(): return lax.ppermute(value, axis, [(i, i ^ mask) for i in range(size)])]
    ppermute x28 -> x29, starting transfers between devices: 35.6 us -> 23 us  [swap(): return lax.ppermute(value, axis, [(i, i ^ mask) for i in range(size)])]
    another operation x3 -> x0, other arithmetic: 3.02 us -> none  [the longest x2 2.99 us: per_device(): both = jnp.stack(w_mine[pair:pair + 2] + line[pair:pair + 2])]
    pallas_call x4, Pallas kernels: 18.4 us -> 16 us  [attend(): pl.pallas_call(functools.partial(attend_kernel, slot, tok, places), out_s...]
    unnamed x49 -> x54, local copies, waits for them, and re-layouts: 5.49 us -> 3.24 us
    pallas_call x5 -> x8, Pallas kernels: 18.6 us -> 20.5 us  [the longest x4 20 us: project(): pl.pallas_call(functools.partial(project_kernel, kind, first_slot, tok, r...]
  transfers between devices with their start and end apart: 28 -> 29, of which waited for: 12 -> 10; matrix products, arithmetic and copies ran while one was open for 4% -> 4% of each run, Pallas kernels for 19% -> 23%
where the time goes in v3:
time: 142 us
  waiting for transfers between devices  69.5 us (49%)
  Pallas kernels  36.5 us (26%)
  starting transfers between devices  23 us (16%)
  other arithmetic  5.95 us (4%)
  local copies, waits for them, and re-layouts  5.64 us (4%)
    ppermute x29, waiting for transfers between devices, swap(): return lax.ppermute(value, axis, [(i, i ^ mask) for i in range(size)])  69.5 us
    ppermute x29, starting transfers between devices, swap(): return lax.ppermute(value, axis, [(i, i ^ mask) for i in range(size)])  23 us
    pallas_call x4, Pallas kernels, project(): pl.pallas_call(functools.partial(project_kernel, kind, first_slot, tok, r...  20 us
    pallas_call x4, Pallas kernels, attend(): pl.pallas_call(functools.partial(attend_kernel, slot, tok, places), out_s...  16 us
    unnamed x54, local copies, waits for them, and re-layouts  3.24 us
  transfers between devices with their start and end apart: 29, of which 10 were waited for; matrix products, arithmetic and copies ran while one was open for 4% of the time, Pallas kernels for 23%

profile of v3, /device:TPU:0, one launch (start us, length us, event | category | flops | bytes accessed | tf_op | source)
XLA Modules:
  0.0 141.7 jit_solution(3450448730265465636)
XLA Ops:
  0.0 1.5 %constant_dynamic-slice_fusion = (bf16[256,768]{1,0:T(8,128)(2,1)S(1)}, bf16[256,768]{1,0:T(8,128)(2,1)S(1)}, bf16[256,768]{1,0:T(8,128)(2,1)S(1)}, bf16[256,768]{1,0:T(8,128)(2,1)S(1)}) fusion(bf16[256,3072]{1,0:T(8,128)(2,1)} %param.9, s32[]{:T(128)S(6)} %select_n.56, s32[]{:T(128)S(6)} %select_n.54, s32[]{:T(128)S(6)} %select_n.53, s32[]{:T(128)S(6)} %select_n.55), kind=kLoop, calls=%fused_computation.59 | loop fusion | bytes 3145744 | tf_op jit(solution)/shard_map/dynamic_slice | solution.py:350
  1.6 0.2 squares.1.refs_0_
  1.8 3.0 %collective-permute-start = (f32[136,128]{1,0:T(8,128)S(1)}, f32[136,128]{1,0:T(8,128)S(1)}, u32[]{:S(2)}, u32[]{:S(2)}) collective-permute-start(f32[136,128]{1,0:T(8,128)S(1)} %squares.1.refs_0_), channel_id=1, source_target_pairs={{0,1},{1,0},{2,3},{3,2},{4,5},{5,4},{6,7},{7,6},{8,9},{9,8},{10,11... | collective-permute-start | bytes 208904 | tf_op jit(solution)/shard_map/side_sums/ppermute | solution.py:24
  4.8 1.5 %collective-permute-start.6 = (bf16[1,256,768]{2,1,0:T(8,128)(2,1)S(1)}, bf16[1,256,768]{2,1,0:T(8,128)(2,1)}, u32[]{:S(2)}, u32[]{:S(2)}) collective-permute-start(bf16[1,256,768]{2,1,0:T(8,128)(2,1)S(1)} %bitcast.52), channel_id=1, source_target_pairs={{0,4},{2,6},{4,0},{6,2},{8,12},{10,14},{12,8},{14,10},{16,20},{18,... | collective-permute-start | bytes 1179656 | tf_op jit(solution)/shard_map/line_w0/ppermute | solution.py:24
  6.3 0.0 copy-start.25
  6.4 0.9 fusion.10
  7.2 2.6 %collective-permute-start.5 = (bf16[288,768]{1,0:T(8,128)(2,1)}, bf16[288,768]{1,0:T(8,128)(2,1)S(1)}, u32[]{:S(2)}, u32[]{:S(2)}) collective-permute-start(bf16[288,768]{1,0:T(8,128)(2,1)} %get-tuple-element.86), channel_id=1, source_target_pairs={{0,16},{2,18},{4,20},{6,22},{8,24},{10,26},{12,28},{14,30},{16,0},... | collective-permute-start | bytes 1327112 | tf_op jit(solution)/shard_map/w_2/ppermute | solution.py:24
  9.8 1.6 %collective-permute-start.4 = (bf16[288,768]{1,0:T(8,128)(2,1)S(1)}, bf16[288,768]{1,0:T(8,128)(2,1)S(1)}, u32[]{:S(2)}, u32[]{:S(2)}) collective-permute-start(bf16[288,768]{1,0:T(8,128)(2,1)S(1)} %get-tuple-element.87), channel_id=1, source_target_pairs={{0,8},{2,10},{4,12},{6,14},{8,0},{10,2},{12,4},{14,6},{16,24},{18,... | collective-permute-start | bytes 1327112 | tf_op jit(solution)/shard_map/w_1/ppermute | solution.py:24
  12.0 0.1 broadcast_multiply_fusion.1
  12.1 0.1 iota_add_fusion
  12.2 0.1 add_add_fusion
  12.3 1.4 %fusion.23 = (f32[4,192,64]{2,1,0:T(8,128)S(1)}, f32[4,192,64]{2,1,0:T(8,128)S(1)}, f32[4,192,64]{2,1,0:T(8,128)S(1)}) fusion(f32[64]{0:T(128)S(1)} %multiply_exponential_fusion, f32[4,192]{1,0:T(4,128)S(1)} %add_convert_fusion), kind=kLoop, calls=%fused_computation.39 | loop fusion | flops 98304 | bytes 593152 | tf_op jit(solution)/shard_map/neg | solution.py:380
  13.8 1.2 pad_maximum_fusion.5
  15.0 0.2 norm.1.refs_2_
  15.2 0.4 collective-permute-start.3
  15.6 0.4 collective-permute-start.2
  16.1 24.6 %collective-permute-done.5.refs_1_ = bf16[288,768]{1,0:T(8,128)(2,1)S(1)} collective-permute-done((bf16[288,768]{1,0:T(8,128)(2,1)}, bf16[288,768]{1,0:T(8,128)(2,1)S(1)}, u32[]{:S(2)}, u32[]{:S(2)}) %collective-permute-start.5) | collective-permute-done | bytes 442400 | tf_op jit(solution)/shard_map/w_2/ppermute | solution.py:24
  40.7 0.5 collective-permute-start.1
  41.2 0.1 unpack.2
  41.3 11.8 %collective-permute-done.3.refs_6_ = bf16[8,136,256]{2,1,0:T(8,128)(2,1)S(1)} collective-permute-done((bf16[8,136,256]{2,1,0:T(8,128)(2,1)S(1)}, bf16[8,136,256]{2,1,0:T(8,128)(2,1)S(1)}, u32[]{:S(2)}, u32[]{:S(2)}) %collective-permute-start.3) | collective-permute-done | bytes 557088 | tf_op jit(solution)/shard_map/x_far_2/ppermute | solution.py:24
  53.2 3.5 %collective-permute-start.10 = (bf16[288,768]{1,0:T(8,128)(2,1)S(1)}, bf16[288,768]{1,0:T(8,128)(2,1)S(1)}, u32[]{:S(2)}, u32[]{:S(2)}) collective-permute-start(bf16[288,768]{1,0:T(8,128)(2,1)S(1)} %get-tuple-element.48), channel_id=1, source_target_pairs={{0,24},{2,26},{4,28},{6,30},{8,16},{10,18},{12,20},{14,22},{16,8},... | collective-permute-start | bytes 1327112 | tf_op jit(solution)/shard_map/w_3/ppermute | solution.py:24
  56.7 0.5 collective-permute-start.9
  57.2 1.5 %collective-permute-start.8 = (bf16[8,136,256]{2,1,0:T(8,128)(2,1)S(1)}, bf16[8,136,256]{2,1,0:T(8,128)(2,1)S(1)}, u32[]{:S(2)}, u32[]{:S(2)}) collective-permute-start(bf16[8,136,256]{2,1,0:T(8,128)(2,1)S(1)} %collective-permute-done.2.refs_4_), channel_id=1, source_target_pairs={{0,1},{1,0},{2,3},{3,2},{4,5},{5,4},{6,7},{7,6},{8,9},{9,8},{10,11... | collective-permute-start | bytes 1671176 | tf_op jit(solution)/shard_map/side_next/ppermute | solution.py:24
  58.7 0.5 collective-permute-start.11
  59.2 8.9 %collective-permute-done.10.refs_0_ = bf16[288,768]{1,0:T(8,128)(2,1)S(1)} collective-permute-done((bf16[288,768]{1,0:T(8,128)(2,1)S(1)}, bf16[288,768]{1,0:T(8,128)(2,1)S(1)}, u32[]{:S(2)}, u32[]{:S(2)}) %collective-permute-start.10) | collective-permute-done | bytes 442400 | tf_op jit(solution)/shard_map/w_3/ppermute | solution.py:24
  68.2 0.6 copy-done.11
  68.8 0.5 collective-permute-start.12
  69.3 13.5 %collective-permute-done.8.refs_5_ = bf16[8,136,256]{2,1,0:T(8,128)(2,1)S(1)} collective-permute-done((bf16[8,136,256]{2,1,0:T(8,128)(2,1)S(1)}, bf16[8,136,256]{2,1,0:T(8,128)(2,1)S(1)}, u32[]{:S(2)}, u32[]{:S(2)}) %collective-permute-start.8) | collective-permute-done | bytes 557088 | tf_op jit(solution)/shard_map/side_next/ppermute | solution.py:24
  82.9 2.9 %collective-permute-done.12.refs_13_.refs_9_ = bf16[1,256,768]{2,1,0:T(8,128)(2,1)} collective-permute-done((bf16[1,256,768]{2,1,0:T(8,128)(2,1)S(1)}, bf16[1,256,768]{2,1,0:T(8,128)(2,1)}, u32[]{:S(2)}, u32[]{:S(2)}) %collective-permute-start.12) | collective-permute-done | bytes 393248 | tf_op jit(solution)/shard_map/line_w3/ppermute | solution.py:24
  85.9 0.5 collective-permute-start.17
  86.4 0.0 collective-permute-start.15
  86.4 0.5 collective-permute-start.16
  86.9 0.7 copy-done.15
  87.6 0.0 collective-permute-start.18
  87.7 0.7 stack.110.refs_1_
  88.3 0.6 pad_maximum_fusion.7.refs_22_
  89.0 2.1 %collective-permute-done.15.refs_16_.refs_12_ = bf16[1,256,768]{2,1,0:T(8,128)(2,1)} collective-permute-done((bf16[1,256,768]{2,1,0:T(8,128)(2,1)S(1)}, bf16[1,256,768]{2,1,0:T(8,128)(2,1)}, u32[]{:S(2)}, u32[]{:S(2)}) %collective-permute-start.15) | collective-permute-done | bytes 393248 | tf_op jit(solution)/shard_map/core_w/ppermute | solution.py:24
  91.1 0.5 collective-permute-start.22
  91.6 0.6 pad_add_fusion.1.refs_0_
  92.3 0.7 copy-done.16
  93.0 0.3 copy-done.13
  93.2 5.4 %keys_values.2.refs_4_ = bf16[3,192,256]{2,1,0:T(8,128)(2,1)} custom-call(s32[16]{0:T(128)} %pad_add_fusion.1.refs_0_, s32[16]{0:T(128)} %stack.110.refs_1_, bf16[8,136,256]{2,1,0:T(8,128)(2,1)} %copy-done.2, bf16[8,136,256]{2,1,0:T(8,128)(2,1)} %copy-done.19, bf16[8,136,256]{2,1,0:T(8,128)(2,1)} %copy-done.18, bf16[8,136,256]{2,1,0:T(8,128)(2,1)} %copy-done.22, ...), custom_call_target="tpu_custom_call" | custom-call | flops 905969664 | bytes 5636096 | tf_op jit(solution)/shard_map/keys_values/pallas_call | solution.py:180
  98.7 0.5 collective-permute-start.19
  99.2 6.5 %queries.2.refs_3_ = bf16[3,4,128,128]{3,2,1,0:T(8,128)(2,1)} custom-call(s32[16]{0:T(128)} %pad_add_fusion.1.refs_0_, s32[16]{0:T(128)} %stack.110.refs_1_, bf16[8,136,256]{2,1,0:T(8,128)(2,1)} %copy-done.2, bf16[8,136,256]{2,1,0:T(8,128)(2,1)} %copy-done.19, bf16[8,136,256]{2,1,0:T(8,128)(2,1)} %copy-done.18, bf16[8,136,256]{2,1,0:T(8,128)(2,1)} %copy-done.22, ...), custom_call_target="tpu_custom_call" | custom-call | flops 1811939328 | bytes 7733248 | tf_op jit(solution)/shard_map/queries/pallas_call | solution.py:180
  105.7 1.9 %collective-permute-done.19.refs_5_ = bf16[3,192,256]{2,1,0:T(8,128)(2,1)S(1)} collective-permute-done((bf16[3,192,256]{2,1,0:T(8,128)(2,1)}, bf16[3,192,256]{2,1,0:T(8,128)(2,1)S(1)}, u32[]{:S(2)}, u32[]{:S(2)}) %collective-permute-start.19) | collective-permute-done | bytes 294944 | tf_op jit(solution)/shard_map/kv_line/ppermute | solution.py:24
  107.7 0.8 copy-done.23
  108.5 3.7 %keys_values.3.refs_8_ = bf16[1,192,256]{2,1,0:T(8,128)(2,1)} custom-call(s32[16]{0:T(128)} %pad_add_fusion.1.refs_0_, s32[16]{0:T(128)} %stack.110.refs_1_, bf16[8,136,256]{2,1,0:T(8,128)(2,1)} %copy-done.20, bf16[8,136,256]{2,1,0:T(8,128)(2,1)} %copy-done.23, bf16[1,256,768]{2,1,0:T(8,128)(2,1)} %bitcast.56, bf16[2,256,768]{2,1,0:T(8,128)(2,1)} %copy-done, ...), custom_call_target="tpu_custom_call" | custom-call | flops 301989888 | bytes 3276800 | tf_op jit(solution)/shard_map/keys_values/pallas_call | solution.py:180
  112.1 0.6 collective-permute-start.23
  112.8 0.2 collective-permute-start.24
  113.0 4.4 %queries.3.refs_3_ = bf16[1,4,128,128]{3,2,1,0:T(8,128)(2,1)} custom-call(s32[16]{0:T(128)} %pad_add_fusion.1.refs_0_, s32[16]{0:T(128)} %stack.110.refs_1_, bf16[8,136,256]{2,1,0:T(8,128)(2,1)} %copy-done.20, bf16[8,136,256]{2,1,0:T(8,128)(2,1)} %copy-done.23, bf16[1,256,768]{2,1,0:T(8,128)(2,1)} %bitcast.57, bf16[2,256,768]{2,1,0:T(8,128)(2,1)} %copy-done, ...), custom_call_target="tpu_custom_call" | custom-call | flops 603979776 | bytes 5373952 | tf_op jit(solution)/shard_map/queries/pallas_call | solution.py:180
  117.4 0.3 collective-permute-done.23.refs_9_
  117.6 0.1 collective-permute-start.25
  117.7 0.1 stack.109.refs_2_
  117.8 1.1 collective-permute-done.25.refs_11_
  119.0 3.8 %attend.5 = bf16[128,512]{1,0:T(8,128)(2,1)S(1)} custom-call(s32[1]{0:T(128)} %copy.8.refs_0_, s32[4]{0:T(128)S(1)} %get-tuple-element.68.refs_1_, s32[16]{0:T(128)S(1)} %stack.109.refs_2_, bf16[3,4,128,128]{3,2,1,0:T(8,128)(2,1)S(1)} %copy-done.4, bf16[3,192,256]{2,1,0:T(8,128)(2,1)S(1)} %copy-done.5, ...), custom_call_target="tpu_custom_call" | custom-call | flops 805306368 | bytes 1572864 | tf_op jit(solution)/shard_map/attend/pallas_call | solution.py:312
  122.7 1.2 collective-permute-start.26
  123.9 4.2 %attend.6 = bf16[128,512]{1,0:T(8,128)(2,1)S(1)} custom-call(s32[1]{0:T(128)} %copy.8.refs_0_, s32[4]{0:T(128)S(1)} %get-tuple-element.68.refs_1_, s32[16]{0:T(128)S(1)} %stack.109.refs_2_, bf16[3,4,128,128]{3,2,1,0:T(8,128)(2,1)S(1)} %copy-done.4, bf16[3,192,256]{2,1,0:T(8,128)(2,1)S(1)} %copy-done.5, ...), custom_call_target="tpu_custom_call" | custom-call | flops 805306368 | bytes 1572864 | tf_op jit(solution)/shard_map/attend/pallas_call | solution.py:312
  128.2 0.1 collective-permute-start.27
  128.2 4.8 %attend.7 = bf16[128,512]{1,0:T(8,128)(2,1)S(1)} custom-call(s32[1]{0:T(128)} %copy.8.refs_0_, s32[4]{0:T(128)S(1)} %get-tuple-element.68.refs_1_, s32[16]{0:T(128)S(1)} %stack.109.refs_2_, bf16[1,4,128,128]{3,2,1,0:T(8,128)(2,1)S(1)} %copy-done.6, bf16[3,192,256]{2,1,0:T(8,128)(2,1)S(1)} %copy-done.5, ...), custom_call_target="tpu_custom_call" | custom-call | flops 805306368 | bytes 1572864 | tf_op jit(solution)/shard_map/attend/pallas_call | solution.py:312
  133.1 2.1 %collective-permute-start.28 = (bf16[128,512]{1,0:T(8,128)(2,1)S(1)}, bf16[128,512]{1,0:T(8,128)(2,1)S(1)}, u32[]{:S(2)}, u32[]{:S(2)}) collective-permute-start(bf16[128,512]{1,0:T(8,128)(2,1)S(1)} %attend.7), channel_id=1, source_target_pairs={{0,24},{2,26},{4,28},{6,30},{8,16},{10,18},{12,20},{14,22},{16,8},... | collective-permute-start | bytes 393224 | tf_op jit(solution)/shard_map/mixed_3/ppermute | solution.py:24
  135.2 3.2 %attend.4 = bf16[128,512]{1,0:T(8,128)(2,1)S(1)} custom-call(s32[1]{0:T(128)} %copy.8.refs_0_, s32[4]{0:T(128)S(1)} %get-tuple-element.68.refs_1_, s32[16]{0:T(128)S(1)} %stack.109.refs_2_, bf16[3,4,128,128]{3,2,1,0:T(8,128)(2,1)S(1)} %copy-done.4, bf16[3,192,256]{2,1,0:T(8,128)(2,1)S(1)} %copy-done.5, ...), custom_call_target="tpu_custom_call" | custom-call | flops 805306368 | bytes 1572864 | tf_op jit(solution)/shard_map/attend/pallas_call | solution.py:312
  138.4 2.4 %collective-permute-done.27 = bf16[128,512]{1,0:T(8,128)(2,1)S(1)} collective-permute-done((bf16[128,512]{1,0:T(8,128)(2,1)S(1)}, bf16[128,512]{1,0:T(8,128)(2,1)S(1)}, u32[]{:S(2)}, u32[]{:S(2)}) %collective-permute-start.27) | collective-permute-done | bytes 131104 | tf_op jit(solution)/shard_map/mixed_2/ppermute | solution.py:24
  140.8 0.1 pad_maximum_fusion.3
  140.9 0.8 pad_maximum_fusion.4
  (84 shorter events, 0.3 us)
Async XLA Ops:
  0.0 1.6 %copy-start.3 = (bf16[128,2048]{1,0:T(8,128)(2,1)S(1)}, bf16[128,2048]{1,0:T(8,128)(2,1)}, u32[]{:S(2)}) copy-start(bf16[128,2048]{1,0:T(8,128)(2,1)} %stream.1) | copy-start | bytes 1572868
  0.0 1.6 %copy-start.7 = (bf16[8,2048]{1,0:T(8,128)(2,1)S(1)}, bf16[8,2048]{1,0:T(8,128)(2,1)}, u32[]{:S(2)}) copy-start(bf16[8,2048]{1,0:T(8,128)(2,1)} %hidden.3) | copy-start | bytes 98308
  0.0 6.3 %copy-start.26 = (s32[8]{0:T(128)S(1)}, s32[8]{0:T(128)}, u32[]{:S(2)}) copy-start(s32[8]{0:T(128)} %param.12) | copy-start | bytes 100
  0.0 6.3 %copy-start.24 = (bf16[2,64,512]{2,1,0:T(8,128)(2,1)S(1)}, bf16[2,64,512]{2,1,0:T(8,128)(2,1)}, u32[]{:S(2)}) copy-start(bf16[2,64,512]{2,1,0:T(8,128)(2,1)} %param.10) | copy-start | bytes 393220
  1.5 81.3 %copy-start.14 = (bf16[256,768]{1,0:T(8,128)(2,1)}, bf16[256,768]{1,0:T(8,128)(2,1)S(1)}, u32[]{:S(2)}) copy-start(bf16[256,768]{1,0:T(8,128)(2,1)S(1)} %get-tuple-element.43) | copy-start | bytes 1179652
  1.8 13.3 %collective-permute-start = (f32[136,128]{1,0:T(8,128)S(1)}, f32[136,128]{1,0:T(8,128)S(1)}, u32[]{:S(2)}, u32[]{:S(2)}) collective-permute-start(f32[136,128]{1,0:T(8,128)S(1)} %squares.1.refs_0_), channel_id=1, source_target_pairs={{0,1},{1,0},{2,3},{3,2},{4,5},{5,4},{6,7},{7,6},{8,9},{9,8},{10,11... | collective-permute-start | bytes 208904 | tf_op jit(solution)/shard_map/side_sums/ppermute | solution.py:24
  4.8 36.6 %collective-permute-start.6 = (bf16[1,256,768]{2,1,0:T(8,128)(2,1)S(1)}, bf16[1,256,768]{2,1,0:T(8,128)(2,1)}, u32[]{:S(2)}, u32[]{:S(2)}) collective-permute-start(bf16[1,256,768]{2,1,0:T(8,128)(2,1)S(1)} %bitcast.52), channel_id=1, source_target_pairs={{0,4},{2,6},{4,0},{6,2},{8,12},{10,14},{12,8},{14,10},{16,20},{18,... | collective-permute-start | bytes 1179656 | tf_op jit(solution)/shard_map/line_w0/ppermute | solution.py:24
  6.3 6.0 %copy-start.25 = (f32[4096]{0:T(1024)S(1)}, f32[4096]{0:T(1024)}, u32[]{:S(2)}) copy-start(f32[4096]{0:T(1024)} %param.8) | copy-start | bytes 49156
  7.2 33.5 %collective-permute-start.5 = (bf16[288,768]{1,0:T(8,128)(2,1)}, bf16[288,768]{1,0:T(8,128)(2,1)S(1)}, u32[]{:S(2)}, u32[]{:S(2)}) collective-permute-start(bf16[288,768]{1,0:T(8,128)(2,1)} %get-tuple-element.86), channel_id=1, source_target_pairs={{0,16},{2,18},{4,20},{6,22},{8,24},{10,26},{12,28},{14,30},{16,0},... | collective-permute-start | bytes 1327112 | tf_op jit(solution)/shard_map/w_2/ppermute | solution.py:24
  9.8 31.4 %collective-permute-start.4 = (bf16[288,768]{1,0:T(8,128)(2,1)S(1)}, bf16[288,768]{1,0:T(8,128)(2,1)S(1)}, u32[]{:S(2)}, u32[]{:S(2)}) collective-permute-start(bf16[288,768]{1,0:T(8,128)(2,1)S(1)} %get-tuple-element.87), channel_id=1, source_target_pairs={{0,8},{2,10},{4,12},{6,14},{8,0},{10,2},{12,4},{14,6},{16,24},{18,... | collective-permute-start | bytes 1327112 | tf_op jit(solution)/shard_map/w_1/ppermute | solution.py:24
  15.2 26.1 %copy-start.2 = (bf16[8,136,256]{2,1,0:T(8,128)(2,1)}, bf16[8,136,256]{2,1,0:T(8,128)(2,1)S(1)}, u32[]{:S(2)}) copy-start(bf16[8,136,256]{2,1,0:T(8,128)(2,1)S(1)} %norm.1.refs_2_) | copy-start | bytes 1671172
  15.2 37.9 %collective-permute-start.3 = (bf16[8,136,256]{2,1,0:T(8,128)(2,1)S(1)}, bf16[8,136,256]{2,1,0:T(8,128)(2,1)S(1)}, u32[]{:S(2)}, u32[]{:S(2)}) collective-permute-start(bf16[8,136,256]{2,1,0:T(8,128)(2,1)S(1)} %norm.1.refs_2_), channel_id=1, source_target_pairs={{0,16},{2,18},{4,20},{6,22},{8,24},{10,26},{12,28},{14,30},{16,0},... | collective-permute-start | bytes 1671176 | tf_op jit(solution)/shard_map/x_far_2/ppermute | solution.py:24
  15.6 37.5 %collective-permute-start.2 = (bf16[8,136,256]{2,1,0:T(8,128)(2,1)S(1)}, bf16[8,136,256]{2,1,0:T(8,128)(2,1)S(1)}, u32[]{:S(2)}, u32[]{:S(2)}) collective-permute-start(bf16[8,136,256]{2,1,0:T(8,128)(2,1)S(1)} %norm.1.refs_2_), channel_id=1, source_target_pairs={{0,8},{2,10},{4,12},{6,14},{8,0},{10,2},{12,4},{14,6},{16,24},{18,... | collective-permute-start | bytes 1671176 | tf_op jit(solution)/shard_map/x_next_1/ppermute | solution.py:24
  40.7 12.4 %collective-permute-start.1 = (bf16[8,136,256]{2,1,0:T(8,128)(2,1)S(1)}, bf16[8,136,256]{2,1,0:T(8,128)(2,1)S(1)}, u32[]{:S(2)}, u32[]{:S(2)}) collective-permute-start(bf16[8,136,256]{2,1,0:T(8,128)(2,1)S(1)} %norm.1.refs_2_), channel_id=1, source_target_pairs={{0,1},{1,0},{2,3},{3,2},{4,5},{5,4},{6,7},{7,6},{8,9},{9,8},{10,11... | collective-permute-start | bytes 1671176 | tf_op jit(solution)/shard_map/side_own/ppermute | solution.py:24
  41.3 26.8 %copy-start.9 = (bf16[96,256]{1,0:T(8,128)(2,1)}, bf16[96,256]{1,0:T(8,128)(2,1)S(1)}, u32[]{:S(2)}) copy-start(bf16[96,256]{1,0:T(8,128)(2,1)S(1)} %get-tuple-element.61.refs_23_) | copy-start | bytes 147460
  41.3 26.8 %copy-start.10 = (bf16[96,256]{1,0:T(8,128)(2,1)}, bf16[96,256]{1,0:T(8,128)(2,1)S(1)}, u32[]{:S(2)}) copy-start(bf16[96,256]{1,0:T(8,128)(2,1)S(1)} %get-tuple-element.62.refs_24_) | copy-start | bytes 147460
  41.3 44.5 %copy-start = (bf16[2,256,768]{2,1,0:T(8,128)(2,1)}, bf16[2,256,768]{2,1,0:T(8,128)(2,1)S(1)}, u32[]{:S(2)}) copy-start(bf16[2,256,768]{2,1,0:T(8,128)(2,1)S(1)} %get-tuple-element.54.refs_9_.refs_5_) | copy-start | bytes 2359300
  53.1 15.0 %copy-start.17 = (bf16[8,136,256]{2,1,0:T(8,128)(2,1)}, bf16[8,136,256]{2,1,0:T(8,128)(2,1)S(1)}, u32[]{:S(2)}) copy-start(bf16[8,136,256]{2,1,0:T(8,128)(2,1)S(1)} %collective-permute-done.3.refs_6_) | copy-start | bytes 1671172
  53.1 15.0 %copy-start.18 = (bf16[8,136,256]{2,1,0:T(8,128)(2,1)}, bf16[8,136,256]{2,1,0:T(8,128)(2,1)S(1)}, u32[]{:S(2)}) copy-start(bf16[8,136,256]{2,1,0:T(8,128)(2,1)S(1)} %collective-permute-done.2.refs_4_) | copy-start | bytes 1671172
  53.1 6.1 %copy-start.19 = (bf16[8,136,256]{2,1,0:T(8,128)(2,1)}, bf16[8,136,256]{2,1,0:T(8,128)(2,1)S(1)}, u32[]{:S(2)}) copy-start(bf16[8,136,256]{2,1,0:T(8,128)(2,1)S(1)} %collective-permute-done.1.refs_3_) | copy-start | bytes 1671172
  53.2 15.0 %collective-permute-start.10 = (bf16[288,768]{1,0:T(8,128)(2,1)S(1)}, bf16[288,768]{1,0:T(8,128)(2,1)S(1)}, u32[]{:S(2)}, u32[]{:S(2)}) collective-permute-start(bf16[288,768]{1,0:T(8,128)(2,1)S(1)} %get-tuple-element.48), channel_id=1, source_target_pairs={{0,24},{2,26},{4,28},{6,30},{8,16},{10,18},{12,20},{14,22},{16,8},... | collective-permute-start | bytes 1327112 | tf_op jit(solution)/shard_map/w_3/ppermute | solution.py:24
  56.7 26.2 %collective-permute-start.9 = (bf16[8,136,256]{2,1,0:T(8,128)(2,1)S(1)}, bf16[8,136,256]{2,1,0:T(8,128)(2,1)S(1)}, u32[]{:S(2)}, u32[]{:S(2)}) collective-permute-start(bf16[8,136,256]{2,1,0:T(8,128)(2,1)S(1)} %collective-permute-done.3.refs_6_), channel_id=1, source_target_pairs={{0,1},{1,0},{2,3},{3,2},{4,5},{5,4},{6,7},{7,6},{8,9},{9,8},{10,11... | collective-permute-start | bytes 1671176 | tf_op jit(solution)/shard_map/side_far/ppermute | solution.py:24
  57.2 25.7 %collective-permute-start.7 = (bf16[8,136,256]{2,1,0:T(8,128)(2,1)S(1)}, bf16[8,136,256]{2,1,0:T(8,128)(2,1)S(1)}, u32[]{:S(2)}, u32[]{:S(2)}) collective-permute-start(bf16[8,136,256]{2,1,0:T(8,128)(2,1)S(1)} %collective-permute-done.3.refs_6_), channel_id=1, source_target_pairs={{0,8},{2,10},{4,12},{6,14},{8,0},{10,2},{12,4},{14,6},{16,24},{18,... | collective-permute-start | bytes 1671176 | tf_op jit(solution)/shard_map/x_last_1/ppermute | solution.py:24
  57.2 25.7 %collective-permute-start.8 = (bf16[8,136,256]{2,1,0:T(8,128)(2,1)S(1)}, bf16[8,136,256]{2,1,0:T(8,128)(2,1)S(1)}, u32[]{:S(2)}, u32[]{:S(2)}) collective-permute-start(bf16[8,136,256]{2,1,0:T(8,128)(2,1)S(1)} %collective-permute-done.2.refs_4_), channel_id=1, source_target_pairs={{0,1},{1,0},{2,3},{3,2},{4,5},{5,4},{6,7},{7,6},{8,9},{9,8},{10,11... | collective-permute-start | bytes 1671176 | tf_op jit(solution)/shard_map/side_next/ppermute | solution.py:24
  58.7 24.2 %collective-permute-start.11 = (bf16[2,256,768]{2,1,0:T(8,128)(2,1)S(1)}, bf16[2,256,768]{2,1,0:T(8,128)(2,1)S(1)}, u32[]{:S(2)}, u32[]{:S(2)}) collective-permute-start(bf16[2,256,768]{2,1,0:T(8,128)(2,1)S(1)} %get-tuple-element.54.refs_9_.refs_5_), channel_id=1, source_target_pairs={{0,4},{2,6},{4,0},{6,2},{8,12},{10,14},{12,8},{14,10},{16,20},{18,... | collective-permute-start | bytes 2359304 | tf_op jit(solution)/shard_map/line_w12/ppermute | solution.py:24
  68.2 0.6 copy-start.11
  68.8 23.4 %copy-start.1 = (bf16[1,256,768]{2,1,0:T(8,128)(2,1)}, bf16[1,256,768]{2,1,0:T(8,128)(2,1)S(1)}, u32[]{:S(2)}) copy-start(bf16[1,256,768]{2,1,0:T(8,128)(2,1)S(1)} %get-tuple-element.55.refs_10_.refs_6_) | copy-start | bytes 1179652
  68.8 17.0 %collective-permute-start.12 = (bf16[1,256,768]{2,1,0:T(8,128)(2,1)S(1)}, bf16[1,256,768]{2,1,0:T(8,128)(2,1)}, u32[]{:S(2)}, u32[]{:S(2)}) collective-permute-start(bf16[1,256,768]{2,1,0:T(8,128)(2,1)S(1)} %get-tuple-element.55.refs_10_.refs_6_), channel_id=1, source_target_pairs={{0,4},{2,6},{4,0},{6,2},{8,12},{10,14},{12,8},{14,10},{16,20},{18,... | collective-permute-start | bytes 1179656 | tf_op jit(solution)/shard_map/line_w3/ppermute | solution.py:24
  82.9 4.0 %copy-start.22 = (bf16[8,136,256]{2,1,0:T(8,128)(2,1)}, bf16[8,136,256]{2,1,0:T(8,128)(2,1)S(1)}, u32[]{:S(2)}) copy-start(bf16[8,136,256]{2,1,0:T(8,128)(2,1)S(1)} %collective-permute-done.8.refs_5_) | copy-start | bytes 1671172
  82.9 4.0 %collective-permute-start.13 = (bf16[1,256,768]{2,1,0:T(8,128)(2,1)S(1)}, bf16[1,256,768]{2,1,0:T(8,128)(2,1)S(1)}, u32[]{:S(2)}, u32[]{:S(2)}) collective-permute-start(bf16[1,256,768]{2,1,0:T(8,128)(2,1)S(1)} %bitcast.53), channel_id=1, source_target_pairs={{0,2},{2,0},{4,6},{6,4},{8,10},{10,8},{12,14},{14,12},{16,18},{18,... | collective-permute-start | bytes 1179656 | tf_op jit(solution)/shard_map/core_w/ppermute | solution.py:24
  82.9 4.0 %copy-start.21 = (bf16[8,136,256]{2,1,0:T(8,128)(2,1)}, bf16[8,136,256]{2,1,0:T(8,128)(2,1)S(1)}, u32[]{:S(2)}) copy-start(bf16[8,136,256]{2,1,0:T(8,128)(2,1)S(1)} %collective-permute-done.9.refs_7_) | copy-start | bytes 1671172
  82.9 4.0 %copy-start.20 = (bf16[8,136,256]{2,1,0:T(8,128)(2,1)}, bf16[8,136,256]{2,1,0:T(8,128)(2,1)S(1)}, u32[]{:S(2)}) copy-start(bf16[8,136,256]{2,1,0:T(8,128)(2,1)S(1)} %collective-permute-done.7.refs_2_) | copy-start | bytes 1671172
  82.9 9.3 %copy-start.12 = (bf16[2,256,768]{2,1,0:T(8,128)(2,1)}, bf16[2,256,768]{2,1,0:T(8,128)(2,1)S(1)}, u32[]{:S(2)}) copy-start(bf16[2,256,768]{2,1,0:T(8,128)(2,1)S(1)} %collective-permute-done.11.refs_12_.refs_8_) | copy-start | bytes 2359300
  85.9 6.4 %collective-permute-start.14 = (bf16[2,256,768]{2,1,0:T(8,128)(2,1)S(1)}, bf16[2,256,768]{2,1,0:T(8,128)(2,1)S(1)}, u32[]{:S(2)}, u32[]{:S(2)}) collective-permute-start(bf16[2,256,768]{2,1,0:T(8,128)(2,1)S(1)} %get-tuple-element.54.refs_9_.refs_5_), channel_id=1, source_target_pairs={{0,2},{2,0},{4,6},{6,4},{8,10},{10,8},{12,14},{14,12},{16,18},{18,... | collective-permute-start | bytes 2359304 | tf_op jit(solution)/shard_map/core_w/ppermute | solution.py:24
  85.9 6.4 %collective-permute-start.17 = (bf16[2,256,768]{2,1,0:T(8,128)(2,1)S(1)}, bf16[2,256,768]{2,1,0:T(8,128)(2,1)}, u32[]{:S(2)}, u32[]{:S(2)}) collective-permute-start(bf16[2,256,768]{2,1,0:T(8,128)(2,1)S(1)} %collective-permute-done.11.refs_12_.refs_8_), channel_id=1, source_target_pairs={{0,2},{2,0},{4,6},{6,4},{8,10},{10,8},{12,14},{14,12},{16,18},{18,... | collective-permute-start | bytes 2359304 | tf_op jit(solution)/shard_map/core_w/ppermute | solution.py:24
  86.4 4.7 %collective-permute-start.15 = (bf16[1,256,768]{2,1,0:T(8,128)(2,1)S(1)}, bf16[1,256,768]{2,1,0:T(8,128)(2,1)}, u32[]{:S(2)}, u32[]{:S(2)}) collective-permute-start(bf16[1,256,768]{2,1,0:T(8,128)(2,1)S(1)} %get-tuple-element.55.refs_10_.refs_6_), channel_id=1, source_target_pairs={{0,2},{2,0},{4,6},{6,4},{8,10},{10,8},{12,14},{14,12},{16,18},{18,... | collective-permute-start | bytes 1179656 | tf_op jit(solution)/shard_map/core_w/ppermute | solution.py:24
  86.4 5.8 %collective-permute-start.16 = (bf16[1,256,768]{2,1,0:T(8,128)(2,1)}, bf16[1,256,768]{2,1,0:T(8,128)(2,1)}, u32[]{:S(2)}, u32[]{:S(2)}) collective-permute-start(bf16[1,256,768]{2,1,0:T(8,128)(2,1)} %collective-permute-done.6.refs_11_.refs_7_), channel_id=1, source_target_pairs={{0,2},{2,0},{4,6},{6,4},{8,10},{10,8},{12,14},{14,12},{16,18},{18,... | collective-permute-start | bytes 1179656 | tf_op jit(solution)/shard_map/core_w/ppermute | solution.py:24
  86.9 0.7 copy-start.15
  87.6 4.6 %collective-permute-start.18 = (bf16[1,256,768]{2,1,0:T(8,128)(2,1)}, bf16[1,256,768]{2,1,0:T(8,128)(2,1)S(1)}, u32[]{:S(2)}, u32[]{:S(2)}) collective-permute-start(bf16[1,256,768]{2,1,0:T(8,128)(2,1)} %collective-permute-done.12.refs_13_.refs_9_), channel_id=1, source_target_pairs={{0,2},{2,0},{4,6},{6,4},{8,10},{10,8},{12,14},{14,12},{16,18},{18,... | collective-permute-start | bytes 1179656 | tf_op jit(solution)/shard_map/core_w/ppermute | solution.py:24
  91.1 16.6 %collective-permute-start.22 = (bf16[8,136,256]{2,1,0:T(8,128)(2,1)}, bf16[8,136,256]{2,1,0:T(8,128)(2,1)S(1)}, u32[]{:S(2)}, u32[]{:S(2)}) collective-permute-start(bf16[8,136,256]{2,1,0:T(8,128)(2,1)} %copy-done.20), channel_id=1, source_target_pairs={{0,1},{1,0},{2,3},{3,2},{4,5},{5,4},{6,7},{7,6},{8,9},{9,8},{10,11... | collective-permute-start | bytes 1671176 | tf_op jit(solution)/shard_map/side_last/ppermute | solution.py:24
  92.2 0.7 copy-start.16
  92.2 1.0 copy-start.13
  98.7 9.0 %collective-permute-start.19 = (bf16[3,192,256]{2,1,0:T(8,128)(2,1)}, bf16[3,192,256]{2,1,0:T(8,128)(2,1)S(1)}, u32[]{:S(2)}, u32[]{:S(2)}) collective-permute-start(bf16[3,192,256]{2,1,0:T(8,128)(2,1)} %keys_values.2.refs_4_), channel_id=1, source_target_pairs={{0,4},{2,6},{4,0},{6,2},{8,12},{10,14},{12,8},{14,10},{16,20},{18,... | collective-permute-start | bytes 884744 | tf_op jit(solution)/shard_map/kv_line/ppermute | solution.py:24
  99.2 19.7 %collective-permute-start.20 = (bf16[3,192,256]{2,1,0:T(8,128)(2,1)}, bf16[3,192,256]{2,1,0:T(8,128)(2,1)S(1)}, u32[]{:S(2)}, u32[]{:S(2)}) collective-permute-start(bf16[3,192,256]{2,1,0:T(8,128)(2,1)} %keys_values.2.refs_4_), channel_id=1, source_target_pairs={{0,2},{2,0},{4,6},{6,4},{8,10},{10,8},{12,14},{14,12},{16,18},{18,... | collective-permute-start | bytes 884744 | tf_op jit(solution)/shard_map/core_kv/ppermute | solution.py:24
  107.7 11.3 %collective-permute-start.21 = (bf16[3,192,256]{2,1,0:T(8,128)(2,1)S(1)}, bf16[3,192,256]{2,1,0:T(8,128)(2,1)S(1)}, u32[]{:S(2)}, u32[]{:S(2)}) collective-permute-start(bf16[3,192,256]{2,1,0:T(8,128)(2,1)S(1)} %collective-permute-done.19.refs_5_), channel_id=1, source_target_pairs={{0,2},{2,0},{4,6},{6,4},{8,10},{10,8},{12,14},{14,12},{16,18},{18,... | collective-permute-start | bytes 884744 | tf_op jit(solution)/shard_map/core_kv_line/ppermute | solution.py:24
  107.7 0.8 copy-start.23
  112.1 6.8 %copy-start.4 = (bf16[3,4,128,128]{3,2,1,0:T(8,128)(2,1)S(1)}, bf16[3,4,128,128]{3,2,1,0:T(8,128)(2,1)}, u32[]{:S(2)}) copy-start(bf16[3,4,128,128]{3,2,1,0:T(8,128)(2,1)} %queries.2.refs_3_) | copy-start | bytes 1179652
  112.1 6.8 %copy-start.5 = (bf16[3,192,256]{2,1,0:T(8,128)(2,1)S(1)}, bf16[3,192,256]{2,1,0:T(8,128)(2,1)}, u32[]{:S(2)}) copy-start(bf16[3,192,256]{2,1,0:T(8,128)(2,1)} %keys_values.2.refs_4_) | copy-start | bytes 884740
  112.1 6.8 %copy-start.8 = (bf16[1,192,256]{2,1,0:T(8,128)(2,1)S(1)}, bf16[1,192,256]{2,1,0:T(8,128)(2,1)}, u32[]{:S(2)}) copy-start(bf16[1,192,256]{2,1,0:T(8,128)(2,1)} %keys_values.3.refs_8_) | copy-start | bytes 294916
  112.1 5.5 %collective-permute-start.23 = (bf16[1,192,256]{2,1,0:T(8,128)(2,1)}, bf16[1,192,256]{2,1,0:T(8,128)(2,1)S(1)}, u32[]{:S(2)}, u32[]{:S(2)}) collective-permute-start(bf16[1,192,256]{2,1,0:T(8,128)(2,1)} %keys_values.3.refs_8_), channel_id=1, source_target_pairs={{0,4},{2,6},{4,0},{6,2},{8,12},{10,14},{12,8},{14,10},{16,20},{18,... | collective-permute-start | bytes 294920 | tf_op jit(solution)/shard_map/kv_line/ppermute | solution.py:24
  112.8 5.1 %collective-permute-start.24 = (bf16[1,192,256]{2,1,0:T(8,128)(2,1)}, bf16[1,192,256]{2,1,0:T(8,128)(2,1)S(1)}, u32[]{:S(2)}, u32[]{:S(2)}) collective-permute-start(bf16[1,192,256]{2,1,0:T(8,128)(2,1)} %keys_values.3.refs_8_), channel_id=1, source_target_pairs={{0,2},{2,0},{4,6},{6,4},{8,10},{10,8},{12,14},{14,12},{16,18},{18,... | collective-permute-start | bytes 294920 | tf_op jit(solution)/shard_map/core_kv/ppermute | solution.py:24
  117.6 1.3 collective-permute-start.25
  122.7 5.5 %copy-start.6 = (bf16[1,4,128,128]{3,2,1,0:T(8,128)(2,1)S(1)}, bf16[1,4,128,128]{3,2,1,0:T(8,128)(2,1)}, u32[]{:S(2)}) copy-start(bf16[1,4,128,128]{3,2,1,0:T(8,128)(2,1)} %queries.3.refs_3_) | copy-start | bytes 393220
  122.7 15.6 %collective-permute-start.26 = (bf16[128,512]{1,0:T(8,128)(2,1)S(1)}, bf16[128,512]{1,0:T(8,128)(2,1)S(1)}, u32[]{:S(2)}, u32[]{:S(2)}) collective-permute-start(bf16[128,512]{1,0:T(8,128)(2,1)S(1)} %attend.5), channel_id=1, source_target_pairs={{0,8},{2,10},{4,12},{6,14},{8,0},{10,2},{12,4},{14,6},{16,24},{18,... | collective-permute-start | bytes 393224 | tf_op jit(solution)/shard_map/mixed_1/ppermute | solution.py:24
  128.2 12.6 %collective-permute-start.27 = (bf16[128,512]{1,0:T(8,128)(2,1)S(1)}, bf16[128,512]{1,0:T(8,128)(2,1)S(1)}, u32[]{:S(2)}, u32[]{:S(2)}) collective-permute-start(bf16[128,512]{1,0:T(8,128)(2,1)S(1)} %attend.6), channel_id=1, source_target_pairs={{0,16},{2,18},{4,20},{6,22},{8,24},{10,26},{12,28},{14,30},{16,0},... | collective-permute-start | bytes 393224 | tf_op jit(solution)/shard_map/mixed_2/ppermute | solution.py:24
  133.1 7.7 %collective-permute-start.28 = (bf16[128,512]{1,0:T(8,128)(2,1)S(1)}, bf16[128,512]{1,0:T(8,128)(2,1)S(1)}, u32[]{:S(2)}, u32[]{:S(2)}) collective-permute-start(bf16[128,512]{1,0:T(8,128)(2,1)S(1)} %attend.7), channel_id=1, source_target_pairs={{0,24},{2,26},{4,28},{6,30},{8,16},{10,18},{12,20},{14,22},{16,8},... | collective-permute-start | bytes 393224 | tf_op jit(solution)/shard_map/mixed_3/ppermute | solution.py:24

commit v4 on v3

--- a/solution.py
+++ b/solution.py
@@ -73,40 +73,50 @@
     )(stream, hidden, gain.reshape(1, -1), *sums)
 
 
-def unpack_kernel(plain, packed, fold, *refs):
-    sources, outs = refs[: plain + packed], refs[plain + packed :]
-    depth = outs[0].shape[1]
-    for i, source in enumerate(sources):
-        outs[0][i] = source[:depth]
-        if i >= plain:
-            extra = source.shape[0] - depth
-            for j in range(fold):
-                lanes = slice(j * 2 * HD, (j + 1) * 2 * HD)
-                outs[1 + i - plain][j * extra : (j + 1) * extra] = source[depth:, lanes]
+def unpack_kernel(plain, fold, sources, *refs):
+    sources, (whole, last, *caches) = refs[:sources], refs[sources:]
+    depth = whole.shape[1]
+    at = 0
+    for n, source in enumerate(sources):
+        if n < plain:
+            whole[at : at + source.shape[0]] = source[...]
+            at += source.shape[0]
+            continue
+        whole[at] = source[:depth]
+        last[n - plain] = source[:depth]
+        at += 1
+        extra = source.shape[0] - depth
+        for j in range(fold):
+            lanes = slice(j * 2 * HD, (j + 1) * 2 * HD)
+            caches[n - plain][j * extra : (j + 1) * extra] = source[depth:, lanes]
 
 
 def unpack(plain, packed, depth, fold):
     extra = packed[0].shape[0] - depth
-    count = len(plain) + len(packed)
+    count = sum(p.shape[0] for p in plain) + len(packed)
     return pl.pallas_call(
-        functools.partial(unpack_kernel, len(plain), len(packed), fold),
-        out_shape=[jax.ShapeDtypeStruct((count, depth, WIDTH), jnp.bfloat16)]
+        functools.partial(unpack_kernel, len(plain), fold, len(plain) + len(packed)),
+        out_shape=[
+            jax.ShapeDtypeStruct((n, depth, WIDTH), jnp.bfloat16) for n in (count, len(packed))
+        ]
         + [jax.ShapeDtypeStruct((fold * extra, 2 * HD), jnp.bfloat16)] * len(packed),
-        in_specs=[VMEM] * count,
-        out_specs=[VMEM] * (1 + len(packed)),
-        compiler_params=pltpu.CompilerParams(vmem_limit_bytes=8 * 2**20),
+        in_specs=[VMEM] * (len(plain) + len(packed)),
+        out_specs=[VMEM] * (2 + len(packed)),
+        compiler_params=pltpu.CompilerParams(vmem_limit_bytes=12 * 2**20),
         cost_estimate=pl.CostEstimate(flops=2 * 10**10, bytes_accessed=10**7, transcendentals=0),
         name="unpack",
     )(*plain, *packed)
 
 
-def project_kernel(kind, first_slot, tok, redo, pitch, n_x, n_w, *refs):
+def project_kernel(kv, tiles, first_slot, tok, redo, pitch, n_x, n_w, *refs):
     x_ids, w_ids = refs[:2]
     x_refs, refs = refs[2 : 2 + sum(n_x)], refs[2 + sum(n_x) :]
     w_refs, refs = refs[:n_w], refs[n_w:]
     chunks = len(n_x)
     cosine, sine, *refs = refs
-    caches, (out, held) = refs[:-2], refs[-2:]
+    caches, outs, held = refs[: chunks * kv], list(refs[chunks * kv : -1]), refs[-1]
+    kv_out = outs.pop(0) if kv else None
+    q_out = outs.pop(0) if outs else None
     span = cosine.shape[1]
     cache_rows = span - tok
 
@@ -134,58 +144,76 @@
         slot = first_slot + chunk
         return value * cosine[slot, first:last] + turned * sine[slot, first:last]
 
-    for chunk in range(chunks):
-        mine = total[chunk * pitch : chunk * pitch + tok + redo]
-        if kind == "queries":
+    def finish_queries():
+        for chunk in range(chunks):
             for head in range(2):
-                value = mine[:tok, head * HD : (head + 1) * HD]
-                out[chunk, head] = rotated(value, chunk, 0, tok).astype(jnp.bfloat16)
-            continue
-        keys = rotated(mine[:tok, :HD], chunk, 0, tok)
-        out[chunk, :tok] = jnp.concatenate([keys, mine[:tok, HD:]], 1).astype(jnp.bfloat16)
-        cache = caches[chunk]
-        offsets = cache[cache_rows : cache_rows + 1, :redo].astype(jnp.float32)
-        row = lax.broadcasted_iota(jnp.int32, (cache_rows, redo), 0).astype(jnp.float32)
-        chosen = (row == offsets).astype(jnp.float32)
-        fresh = jnp.dot(
-            chosen,
-            mine[tok:],
-            preferred_element_type=jnp.float32,
-            precision=lax.Precision.HIGHEST,
-        )
-        turned = rotated(fresh[:, :HD], chunk, tok, span)
-        fresh = jnp.concatenate([turned, fresh[:, HD:]], 1)
-        hit = jnp.sum(chosen, axis=1, keepdims=True) > 0.5
-        kept = cache[:cache_rows].astype(jnp.float32)
-        out[chunk, tok:] = jnp.where(hit, fresh, kept).astype(jnp.bfloat16)
-
-
-def project(kind, first_slot, x_chunks, x_ids, w_parts, w_ids, cosine, sine, caches, tok, redo):
+                value = total[chunk * pitch : chunk * pitch + tok, head * HD : (head + 1) * HD]
+                q_out[chunk, head] = rotated(value, chunk, 0, tok).astype(jnp.bfloat16)
+
+    def finish_kv():
+        for chunk in range(chunks):
+            mine = total[chunk * pitch : chunk * pitch + tok + redo]
+            keys = rotated(mine[:tok, :HD], chunk, 0, tok)
+            kv_out[chunk, :tok] = jnp.concatenate([keys, mine[:tok, HD:]], 1).astype(jnp.bfloat16)
+            cache = caches[chunk]
+            offsets = cache[cache_rows : cache_rows + 1, :redo].astype(jnp.float32)
+            row = lax.broadcasted_iota(jnp.int32, (cache_rows, redo), 0).astype(jnp.float32)
+            chosen = (row == offsets).astype(jnp.float32)
+            fresh = jnp.dot(
+                chosen,
+                mine[tok:],
+                preferred_element_type=jnp.float32,
+                precision=lax.Precision.HIGHEST,
+            )
+            turned = rotated(fresh[:, :HD], chunk, tok, span)
+            fresh = jnp.concatenate([turned, fresh[:, HD:]], 1)
+            hit = jnp.sum(chosen, axis=1, keepdims=True) > 0.5
+            kept = cache[:cache_rows].astype(jnp.float32)
+            kv_out[chunk, tok:] = jnp.where(hit, fresh, kept).astype(jnp.bfloat16)
+
+    if kv and tiles > 1:
+        pl.when(pl.program_id(0) == 0)(finish_kv)
+        pl.when(pl.program_id(0) > 0)(finish_queries)
+    elif kv:
+        finish_kv()
+    else:
+        finish_queries()
+
+
+def project(kv, q, first_slot, x_chunks, x_ids, w_parts, w_ids, cosine, sine, caches, tok, redo):
     chunks = len(x_chunks)
     blocks = sum(p.shape[0] for p in x_chunks[0])
     span = cosine.shape[1]
     pitch = -(-(tok + redo) // 16) * 16
     full = lambda a: pl.BlockSpec(a.shape, lambda t, n=a.ndim: (0,) * n)
-    tiles, first = (2, 0) if kind == "queries" else (1, 2)
-    w_spec = lambda a: pl.BlockSpec((a.shape[0], FEATS, FEATS), lambda t: (0, 0, first + t))
-    if kind == "queries":
-        out_shape = jax.ShapeDtypeStruct((chunks, GROUP, tok, HD), jnp.bfloat16)
-        out_spec = pl.BlockSpec((chunks, 2, tok, HD), lambda t: (0, t, 0, 0))
+    q_tiles = WIDTH // FEATS - 1
+    tiles = kv + q * q_tiles
+    w_spec = lambda a: pl.BlockSpec(
+        (a.shape[0], FEATS, FEATS),
+        lambda t: (0, 0, lax.rem(t + q_tiles, q_tiles + 1) if kv else t),
+    )
+    out_shape, out_specs = [], []
+    if kv:
+        out_shape.append(jax.ShapeDtypeStruct((chunks, span, 2 * HD), jnp.bfloat16))
+        out_specs.append(full(out_shape[0]))
+    else:
         caches = []
-    else:
-        out_shape = jax.ShapeDtypeStruct((chunks, span, 2 * HD), jnp.bfloat16)
-        out_spec = full(out_shape)
+    if q:
+        out_shape.append(jax.ShapeDtypeStruct((chunks, GROUP, tok, HD), jnp.bfloat16))
+        out_specs.append(
+            pl.BlockSpec((chunks, 2, tok, HD), lambda t: (0, jnp.maximum(t - kv, 0), 0, 0))
+        )
     x_parts = [p for chunk in x_chunks for p in chunk]
     n_x = [len(chunk) for chunk in x_chunks]
     return pl.pallas_call(
-        functools.partial(project_kernel, kind, first_slot, tok, redo, pitch, n_x, len(w_parts)),
+        functools.partial(project_kernel, kv, tiles, first_slot, tok, redo, pitch, n_x, len(w_parts)),
         grid=(tiles,),
         out_shape=out_shape,
         in_specs=[SMEM, SMEM]
         + [full(a) for a in x_parts]
         + [w_spec(a) for a in w_parts]
         + [full(a) for a in (cosine, sine, *caches)],
-        out_specs=out_spec,
+        out_specs=out_specs,
         scratch_shapes=[pltpu.VMEM((blocks, chunks * pitch, FEATS), jnp.bfloat16)],
         compiler_params=pltpu.CompilerParams(vmem_limit_bytes=56 * 2**20),
         cost_estimate=pl.CostEstimate(
@@ -193,7 +221,7 @@
             bytes_accessed=2 * blocks * FEATS * (FEATS * tiles + chunks * pitch),
             transcendentals=0,
         ),
-        name=kind,
+        name="_".join(["keys_values"] * kv + ["queries"] * q),
     )(x_ids, w_ids, *x_parts, *w_parts, cosine, sine, *caches)
 
 
@@ -369,15 +397,17 @@
     def folded(cache):
         return jnp.concatenate([cache[i * extra : (i + 1) * extra] for i in range(fold)], 1)
 
-    half = HD // 2
-    freq = jnp.exp(-math.log(1000000.0) * jnp.arange(half, dtype=jnp.float32) * 2.0 / (2 * half))
-    q_ids = jnp.stack([(plane ^ k) * crew + inner for k in range(heads)]).astype(jnp.int32)
-    token_ids = q_ids[:, None] * tok + jnp.arange(tok, dtype=jnp.int32) + begin
-    row_ids = q_ids[:, None] * cache_rows + jnp.arange(cache_rows, dtype=jnp.int32)
-    angle = jnp.concatenate([token_ids, row_ids], 1).astype(jnp.float32)[..., None] * freq
-    cosine, sine = jnp.cos(angle), jnp.sin(angle)
-    cosine = jnp.concatenate([cosine, cosine], -1)
-    sine = jnp.concatenate([-sine, sine], -1)
+    def tables(plane):
+        half = HD // 2
+        freq = jnp.exp(
+            -math.log(1000000.0) * jnp.arange(half, dtype=jnp.float32) * 2.0 / (2 * half)
+        )
+        q_ids = jnp.stack([(plane ^ k) * crew + inner for k in range(heads)]).astype(jnp.int32)
+        token_ids = q_ids[:, None] * tok + jnp.arange(tok, dtype=jnp.int32) + begin
+        row_ids = q_ids[:, None] * cache_rows + jnp.arange(cache_rows, dtype=jnp.int32)
+        angle = jnp.concatenate([token_ids, row_ids], 1).astype(jnp.float32)[..., None] * freq
+        cosine, sine = jnp.cos(angle), jnp.sin(angle)
+        return q_ids, jnp.concatenate([cosine, cosine], -1), jnp.concatenate([-sine, sine], -1)
 
     count = wide // FEATS
     groups = [[i * crew + j for j in range(crew)] for i in range(heads)]
@@ -393,40 +423,46 @@
             return swap(value, "seq", seq, 1, f"core_{name}")
 
         depth = w_qkv.shape[0]
-        w_sent = [jnp.concatenate([w, folded(c)], 0) for w, c in zip(w_cut, caches)]
+        w_sent = [jnp.concatenate([w, folded(c)], 0) for w, c in zip(w_cut[:3], caches)]
         w_own = w_cut[0][None]
         w_1, w_2 = across(w_sent[1], 1, "w"), across(w_sent[2], 2, "w")
         far, next_x = across(own, 2, "x_far"), across(own, 1, "x_next")
-        own_side, w_line = sides(own, "own"), line(w_own, "w0")
-        w_mid, *cache_mid = unpack([], [w_1, w_2], depth, fold)
-        own, own_side, next_x, far, w_mid, cache_mid, w_3, w_line, cosine, sine = (
-            lax.optimization_barrier(
-                (own, own_side, next_x, far, w_mid, cache_mid, w_sent[3], w_line, cosine, sine)
-            )
-        )
-        w_3 = across(w_3, 3, "w")
-        last = across(far, 1, "x_last")
-        next_side, far_side = sides(next_x, "next"), sides(far, "far")
-        w_mid_line = line(w_mid, "w12")
-        w_last, cache_last = unpack([], [w_3], depth, fold)
-        w_last_line = line(w_last, "w3")
-        last, next_side, far_side, w_last, w_mid, w_mid_line, w_last_line, w_line = (
-            lax.optimization_barrier(
-                (last, next_side, far_side, w_last, w_mid, w_mid_line, w_last_line, w_line)
-            )
-        )
-        caches = [caches[0], *cache_mid, cache_last]
-        last_side = sides(last, "last")
-        w_parts = [w_own, w_mid, w_last, w_line, w_mid_line, w_last_line]
-        w_parts += [core(w, "w") for w in w_parts]
-        x_chunks = [[own, own_side], [next_x, next_side], [far, far_side], [last, last_side]]
+        own_side, w_line = sides(own, "own"), line(after(w_own, w_2), "w0")
+        w_some, w_mid, *cache_mid = unpack([w_own], [w_1, w_2], depth, fold)
+        late, late_cache, _ = lax.optimization_barrier((plane, caches[3], w_2))
+        w_sent_3 = jnp.concatenate([w_cut[3], folded(late_cache)], 0)
+        q_ids, cosine, sine = tables(late)
         ids = jnp.arange(count, dtype=jnp.int32)
         x_ids = jnp.concatenate([side * count + ids, (1 - side) * count + ids])
         w_ids = [
-            (plane ^ k) * crew + (inner ^ turn) for turn in (0, 2, 1, 3) for k in range(heads)
+            (late ^ k) * crew + (inner ^ turn) for turn in (0, 2, 1, 3) for k in range(heads)
         ]
         w_ids = jnp.stack(w_ids).astype(jnp.int32)
+        kv_ids = [(late ^ k) * crew + (inner ^ turn) for k in range(heads) for turn in (0, 2, 1, 3)]
+        kv_ids = jnp.stack(kv_ids).astype(jnp.int32)
+        numbers = (q_ids, cosine, sine, x_ids, w_ids, kv_ids)
+        own, own_side, next_x, far, w_some, w_mid, cache_mid, w_3, w_line, numbers = (
+            lax.optimization_barrier(
+                (own, own_side, next_x, far, w_some, w_mid, cache_mid, w_sent_3, w_line, numbers)
+            )
+        )
+        q_ids, cosine, sine, x_ids, w_ids, kv_ids = numbers
+        next_side, far_side = sides(next_x, "next"), sides(far, "far")
+        w_3 = across(w_3, 3, "w")
+        last = across(far, 1, "x_last")
+        w_mid_line = line(w_mid, "w12")
+        w_all, w_last, cache_last = unpack([w_some], [w_3], depth, fold)
+        w_last_line = line(w_last, "w3")
+        last, next_side, far_side, w_all, w_mid_line, w_last_line, w_line = lax.optimization_barrier(
+            (last, next_side, far_side, w_all, w_mid_line, w_last_line, w_line)
+        )
+        caches = [caches[0], *cache_mid, cache_last]
+        last_side = sides(last, "last")
+        w_parts = [w_all, w_line, w_mid_line, w_last_line]
+        w_parts += [core(w, "w") for w in w_parts]
+        x_chunks = [[own, own_side], [next_x, next_side], [far, far_side], [last, last_side]]
     else:
+        q_ids, cosine, sine = tables(plane)
         caches = [across(c, k) for k, c in enumerate(caches)]
         members = [
             [(i * crew + j) * tp + t for i in range(heads) for t in range(tp)] for j in range(crew)
@@ -447,25 +483,26 @@
             [(plane ^ k) * per + jnp.arange(per, dtype=jnp.int32) for k in range(heads)]
         )
 
-    def projected(kind, slots):
+    def projected(kv, q, slots):
         chunks = [x_chunks[k] for k in slots]
         some = [caches[k] for k in slots]
-        return project(kind, slots[0], chunks, x_ids, w_parts, w_ids, cosine, sine, some, tok, redo)
-
-    calls = ((0, 1, 2), (3,)) if squared else (tuple(range(heads)),)
-    kv_new = [projected("keys_values", slots) for slots in calls]
-    queries = [projected("queries", slots) for slots in calls]
+        return project(kv, q, slots[0], chunks, x_ids, w_parts, w_ids, cosine, sine, some, tok, redo)
+
+    if squared:
+        kv_some, q_some = projected(True, True, (0, 1, 2))
+        kv_new, queries = [kv_some, *projected(True, False, (3,))], [q_some]
+        x_chunks[3][0] = after(last, kv_new[1])
+        queries += projected(False, True, (3,))
+    else:
+        kv_new, queries = [[value] for value in projected(True, True, tuple(range(heads)))]
 
     if squared:
         kv_parts, places = [], []
-        for mine, some in zip(kv_new, queries):
-            far = swap(mine, "seq", seq, 2, "kv_line")
-            far, some = lax.optimization_barrier((far, some))
+        fars = [swap(mine, "seq", seq, 2, "kv_line") for mine in kv_new]
+        fars = lax.optimization_barrier((*fars, queries[1]))
+        for mine, far in zip(kv_new, fars):
             places += [(len(kv_parts) + n, i) for i in range(mine.shape[0]) for n in range(4)]
             kv_parts += [mine, far, core(mine, "kv"), core(far, "kv_line")]
-        turns = (0, 2, 1, 3)
-        kv_ids = jnp.stack([(plane ^ k) * crew + (inner ^ turn) for k in range(4) for turn in turns])
-        kv_ids = kv_ids.astype(jnp.int32)
     else:
         kv_parts = [
             lax.all_gather(kv_new[0][k : k + 1], "seq", axis=0, tiled=True, axis_index_groups=groups)
@@ -479,6 +516,10 @@
     back = [None] * heads
     for k in reversed(range(heads)):
         some, index = (queries[k // 3], k % 3) if squared else (queries[0], k)
+        if k + 2 < heads:
+            some = after(some, mixed, back[k + 2])
+        elif k + 1 < heads:
+            some = after(some, mixed)
         mixed = attend(k, prefix_len, some, index, q_ids, kv_parts, places, kv_ids, tok)
         back[k] = across(mixed, k, "mixed")
     back = jnp.stack(back)

time: 142 us -> 137 us (0.965)
  waiting for transfers between devices: 69.5 us -> 56.9 us
  starting transfers between devices: 23 us -> 28.2 us
  local copies, waits for them, and re-layouts: 5.64 us -> 8.44 us
  other arithmetic: 5.95 us -> 7.56 us
  Pallas kernels: 36.5 us -> 35 us
    ppermute x29 -> x27, waiting for transfers between devices: 69.5 us -> 56.9 us  [swap(): return lax.ppermute(value, axis, [(i, i ^ mask) for i in range(size)])]
    ppermute x29 -> x27, starting transfers between devices: 23 us -> 28.2 us  [swap(): return lax.ppermute(value, axis, [(i, i ^ mask) for i in range(size)])]
    pallas_call x6 -> x5, Pallas kernels: 20.1 us -> 16.7 us  [the longest x3 16.4 us: project(): pl.pallas_call(functools.partial(project_kernel, kv, tiles, first_slot, t...]
    unnamed x54 -> x52, local copies, waits for them, and re-layouts: 3.24 us -> 5.36 us
    pallas_call x4, Pallas kernels: 16 us -> 17.9 us  [attend(): pl.pallas_call(functools.partial(attend_kernel, slot, tok, places), out_s...]
    concatenate x2 -> x4, other arithmetic: 2.09 us -> 3.72 us  [the longest x1 1.02 us: per_device(): w_sent_3 = jnp.concatenate([w_cut[3], folded(late_cache)], 0)]
  transfers between devices with their start and end apart: 29 -> 27, of which waited for: 10 -> 15; matrix products, arithmetic and copies ran while one was open for 4% -> 5% of each run, Pallas kernels for 23% -> 22%
where the time goes in v4:
time: 137 us
  waiting for transfers between devices  56.9 us (42%)
  Pallas kernels  35 us (26%)
  starting transfers between devices  28.2 us (21%)
  local copies, waits for them, and re-layouts  8.44 us (6%)
  other arithmetic  7.56 us (6%)
    ppermute x27, waiting for transfers between devices, swap(): return lax.ppermute(value, axis, [(i, i ^ mask) for i in range(size)])  56.9 us
    ppermute x27, starting transfers between devices, swap(): return lax.ppermute(value, axis, [(i, i ^ mask) for i in range(size)])  28.2 us
    pallas_call x4, Pallas kernels, attend(): pl.pallas_call(functools.partial(attend_kernel, slot, tok, places), out_s...  17.9 us
    pallas_call x3, Pallas kernels, project(): pl.pallas_call(functools.partial(project_kernel, kv, tiles, first_slot, t...  16.4 us
    unnamed x52, local copies, waits for them, and re-layouts  5.36 us
  transfers between devices with their start and end apart: 27, of which 15 were waited for; matrix products, arithmetic and copies ran while one was open for 5% of the time, Pallas kernels for 22%

profile of v4, /device:TPU:0, one launch (start us, length us, event | category | flops | bytes accessed | tf_op | source)
XLA Modules:
  0.0 137.0 jit_solution(13571998378005247110)
XLA Ops:
  0.0 2.3 %constant_dynamic-slice_fusion = (bf16[256,768]{1,0:T(8,128)(2,1)}, bf16[256,768]{1,0:T(8,128)(2,1)S(1)}, bf16[256,768]{1,0:T(8,128)(2,1)S(1)}, bf16[256,768]{1,0:T(8,128)(2,1)S(1)}) fusion(bf16[256,3072]{1,0:T(8,128)(2,1)} %param.9, s32[]{:T(128)S(6)} %select_n.55, s32[]{:T(128)S(6)} %select_n.53, s32[]{:T(128)S(6)} %select_n.52, s32[]{:T(128)S(6)} %select_n.54), kind=kLoop, calls=%fused_computation.50 | loop fusion | bytes 3145744 | tf_op jit(solution)/shard_map/dynamic_slice | solution.py:378
  2.4 0.8 fusion.7
  3.2 4.0 %collective-permute-start.5 = (bf16[288,768]{1,0:T(8,128)(2,1)S(1)}, bf16[288,768]{1,0:T(8,128)(2,1)S(1)}, u32[]{:S(2)}, u32[]{:S(2)}) collective-permute-start(bf16[288,768]{1,0:T(8,128)(2,1)S(1)} %get-tuple-element.120), channel_id=1, source_target_pairs={{0,16},{2,18},{4,20},{6,22},{8,24},{10,26},{12,28},{14,30},{16,0},... | collective-permute-start | bytes 1327112 | tf_op jit(solution)/shard_map/w_2/ppermute | solution.py:24
  7.2 1.6 %collective-permute-start.4 = (bf16[288,768]{1,0:T(8,128)(2,1)}, bf16[288,768]{1,0:T(8,128)(2,1)S(1)}, u32[]{:S(2)}, u32[]{:S(2)}) collective-permute-start(bf16[288,768]{1,0:T(8,128)(2,1)} %get-tuple-element.121), channel_id=1, source_target_pairs={{0,8},{2,10},{4,12},{6,14},{8,0},{10,2},{12,4},{14,6},{16,24},{18,... | collective-permute-start | bytes 1327112 | tf_op jit(solution)/shard_map/w_1/ppermute | solution.py:24
  8.8 0.2 squares.1.refs_0_
  9.0 1.5 %collective-permute-start = (f32[136,128]{1,0:T(8,128)S(1)}, f32[136,128]{1,0:T(8,128)S(1)}, u32[]{:S(2)}, u32[]{:S(2)}) collective-permute-start(f32[136,128]{1,0:T(8,128)S(1)} %squares.1.refs_0_), channel_id=1, source_target_pairs={{0,1},{1,0},{2,3},{3,2},{4,5},{5,4},{6,7},{7,6},{8,9},{9,8},{10,11... | collective-permute-start | bytes 208904 | tf_op jit(solution)/shard_map/side_sums/ppermute | solution.py:24
  11.3 0.6 pad_maximum_fusion.6
  11.9 0.6 pad_add_fusion.1.refs_0_
  12.5 0.9 collective-permute-done.refs_1_
  13.3 0.2 norm.1.refs_2_
  13.6 1.6 %collective-permute-start.1 = (bf16[8,136,256]{2,1,0:T(8,128)(2,1)S(1)}, bf16[8,136,256]{2,1,0:T(8,128)(2,1)}, u32[]{:S(2)}, u32[]{:S(2)}) collective-permute-start(bf16[8,136,256]{2,1,0:T(8,128)(2,1)S(1)} %norm.1.refs_2_), channel_id=1, source_target_pairs={{0,1},{1,0},{2,3},{3,2},{4,5},{5,4},{6,7},{7,6},{8,9},{9,8},{10,11... | collective-permute-start | bytes 1671176 | tf_op jit(solution)/shard_map/side_own/ppermute | solution.py:24
  15.2 0.4 collective-permute-start.2
  15.6 0.3 collective-permute-start.3
  15.9 11.9 %collective-permute-done.5.refs_2_ = bf16[288,768]{1,0:T(8,128)(2,1)S(1)} collective-permute-done((bf16[288,768]{1,0:T(8,128)(2,1)S(1)}, bf16[288,768]{1,0:T(8,128)(2,1)S(1)}, u32[]{:S(2)}, u32[]{:S(2)}) %collective-permute-start.5) | collective-permute-done | bytes 442400 | tf_op jit(solution)/shard_map/w_2/ppermute | solution.py:24
  28.0 1.8 %collective-permute-start.6 = (bf16[1,256,768]{2,1,0:T(8,128)(2,1)S(1)}, bf16[1,256,768]{2,1,0:T(8,128)(2,1)S(1)}, u32[]{:S(2)}, u32[]{:S(2)}) collective-permute-start(bf16[1,256,768]{2,1,0:T(8,128)(2,1)S(1)} %bitcast.50), channel_id=1, source_target_pairs={{0,4},{2,6},{4,0},{6,2},{8,12},{10,14},{12,8},{14,10},{16,20},{18,... | collective-permute-start | bytes 1179656 | tf_op jit(solution)/shard_map/line_w0/ppermute | solution.py:24
  29.9 1.4 %fusion.16 = (f32[4,192,64]{2,1,0:T(8,128)S(1)}, f32[4,192,64]{2,1,0:T(8,128)S(1)}, f32[4,192,64]{2,1,0:T(8,128)S(1)}) fusion(f32[64]{0:T(128)S(1)} %multiply_exponential_fusion, f32[4,192]{1,0:T(4,128)S(1)} %add_convert_fusion), kind=kLoop, calls=%fused_computation.32 | loop fusion | flops 98304 | bytes 593152 | tf_op jit(solution)/shard_map/neg | solution.py:410
  31.3 9.4 %collective-permute-done.4.refs_1_ = bf16[288,768]{1,0:T(8,128)(2,1)S(1)} collective-permute-done((bf16[288,768]{1,0:T(8,128)(2,1)}, bf16[288,768]{1,0:T(8,128)(2,1)S(1)}, u32[]{:S(2)}, u32[]{:S(2)}) %collective-permute-start.4) | collective-permute-done | bytes 442400 | tf_op jit(solution)/shard_map/w_1/ppermute | solution.py:24
  41.0 0.6 copy-done.6
  41.6 0.6 copy-done.7
  42.2 1.1 copy-done.11
  43.2 0.9 pad_maximum_fusion.4.refs_16_.refs_12_
  44.2 1.0 pad_maximum_fusion.5.refs_17_.refs_13_
  45.2 0.6 stack.109.refs_1_
  45.8 1.0 maximum_maximum_fusion
  46.9 4.5 %collective-permute-done.2.refs_4_ = bf16[8,136,256]{2,1,0:T(8,128)(2,1)} collective-permute-done((bf16[8,136,256]{2,1,0:T(8,128)(2,1)S(1)}, bf16[8,136,256]{2,1,0:T(8,128)(2,1)}, u32[]{:S(2)}, u32[]{:S(2)}) %collective-permute-start.2) | collective-permute-done | bytes 557088 | tf_op jit(solution)/shard_map/x_next_1/ppermute | solution.py:24
  51.4 2.6 %collective-permute-start.10 = (bf16[288,768]{1,0:T(8,128)(2,1)S(1)}, bf16[288,768]{1,0:T(8,128)(2,1)S(1)}, u32[]{:S(2)}, u32[]{:S(2)}) collective-permute-start(bf16[288,768]{1,0:T(8,128)(2,1)S(1)} %maximum_maximum_fusion), channel_id=1, source_target_pairs={{0,24},{2,26},{4,28},{6,30},{8,16},{10,18},{12,20},{14,22},{16,8},... | collective-permute-start | bytes 1327112 | tf_op jit(solution)/shard_map/w_3/ppermute | solution.py:24
  54.0 0.2 collective-permute-start.7
  54.1 1.5 %collective-permute-start.9 = (bf16[8,136,256]{2,1,0:T(8,128)(2,1)}, bf16[8,136,256]{2,1,0:T(8,128)(2,1)S(1)}, u32[]{:S(2)}, u32[]{:S(2)}) collective-permute-start(bf16[8,136,256]{2,1,0:T(8,128)(2,1)} %collective-permute-done.3.refs_6_), channel_id=1, source_target_pairs={{0,1},{1,0},{2,3},{3,2},{4,5},{5,4},{6,7},{7,6},{8,9},{9,8},{10,11... | collective-permute-start | bytes 1671176 | tf_op jit(solution)/shard_map/side_far/ppermute | solution.py:24
  55.6 1.5 %collective-permute-start.11 = (bf16[2,256,768]{2,1,0:T(8,128)(2,1)S(1)}, bf16[2,256,768]{2,1,0:T(8,128)(2,1)S(1)}, u32[]{:S(2)}, u32[]{:S(2)}) collective-permute-start(bf16[2,256,768]{2,1,0:T(8,128)(2,1)S(1)} %get-tuple-element.74), channel_id=1, source_target_pairs={{0,4},{2,6},{4,0},{6,2},{8,12},{10,14},{12,8},{14,10},{16,20},{18,... | collective-permute-start | bytes 2359304 | tf_op jit(solution)/shard_map/line_w12/ppermute | solution.py:24
  57.1 0.5 collective-permute-start.8
  57.6 8.8 %collective-permute-done.10.refs_1_ = bf16[288,768]{1,0:T(8,128)(2,1)S(1)} collective-permute-done((bf16[288,768]{1,0:T(8,128)(2,1)S(1)}, bf16[288,768]{1,0:T(8,128)(2,1)S(1)}, u32[]{:S(2)}, u32[]{:S(2)}) %collective-permute-start.10) | collective-permute-done | bytes 442400 | tf_op jit(solution)/shard_map/w_3/ppermute | solution.py:24
  66.5 0.6 copy-done.8
  67.2 1.6 %collective-permute-start.12 = (bf16[1,256,768]{2,1,0:T(8,128)(2,1)S(1)}, bf16[1,256,768]{2,1,0:T(8,128)(2,1)S(1)}, u32[]{:S(2)}, u32[]{:S(2)}) collective-permute-start(bf16[1,256,768]{2,1,0:T(8,128)(2,1)S(1)} %get-tuple-element.75), channel_id=1, source_target_pairs={{0,4},{2,6},{4,0},{6,2},{8,12},{10,14},{12,8},{14,10},{16,20},{18,... | collective-permute-start | bytes 1179656 | tf_op jit(solution)/shard_map/line_w3/ppermute | solution.py:24
  68.7 7.3 %collective-permute-done.7.refs_2_ = bf16[8,136,256]{2,1,0:T(8,128)(2,1)S(1)} collective-permute-done((bf16[8,136,256]{2,1,0:T(8,128)(2,1)}, bf16[8,136,256]{2,1,0:T(8,128)(2,1)S(1)}, u32[]{:S(2)}, u32[]{:S(2)}) %collective-permute-start.7) | collective-permute-done | bytes 557088 | tf_op jit(solution)/shard_map/x_last_1/ppermute | solution.py:24
  76.0 3.2 %collective-permute-done.8.refs_5_ = bf16[8,136,256]{2,1,0:T(8,128)(2,1)S(1)} collective-permute-done((bf16[8,136,256]{2,1,0:T(8,128)(2,1)}, bf16[8,136,256]{2,1,0:T(8,128)(2,1)S(1)}, u32[]{:S(2)}, u32[]{:S(2)}) %collective-permute-start.8) | collective-permute-done | bytes 557088 | tf_op jit(solution)/shard_map/side_next/ppermute | solution.py:24
  79.2 2.4 %collective-permute-done.12.refs_11_.refs_7_ = bf16[1,256,768]{2,1,0:T(8,128)(2,1)S(1)} collective-permute-done((bf16[1,256,768]{2,1,0:T(8,128)(2,1)S(1)}, bf16[1,256,768]{2,1,0:T(8,128)(2,1)S(1)}, u32[]{:S(2)}, u32[]{:S(2)}) %collective-permute-start.12) | collective-permute-done | bytes 393248 | tf_op jit(solution)/shard_map/line_w3/ppermute | solution.py:24
  81.7 0.5 collective-permute-start.15
  82.3 0.4 collective-permute-start.16
  82.7 0.5 collective-permute-start.17
  83.2 3.6 %collective-permute-done.14.refs_13_.refs_9_ = bf16[1,256,768]{2,1,0:T(8,128)(2,1)S(1)} collective-permute-done((bf16[1,256,768]{2,1,0:T(8,128)(2,1)S(1)}, bf16[1,256,768]{2,1,0:T(8,128)(2,1)S(1)}, u32[]{:S(2)}, u32[]{:S(2)}) %collective-permute-start.14) | collective-permute-done | bytes 393248 | tf_op jit(solution)/shard_map/core_w/ppermute | solution.py:24
  86.8 0.6 collective-permute-done.16.refs_15_.refs_11_
  87.4 0.1 copy-done.18
  87.6 0.6 copy-done.19
  88.1 0.3 copy-done.15
  88.4 0.5 copy-done.13
  88.9 8.5 %keys_values_queries.1 = (bf16[3,192,256]{2,1,0:T(8,128)(2,1)}, bf16[3,4,128,128]{3,2,1,0:T(8,128)(2,1)}) custom-call(s32[16]{0:T(128)} %pad_add_fusion.1.refs_0_, s32[16]{0:T(128)} %stack.109.refs_1_, bf16[8,136,256]{2,1,0:T(8,128)(2,1)} %copy-done.1, bf16[8,136,256]{2,1,0:T(8,128)(2,1)} %collective-permute-done.1.refs_3_, ...), custom_call_target="tpu_custom_call" | custom-call | flops 2717908992 | bytes 9830400 | tf_op jit(solution)/shard_map/keys_values_queries/pallas_call | solution.py:208
  97.4 1.6 %collective-permute-start.18 = (bf16[3,192,256]{2,1,0:T(8,128)(2,1)}, bf16[3,192,256]{2,1,0:T(8,128)(2,1)S(1)}, u32[]{:S(2)}, u32[]{:S(2)}) collective-permute-start(bf16[3,192,256]{2,1,0:T(8,128)(2,1)} %get-tuple-element.91.refs_4_), channel_id=1, source_target_pairs={{0,4},{2,6},{4,0},{6,2},{8,12},{10,14},{12,8},{14,10},{16,20},{18,... | collective-permute-start | bytes 884744 | tf_op jit(solution)/shard_map/kv_line/ppermute | solution.py:24
  99.0 3.7 %keys_values.1.refs_8_ = bf16[1,192,256]{2,1,0:T(8,128)(2,1)} custom-call(s32[16]{0:T(128)} %pad_add_fusion.1.refs_0_, s32[16]{0:T(128)} %stack.109.refs_1_, bf16[8,136,256]{2,1,0:T(8,128)(2,1)} %copy-done.20, bf16[8,136,256]{2,1,0:T(8,128)(2,1)} %collective-permute-done.17.refs_3_, bf16[4,256,768]{2,1,0:T(8,128)(2,1)} %copy-done, ...), custom_call_target="tpu_custom_call" | custom-call | flops 301989888 | bytes 3276800 | tf_op jit(solution)/shard_map/keys_values/pallas_call | solution.py:208
  102.6 0.5 collective-permute-start.19
  103.2 4.3 %queries.1.refs_3_ = bf16[1,4,128,128]{3,2,1,0:T(8,128)(2,1)} custom-call(s32[16]{0:T(128)} %pad_add_fusion.1.refs_0_, s32[16]{0:T(128)} %stack.109.refs_1_, bf16[8,136,256]{2,1,0:T(8,128)(2,1)} %copy-done.20, bf16[8,136,256]{2,1,0:T(8,128)(2,1)} %collective-permute-done.17.refs_3_, bf16[4,256,768]{2,1,0:T(8,128)(2,1)} %copy-done, ...), custom_call_target="tpu_custom_call" | custom-call | flops 603979776 | bytes 5373952 | tf_op jit(solution)/shard_map/queries/pallas_call | solution.py:208
  107.5 1.4 %collective-permute-done.19.refs_9_ = bf16[1,192,256]{2,1,0:T(8,128)(2,1)S(1)} collective-permute-done((bf16[1,192,256]{2,1,0:T(8,128)(2,1)}, bf16[1,192,256]{2,1,0:T(8,128)(2,1)S(1)}, u32[]{:S(2)}, u32[]{:S(2)}) %collective-permute-start.19) | collective-permute-done | bytes 98336 | tf_op jit(solution)/shard_map/kv_line/ppermute | solution.py:24
  108.9 0.5 collective-permute-start.22
  109.4 1.1 collective-permute-done.22.refs_10_
  110.6 0.1 collective-permute-done.23.refs_11_
  110.7 0.9 copy-done.3
  111.6 5.5 %attend.4 = bf16[128,512]{1,0:T(8,128)(2,1)S(1)} custom-call(s32[1]{0:T(128)} %copy.8.refs_0_, s32[4]{0:T(128)S(1)} %get-tuple-element.63.refs_1_, s32[16]{0:T(128)S(1)} %stack.110.refs_2_, bf16[1,4,128,128]{3,2,1,0:T(8,128)(2,1)S(1)} %copy-done.3, bf16[3,192,256]{2,1,0:T(8,128)(2,1)S(1)} %copy-done.10, ...), custom_call_target="tpu_custom_call" | custom-call | flops 805306368 | bytes 1572864 | tf_op jit(solution)/shard_map/attend/pallas_call | solution.py:340
  117.2 4.7 %attend.5 = bf16[128,512]{1,0:T(8,128)(2,1)S(1)} custom-call(s32[1]{0:T(128)} %copy.8.refs_0_, s32[4]{0:T(128)S(1)} %get-tuple-element.63.refs_1_, s32[16]{0:T(128)S(1)} %stack.110.refs_2_, bf16[3,4,128,128]{3,2,1,0:T(8,128)(2,1)S(1)} %copy-done.9, bf16[3,192,256]{2,1,0:T(8,128)(2,1)S(1)} %copy-done.10, ...), custom_call_target="tpu_custom_call" | custom-call | flops 805306368 | bytes 1572864 | tf_op jit(solution)/shard_map/attend/pallas_call | solution.py:340
  121.9 1.9 %collective-permute-start.25 = (bf16[128,512]{1,0:T(8,128)(2,1)S(1)}, bf16[128,512]{1,0:T(8,128)(2,1)S(1)}, u32[]{:S(2)}, u32[]{:S(2)}) collective-permute-start(bf16[128,512]{1,0:T(8,128)(2,1)S(1)} %attend.5), channel_id=1, source_target_pairs={{0,16},{2,18},{4,20},{6,22},{8,24},{10,26},{12,28},{14,30},{16,0},... | collective-permute-start | bytes 393224 | tf_op jit(solution)/shard_map/mixed_2/ppermute | solution.py:24
  123.8 0.8 collective-permute-done.24
  124.6 4.1 %attend.6 = bf16[128,512]{1,0:T(8,128)(2,1)S(1)} custom-call(s32[1]{0:T(128)} %copy.8.refs_0_, s32[4]{0:T(128)S(1)} %get-tuple-element.63.refs_1_, s32[16]{0:T(128)S(1)} %stack.110.refs_2_, bf16[3,4,128,128]{3,2,1,0:T(8,128)(2,1)S(1)} %copy-done.9, bf16[3,192,256]{2,1,0:T(8,128)(2,1)S(1)} %copy-done.10, ...), custom_call_target="tpu_custom_call" | custom-call | flops 805306368 | bytes 1572864 | tf_op jit(solution)/shard_map/attend/pallas_call | solution.py:340
  128.7 2.8 %collective-permute-start.26 = (bf16[128,512]{1,0:T(8,128)(2,1)S(1)}, bf16[128,512]{1,0:T(8,128)(2,1)S(1)}, u32[]{:S(2)}, u32[]{:S(2)}) collective-permute-start(bf16[128,512]{1,0:T(8,128)(2,1)S(1)} %attend.6), channel_id=1, source_target_pairs={{0,8},{2,10},{4,12},{6,14},{8,0},{10,2},{12,4},{14,6},{16,24},{18,... | collective-permute-start | bytes 393224 | tf_op jit(solution)/shard_map/mixed_1/ppermute | solution.py:24
  131.5 0.9 collective-permute-done.25
  132.4 3.6 %attend.7 = bf16[128,512]{1,0:T(8,128)(2,1)S(1)} custom-call(s32[1]{0:T(128)} %copy.8.refs_0_, s32[4]{0:T(128)S(1)} %get-tuple-element.63.refs_1_, s32[16]{0:T(128)S(1)} %stack.110.refs_2_, bf16[3,4,128,128]{3,2,1,0:T(8,128)(2,1)S(1)} %copy-done.9, bf16[3,192,256]{2,1,0:T(8,128)(2,1)S(1)} %copy-done.10, ...), custom_call_target="tpu_custom_call" | custom-call | flops 805306368 | bytes 1572864 | tf_op jit(solution)/shard_map/attend/pallas_call | solution.py:340
  136.2 0.8 pad_maximum_fusion.3
  (79 shorter events, 1.2 us)
Async XLA Ops:
  0.0 2.3 %copy-start.25 = (s32[8]{0:T(128)S(1)}, s32[8]{0:T(128)}, u32[]{:S(2)}) copy-start(s32[8]{0:T(128)} %param.12) | copy-start | bytes 100
  0.0 2.3 %copy-start.23 = (bf16[2,64,512]{2,1,0:T(8,128)(2,1)S(1)}, bf16[2,64,512]{2,1,0:T(8,128)(2,1)}, u32[]{:S(2)}) copy-start(bf16[2,64,512]{2,1,0:T(8,128)(2,1)} %param.10) | copy-start | bytes 393220
  2.3 6.6 %copy-start.2 = (bf16[128,2048]{1,0:T(8,128)(2,1)S(1)}, bf16[128,2048]{1,0:T(8,128)(2,1)}, u32[]{:S(2)}) copy-start(bf16[128,2048]{1,0:T(8,128)(2,1)} %stream.1) | copy-start | bytes 1572868
  2.3 6.6 %copy-start.4 = (bf16[8,2048]{1,0:T(8,128)(2,1)S(1)}, bf16[8,2048]{1,0:T(8,128)(2,1)}, u32[]{:S(2)}) copy-start(bf16[8,2048]{1,0:T(8,128)(2,1)} %hidden.3) | copy-start | bytes 98308
  2.3 8.9 %copy-start.24 = (f32[4096]{0:T(1024)S(1)}, f32[4096]{0:T(1024)}, u32[]{:S(2)}) copy-start(f32[4096]{0:T(1024)} %param.8) | copy-start | bytes 49156
  3.2 24.6 %collective-permute-start.5 = (bf16[288,768]{1,0:T(8,128)(2,1)S(1)}, bf16[288,768]{1,0:T(8,128)(2,1)S(1)}, u32[]{:S(2)}, u32[]{:S(2)}) collective-permute-start(bf16[288,768]{1,0:T(8,128)(2,1)S(1)} %get-tuple-element.120), channel_id=1, source_target_pairs={{0,16},{2,18},{4,20},{6,22},{8,24},{10,26},{12,28},{14,30},{16,0},... | collective-permute-start | bytes 1327112 | tf_op jit(solution)/shard_map/w_2/ppermute | solution.py:24
  7.2 33.6 %collective-permute-start.4 = (bf16[288,768]{1,0:T(8,128)(2,1)}, bf16[288,768]{1,0:T(8,128)(2,1)S(1)}, u32[]{:S(2)}, u32[]{:S(2)}) collective-permute-start(bf16[288,768]{1,0:T(8,128)(2,1)} %get-tuple-element.121), channel_id=1, source_target_pairs={{0,8},{2,10},{4,12},{6,14},{8,0},{10,2},{12,4},{14,6},{16,24},{18,... | collective-permute-start | bytes 1327112 | tf_op jit(solution)/shard_map/w_1/ppermute | solution.py:24
  9.0 4.3 %collective-permute-start = (f32[136,128]{1,0:T(8,128)S(1)}, f32[136,128]{1,0:T(8,128)S(1)}, u32[]{:S(2)}, u32[]{:S(2)}) collective-permute-start(f32[136,128]{1,0:T(8,128)S(1)} %squares.1.refs_0_), channel_id=1, source_target_pairs={{0,1},{1,0},{2,3},{3,2},{4,5},{5,4},{6,7},{7,6},{8,9},{9,8},{10,11... | collective-permute-start | bytes 208904 | tf_op jit(solution)/shard_map/side_sums/ppermute | solution.py:24
  13.6 27.4 %copy-start.1 = (bf16[8,136,256]{2,1,0:T(8,128)(2,1)}, bf16[8,136,256]{2,1,0:T(8,128)(2,1)S(1)}, u32[]{:S(2)}) copy-start(bf16[8,136,256]{2,1,0:T(8,128)(2,1)S(1)} %norm.1.refs_2_) | copy-start | bytes 1671172
  13.6 33.3 %collective-permute-start.1 = (bf16[8,136,256]{2,1,0:T(8,128)(2,1)S(1)}, bf16[8,136,256]{2,1,0:T(8,128)(2,1)}, u32[]{:S(2)}, u32[]{:S(2)}) collective-permute-start(bf16[8,136,256]{2,1,0:T(8,128)(2,1)S(1)} %norm.1.refs_2_), channel_id=1, source_target_pairs={{0,1},{1,0},{2,3},{3,2},{4,5},{5,4},{6,7},{7,6},{8,9},{9,8},{10,11... | collective-permute-start | bytes 1671176 | tf_op jit(solution)/shard_map/side_own/ppermute | solution.py:24
  15.2 36.2 %collective-permute-start.2 = (bf16[8,136,256]{2,1,0:T(8,128)(2,1)S(1)}, bf16[8,136,256]{2,1,0:T(8,128)(2,1)}, u32[]{:S(2)}, u32[]{:S(2)}) collective-permute-start(bf16[8,136,256]{2,1,0:T(8,128)(2,1)S(1)} %norm.1.refs_2_), channel_id=1, source_target_pairs={{0,8},{2,10},{4,12},{6,14},{8,0},{10,2},{12,4},{14,6},{16,24},{18,... | collective-permute-start | bytes 1671176 | tf_op jit(solution)/shard_map/x_next_1/ppermute | solution.py:24
  15.6 35.8 %collective-permute-start.3 = (bf16[8,136,256]{2,1,0:T(8,128)(2,1)S(1)}, bf16[8,136,256]{2,1,0:T(8,128)(2,1)}, u32[]{:S(2)}, u32[]{:S(2)}) collective-permute-start(bf16[8,136,256]{2,1,0:T(8,128)(2,1)S(1)} %norm.1.refs_2_), channel_id=1, source_target_pairs={{0,16},{2,18},{4,20},{6,22},{8,24},{10,26},{12,28},{14,30},{16,0},... | collective-permute-start | bytes 1671176 | tf_op jit(solution)/shard_map/x_far_2/ppermute | solution.py:24
  28.0 23.4 %collective-permute-start.6 = (bf16[1,256,768]{2,1,0:T(8,128)(2,1)S(1)}, bf16[1,256,768]{2,1,0:T(8,128)(2,1)S(1)}, u32[]{:S(2)}, u32[]{:S(2)}) collective-permute-start(bf16[1,256,768]{2,1,0:T(8,128)(2,1)S(1)} %bitcast.50), channel_id=1, source_target_pairs={{0,4},{2,6},{4,0},{6,2},{8,12},{10,14},{12,8},{14,10},{16,20},{18,... | collective-permute-start | bytes 1179656 | tf_op jit(solution)/shard_map/line_w0/ppermute | solution.py:24
  40.9 0.6 copy-start.6
  41.6 0.6 copy-start.7
  42.2 1.1 copy-start.11
  43.2 23.2 %copy-start.12 = (bf16[3,256,768]{2,1,0:T(8,128)(2,1)S(1)}, bf16[3,256,768]{2,1,0:T(8,128)(2,1)}, u32[]{:S(2)}) copy-start(bf16[3,256,768]{2,1,0:T(8,128)(2,1)} %copy-done.11) | copy-start | bytes 3538948
  51.4 30.8 %copy-start.16 = (bf16[1,256,768]{2,1,0:T(8,128)(2,1)}, bf16[1,256,768]{2,1,0:T(8,128)(2,1)S(1)}, u32[]{:S(2)}) copy-start(bf16[1,256,768]{2,1,0:T(8,128)(2,1)S(1)} %collective-permute-done.6.refs_9_.refs_5_) | copy-start | bytes 1179652
  51.4 15.0 %collective-permute-start.10 = (bf16[288,768]{1,0:T(8,128)(2,1)S(1)}, bf16[288,768]{1,0:T(8,128)(2,1)S(1)}, u32[]{:S(2)}, u32[]{:S(2)}) collective-permute-start(bf16[288,768]{1,0:T(8,128)(2,1)S(1)} %maximum_maximum_fusion), channel_id=1, source_target_pairs={{0,24},{2,26},{4,28},{6,30},{8,16},{10,18},{12,20},{14,22},{16,8},... | collective-permute-start | bytes 1327112 | tf_op jit(solution)/shard_map/w_3/ppermute | solution.py:24
  54.0 22.0 %collective-permute-start.7 = (bf16[8,136,256]{2,1,0:T(8,128)(2,1)}, bf16[8,136,256]{2,1,0:T(8,128)(2,1)S(1)}, u32[]{:S(2)}, u32[]{:S(2)}) collective-permute-start(bf16[8,136,256]{2,1,0:T(8,128)(2,1)} %collective-permute-done.3.refs_6_), channel_id=1, source_target_pairs={{0,8},{2,10},{4,12},{6,14},{8,0},{10,2},{12,4},{14,6},{16,24},{18,... | collective-permute-start | bytes 1671176 | tf_op jit(solution)/shard_map/x_last_1/ppermute | solution.py:24
  54.1 25.1 %collective-permute-start.9 = (bf16[8,136,256]{2,1,0:T(8,128)(2,1)}, bf16[8,136,256]{2,1,0:T(8,128)(2,1)S(1)}, u32[]{:S(2)}, u32[]{:S(2)}) collective-permute-start(bf16[8,136,256]{2,1,0:T(8,128)(2,1)} %collective-permute-done.3.refs_6_), channel_id=1, source_target_pairs={{0,1},{1,0},{2,3},{3,2},{4,5},{5,4},{6,7},{7,6},{8,9},{9,8},{10,11... | collective-permute-start | bytes 1671176 | tf_op jit(solution)/shard_map/side_far/ppermute | solution.py:24
  55.6 23.6 %collective-permute-start.11 = (bf16[2,256,768]{2,1,0:T(8,128)(2,1)S(1)}, bf16[2,256,768]{2,1,0:T(8,128)(2,1)S(1)}, u32[]{:S(2)}, u32[]{:S(2)}) collective-permute-start(bf16[2,256,768]{2,1,0:T(8,128)(2,1)S(1)} %get-tuple-element.74), channel_id=1, source_target_pairs={{0,4},{2,6},{4,0},{6,2},{8,12},{10,14},{12,8},{14,10},{16,20},{18,... | collective-permute-start | bytes 2359304 | tf_op jit(solution)/shard_map/line_w12/ppermute | solution.py:24
  57.1 22.1 %collective-permute-start.8 = (bf16[8,136,256]{2,1,0:T(8,128)(2,1)}, bf16[8,136,256]{2,1,0:T(8,128)(2,1)S(1)}, u32[]{:S(2)}, u32[]{:S(2)}) collective-permute-start(bf16[8,136,256]{2,1,0:T(8,128)(2,1)} %collective-permute-done.2.refs_4_), channel_id=1, source_target_pairs={{0,1},{1,0},{2,3},{3,2},{4,5},{5,4},{6,7},{7,6},{8,9},{9,8},{10,11... | collective-permute-start | bytes 1671176 | tf_op jit(solution)/shard_map/side_next/ppermute | solution.py:24
  66.5 0.6 copy-start.8
  67.2 20.2 %copy-start = (bf16[4,256,768]{2,1,0:T(8,128)(2,1)}, bf16[4,256,768]{2,1,0:T(8,128)(2,1)S(1)}, u32[]{:S(2)}) copy-start(bf16[4,256,768]{2,1,0:T(8,128)(2,1)S(1)} %get-tuple-element.79.refs_8_.refs_4_) | copy-start | bytes 4718596
  67.2 14.5 %collective-permute-start.12 = (bf16[1,256,768]{2,1,0:T(8,128)(2,1)S(1)}, bf16[1,256,768]{2,1,0:T(8,128)(2,1)S(1)}, u32[]{:S(2)}, u32[]{:S(2)}) collective-permute-start(bf16[1,256,768]{2,1,0:T(8,128)(2,1)S(1)} %get-tuple-element.75), channel_id=1, source_target_pairs={{0,4},{2,6},{4,0},{6,2},{8,12},{10,14},{12,8},{14,10},{16,20},{18,... | collective-permute-start | bytes 1179656 | tf_op jit(solution)/shard_map/line_w3/ppermute | solution.py:24
  76.0 21.4 %copy-start.20 = (bf16[8,136,256]{2,1,0:T(8,128)(2,1)}, bf16[8,136,256]{2,1,0:T(8,128)(2,1)S(1)}, u32[]{:S(2)}) copy-start(bf16[8,136,256]{2,1,0:T(8,128)(2,1)S(1)} %collective-permute-done.7.refs_2_) | copy-start | bytes 1671172
  79.2 2.4 %copy-start.22 = (bf16[8,136,256]{2,1,0:T(8,128)(2,1)}, bf16[8,136,256]{2,1,0:T(8,128)(2,1)S(1)}, u32[]{:S(2)}) copy-start(bf16[8,136,256]{2,1,0:T(8,128)(2,1)S(1)} %collective-permute-done.8.refs_5_) | copy-start | bytes 1671172
  79.2 2.4 %copy-start.21 = (bf16[8,136,256]{2,1,0:T(8,128)(2,1)}, bf16[8,136,256]{2,1,0:T(8,128)(2,1)S(1)}, u32[]{:S(2)}) copy-start(bf16[8,136,256]{2,1,0:T(8,128)(2,1)S(1)} %collective-permute-done.9.refs_7_) | copy-start | bytes 1671172
  79.2 8.2 %copy-start.14 = (bf16[2,256,768]{2,1,0:T(8,128)(2,1)}, bf16[2,256,768]{2,1,0:T(8,128)(2,1)S(1)}, u32[]{:S(2)}) copy-start(bf16[2,256,768]{2,1,0:T(8,128)(2,1)S(1)} %collective-permute-done.11.refs_10_.refs_6_) | copy-start | bytes 2359300
  81.6 5.8 %copy-start.17 = (bf16[1,256,768]{2,1,0:T(8,128)(2,1)}, bf16[1,256,768]{2,1,0:T(8,128)(2,1)S(1)}, u32[]{:S(2)}) copy-start(bf16[1,256,768]{2,1,0:T(8,128)(2,1)S(1)} %collective-permute-done.12.refs_11_.refs_7_) | copy-start | bytes 1179652
  81.6 5.7 %collective-permute-start.13 = (bf16[4,256,768]{2,1,0:T(8,128)(2,1)S(1)}, bf16[4,256,768]{2,1,0:T(8,128)(2,1)S(1)}, u32[]{:S(2)}, u32[]{:S(2)}) collective-permute-start(bf16[4,256,768]{2,1,0:T(8,128)(2,1)S(1)} %get-tuple-element.79.refs_8_.refs_4_), channel_id=1, source_target_pairs={{0,2},{2,0},{4,6},{6,4},{8,10},{10,8},{12,14},{14,12},{16,18},{18,... | collective-permute-start | bytes 4718600 | tf_op jit(solution)/shard_map/core_w/ppermute | solution.py:24
  81.7 5.7 %collective-permute-start.15 = (bf16[2,256,768]{2,1,0:T(8,128)(2,1)S(1)}, bf16[2,256,768]{2,1,0:T(8,128)(2,1)S(1)}, u32[]{:S(2)}, u32[]{:S(2)}) collective-permute-start(bf16[2,256,768]{2,1,0:T(8,128)(2,1)S(1)} %collective-permute-done.11.refs_10_.refs_6_), channel_id=1, source_target_pairs={{0,2},{2,0},{4,6},{6,4},{8,10},{10,8},{12,14},{14,12},{16,18},{18,... | collective-permute-start | bytes 2359304 | tf_op jit(solution)/shard_map/core_w/ppermute | solution.py:24
  82.2 4.6 %collective-permute-start.14 = (bf16[1,256,768]{2,1,0:T(8,128)(2,1)S(1)}, bf16[1,256,768]{2,1,0:T(8,128)(2,1)S(1)}, u32[]{:S(2)}, u32[]{:S(2)}) collective-permute-start(bf16[1,256,768]{2,1,0:T(8,128)(2,1)S(1)} %collective-permute-done.6.refs_9_.refs_5_), channel_id=1, source_target_pairs={{0,2},{2,0},{4,6},{6,4},{8,10},{10,8},{12,14},{14,12},{16,18},{18,... | collective-permute-start | bytes 1179656 | tf_op jit(solution)/shard_map/core_w/ppermute | solution.py:24
  82.3 5.1 %collective-permute-start.16 = (bf16[1,256,768]{2,1,0:T(8,128)(2,1)S(1)}, bf16[1,256,768]{2,1,0:T(8,128)(2,1)S(1)}, u32[]{:S(2)}, u32[]{:S(2)}) collective-permute-start(bf16[1,256,768]{2,1,0:T(8,128)(2,1)S(1)} %collective-permute-done.12.refs_11_.refs_7_), channel_id=1, source_target_pairs={{0,2},{2,0},{4,6},{6,4},{8,10},{10,8},{12,14},{14,12},{16,18},{18,... | collective-permute-start | bytes 1179656 | tf_op jit(solution)/shard_map/core_w/ppermute | solution.py:24
  82.7 16.2 %collective-permute-start.17 = (bf16[8,136,256]{2,1,0:T(8,128)(2,1)S(1)}, bf16[8,136,256]{2,1,0:T(8,128)(2,1)}, u32[]{:S(2)}, u32[]{:S(2)}) collective-permute-start(bf16[8,136,256]{2,1,0:T(8,128)(2,1)S(1)} %collective-permute-done.7.refs_2_), channel_id=1, source_target_pairs={{0,1},{1,0},{2,3},{3,2},{4,5},{5,4},{6,7},{7,6},{8,9},{9,8},{10,11... | collective-permute-start | bytes 1671176 | tf_op jit(solution)/shard_map/side_last/ppermute | solution.py:24
  86.8 0.8 copy-start.18
  87.4 0.8 copy-start.19
  87.4 1.1 copy-start.15
  87.4 1.5 %copy-start.13 = (bf16[4,256,768]{2,1,0:T(8,128)(2,1)}, bf16[4,256,768]{2,1,0:T(8,128)(2,1)S(1)}, u32[]{:S(2)}) copy-start(bf16[4,256,768]{2,1,0:T(8,128)(2,1)S(1)} %collective-permute-done.13.refs_12_.refs_8_) | copy-start | bytes 4718596
  97.4 11.5 %collective-permute-start.18 = (bf16[3,192,256]{2,1,0:T(8,128)(2,1)}, bf16[3,192,256]{2,1,0:T(8,128)(2,1)S(1)}, u32[]{:S(2)}, u32[]{:S(2)}) collective-permute-start(bf16[3,192,256]{2,1,0:T(8,128)(2,1)} %get-tuple-element.91.refs_4_), channel_id=1, source_target_pairs={{0,4},{2,6},{4,0},{6,2},{8,12},{10,14},{12,8},{14,10},{16,20},{18,... | collective-permute-start | bytes 884744 | tf_op jit(solution)/shard_map/kv_line/ppermute | solution.py:24
  99.0 4.2 %copy-start.10 = (bf16[3,192,256]{2,1,0:T(8,128)(2,1)S(1)}, bf16[3,192,256]{2,1,0:T(8,128)(2,1)}, u32[]{:S(2)}) copy-start(bf16[3,192,256]{2,1,0:T(8,128)(2,1)} %get-tuple-element.91.refs_4_) | copy-start | bytes 884740
  102.6 6.2 %copy-start.5 = (bf16[1,192,256]{2,1,0:T(8,128)(2,1)S(1)}, bf16[1,192,256]{2,1,0:T(8,128)(2,1)}, u32[]{:S(2)}) copy-start(bf16[1,192,256]{2,1,0:T(8,128)(2,1)} %keys_values.1.refs_8_) | copy-start | bytes 294916
  102.6 6.2 %collective-permute-start.19 = (bf16[1,192,256]{2,1,0:T(8,128)(2,1)}, bf16[1,192,256]{2,1,0:T(8,128)(2,1)S(1)}, u32[]{:S(2)}, u32[]{:S(2)}) collective-permute-start(bf16[1,192,256]{2,1,0:T(8,128)(2,1)} %keys_values.1.refs_8_), channel_id=1, source_target_pairs={{0,4},{2,6},{4,0},{6,2},{8,12},{10,14},{12,8},{14,10},{16,20},{18,... | collective-permute-start | bytes 294920 | tf_op jit(solution)/shard_map/kv_line/ppermute | solution.py:24
  103.2 7.4 %collective-permute-start.20 = (bf16[3,192,256]{2,1,0:T(8,128)(2,1)S(1)}, bf16[3,192,256]{2,1,0:T(8,128)(2,1)S(1)}, u32[]{:S(2)}, u32[]{:S(2)}) collective-permute-start(bf16[3,192,256]{2,1,0:T(8,128)(2,1)S(1)} %copy-done.10), channel_id=1, source_target_pairs={{0,2},{2,0},{4,6},{6,4},{8,10},{10,8},{12,14},{14,12},{16,18},{18,... | collective-permute-start | bytes 884744 | tf_op jit(solution)/shard_map/core_kv/ppermute | solution.py:24
  103.2 14.0 %copy-start.9 = (bf16[3,4,128,128]{3,2,1,0:T(8,128)(2,1)S(1)}, bf16[3,4,128,128]{3,2,1,0:T(8,128)(2,1)}, u32[]{:S(2)}) copy-start(bf16[3,4,128,128]{3,2,1,0:T(8,128)(2,1)} %get-tuple-element.96.refs_3_) | copy-start | bytes 1179652
  108.9 1.9 %collective-permute-start.21 = (bf16[3,192,256]{2,1,0:T(8,128)(2,1)S(1)}, bf16[3,192,256]{2,1,0:T(8,128)(2,1)S(1)}, u32[]{:S(2)}, u32[]{:S(2)}) collective-permute-start(bf16[3,192,256]{2,1,0:T(8,128)(2,1)S(1)} %collective-permute-done.18.refs_5_), channel_id=1, source_target_pairs={{0,2},{2,0},{4,6},{6,4},{8,10},{10,8},{12,14},{14,12},{16,18},{18,... | collective-permute-start | bytes 884744 | tf_op jit(solution)/shard_map/core_kv_line/ppermute | solution.py:24
  108.9 1.7 %collective-permute-start.22 = (bf16[1,192,256]{2,1,0:T(8,128)(2,1)S(1)}, bf16[1,192,256]{2,1,0:T(8,128)(2,1)S(1)}, u32[]{:S(2)}, u32[]{:S(2)}) collective-permute-start(bf16[1,192,256]{2,1,0:T(8,128)(2,1)S(1)} %copy-done.5), channel_id=1, source_target_pairs={{0,2},{2,0},{4,6},{6,4},{8,10},{10,8},{12,14},{14,12},{16,18},{18,... | collective-permute-start | bytes 294920 | tf_op jit(solution)/shard_map/core_kv/ppermute | solution.py:24
  109.4 1.4 collective-permute-start.23
  110.7 0.9 copy-start.3
  117.1 7.5 %collective-permute-start.24 = (bf16[128,512]{1,0:T(8,128)(2,1)S(1)}, bf16[128,512]{1,0:T(8,128)(2,1)S(1)}, u32[]{:S(2)}, u32[]{:S(2)}) collective-permute-start(bf16[128,512]{1,0:T(8,128)(2,1)S(1)} %attend.4), channel_id=1, source_target_pairs={{0,24},{2,26},{4,28},{6,30},{8,16},{10,18},{12,20},{14,22},{16,8},... | collective-permute-start | bytes 393224 | tf_op jit(solution)/shard_map/mixed_3/ppermute | solution.py:24
  121.9 10.5 %collective-permute-start.25 = (bf16[128,512]{1,0:T(8,128)(2,1)S(1)}, bf16[128,512]{1,0:T(8,128)(2,1)S(1)}, u32[]{:S(2)}, u32[]{:S(2)}) collective-permute-start(bf16[128,512]{1,0:T(8,128)(2,1)S(1)} %attend.5), channel_id=1, source_target_pairs={{0,16},{2,18},{4,20},{6,22},{8,24},{10,26},{12,28},{14,30},{16,0},... | collective-permute-start | bytes 393224 | tf_op jit(solution)/shard_map/mixed_2/ppermute | solution.py:24
  128.7 7.4 %collective-permute-start.26 = (bf16[128,512]{1,0:T(8,128)(2,1)S(1)}, bf16[128,512]{1,0:T(8,128)(2,1)S(1)}, u32[]{:S(2)}, u32[]{:S(2)}) collective-permute-start(bf16[128,512]{1,0:T(8,128)(2,1)S(1)} %attend.6), channel_id=1, source_target_pairs={{0,8},{2,10},{4,12},{6,14},{8,0},{10,2},{12,4},{14,6},{16,24},{18,... | collective-permute-start | bytes 393224 | tf_op jit(solution)/shard_map/mixed_1/ppermute | solution.py:24

commit v5 on v4

--- a/solution.py
+++ b/solution.py
@@ -106,6 +106,43 @@
         cost_estimate=pl.CostEstimate(flops=2 * 10**10, bytes_accessed=10**7, transcendentals=0),
         name="unpack",
     )(*plain, *packed)
+
+
+def join_kernel(*refs):
+    at = 0
+    for ref in refs[:-1]:
+        refs[-1][at : at + ref.shape[0]] = ref[...]
+        at += ref.shape[0]
+
+
+def join(parts):
+    count = sum(p.shape[0] for p in parts)
+    return pl.pallas_call(
+        join_kernel,
+        out_shape=jax.ShapeDtypeStruct((count, *parts[0].shape[1:]), parts[0].dtype),
+        in_specs=[VMEM] * len(parts),
+        out_specs=VMEM,
+        compiler_params=pltpu.CompilerParams(vmem_limit_bytes=12 * 2**20),
+        name="join",
+    )(*parts)
+
+
+def half_kernel(value, out):
+    out[...] = value[...]
+
+
+def half(value, index):
+    shape = (value.shape[0] // 2, *value.shape[1:])
+    return pl.pallas_call(
+        half_kernel,
+        grid=(1,),
+        out_shape=jax.ShapeDtypeStruct(shape, value.dtype),
+        in_specs=[pl.BlockSpec(shape, lambda t: (index, 0, 0))],
+        out_specs=pl.BlockSpec(shape, lambda t: (0, 0, 0)),
+        compiler_params=pltpu.CompilerParams(vmem_limit_bytes=8 * 2**20),
+        cost_estimate=pl.CostEstimate(flops=2 * 10**10, bytes_accessed=10**6, transcendentals=0),
+        name="half",
+    )(value)
 
 
 def project_kernel(kv, tiles, first_slot, tok, redo, pitch, n_x, n_w, *refs):
@@ -215,7 +252,7 @@
         + [full(a) for a in (cosine, sine, *caches)],
         out_specs=out_specs,
         scratch_shapes=[pltpu.VMEM((blocks, chunks * pitch, FEATS), jnp.bfloat16)],
-        compiler_params=pltpu.CompilerParams(vmem_limit_bytes=56 * 2**20),
+        compiler_params=pltpu.CompilerParams(vmem_limit_bytes=32 * 2**20),
         cost_estimate=pl.CostEstimate(
             flops=2 * chunks * pitch * blocks * FEATS * FEATS * tiles,
             bytes_accessed=2 * blocks * FEATS * (FEATS * tiles + chunks * pitch),
@@ -225,125 +262,127 @@
     )(x_ids, w_ids, *x_parts, *w_parts, cosine, sine, *caches)
 
 
-def attend_kernel(slot, tok, places, *refs):
-    begin_ref, q_ids, kv_ids, q_ref = refs[:4]
-    kv_refs = refs[4:-5]
-    out, scores, top, total, accum = refs[-5:]
+def attend_kernel(slots, tok, places, *refs):
+    begin_ref, q_ids, kv_ids = refs[:3]
+    count = len(slots)
+    q_refs, refs = refs[3 : 3 + count], refs[3 + count :]
+    kv_refs, refs = refs[: -count - 4], refs[-count - 4 :]
+    outs, (scores, top, total, accum) = refs[:count], refs[count:]
     begin = begin_ref[0]
-    q_id = q_ids[slot]
     heads = GROUP * tok
     scale = math.log2(math.e) / math.sqrt(HD)
     span = kv_refs[0].shape[1]
     cache_rows = span - tok
-    top[...] = jnp.full(top.shape, FAR, jnp.float32)
-    total[...] = jnp.zeros(total.shape, jnp.float32)
-    accum[...] = jnp.zeros(accum.shape, jnp.float32)
-
-    def score(column, keys, allowed):
-        value = lax.dot_general(
-            q_ref[0].reshape(heads, HD),
-            keys,
-            (((1,), (1,)), ((), ())),
-            preferred_element_type=jnp.float32,
-        )
-        if allowed is not None:
-            value = jnp.where(allowed(value.shape), value, FAR)
-        scores[:, column : column + value.shape[1]] = value
-        most = top[...]
-        for lane in range(0, value.shape[1], HD):
-            most = jnp.maximum(most, value[:, lane : lane + HD])
-        top[...] = most
-
-    def mix(column, values):
-        weights = []
-        some = total[...]
-        most = top[...]
-        for lane in range(0, values.shape[0], HD):
-            part = scores[:, column + lane : column + lane + HD]
-            weight = jnp.exp2(part * scale - most)
-            some = some + weight
-            weights.append(weight.astype(jnp.bfloat16))
-        total[...] = some
-        accum[...] += jnp.dot(
-            jnp.concatenate(weights, 1), values, preferred_element_type=jnp.float32
-        )
-
-    pending = []
+    groups = []
     for at in range(0, len(places), 4):
         group = places[at : at + 4]
         ids = [kv_ids[at + i] for i in range(len(group))]
-        least = functools.reduce(jnp.minimum, ids)
-        most = functools.reduce(jnp.maximum, ids)
-        base = at * span
-
-        def rows(first, last, half, group=group):
+        least, most = functools.reduce(jnp.minimum, ids), functools.reduce(jnp.maximum, ids)
+        groups.append((group, ids, least, most, at * span))
+
+    for n, slot in enumerate(slots):
+        q_id = q_ids[slot]
+        top[...] = jnp.full(top.shape, FAR, jnp.float32)
+        total[...] = jnp.zeros(total.shape, jnp.float32)
+        accum[...] = jnp.zeros(accum.shape, jnp.float32)
+
+        def rows(group, first, last, half):
             return jnp.concatenate(
-                [kv_refs[n][i, first:last, half * HD : (half + 1) * HD] for n, i in group], 0
+                [kv_refs[r][i, first:last, half * HD : (half + 1) * HD] for r, i in group], 0
             )
 
-        def starts(shape, step, ids=ids):
-            column = lax.broadcasted_iota(jnp.int32, shape, 1)
-            which = column // step
-            first = jnp.zeros(shape, jnp.int32)
-            for i, one in enumerate(ids):
-                first = jnp.where(which == i, one * step, first)
-            return first + column % step
-
-        def causal(shape, starts=starts):
-            row = lax.broadcasted_iota(jnp.int32, shape, 0)
-            return starts(shape, tok) <= q_id * tok + row % tok
-
-        def prefix(shape, starts=starts):
-            return starts(shape, cache_rows) < begin
-
-        shift = len(group) * tok
-
-        @pl.when((most + 1) * cache_rows <= begin)
-        def _(rows=rows, base=base):
-            score(base + shift, rows(tok, span, 0), None)
-
-        @pl.when(((most + 1) * cache_rows > begin) & (least * cache_rows < begin))
-        def _(rows=rows, prefix=prefix, base=base):
-            score(base + shift, rows(tok, span, 0), prefix)
-
-        @pl.when(most < q_id)
-        def _(rows=rows, base=base):
-            score(base, rows(0, tok, 0), None)
-
-        @pl.when((most >= q_id) & (least <= q_id))
-        def _(rows=rows, causal=causal, base=base):
-            score(base, rows(0, tok, 0), causal)
-
-        pending.append((least * cache_rows < begin, least <= q_id, rows, base, shift))
-
-    peak = jnp.max(top[...], axis=1, keepdims=True) * scale
-    top[...] = jnp.broadcast_to(peak, top.shape)
-    for cached, streamed, rows, base, shift in pending:
-
-        @pl.when(cached)
-        def _(rows=rows, base=base, shift=shift):
-            mix(base + shift, rows(tok, span, 1))
-
-        @pl.when(streamed)
-        def _(rows=rows, base=base):
-            mix(base, rows(0, tok, 1))
-
-    mixed = (accum[...] / jnp.sum(total[...], axis=1, keepdims=True)).astype(jnp.bfloat16)
-    for head in range(GROUP):
-        out[:, head * HD : (head + 1) * HD] = mixed[head * tok : (head + 1) * tok]
-
-
-def attend(slot, begin, queries, index, q_ids, kv_parts, places, kv_ids, tok):
+        def score(column, keys, allowed, n=n):
+            value = lax.dot_general(
+                q_refs[n][0].reshape(heads, HD),
+                keys,
+                (((1,), (1,)), ((), ())),
+                preferred_element_type=jnp.float32,
+            )
+            if allowed is not None:
+                value = jnp.where(allowed(value.shape), value, FAR)
+            scores[:, column : column + value.shape[1]] = value
+            most = top[...]
+            for lane in range(0, value.shape[1], HD):
+                most = jnp.maximum(most, value[:, lane : lane + HD])
+            top[...] = most
+
+        def mix(column, values):
+            weights = []
+            some = total[...]
+            most = top[...]
+            for lane in range(0, values.shape[0], HD):
+                part = scores[:, column + lane : column + lane + HD]
+                weight = jnp.exp2(part * scale - most)
+                some = some + weight
+                weights.append(weight.astype(jnp.bfloat16))
+            total[...] = some
+            accum[...] += jnp.dot(
+                jnp.concatenate(weights, 1), values, preferred_element_type=jnp.float32
+            )
+
+        for group, ids, least, most, base in groups:
+            shift = len(group) * tok
+
+            def starts(shape, step, ids=ids):
+                column = lax.broadcasted_iota(jnp.int32, shape, 1)
+                which = column // step
+                first = jnp.zeros(shape, jnp.int32)
+                for i, one in enumerate(ids):
+                    first = jnp.where(which == i, one * step, first)
+                return first + column % step
+
+            def causal(shape, starts=starts):
+                row = lax.broadcasted_iota(jnp.int32, (shape[0], 1), 0)
+                return starts((1, shape[1]), tok) <= q_id * tok + row % tok
+
+            def prefix(shape, starts=starts):
+                return starts((1, shape[1]), cache_rows) < begin
+
+            @pl.when((most + 1) * cache_rows <= begin)
+            def _(group=group, base=base):
+                score(base + shift, rows(group, tok, span, 0), None)
+
+            @pl.when(((most + 1) * cache_rows > begin) & (least * cache_rows < begin))
+            def _(group=group, prefix=prefix, base=base):
+                score(base + shift, rows(group, tok, span, 0), prefix)
+
+            @pl.when(most < q_id)
+            def _(group=group, base=base):
+                score(base, rows(group, 0, tok, 0), None)
+
+            @pl.when((most >= q_id) & (least <= q_id))
+            def _(group=group, causal=causal, base=base):
+                score(base, rows(group, 0, tok, 0), causal)
+
+        peak = jnp.max(top[...], axis=1, keepdims=True) * scale
+        top[...] = jnp.broadcast_to(peak, top.shape)
+        for group, ids, least, most, base in groups:
+            shift = len(group) * tok
+
+            @pl.when(least * cache_rows < begin)
+            def _(group=group, base=base):
+                mix(base + shift, rows(group, tok, span, 1))
+
+            @pl.when(least <= q_id)
+            def _(group=group, base=base):
+                mix(base, rows(group, 0, tok, 1))
+
+        mixed = (accum[...] / jnp.sum(total[...], axis=1, keepdims=True)).astype(jnp.bfloat16)
+        for head in range(GROUP):
+            outs[n][:, head * HD : (head + 1) * HD] = mixed[head * tok : (head + 1) * tok]
+
+
+def attend(slots, begin, queries, q_ids, kv_parts, places, kv_ids, tok):
     span = kv_parts[0].shape[1]
     n_rows = len(places) * span
     heads = GROUP * tok
-    return pl.pallas_call(
-        functools.partial(attend_kernel, slot, tok, places),
-        out_shape=jax.ShapeDtypeStruct((tok, GROUP * HD), jnp.bfloat16),
+    q_specs = [pl.BlockSpec((1, GROUP, tok, HD), lambda t, i=i: (i, 0, 0, 0)) for _, i in queries]
+    return pl.pallas_call(
+        functools.partial(attend_kernel, slots, tok, places),
         grid=(1,),
-        in_specs=[SMEM, SMEM, SMEM, pl.BlockSpec((1, GROUP, tok, HD), lambda t: (index, 0, 0, 0))]
-        + [VMEM] * len(kv_parts),
-        out_specs=VMEM,
+        out_shape=[jax.ShapeDtypeStruct((tok, GROUP * HD), jnp.bfloat16)] * len(slots),
+        in_specs=[SMEM, SMEM, SMEM] + q_specs + [VMEM] * len(kv_parts),
+        out_specs=[VMEM] * len(slots),
         scratch_shapes=[
             pltpu.VMEM((heads, n_rows), jnp.float32),
             pltpu.VMEM((heads, HD), jnp.float32),
@@ -352,12 +391,12 @@
         ],
         compiler_params=pltpu.CompilerParams(vmem_limit_bytes=8 * 2**20 + 5 * heads * n_rows),
         cost_estimate=pl.CostEstimate(
-            flops=4 * heads * n_rows * HD,
+            flops=4 * len(slots) * heads * n_rows * HD,
             bytes_accessed=4 * n_rows * HD,
-            transcendentals=heads * n_rows,
+            transcendentals=len(slots) * heads * n_rows,
         ),
         name="attend",
-    )(begin, q_ids, kv_ids, queries, *kv_parts)
+    )(begin, q_ids, kv_ids, *[q for q, _ in queries], *kv_parts)
 
 
 def per_device(
@@ -426,17 +465,19 @@
         w_sent = [jnp.concatenate([w, folded(c)], 0) for w, c in zip(w_cut[:3], caches)]
         w_own = w_cut[0][None]
         w_1, w_2 = across(w_sent[1], 1, "w"), across(w_sent[2], 2, "w")
-        far, next_x = across(own, 2, "x_far"), across(own, 1, "x_next")
-        own_side, w_line = sides(own, "own"), line(after(w_own, w_2), "w0")
-        w_some, w_mid, *cache_mid = unpack([w_own], [w_1, w_2], depth, fold)
+        far, next_x = across(after(own, w_2), 2, "x_far"), across(own, 1, "x_next")
+        own_side = sides(own, "own")
+        w_some, _, cache_2 = unpack([w_own], [w_2], depth, fold)
+        w_line = line(w_some, "w02")
+        w_some, w_mid, cache_1 = unpack([w_some], [w_1], depth, fold)
+        cache_mid = (cache_1, cache_2)
         late, late_cache, _ = lax.optimization_barrier((plane, caches[3], w_2))
         w_sent_3 = jnp.concatenate([w_cut[3], folded(late_cache)], 0)
         q_ids, cosine, sine = tables(late)
         ids = jnp.arange(count, dtype=jnp.int32)
         x_ids = jnp.concatenate([side * count + ids, (1 - side) * count + ids])
-        w_ids = [
-            (late ^ k) * crew + (inner ^ turn) for turn in (0, 2, 1, 3) for k in range(heads)
-        ]
+        order = ((0, 0), (2, 0), (1, 0), (0, 2), (2, 2), (1, 2), (3, 0), (3, 2))
+        w_ids = [(late ^ k) * crew + (inner ^ turn ^ flip) for flip in (0, 1) for k, turn in order]
         w_ids = jnp.stack(w_ids).astype(jnp.int32)
         kv_ids = [(late ^ k) * crew + (inner ^ turn) for k in range(heads) for turn in (0, 2, 1, 3)]
         kv_ids = jnp.stack(kv_ids).astype(jnp.int32)
@@ -450,17 +491,22 @@
         next_side, far_side = sides(next_x, "next"), sides(far, "far")
         w_3 = across(w_3, 3, "w")
         last = across(far, 1, "x_last")
-        w_mid_line = line(w_mid, "w12")
-        w_all, w_last, cache_last = unpack([w_some], [w_3], depth, fold)
+        w_mid_line = line(w_mid, "w1")
+        w_last, _, cache_last = unpack([], [w_3], depth, fold)
         w_last_line = line(w_last, "w3")
-        last, next_side, far_side, w_all, w_mid_line, w_last_line, w_line = lax.optimization_barrier(
-            (last, next_side, far_side, w_all, w_mid_line, w_last_line, w_line)
+        w_some = join([w_some, w_line, w_mid_line])
+        w_some_core = core(w_some, "w")
+        last_low, far_high = half(last, 0), half(far_side, 1)
+        moved = (last, next_side, far_side, w_last, w_last_line, w_some)
+        moved, w_some_core, last_low, far_high = lax.optimization_barrier(
+            (moved, w_some_core, last_low, far_high)
         )
+        last, next_side, far_side, w_last, w_last_line, w_some = moved
         caches = [caches[0], *cache_mid, cache_last]
-        last_side = sides(last, "last")
-        w_parts = [w_all, w_line, w_mid_line, w_last_line]
-        w_parts += [core(w, "w") for w in w_parts]
-        x_chunks = [[own, own_side], [next_x, next_side], [far, far_side], [last, last_side]]
+        last_side = [sides(last_low, "last"), across(far_high, 1, "x_last_side")]
+        w_parts = [w_some, w_last, w_last_line]
+        w_parts += [w_some_core, core(w_last, "w3"), core(w_last_line, "w3_line")]
+        x_chunks = [[own, own_side], [next_x, next_side], [far, far_side], [last, *last_side]]
     else:
         q_ids, cosine, sine = tables(plane)
         caches = [across(c, k) for k, c in enumerate(caches)]
@@ -489,10 +535,10 @@
         return project(kv, q, slots[0], chunks, x_ids, w_parts, w_ids, cosine, sine, some, tok, redo)
 
     if squared:
-        kv_some, q_some = projected(True, True, (0, 1, 2))
-        kv_new, queries = [kv_some, *projected(True, False, (3,))], [q_some]
-        x_chunks[3][0] = after(last, kv_new[1])
-        queries += projected(False, True, (3,))
+        kv_new = [*projected(True, False, (0, 1, 2)), *projected(True, False, (3,))]
+        for chunk in x_chunks:
+            chunk[0] = after(chunk[0], kv_new[1])
+        queries = [*projected(False, True, (0, 1, 2)), *projected(False, True, (3,))]
     else:
         kv_new, queries = [[value] for value in projected(True, True, tuple(range(heads)))]
 
@@ -514,14 +560,14 @@
         )
 
     back = [None] * heads
-    for k in reversed(range(heads)):
-        some, index = (queries[k // 3], k % 3) if squared else (queries[0], k)
-        if k + 2 < heads:
-            some = after(some, mixed, back[k + 2])
-        elif k + 1 < heads:
-            some = after(some, mixed)
-        mixed = attend(k, prefix_len, some, index, q_ids, kv_parts, places, kv_ids, tok)
-        back[k] = across(mixed, k, "mixed")
+    for slots in tuple((k,) for k in reversed(range(heads))):
+        some = [(queries[k // 3], k % 3) if squared else (queries[0], k) for k in slots]
+        if squared and slots != (3,):
+            earlier = [value for value in back[slots[0] + 2 :][:1] if value is not None]
+            some = [(after(some[0][0], *mixed, *earlier), some[0][1])]
+        mixed = attend(slots, prefix_len, some, q_ids, kv_parts, places, kv_ids, tok)
+        for k, value in zip(slots, mixed):
+            back[k] = across(value, k, "mixed")
     back = jnp.stack(back)
     columns = [lax.dynamic_index_in_dim(back, plane ^ h, 0, keepdims=False) for h in range(heads)]
     return jnp.concatenate(columns, 1)

time: 137 us -> 130 us (0.949)
  Pallas kernels: 35 us -> 29 us
  waiting for transfers between devices: 56.9 us -> 60.4 us
  other arithmetic: 7.56 us -> 4.69 us
  local copies, waits for them, and re-layouts: 8.44 us -> 6.47 us
    pallas_call x3 -> x4, Pallas kernels: 16.4 us -> 9.17 us  [project(): pl.pallas_call(functools.partial(project_kernel, kv, tiles, first_slot, t...]
    ppermute x27, waiting for transfers between devices: 56.9 us -> 60.4 us  [swap(): return lax.ppermute(value, axis, [(i, i ^ mask) for i in range(size)])]
    pallas_call x2 -> x3, Pallas kernels: 0.26 us -> 3.25 us  [unpack(): pl.pallas_call(functools.partial(unpack_kernel, len(plain), fold, len(pla...]
    pallas_call x4 -> x7, Pallas kernels: 17.9 us -> 16.2 us  [the longest x4 16 us: attend(): pl.pallas_call(functools.partial(attend_kernel, slots, tok, places), grid...]
    unnamed x52 -> x32, local copies, waits for them, and re-layouts: 5.36 us -> 4.65 us
  transfers between devices with their start and end apart: 27 -> 27, of which waited for: 15 -> 17; matrix products, arithmetic and copies ran while one was open for 5% -> 3% of each run, Pallas kernels for 22% -> 18%
where the time goes in v5:
time: 130 us; the launch traced here: 129 us
  waiting for transfers between devices  60.4 us (46%)
  Pallas kernels  29 us (22%)
  starting transfers between devices  27.8 us (21%)
  local copies, waits for them, and re-layouts  6.47 us (5%)
  other arithmetic  4.69 us (4%)
    ppermute x27, waiting for transfers between devices, swap(): return lax.ppermute(value, axis, [(i, i ^ mask) for i in range(size)])  60.4 us
    ppermute x27, starting transfers between devices, swap(): return lax.ppermute(value, axis, [(i, i ^ mask) for i in range(size)])  27.8 us
    pallas_call x4, Pallas kernels, attend(): pl.pallas_call(functools.partial(attend_kernel, slots, tok, places), grid...  16 us
    pallas_call x4, Pallas kernels, project(): pl.pallas_call(functools.partial(project_kernel, kv, tiles, first_slot, t...  9.17 us
    unnamed x32, local copies, waits for them, and re-layouts  4.65 us
    pallas_call x3, Pallas kernels, unpack(): pl.pallas_call(functools.partial(unpack_kernel, len(plain), fold, len(pla...  3.25 us
  transfers between devices with their start and end apart: 27, of which 17 were waited for; matrix products, arithmetic and copies ran while one was open for 3% of the time, Pallas kernels for 18%

profile of v5, /device:TPU:0, one launch (start us, length us, event | category | flops | bytes accessed | tf_op | source)
XLA Modules:
  0.0 129.3 jit_solution(12356889211025330927)
XLA Ops:
  0.0 1.5 %constant_dynamic-slice_fusion = (bf16[256,768]{1,0:T(8,128)(2,1)S(1)}, bf16[256,768]{1,0:T(8,128)(2,1)S(1)}, bf16[256,768]{1,0:T(8,128)(2,1)S(1)}, bf16[256,768]{1,0:T(8,128)(2,1)S(1)}) fusion(bf16[256,3072]{1,0:T(8,128)(2,1)} %param.9, s32[]{:T(128)S(6)} %select_n.55, s32[]{:T(128)S(6)} %select_n.53, s32[]{:T(128)S(6)} %select_n.52, s32[]{:T(128)S(6)} %select_n.54), kind=kLoop, calls=%fused_computation.50 | loop fusion | bytes 3145744 | tf_op jit(solution)/shard_map/dynamic_slice | solution.py:417
  1.6 0.2 squares.1.refs_0_
  1.8 3.0 %collective-permute-start = (f32[136,128]{1,0:T(8,128)S(1)}, f32[136,128]{1,0:T(8,128)S(1)}, u32[]{:S(2)}, u32[]{:S(2)}) collective-permute-start(f32[136,128]{1,0:T(8,128)S(1)} %squares.1.refs_0_), channel_id=1, source_target_pairs={{0,1},{1,0},{2,3},{3,2},{4,5},{5,4},{6,7},{7,6},{8,9},{9,8},{10,11... | collective-permute-start | bytes 208904 | tf_op jit(solution)/shard_map/side_sums/ppermute | solution.py:24
  4.9 1.0 fusion.7
  5.8 1.6 %collective-permute-start.5 = (bf16[288,768]{1,0:T(8,128)(2,1)}, bf16[288,768]{1,0:T(8,128)(2,1)}, u32[]{:S(2)}, u32[]{:S(2)}) collective-permute-start(bf16[288,768]{1,0:T(8,128)(2,1)} %get-tuple-element.126), channel_id=1, source_target_pairs={{0,8},{2,10},{4,12},{6,14},{8,0},{10,2},{12,4},{14,6},{16,24},{18,... | collective-permute-start | bytes 1327112 | tf_op jit(solution)/shard_map/w_1/ppermute | solution.py:24
  7.4 2.6 %collective-permute-start.3 = (bf16[288,768]{1,0:T(8,128)(2,1)}, bf16[288,768]{1,0:T(8,128)(2,1)S(1)}, u32[]{:S(2)}, u32[]{:S(2)}) collective-permute-start(bf16[288,768]{1,0:T(8,128)(2,1)} %get-tuple-element.127), channel_id=1, source_target_pairs={{0,16},{2,18},{4,20},{6,22},{8,24},{10,26},{12,28},{14,30},{16,0},... | collective-permute-start | bytes 1327112 | tf_op jit(solution)/shard_map/w_2/ppermute | solution.py:24
  10.7 0.6 pad_maximum_fusion.6
  11.4 0.2 norm.1.refs_2_
  11.6 0.5 collective-permute-start.2
  12.1 0.5 collective-permute-start.1
  12.7 15.4 %collective-permute-done.3.refs_1_ = bf16[288,768]{1,0:T(8,128)(2,1)S(1)} collective-permute-done((bf16[288,768]{1,0:T(8,128)(2,1)}, bf16[288,768]{1,0:T(8,128)(2,1)S(1)}, u32[]{:S(2)}, u32[]{:S(2)}) %collective-permute-start.3) | collective-permute-done | bytes 442400 | tf_op jit(solution)/shard_map/w_2/ppermute | solution.py:24
  28.1 0.8 copy-done.2
  29.0 3.0 %collective-permute-start.4 = (bf16[8,136,256]{2,1,0:T(8,128)(2,1)S(1)}, bf16[8,136,256]{2,1,0:T(8,128)(2,1)S(1)}, u32[]{:S(2)}, u32[]{:S(2)}) collective-permute-start(bf16[8,136,256]{2,1,0:T(8,128)(2,1)S(1)} %norm.1.refs_2_), channel_id=1, source_target_pairs={{0,16},{2,18},{4,20},{6,22},{8,24},{10,26},{12,28},{14,30},{16,0},... | collective-permute-start | bytes 1671176 | tf_op jit(solution)/shard_map/x_far_2/ppermute | solution.py:24
  32.1 1.0 copy-done.3
  33.1 1.1 unpack.3
  34.2 1.5 %collective-permute-start.6 = (bf16[2,256,768]{2,1,0:T(8,128)(2,1)}, bf16[2,256,768]{2,1,0:T(8,128)(2,1)S(1)}, u32[]{:S(2)}, u32[]{:S(2)}) collective-permute-start(bf16[2,256,768]{2,1,0:T(8,128)(2,1)} %get-tuple-element.58.refs_0_), channel_id=1, source_target_pairs={{0,4},{2,6},{4,0},{6,2},{8,12},{10,14},{12,8},{14,10},{16,20},{18,... | collective-permute-start | bytes 2359304 | tf_op jit(solution)/shard_map/line_w02/ppermute | solution.py:24
  35.8 0.1 stack.117.refs_1_
  36.0 1.4 %unpack.4 = (bf16[3,256,768]{2,1,0:T(8,128)(2,1)S(1)}, bf16[1,256,768]{2,1,0:T(8,128)(2,1)S(1)}, bf16[96,256]{1,0:T(8,128)(2,1)S(1)}) custom-call(bf16[2,256,768]{2,1,0:T(8,128)(2,1)} %get-tuple-element.58.refs_0_, bf16[288,768]{1,0:T(8,128)(2,1)} %collective-permute-done.5.refs_1_), custom_call_target="tpu_custom_call" | custom-call | flops 20000000000 | bytes 10000000 | tf_op jit(solution)/shard_map/unpack/pallas_call | solution.py:97
  37.3 1.4 %fusion.16 = (f32[4,192,64]{2,1,0:T(8,128)S(1)}, f32[4,192,64]{2,1,0:T(8,128)S(1)}, f32[4,192,64]{2,1,0:T(8,128)S(1)}) fusion(f32[64]{0:T(128)S(1)} %multiply_exponential_fusion, f32[4,192]{1,0:T(4,128)S(1)} %add_convert_fusion), kind=kLoop, calls=%fused_computation.32 | loop fusion | flops 98304 | bytes 593152 | tf_op jit(solution)/shard_map/neg | solution.py:449
  38.8 0.2 pad_maximum_fusion.4.refs_11_.refs_14_
  39.0 0.2 pad_maximum_fusion.5.refs_12_.refs_15_
  39.2 10.7 %collective-permute-done.2.refs_4_ = bf16[8,136,256]{2,1,0:T(8,128)(2,1)S(1)} collective-permute-done((bf16[8,136,256]{2,1,0:T(8,128)(2,1)S(1)}, bf16[8,136,256]{2,1,0:T(8,128)(2,1)S(1)}, u32[]{:S(2)}, u32[]{:S(2)}) %collective-permute-start.2) | collective-permute-done | bytes 557088 | tf_op jit(solution)/shard_map/x_next_1/ppermute | solution.py:24
  49.9 10.2 %collective-permute-done.4.refs_6_ = bf16[8,136,256]{2,1,0:T(8,128)(2,1)S(1)} collective-permute-done((bf16[8,136,256]{2,1,0:T(8,128)(2,1)S(1)}, bf16[8,136,256]{2,1,0:T(8,128)(2,1)S(1)}, u32[]{:S(2)}, u32[]{:S(2)}) %collective-permute-start.4) | collective-permute-done | bytes 557088 | tf_op jit(solution)/shard_map/x_far_2/ppermute | solution.py:24
  60.1 1.9 %collective-permute-start.10 = (bf16[288,768]{1,0:T(8,128)(2,1)S(1)}, bf16[288,768]{1,0:T(8,128)(2,1)S(1)}, u32[]{:S(2)}, u32[]{:S(2)}) collective-permute-start(bf16[288,768]{1,0:T(8,128)(2,1)S(1)} %maximum_maximum_fusion), channel_id=1, source_target_pairs={{0,24},{2,26},{4,28},{6,30},{8,16},{10,18},{12,20},{14,22},{16,8},... | collective-permute-start | bytes 1327112 | tf_op jit(solution)/shard_map/w_3/ppermute | solution.py:24
  62.0 1.5 %collective-permute-start.12 = (bf16[1,256,768]{2,1,0:T(8,128)(2,1)S(1)}, bf16[1,256,768]{2,1,0:T(8,128)(2,1)S(1)}, u32[]{:S(2)}, u32[]{:S(2)}) collective-permute-start(bf16[1,256,768]{2,1,0:T(8,128)(2,1)S(1)} %get-tuple-element.78), channel_id=1, source_target_pairs={{0,4},{2,6},{4,0},{6,2},{8,12},{10,14},{12,8},{14,10},{16,20},{18,... | collective-permute-start | bytes 1179656 | tf_op jit(solution)/shard_map/line_w1/ppermute | solution.py:24
  63.5 0.5 collective-permute-start.9
  64.0 1.5 %collective-permute-start.8 = (bf16[8,136,256]{2,1,0:T(8,128)(2,1)S(1)}, bf16[8,136,256]{2,1,0:T(8,128)(2,1)S(1)}, u32[]{:S(2)}, u32[]{:S(2)}) collective-permute-start(bf16[8,136,256]{2,1,0:T(8,128)(2,1)S(1)} %collective-permute-done.2.refs_4_), channel_id=1, source_target_pairs={{0,1},{1,0},{2,3},{3,2},{4,5},{5,4},{6,7},{7,6},{8,9},{9,8},{10,11... | collective-permute-start | bytes 1671176 | tf_op jit(solution)/shard_map/side_next/ppermute | solution.py:24
  65.5 4.3 %collective-permute-done.12.refs_2_ = bf16[1,256,768]{2,1,0:T(8,128)(2,1)S(1)} collective-permute-done((bf16[1,256,768]{2,1,0:T(8,128)(2,1)S(1)}, bf16[1,256,768]{2,1,0:T(8,128)(2,1)S(1)}, u32[]{:S(2)}, u32[]{:S(2)}) %collective-permute-start.12) | collective-permute-done | bytes 393248 | tf_op jit(solution)/shard_map/line_w1/ppermute | solution.py:24
  69.8 0.2 join.1.refs_5_.refs_8_
  70.0 0.4 collective-permute-done.10.refs_0_
  70.4 0.8 unpack.5
  71.2 1.5 %collective-permute-start.11 = (bf16[1,256,768]{2,1,0:T(8,128)(2,1)S(1)}, bf16[1,256,768]{2,1,0:T(8,128)(2,1)S(1)}, u32[]{:S(2)}, u32[]{:S(2)}) collective-permute-start(bf16[1,256,768]{2,1,0:T(8,128)(2,1)S(1)} %get-tuple-element.83.refs_6_.refs_9_), channel_id=1, source_target_pairs={{0,4},{2,6},{4,0},{6,2},{8,12},{10,14},{12,8},{14,10},{16,20},{18,... | collective-permute-start | bytes 1179656 | tf_op jit(solution)/shard_map/line_w3/ppermute | solution.py:24
  72.7 0.4 collective-permute-done.9.value.refs_7_
  73.1 3.2 %collective-permute-done.7.value.refs_2_ = bf16[8,136,256]{2,1,0:T(8,128)(2,1)S(1)} collective-permute-done((bf16[8,136,256]{2,1,0:T(8,128)(2,1)S(1)}, bf16[8,136,256]{2,1,0:T(8,128)(2,1)S(1)}, u32[]{:S(2)}, u32[]{:S(2)}) %collective-permute-start.7) | collective-permute-done | bytes 557088 | tf_op jit(solution)/shard_map/x_last_1/ppermute | solution.py:24
  76.3 2.7 %collective-permute-done.8.refs_5_ = bf16[8,136,256]{2,1,0:T(8,128)(2,1)S(1)} collective-permute-done((bf16[8,136,256]{2,1,0:T(8,128)(2,1)S(1)}, bf16[8,136,256]{2,1,0:T(8,128)(2,1)S(1)}, u32[]{:S(2)}, u32[]{:S(2)}) %collective-permute-start.8) | collective-permute-done | bytes 557088 | tf_op jit(solution)/shard_map/side_next/ppermute | solution.py:24
  79.0 3.3 %collective-permute-done.11.refs_7_.refs_10_ = bf16[1,256,768]{2,1,0:T(8,128)(2,1)S(1)} collective-permute-done((bf16[1,256,768]{2,1,0:T(8,128)(2,1)S(1)}, bf16[1,256,768]{2,1,0:T(8,128)(2,1)S(1)}, u32[]{:S(2)}, u32[]{:S(2)}) %collective-permute-start.11) | collective-permute-done | bytes 393248 | tf_op jit(solution)/shard_map/line_w3/ppermute | solution.py:24
  82.3 0.5 collective-permute-start.17
  82.8 0.5 collective-permute-start.14
  83.4 0.1 collective-permute-start.15
  83.5 0.6 collective-permute-done.16.refs_9_.refs_12_
  84.1 0.6 collective-permute-done.17.refs_10_.refs_13_
  84.6 2.4 %keys_values.3.refs_4_ = bf16[3,192,256]{2,1,0:T(8,128)(2,1)S(1)} custom-call(s32[16]{0:T(128)S(1)} %pad_add_fusion.1.refs_0_, s32[16]{0:T(128)S(1)} %stack.117.refs_1_, bf16[8,136,256]{2,1,0:T(8,128)(2,1)S(1)} %norm.1.refs_2_, bf16[8,136,256]{2,1,0:T(8,128)(2,1)S(1)} %collective-permute-done.1.refs_3_, ...), custom_call_target="tpu_custom_call" | custom-call | flops 905969664 | bytes 5636096 | tf_op jit(solution)/shard_map/keys_values/pallas_call | solution.py:245
  87.1 1.6 %collective-permute-start.18 = (bf16[3,192,256]{2,1,0:T(8,128)(2,1)S(1)}, bf16[3,192,256]{2,1,0:T(8,128)(2,1)S(1)}, u32[]{:S(2)}, u32[]{:S(2)}) collective-permute-start(bf16[3,192,256]{2,1,0:T(8,128)(2,1)S(1)} %keys_values.3.refs_4_), channel_id=1, source_target_pairs={{0,4},{2,6},{4,0},{6,2},{8,12},{10,14},{12,8},{14,10},{16,20},{18,... | collective-permute-start | bytes 884744 | tf_op jit(solution)/shard_map/kv_line/ppermute | solution.py:24
  88.6 2.8 %collective-permute-done.14.refs_3_ = bf16[4,136,256]{2,1,0:T(8,128)(2,1)S(1)} collective-permute-done((bf16[4,136,256]{2,1,0:T(8,128)(2,1)S(1)}, bf16[4,136,256]{2,1,0:T(8,128)(2,1)S(1)}, u32[]{:S(2)}, u32[]{:S(2)}) %collective-permute-start.14) | collective-permute-done | bytes 278560 | tf_op jit(solution)/shard_map/side_last/ppermute | solution.py:24
  91.4 0.2 collective-permute-done.15.refs_4_
  91.6 1.4 %keys_values.2.refs_8_ = bf16[1,192,256]{2,1,0:T(8,128)(2,1)S(1)} custom-call(s32[16]{0:T(128)S(1)} %pad_add_fusion.1.refs_0_, s32[16]{0:T(128)S(1)} %stack.117.refs_1_, bf16[8,136,256]{2,1,0:T(8,128)(2,1)S(1)} %collective-permute-done.7.value.refs_2_, bf16[4,136,256]{2,1,0:T(8,128)(2,1)S(1)} %collective-permute-done.14.refs_3_, ...), custom_call_target="tpu_custom_call" | custom-call | flops 301989888 | bytes 3276800 | tf_op jit(solution)/shard_map/keys_values/pallas_call | solution.py:245
  93.1 1.6 %collective-permute-start.19 = (bf16[1,192,256]{2,1,0:T(8,128)(2,1)S(1)}, bf16[1,192,256]{2,1,0:T(8,128)(2,1)S(1)}, u32[]{:S(2)}, u32[]{:S(2)}) collective-permute-start(bf16[1,192,256]{2,1,0:T(8,128)(2,1)S(1)} %keys_values.2.refs_8_), channel_id=1, source_target_pairs={{0,4},{2,6},{4,0},{6,2},{8,12},{10,14},{12,8},{14,10},{16,20},{18,... | collective-permute-start | bytes 294920 | tf_op jit(solution)/shard_map/kv_line/ppermute | solution.py:24
  94.6 2.0 %queries.3.refs_3_ = bf16[1,4,128,128]{3,2,1,0:T(8,128)(2,1)S(1)} custom-call(s32[16]{0:T(128)S(1)} %pad_add_fusion.1.refs_0_, s32[16]{0:T(128)S(1)} %stack.117.refs_1_, bf16[8,136,256]{2,1,0:T(8,128)(2,1)S(1)} %collective-permute-done.7.value.refs_2_, bf16[4,136,256]{2,1,0:T(8,128)(2,1)S(1)} %collective-permute-done.14.refs_3_, ...), custom_call_target="tpu_custom_call" | custom-call | flops 603979776 | bytes 5373952 | tf_op jit(solution)/shard_map/queries/pallas_call | solution.py:245
  96.6 1.7 %collective-permute-done.19.refs_9_ = bf16[1,192,256]{2,1,0:T(8,128)(2,1)S(1)} collective-permute-done((bf16[1,192,256]{2,1,0:T(8,128)(2,1)S(1)}, bf16[1,192,256]{2,1,0:T(8,128)(2,1)S(1)}, u32[]{:S(2)}, u32[]{:S(2)}) %collective-permute-start.19) | collective-permute-done | bytes 98336 | tf_op jit(solution)/shard_map/kv_line/ppermute | solution.py:24
  98.3 0.5 collective-permute-start.22
  98.8 1.2 collective-permute-done.22.refs_10_
  100.0 0.1 collective-permute-done.23.refs_11_
  100.1 5.0 %attend.4 = bf16[128,512]{1,0:T(8,128)(2,1)S(1)} custom-call(s32[1]{0:T(128)} %copy.8.refs_0_, s32[4]{0:T(128)S(1)} %get-tuple-element.67.refs_1_, s32[16]{0:T(128)S(1)} %stack.122.refs_2_, bf16[1,4,128,128]{3,2,1,0:T(8,128)(2,1)S(1)} %queries.3.refs_3_, bf16[3,192,256]{2,1,0:T(8,128)(2,1)S(1)} %keys_values.3.refs_4_, ...), custom_call_target="tpu_custom_call" | custom-call | flops 805306368 | bytes 1572864 | tf_op jit(solution)/shard_map/attend/pallas_call | solution.py:380
  105.2 0.2 collective-permute-start.24
  105.3 3.4 %queries.2.refs_3_ = bf16[3,4,128,128]{3,2,1,0:T(8,128)(2,1)S(1)} custom-call(s32[16]{0:T(128)S(1)} %pad_add_fusion.1.refs_0_, s32[16]{0:T(128)S(1)} %stack.117.refs_1_, bf16[8,136,256]{2,1,0:T(8,128)(2,1)S(1)} %norm.1.refs_2_, bf16[8,136,256]{2,1,0:T(8,128)(2,1)S(1)} %collective-permute-done.1.refs_3_, ...), custom_call_target="tpu_custom_call" | custom-call | flops 1811939328 | bytes 7733248 | tf_op jit(solution)/shard_map/queries/pallas_call | solution.py:245
  108.7 4.2 %attend.5 = bf16[128,512]{1,0:T(8,128)(2,1)S(1)} custom-call(s32[1]{0:T(128)} %copy.8.refs_0_, s32[4]{0:T(128)S(1)} %get-tuple-element.67.refs_1_, s32[16]{0:T(128)S(1)} %stack.122.refs_2_, bf16[3,4,128,128]{3,2,1,0:T(8,128)(2,1)S(1)} %queries.2.refs_3_, bf16[3,192,256]{2,1,0:T(8,128)(2,1)S(1)} %keys_values.3.refs_4_, ...), custom_call_target="tpu_custom_call" | custom-call | flops 805306368 | bytes 1572864 | tf_op jit(solution)/shard_map/attend/pallas_call | solution.py:380
  113.1 3.6 %attend.6 = bf16[128,512]{1,0:T(8,128)(2,1)S(1)} custom-call(s32[1]{0:T(128)} %copy.8.refs_0_, s32[4]{0:T(128)S(1)} %get-tuple-element.67.refs_1_, s32[16]{0:T(128)S(1)} %stack.122.refs_2_, bf16[3,4,128,128]{3,2,1,0:T(8,128)(2,1)S(1)} %queries.2.refs_3_, bf16[3,192,256]{2,1,0:T(8,128)(2,1)S(1)} %keys_values.3.refs_4_, ...), custom_call_target="tpu_custom_call" | custom-call | flops 805306368 | bytes 1572864 | tf_op jit(solution)/shard_map/attend/pallas_call | solution.py:380
  116.7 3.1 %collective-permute-start.26 = (bf16[128,512]{1,0:T(8,128)(2,1)S(1)}, bf16[128,512]{1,0:T(8,128)(2,1)S(1)}, u32[]{:S(2)}, u32[]{:S(2)}) collective-permute-start(bf16[128,512]{1,0:T(8,128)(2,1)S(1)} %attend.6), channel_id=1, source_target_pairs={{0,8},{2,10},{4,12},{6,14},{8,0},{10,2},{12,4},{14,6},{16,24},{18,... | collective-permute-start | bytes 393224 | tf_op jit(solution)/shard_map/mixed_1/ppermute | solution.py:24
  119.8 2.5 %collective-permute-done.25 = bf16[128,512]{1,0:T(8,128)(2,1)S(1)} collective-permute-done((bf16[128,512]{1,0:T(8,128)(2,1)S(1)}, bf16[128,512]{1,0:T(8,128)(2,1)S(1)}, u32[]{:S(2)}, u32[]{:S(2)}) %collective-permute-start.25) | collective-permute-done | bytes 131104 | tf_op jit(solution)/shard_map/mixed_2/ppermute | solution.py:24
  122.3 1.0 copy-done.5
  123.3 1.0 copy-done.7
  124.2 0.9 copy-done.9
  125.1 3.2 %attend.7 = bf16[128,512]{1,0:T(8,128)(2,1)S(1)} custom-call(s32[1]{0:T(128)} %copy.8.refs_0_, s32[4]{0:T(128)S(1)} %get-tuple-element.67.refs_1_, s32[16]{0:T(128)S(1)} %stack.122.refs_2_, bf16[3,4,128,128]{3,2,1,0:T(8,128)(2,1)S(1)} %queries.2.refs_3_, bf16[3,192,256]{2,1,0:T(8,128)(2,1)S(1)} %keys_values.3.refs_4_, ...), custom_call_target="tpu_custom_call" | custom-call | flops 805306368 | bytes 1572864 | tf_op jit(solution)/shard_map/attend/pallas_call | solution.py:380
  128.5 0.8 pad_maximum_fusion.3
  (64 shorter events, 0.9 us)
Async XLA Ops:
  0.0 1.6 %copy-start = (bf16[128,2048]{1,0:T(8,128)(2,1)S(1)}, bf16[128,2048]{1,0:T(8,128)(2,1)}, u32[]{:S(2)}) copy-start(bf16[128,2048]{1,0:T(8,128)(2,1)} %stream.1) | copy-start | bytes 1572868
  0.0 1.6 %copy-start.1 = (bf16[8,2048]{1,0:T(8,128)(2,1)S(1)}, bf16[8,2048]{1,0:T(8,128)(2,1)}, u32[]{:S(2)}) copy-start(bf16[8,2048]{1,0:T(8,128)(2,1)} %hidden.3) | copy-start | bytes 98308
  0.0 4.8 %copy-start.15 = (s32[8]{0:T(128)S(1)}, s32[8]{0:T(128)}, u32[]{:S(2)}) copy-start(s32[8]{0:T(128)} %param.12) | copy-start | bytes 100
  0.0 4.8 %copy-start.11 = (bf16[2,64,512]{2,1,0:T(8,128)(2,1)S(1)}, bf16[2,64,512]{2,1,0:T(8,128)(2,1)}, u32[]{:S(2)}) copy-start(bf16[2,64,512]{2,1,0:T(8,128)(2,1)} %param.10) | copy-start | bytes 393220
  1.5 9.1 %copy-start.14 = (f32[4096]{0:T(1024)S(1)}, f32[4096]{0:T(1024)}, u32[]{:S(2)}) copy-start(f32[4096]{0:T(1024)} %param.8) | copy-start | bytes 49156
  1.8 9.7 %collective-permute-start = (f32[136,128]{1,0:T(8,128)S(1)}, f32[136,128]{1,0:T(8,128)S(1)}, u32[]{:S(2)}, u32[]{:S(2)}) collective-permute-start(f32[136,128]{1,0:T(8,128)S(1)} %squares.1.refs_0_), channel_id=1, source_target_pairs={{0,1},{1,0},{2,3},{3,2},{4,5},{5,4},{6,7},{7,6},{8,9},{9,8},{10,11... | collective-permute-start | bytes 208904 | tf_op jit(solution)/shard_map/side_sums/ppermute | solution.py:24
  5.8 30.1 %collective-permute-start.5 = (bf16[288,768]{1,0:T(8,128)(2,1)}, bf16[288,768]{1,0:T(8,128)(2,1)}, u32[]{:S(2)}, u32[]{:S(2)}) collective-permute-start(bf16[288,768]{1,0:T(8,128)(2,1)} %get-tuple-element.126), channel_id=1, source_target_pairs={{0,8},{2,10},{4,12},{6,14},{8,0},{10,2},{12,4},{14,6},{16,24},{18,... | collective-permute-start | bytes 1327112 | tf_op jit(solution)/shard_map/w_1/ppermute | solution.py:24
  7.4 20.7 %collective-permute-start.3 = (bf16[288,768]{1,0:T(8,128)(2,1)}, bf16[288,768]{1,0:T(8,128)(2,1)S(1)}, u32[]{:S(2)}, u32[]{:S(2)}) collective-permute-start(bf16[288,768]{1,0:T(8,128)(2,1)} %get-tuple-element.127), channel_id=1, source_target_pairs={{0,16},{2,18},{4,20},{6,22},{8,24},{10,26},{12,28},{14,30},{16,0},... | collective-permute-start | bytes 1327112 | tf_op jit(solution)/shard_map/w_2/ppermute | solution.py:24
  11.6 38.3 %collective-permute-start.2 = (bf16[8,136,256]{2,1,0:T(8,128)(2,1)S(1)}, bf16[8,136,256]{2,1,0:T(8,128)(2,1)S(1)}, u32[]{:S(2)}, u32[]{:S(2)}) collective-permute-start(bf16[8,136,256]{2,1,0:T(8,128)(2,1)S(1)} %norm.1.refs_2_), channel_id=1, source_target_pairs={{0,8},{2,10},{4,12},{6,14},{8,0},{10,2},{12,4},{14,6},{16,24},{18,... | collective-permute-start | bytes 1671176 | tf_op jit(solution)/shard_map/x_next_1/ppermute | solution.py:24
  12.1 37.8 %collective-permute-start.1 = (bf16[8,136,256]{2,1,0:T(8,128)(2,1)S(1)}, bf16[8,136,256]{2,1,0:T(8,128)(2,1)S(1)}, u32[]{:S(2)}, u32[]{:S(2)}) collective-permute-start(bf16[8,136,256]{2,1,0:T(8,128)(2,1)S(1)} %norm.1.refs_2_), channel_id=1, source_target_pairs={{0,1},{1,0},{2,3},{3,2},{4,5},{5,4},{6,7},{7,6},{8,9},{9,8},{10,11... | collective-permute-start | bytes 1671176 | tf_op jit(solution)/shard_map/side_own/ppermute | solution.py:24
  28.1 0.8 copy-start.2
  29.0 31.1 %collective-permute-start.4 = (bf16[8,136,256]{2,1,0:T(8,128)(2,1)S(1)}, bf16[8,136,256]{2,1,0:T(8,128)(2,1)S(1)}, u32[]{:S(2)}, u32[]{:S(2)}) collective-permute-start(bf16[8,136,256]{2,1,0:T(8,128)(2,1)S(1)} %norm.1.refs_2_), channel_id=1, source_target_pairs={{0,16},{2,18},{4,20},{6,22},{8,24},{10,26},{12,28},{14,30},{16,0},... | collective-permute-start | bytes 1671176 | tf_op jit(solution)/shard_map/x_far_2/ppermute | solution.py:24
  32.1 1.0 copy-start.3
  34.2 25.9 %collective-permute-start.6 = (bf16[2,256,768]{2,1,0:T(8,128)(2,1)}, bf16[2,256,768]{2,1,0:T(8,128)(2,1)S(1)}, u32[]{:S(2)}, u32[]{:S(2)}) collective-permute-start(bf16[2,256,768]{2,1,0:T(8,128)(2,1)} %get-tuple-element.58.refs_0_), channel_id=1, source_target_pairs={{0,4},{2,6},{4,0},{6,2},{8,12},{10,14},{12,8},{14,10},{16,20},{18,... | collective-permute-start | bytes 2359304 | tf_op jit(solution)/shard_map/line_w02/ppermute | solution.py:24
  37.3 1.8 %copy-start.10 = (bf16[96,256]{1,0:T(8,128)(2,1)S(1)}, bf16[96,256]{1,0:T(8,128)(2,1)}, u32[]{:S(2)}) copy-start(bf16[96,256]{1,0:T(8,128)(2,1)} %get-tuple-element.65) | copy-start | bytes 147460
  60.1 10.3 %collective-permute-start.10 = (bf16[288,768]{1,0:T(8,128)(2,1)S(1)}, bf16[288,768]{1,0:T(8,128)(2,1)S(1)}, u32[]{:S(2)}, u32[]{:S(2)}) collective-permute-start(bf16[288,768]{1,0:T(8,128)(2,1)S(1)} %maximum_maximum_fusion), channel_id=1, source_target_pairs={{0,24},{2,26},{4,28},{6,30},{8,16},{10,18},{12,20},{14,22},{16,8},... | collective-permute-start | bytes 1327112 | tf_op jit(solution)/shard_map/w_3/ppermute | solution.py:24
  62.0 7.8 %collective-permute-start.12 = (bf16[1,256,768]{2,1,0:T(8,128)(2,1)S(1)}, bf16[1,256,768]{2,1,0:T(8,128)(2,1)S(1)}, u32[]{:S(2)}, u32[]{:S(2)}) collective-permute-start(bf16[1,256,768]{2,1,0:T(8,128)(2,1)S(1)} %get-tuple-element.78), channel_id=1, source_target_pairs={{0,4},{2,6},{4,0},{6,2},{8,12},{10,14},{12,8},{14,10},{16,20},{18,... | collective-permute-start | bytes 1179656 | tf_op jit(solution)/shard_map/line_w1/ppermute | solution.py:24
  63.5 9.6 %collective-permute-start.9 = (bf16[8,136,256]{2,1,0:T(8,128)(2,1)S(1)}, bf16[8,136,256]{2,1,0:T(8,128)(2,1)S(1)}, u32[]{:S(2)}, u32[]{:S(2)}) collective-permute-start(bf16[8,136,256]{2,1,0:T(8,128)(2,1)S(1)} %collective-permute-done.4.refs_6_), channel_id=1, source_target_pairs={{0,1},{1,0},{2,3},{3,2},{4,5},{5,4},{6,7},{7,6},{8,9},{9,8},{10,11... | collective-permute-start | bytes 1671176 | tf_op jit(solution)/shard_map/side_far/ppermute | solution.py:24
  64.0 12.3 %collective-permute-start.7 = (bf16[8,136,256]{2,1,0:T(8,128)(2,1)S(1)}, bf16[8,136,256]{2,1,0:T(8,128)(2,1)S(1)}, u32[]{:S(2)}, u32[]{:S(2)}) collective-permute-start(bf16[8,136,256]{2,1,0:T(8,128)(2,1)S(1)} %collective-permute-done.4.refs_6_), channel_id=1, source_target_pairs={{0,8},{2,10},{4,12},{6,14},{8,0},{10,2},{12,4},{14,6},{16,24},{18,... | collective-permute-start | bytes 1671176 | tf_op jit(solution)/shard_map/x_last_1/ppermute | solution.py:24
  64.0 15.0 %collective-permute-start.8 = (bf16[8,136,256]{2,1,0:T(8,128)(2,1)S(1)}, bf16[8,136,256]{2,1,0:T(8,128)(2,1)S(1)}, u32[]{:S(2)}, u32[]{:S(2)}) collective-permute-start(bf16[8,136,256]{2,1,0:T(8,128)(2,1)S(1)} %collective-permute-done.2.refs_4_), channel_id=1, source_target_pairs={{0,1},{1,0},{2,3},{3,2},{4,5},{5,4},{6,7},{7,6},{8,9},{9,8},{10,11... | collective-permute-start | bytes 1671176 | tf_op jit(solution)/shard_map/side_next/ppermute | solution.py:24
  69.9 12.4 %collective-permute-start.13 = (bf16[6,256,768]{2,1,0:T(8,128)(2,1)S(1)}, bf16[6,256,768]{2,1,0:T(8,128)(2,1)S(1)}, u32[]{:S(2)}, u32[]{:S(2)}) collective-permute-start(bf16[6,256,768]{2,1,0:T(8,128)(2,1)S(1)} %join.1.refs_5_.refs_8_), channel_id=1, source_target_pairs={{0,2},{2,0},{4,6},{6,4},{8,10},{10,8},{12,14},{14,12},{16,18},{18,... | collective-permute-start | bytes 7077896 | tf_op jit(solution)/shard_map/core_w/ppermute | solution.py:24
  71.2 11.1 %collective-permute-start.11 = (bf16[1,256,768]{2,1,0:T(8,128)(2,1)S(1)}, bf16[1,256,768]{2,1,0:T(8,128)(2,1)S(1)}, u32[]{:S(2)}, u32[]{:S(2)}) collective-permute-start(bf16[1,256,768]{2,1,0:T(8,128)(2,1)S(1)} %get-tuple-element.83.refs_6_.refs_9_), channel_id=1, source_target_pairs={{0,4},{2,6},{4,0},{6,2},{8,12},{10,14},{12,8},{14,10},{16,20},{18,... | collective-permute-start | bytes 1179656 | tf_op jit(solution)/shard_map/line_w3/ppermute | solution.py:24
  82.3 1.7 %collective-permute-start.16 = (bf16[1,256,768]{2,1,0:T(8,128)(2,1)S(1)}, bf16[1,256,768]{2,1,0:T(8,128)(2,1)S(1)}, u32[]{:S(2)}, u32[]{:S(2)}) collective-permute-start(bf16[1,256,768]{2,1,0:T(8,128)(2,1)S(1)} %get-tuple-element.83.refs_6_.refs_9_), channel_id=1, source_target_pairs={{0,2},{2,0},{4,6},{6,4},{8,10},{10,8},{12,14},{14,12},{16,18},{18,... | collective-permute-start | bytes 1179656 | tf_op jit(solution)/shard_map/core_w3/ppermute | solution.py:24
  82.3 2.3 %collective-permute-start.17 = (bf16[1,256,768]{2,1,0:T(8,128)(2,1)S(1)}, bf16[1,256,768]{2,1,0:T(8,128)(2,1)S(1)}, u32[]{:S(2)}, u32[]{:S(2)}) collective-permute-start(bf16[1,256,768]{2,1,0:T(8,128)(2,1)S(1)} %collective-permute-done.11.refs_7_.refs_10_), channel_id=1, source_target_pairs={{0,2},{2,0},{4,6},{6,4},{8,10},{10,8},{12,14},{14,12},{16,18},{18,... | collective-permute-start | bytes 1179656 | tf_op jit(solution)/shard_map/core_w3_line/ppermute | solution.py:24
  82.8 8.6 %collective-permute-start.14 = (bf16[4,136,256]{2,1,0:T(8,128)(2,1)S(1)}, bf16[4,136,256]{2,1,0:T(8,128)(2,1)S(1)}, u32[]{:S(2)}, u32[]{:S(2)}) collective-permute-start(bf16[4,136,256]{2,1,0:T(8,128)(2,1)S(1)} %half.2), channel_id=1, source_target_pairs={{0,1},{1,0},{2,3},{3,2},{4,5},{5,4},{6,7},{7,6},{8,9},{9,8},{10,11... | collective-permute-start | bytes 835592 | tf_op jit(solution)/shard_map/side_last/ppermute | solution.py:24
  83.4 8.3 %collective-permute-start.15 = (bf16[4,136,256]{2,1,0:T(8,128)(2,1)S(1)}, bf16[4,136,256]{2,1,0:T(8,128)(2,1)S(1)}, u32[]{:S(2)}, u32[]{:S(2)}) collective-permute-start(bf16[4,136,256]{2,1,0:T(8,128)(2,1)S(1)} %half.3), channel_id=1, source_target_pairs={{0,8},{2,10},{4,12},{6,14},{8,0},{10,2},{12,4},{14,6},{16,24},{18,... | collective-permute-start | bytes 835592 | tf_op jit(solution)/shard_map/x_last_side_1/ppermute | solution.py:24
  87.1 11.2 %collective-permute-start.18 = (bf16[3,192,256]{2,1,0:T(8,128)(2,1)S(1)}, bf16[3,192,256]{2,1,0:T(8,128)(2,1)S(1)}, u32[]{:S(2)}, u32[]{:S(2)}) collective-permute-start(bf16[3,192,256]{2,1,0:T(8,128)(2,1)S(1)} %keys_values.3.refs_4_), channel_id=1, source_target_pairs={{0,4},{2,6},{4,0},{6,2},{8,12},{10,14},{12,8},{14,10},{16,20},{18,... | collective-permute-start | bytes 884744 | tf_op jit(solution)/shard_map/kv_line/ppermute | solution.py:24
  93.1 5.2 %collective-permute-start.19 = (bf16[1,192,256]{2,1,0:T(8,128)(2,1)S(1)}, bf16[1,192,256]{2,1,0:T(8,128)(2,1)S(1)}, u32[]{:S(2)}, u32[]{:S(2)}) collective-permute-start(bf16[1,192,256]{2,1,0:T(8,128)(2,1)S(1)} %keys_values.2.refs_8_), channel_id=1, source_target_pairs={{0,4},{2,6},{4,0},{6,2},{8,12},{10,14},{12,8},{14,10},{16,20},{18,... | collective-permute-start | bytes 294920 | tf_op jit(solution)/shard_map/kv_line/ppermute | solution.py:24
  94.6 5.4 %collective-permute-start.20 = (bf16[3,192,256]{2,1,0:T(8,128)(2,1)S(1)}, bf16[3,192,256]{2,1,0:T(8,128)(2,1)S(1)}, u32[]{:S(2)}, u32[]{:S(2)}) collective-permute-start(bf16[3,192,256]{2,1,0:T(8,128)(2,1)S(1)} %keys_values.3.refs_4_), channel_id=1, source_target_pairs={{0,2},{2,0},{4,6},{6,4},{8,10},{10,8},{12,14},{14,12},{16,18},{18,... | collective-permute-start | bytes 884744 | tf_op jit(solution)/shard_map/core_kv/ppermute | solution.py:24
  98.3 1.9 %collective-permute-start.21 = (bf16[3,192,256]{2,1,0:T(8,128)(2,1)S(1)}, bf16[3,192,256]{2,1,0:T(8,128)(2,1)S(1)}, u32[]{:S(2)}, u32[]{:S(2)}) collective-permute-start(bf16[3,192,256]{2,1,0:T(8,128)(2,1)S(1)} %collective-permute-done.18.refs_5_), channel_id=1, source_target_pairs={{0,2},{2,0},{4,6},{6,4},{8,10},{10,8},{12,14},{14,12},{16,18},{18,... | collective-permute-start | bytes 884744 | tf_op jit(solution)/shard_map/core_kv_line/ppermute | solution.py:24
  98.3 1.7 %collective-permute-start.22 = (bf16[1,192,256]{2,1,0:T(8,128)(2,1)S(1)}, bf16[1,192,256]{2,1,0:T(8,128)(2,1)S(1)}, u32[]{:S(2)}, u32[]{:S(2)}) collective-permute-start(bf16[1,192,256]{2,1,0:T(8,128)(2,1)S(1)} %keys_values.2.refs_8_), channel_id=1, source_target_pairs={{0,2},{2,0},{4,6},{6,4},{8,10},{10,8},{12,14},{14,12},{16,18},{18,... | collective-permute-start | bytes 294920 | tf_op jit(solution)/shard_map/core_kv/ppermute | solution.py:24
  98.8 1.4 %collective-permute-start.23 = (bf16[1,192,256]{2,1,0:T(8,128)(2,1)S(1)}, bf16[1,192,256]{2,1,0:T(8,128)(2,1)S(1)}, u32[]{:S(2)}, u32[]{:S(2)}) collective-permute-start(bf16[1,192,256]{2,1,0:T(8,128)(2,1)S(1)} %collective-permute-done.19.refs_9_), channel_id=1, source_target_pairs={{0,2},{2,0},{4,6},{6,4},{8,10},{10,8},{12,14},{14,12},{16,18},{18,... | collective-permute-start | bytes 294920 | tf_op jit(solution)/shard_map/core_kv_line/ppermute | solution.py:24
  100.0 13.1 %copy-start.4 = (bf16[3,192,256]{2,1,0:T(8,128)(2,1)}, bf16[3,192,256]{2,1,0:T(8,128)(2,1)S(1)}, u32[]{:S(2)}) copy-start(bf16[3,192,256]{2,1,0:T(8,128)(2,1)S(1)} %collective-permute-done.20.refs_6_) | copy-start | bytes 884740
  100.1 12.9 %copy-start.8 = (bf16[1,192,256]{2,1,0:T(8,128)(2,1)}, bf16[1,192,256]{2,1,0:T(8,128)(2,1)S(1)}, u32[]{:S(2)}) copy-start(bf16[1,192,256]{2,1,0:T(8,128)(2,1)S(1)} %collective-permute-done.23.refs_11_) | copy-start | bytes 294916
  100.1 12.9 %copy-start.6 = (bf16[3,192,256]{2,1,0:T(8,128)(2,1)}, bf16[3,192,256]{2,1,0:T(8,128)(2,1)S(1)}, u32[]{:S(2)}) copy-start(bf16[3,192,256]{2,1,0:T(8,128)(2,1)S(1)} %collective-permute-done.21.refs_7_) | copy-start | bytes 884740
  105.2 7.9 %collective-permute-start.24 = (bf16[128,512]{1,0:T(8,128)(2,1)S(1)}, bf16[128,512]{1,0:T(8,128)(2,1)S(1)}, u32[]{:S(2)}, u32[]{:S(2)}) collective-permute-start(bf16[128,512]{1,0:T(8,128)(2,1)S(1)} %attend.4), channel_id=1, source_target_pairs={{0,24},{2,26},{4,28},{6,30},{8,16},{10,18},{12,20},{14,22},{16,8},... | collective-permute-start | bytes 393224 | tf_op jit(solution)/shard_map/mixed_3/ppermute | solution.py:24
  113.0 9.4 %collective-permute-start.25 = (bf16[128,512]{1,0:T(8,128)(2,1)S(1)}, bf16[128,512]{1,0:T(8,128)(2,1)S(1)}, u32[]{:S(2)}, u32[]{:S(2)}) collective-permute-start(bf16[128,512]{1,0:T(8,128)(2,1)S(1)} %attend.5), channel_id=1, source_target_pairs={{0,16},{2,18},{4,20},{6,22},{8,24},{10,26},{12,28},{14,30},{16,0},... | collective-permute-start | bytes 393224 | tf_op jit(solution)/shard_map/mixed_2/ppermute | solution.py:24
  113.1 3.6 %copy-start.12 = (bf16[128,512]{1,0:T(8,128)(2,1)}, bf16[128,512]{1,0:T(8,128)(2,1)S(1)}, u32[]{:S(2)}) copy-start(bf16[128,512]{1,0:T(8,128)(2,1)S(1)} %collective-permute-done.24) | copy-start | bytes 393220
  116.7 11.6 %collective-permute-start.26 = (bf16[128,512]{1,0:T(8,128)(2,1)S(1)}, bf16[128,512]{1,0:T(8,128)(2,1)S(1)}, u32[]{:S(2)}, u32[]{:S(2)}) collective-permute-start(bf16[128,512]{1,0:T(8,128)(2,1)S(1)} %attend.6), channel_id=1, source_target_pairs={{0,8},{2,10},{4,12},{6,14},{8,0},{10,2},{12,4},{14,6},{16,24},{18,... | collective-permute-start | bytes 393224 | tf_op jit(solution)/shard_map/mixed_1/ppermute | solution.py:24
  122.3 1.0 copy-start.5
  123.3 1.0 copy-start.7
  124.2 0.9 copy-start.9
  125.1 3.2 %copy-start.13 = (bf16[128,512]{1,0:T(8,128)(2,1)S(1)}, bf16[128,512]{1,0:T(8,128)(2,1)}, u32[]{:S(2)}) copy-start(bf16[128,512]{1,0:T(8,128)(2,1)} %copy-done.12) | copy-start | bytes 393220

commit v6 on v5

--- a/solution.py
+++ b/solution.py
@@ -539,6 +539,7 @@
         for chunk in x_chunks:
             chunk[0] = after(chunk[0], kv_new[1])
         queries = [*projected(False, True, (0, 1, 2)), *projected(False, True, (3,))]
+        queries = list(lax.optimization_barrier(tuple(queries)))
     else:
         kv_new, queries = [[value] for value in projected(True, True, tuple(range(heads)))]
 
@@ -563,7 +564,7 @@
     for slots in tuple((k,) for k in reversed(range(heads))):
         some = [(queries[k // 3], k % 3) if squared else (queries[0], k) for k in slots]
         if squared and slots != (3,):
-            earlier = [value for value in back[slots[0] + 2 :][:1] if value is not None]
+            earlier = back[3:] if slots == (0,) else []
             some = [(after(some[0][0], *mixed, *earlier), some[0][1])]
         mixed = attend(slots, prefix_len, some, q_ids, kv_parts, places, kv_ids, tok)
         for k, value in zip(slots, mixed):

time: 130 us -> 128 us (0.985)
  waiting for transfers between devices: 60.4 us -> 57.4 us
  Pallas kernels: 29 us -> 30.9 us
  local copies, waits for them, and re-layouts: 6.47 us -> 4.6 us
  starting transfers between devices: 27.8 us -> 29.6 us
    ppermute x27, waiting for transfers between devices: 60.4 us -> 57.4 us  [swap(): return lax.ppermute(value, axis, [(i, i ^ mask) for i in range(size)])]
    unnamed x32 -> x20, local copies, waits for them, and re-layouts: 4.65 us -> 2.77 us
    ppermute x27, starting transfers between devices: 27.8 us -> 29.6 us  [swap(): return lax.ppermute(value, axis, [(i, i ^ mask) for i in range(size)])]
    pallas_call x4, Pallas kernels: 16 us -> 17.8 us  [attend(): pl.pallas_call(functools.partial(attend_kernel, slots, tok, places), grid...]
  transfers between devices with their start and end apart: 27 -> 27, of which waited for: 17 -> 16; matrix products, arithmetic and copies ran while one was open for 3% -> 3% of each run, Pallas kernels for 18% -> 20%
where the time goes in v6:
time: 128 us
  waiting for transfers between devices  57.4 us (45%)
  Pallas kernels  30.9 us (24%)
  starting transfers between devices  29.6 us (23%)
  other arithmetic  4.68 us (4%)
  local copies, waits for them, and re-layouts  4.6 us (4%)
    ppermute x27, waiting for transfers between devices, swap(): return lax.ppermute(value, axis, [(i, i ^ mask) for i in range(size)])  57.4 us
    ppermute x27, starting transfers between devices, swap(): return lax.ppermute(value, axis, [(i, i ^ mask) for i in range(size)])  29.6 us
    pallas_call x4, Pallas kernels, attend(): pl.pallas_call(functools.partial(attend_kernel, slots, tok, places), grid...  17.8 us
    pallas_call x4, Pallas kernels, project(): pl.pallas_call(functools.partial(project_kernel, kv, tiles, first_slot, t...  9.2 us
    pallas_call x3, Pallas kernels, unpack(): pl.pallas_call(functools.partial(unpack_kernel, len(plain), fold, len(pla...  3.3 us
    unnamed x20, local copies, waits for them, and re-layouts  2.77 us
  transfers between devices with their start and end apart: 27, of which 16 were waited for; matrix products, arithmetic and copies ran while one was open for 3% of the time, Pallas kernels for 20%

profile of v6, /device:TPU:0, one launch (start us, length us, event | category | flops | bytes accessed | tf_op | source)
XLA Modules:
  0.0 128.1 jit_solution(4931472325500045485)
XLA Ops:
  0.0 1.5 %constant_dynamic-slice_fusion = (bf16[256,768]{1,0:T(8,128)(2,1)S(1)}, bf16[256,768]{1,0:T(8,128)(2,1)S(1)}, bf16[256,768]{1,0:T(8,128)(2,1)S(1)}, bf16[256,768]{1,0:T(8,128)(2,1)S(1)}) fusion(bf16[256,3072]{1,0:T(8,128)(2,1)} %param.9, s32[]{:T(128)S(6)} %select_n.55, s32[]{:T(128)S(6)} %select_n.53, s32[]{:T(128)S(6)} %select_n.52, s32[]{:T(128)S(6)} %select_n.54), kind=kLoop, calls=%fused_computation.50 | loop fusion | bytes 3145744 | tf_op jit(solution)/shard_map/dynamic_slice | solution.py:417
  1.6 0.2 squares.1.refs_0_
  1.8 3.0 %collective-permute-start = (f32[136,128]{1,0:T(8,128)S(1)}, f32[136,128]{1,0:T(8,128)S(1)}, u32[]{:S(2)}, u32[]{:S(2)}) collective-permute-start(f32[136,128]{1,0:T(8,128)S(1)} %squares.1.refs_0_), channel_id=1, source_target_pairs={{0,1},{1,0},{2,3},{3,2},{4,5},{5,4},{6,7},{7,6},{8,9},{9,8},{10,11... | collective-permute-start | bytes 208904 | tf_op jit(solution)/shard_map/side_sums/ppermute | solution.py:24
  4.9 1.0 fusion.7
  5.8 1.6 %collective-permute-start.5 = (bf16[288,768]{1,0:T(8,128)(2,1)}, bf16[288,768]{1,0:T(8,128)(2,1)}, u32[]{:S(2)}, u32[]{:S(2)}) collective-permute-start(bf16[288,768]{1,0:T(8,128)(2,1)} %get-tuple-element.130), channel_id=1, source_target_pairs={{0,8},{2,10},{4,12},{6,14},{8,0},{10,2},{12,4},{14,6},{16,24},{18,... | collective-permute-start | bytes 1327112 | tf_op jit(solution)/shard_map/w_1/ppermute | solution.py:24
  7.4 2.6 %collective-permute-start.3 = (bf16[288,768]{1,0:T(8,128)(2,1)}, bf16[288,768]{1,0:T(8,128)(2,1)S(1)}, u32[]{:S(2)}, u32[]{:S(2)}) collective-permute-start(bf16[288,768]{1,0:T(8,128)(2,1)} %get-tuple-element.131), channel_id=1, source_target_pairs={{0,16},{2,18},{4,20},{6,22},{8,24},{10,26},{12,28},{14,30},{16,0},... | collective-permute-start | bytes 1327112 | tf_op jit(solution)/shard_map/w_2/ppermute | solution.py:24
  10.7 0.6 pad_maximum_fusion.6
  11.4 0.2 norm.1.refs_2_
  11.6 0.5 collective-permute-start.2
  12.1 0.5 collective-permute-start.1
  12.6 15.5 %collective-permute-done.3.refs_1_ = bf16[288,768]{1,0:T(8,128)(2,1)S(1)} collective-permute-done((bf16[288,768]{1,0:T(8,128)(2,1)}, bf16[288,768]{1,0:T(8,128)(2,1)S(1)}, u32[]{:S(2)}, u32[]{:S(2)}) %collective-permute-start.3) | collective-permute-done | bytes 442400 | tf_op jit(solution)/shard_map/w_2/ppermute | solution.py:24
  28.1 0.8 copy-done.2
  29.0 3.0 %collective-permute-start.4 = (bf16[8,136,256]{2,1,0:T(8,128)(2,1)S(1)}, bf16[8,136,256]{2,1,0:T(8,128)(2,1)S(1)}, u32[]{:S(2)}, u32[]{:S(2)}) collective-permute-start(bf16[8,136,256]{2,1,0:T(8,128)(2,1)S(1)} %norm.1.refs_2_), channel_id=1, source_target_pairs={{0,16},{2,18},{4,20},{6,22},{8,24},{10,26},{12,28},{14,30},{16,0},... | collective-permute-start | bytes 1671176 | tf_op jit(solution)/shard_map/x_far_2/ppermute | solution.py:24
  32.1 1.0 copy-done.3
  33.1 1.1 unpack.3
  34.2 1.5 %collective-permute-start.6 = (bf16[2,256,768]{2,1,0:T(8,128)(2,1)}, bf16[2,256,768]{2,1,0:T(8,128)(2,1)S(1)}, u32[]{:S(2)}, u32[]{:S(2)}) collective-permute-start(bf16[2,256,768]{2,1,0:T(8,128)(2,1)} %get-tuple-element.60.refs_0_), channel_id=1, source_target_pairs={{0,4},{2,6},{4,0},{6,2},{8,12},{10,14},{12,8},{14,10},{16,20},{18,... | collective-permute-start | bytes 2359304 | tf_op jit(solution)/shard_map/line_w02/ppermute | solution.py:24
  35.7 0.1 stack.122.refs_2_
  35.8 0.1 stack.117.refs_1_
  36.0 1.4 %unpack.4 = (bf16[3,256,768]{2,1,0:T(8,128)(2,1)S(1)}, bf16[1,256,768]{2,1,0:T(8,128)(2,1)S(1)}, bf16[96,256]{1,0:T(8,128)(2,1)S(1)}) custom-call(bf16[2,256,768]{2,1,0:T(8,128)(2,1)} %get-tuple-element.60.refs_0_, bf16[288,768]{1,0:T(8,128)(2,1)} %collective-permute-done.5.refs_1_), custom_call_target="tpu_custom_call" | custom-call | flops 20000000000 | bytes 10000000 | tf_op jit(solution)/shard_map/unpack/pallas_call | solution.py:97
  37.4 1.4 %fusion.16 = (f32[4,192,64]{2,1,0:T(8,128)S(1)}, f32[4,192,64]{2,1,0:T(8,128)S(1)}, f32[4,192,64]{2,1,0:T(8,128)S(1)}) fusion(f32[64]{0:T(128)S(1)} %multiply_exponential_fusion, f32[4,192]{1,0:T(4,128)S(1)} %add_convert_fusion), kind=kLoop, calls=%fused_computation.32 | loop fusion | flops 98304 | bytes 593152 | tf_op jit(solution)/shard_map/neg | solution.py:449
  38.8 0.2 pad_maximum_fusion.4.refs_11_.refs_14_
  39.0 0.2 pad_maximum_fusion.5.refs_12_.refs_15_
  39.2 10.7 %collective-permute-done.2.refs_4_ = bf16[8,136,256]{2,1,0:T(8,128)(2,1)S(1)} collective-permute-done((bf16[8,136,256]{2,1,0:T(8,128)(2,1)S(1)}, bf16[8,136,256]{2,1,0:T(8,128)(2,1)S(1)}, u32[]{:S(2)}, u32[]{:S(2)}) %collective-permute-start.2) | collective-permute-done | bytes 557088 | tf_op jit(solution)/shard_map/x_next_1/ppermute | solution.py:24
  49.9 10.2 %collective-permute-done.4.refs_6_ = bf16[8,136,256]{2,1,0:T(8,128)(2,1)S(1)} collective-permute-done((bf16[8,136,256]{2,1,0:T(8,128)(2,1)S(1)}, bf16[8,136,256]{2,1,0:T(8,128)(2,1)S(1)}, u32[]{:S(2)}, u32[]{:S(2)}) %collective-permute-start.4) | collective-permute-done | bytes 557088 | tf_op jit(solution)/shard_map/x_far_2/ppermute | solution.py:24
  60.1 1.9 %collective-permute-start.10 = (bf16[288,768]{1,0:T(8,128)(2,1)S(1)}, bf16[288,768]{1,0:T(8,128)(2,1)S(1)}, u32[]{:S(2)}, u32[]{:S(2)}) collective-permute-start(bf16[288,768]{1,0:T(8,128)(2,1)S(1)} %maximum_maximum_fusion), channel_id=1, source_target_pairs={{0,24},{2,26},{4,28},{6,30},{8,16},{10,18},{12,20},{14,22},{16,8},... | collective-permute-start | bytes 1327112 | tf_op jit(solution)/shard_map/w_3/ppermute | solution.py:24
  62.0 1.5 %collective-permute-start.12 = (bf16[1,256,768]{2,1,0:T(8,128)(2,1)S(1)}, bf16[1,256,768]{2,1,0:T(8,128)(2,1)S(1)}, u32[]{:S(2)}, u32[]{:S(2)}) collective-permute-start(bf16[1,256,768]{2,1,0:T(8,128)(2,1)S(1)} %get-tuple-element.80), channel_id=1, source_target_pairs={{0,4},{2,6},{4,0},{6,2},{8,12},{10,14},{12,8},{14,10},{16,20},{18,... | collective-permute-start | bytes 1179656 | tf_op jit(solution)/shard_map/line_w1/ppermute | solution.py:24
  63.5 0.5 collective-permute-start.9
  64.0 1.5 %collective-permute-start.8 = (bf16[8,136,256]{2,1,0:T(8,128)(2,1)S(1)}, bf16[8,136,256]{2,1,0:T(8,128)(2,1)S(1)}, u32[]{:S(2)}, u32[]{:S(2)}) collective-permute-start(bf16[8,136,256]{2,1,0:T(8,128)(2,1)S(1)} %collective-permute-done.2.refs_4_), channel_id=1, source_target_pairs={{0,1},{1,0},{2,3},{3,2},{4,5},{5,4},{6,7},{7,6},{8,9},{9,8},{10,11... | collective-permute-start | bytes 1671176 | tf_op jit(solution)/shard_map/side_next/ppermute | solution.py:24
  65.5 4.3 %collective-permute-done.12.refs_2_ = bf16[1,256,768]{2,1,0:T(8,128)(2,1)S(1)} collective-permute-done((bf16[1,256,768]{2,1,0:T(8,128)(2,1)S(1)}, bf16[1,256,768]{2,1,0:T(8,128)(2,1)S(1)}, u32[]{:S(2)}, u32[]{:S(2)}) %collective-permute-start.12) | collective-permute-done | bytes 393248 | tf_op jit(solution)/shard_map/line_w1/ppermute | solution.py:24
  69.8 0.2 join.1.refs_5_.refs_8_
  70.0 0.4 collective-permute-done.10.refs_0_
  70.4 0.8 unpack.5
  71.2 1.5 %collective-permute-start.11 = (bf16[1,256,768]{2,1,0:T(8,128)(2,1)S(1)}, bf16[1,256,768]{2,1,0:T(8,128)(2,1)S(1)}, u32[]{:S(2)}, u32[]{:S(2)}) collective-permute-start(bf16[1,256,768]{2,1,0:T(8,128)(2,1)S(1)} %get-tuple-element.85.refs_6_.refs_9_), channel_id=1, source_target_pairs={{0,4},{2,6},{4,0},{6,2},{8,12},{10,14},{12,8},{14,10},{16,20},{18,... | collective-permute-start | bytes 1179656 | tf_op jit(solution)/shard_map/line_w3/ppermute | solution.py:24
  72.7 0.4 collective-permute-done.9.value.refs_7_
  73.1 3.2 %collective-permute-done.7.value.refs_2_ = bf16[8,136,256]{2,1,0:T(8,128)(2,1)S(1)} collective-permute-done((bf16[8,136,256]{2,1,0:T(8,128)(2,1)S(1)}, bf16[8,136,256]{2,1,0:T(8,128)(2,1)S(1)}, u32[]{:S(2)}, u32[]{:S(2)}) %collective-permute-start.7) | collective-permute-done | bytes 557088 | tf_op jit(solution)/shard_map/x_last_1/ppermute | solution.py:24
  76.3 2.7 %collective-permute-done.8.refs_5_ = bf16[8,136,256]{2,1,0:T(8,128)(2,1)S(1)} collective-permute-done((bf16[8,136,256]{2,1,0:T(8,128)(2,1)S(1)}, bf16[8,136,256]{2,1,0:T(8,128)(2,1)S(1)}, u32[]{:S(2)}, u32[]{:S(2)}) %collective-permute-start.8) | collective-permute-done | bytes 557088 | tf_op jit(solution)/shard_map/side_next/ppermute | solution.py:24
  79.0 3.3 %collective-permute-done.11.refs_7_.refs_10_ = bf16[1,256,768]{2,1,0:T(8,128)(2,1)S(1)} collective-permute-done((bf16[1,256,768]{2,1,0:T(8,128)(2,1)S(1)}, bf16[1,256,768]{2,1,0:T(8,128)(2,1)S(1)}, u32[]{:S(2)}, u32[]{:S(2)}) %collective-permute-start.11) | collective-permute-done | bytes 393248 | tf_op jit(solution)/shard_map/line_w3/ppermute | solution.py:24
  82.3 0.5 collective-permute-start.17
  82.8 0.5 collective-permute-start.14
  83.3 0.1 collective-permute-start.15
  83.5 0.6 collective-permute-done.16.refs_9_.refs_12_
  84.0 0.6 collective-permute-done.17.refs_10_.refs_13_
  84.6 2.4 %keys_values.3.refs_4_ = bf16[3,192,256]{2,1,0:T(8,128)(2,1)S(1)} custom-call(s32[16]{0:T(128)S(1)} %pad_add_fusion.1.refs_0_, s32[16]{0:T(128)S(1)} %stack.117.refs_1_, bf16[8,136,256]{2,1,0:T(8,128)(2,1)S(1)} %norm.1.refs_2_, bf16[8,136,256]{2,1,0:T(8,128)(2,1)S(1)} %collective-permute-done.1.refs_3_, ...), custom_call_target="tpu_custom_call" | custom-call | flops 905969664 | bytes 5636096 | tf_op jit(solution)/shard_map/keys_values/pallas_call | solution.py:245
  87.0 1.6 %collective-permute-start.18 = (bf16[3,192,256]{2,1,0:T(8,128)(2,1)S(1)}, bf16[3,192,256]{2,1,0:T(8,128)(2,1)S(1)}, u32[]{:S(2)}, u32[]{:S(2)}) collective-permute-start(bf16[3,192,256]{2,1,0:T(8,128)(2,1)S(1)} %keys_values.3.refs_4_), channel_id=1, source_target_pairs={{0,4},{2,6},{4,0},{6,2},{8,12},{10,14},{12,8},{14,10},{16,20},{18,... | collective-permute-start | bytes 884744 | tf_op jit(solution)/shard_map/kv_line/ppermute | solution.py:24
  88.6 2.8 %collective-permute-done.14.refs_3_ = bf16[4,136,256]{2,1,0:T(8,128)(2,1)S(1)} collective-permute-done((bf16[4,136,256]{2,1,0:T(8,128)(2,1)S(1)}, bf16[4,136,256]{2,1,0:T(8,128)(2,1)S(1)}, u32[]{:S(2)}, u32[]{:S(2)}) %collective-permute-start.14) | collective-permute-done | bytes 278560 | tf_op jit(solution)/shard_map/side_last/ppermute | solution.py:24
  91.4 0.2 collective-permute-done.15.refs_4_
  91.6 1.4 %keys_values.2.refs_8_ = bf16[1,192,256]{2,1,0:T(8,128)(2,1)S(1)} custom-call(s32[16]{0:T(128)S(1)} %pad_add_fusion.1.refs_0_, s32[16]{0:T(128)S(1)} %stack.117.refs_1_, bf16[8,136,256]{2,1,0:T(8,128)(2,1)S(1)} %collective-permute-done.7.value.refs_2_, bf16[4,136,256]{2,1,0:T(8,128)(2,1)S(1)} %collective-permute-done.14.refs_3_, ...), custom_call_target="tpu_custom_call" | custom-call | flops 301989888 | bytes 3276800 | tf_op jit(solution)/shard_map/keys_values/pallas_call | solution.py:245
  93.0 1.6 %collective-permute-start.19 = (bf16[1,192,256]{2,1,0:T(8,128)(2,1)S(1)}, bf16[1,192,256]{2,1,0:T(8,128)(2,1)S(1)}, u32[]{:S(2)}, u32[]{:S(2)}) collective-permute-start(bf16[1,192,256]{2,1,0:T(8,128)(2,1)S(1)} %keys_values.2.refs_8_), channel_id=1, source_target_pairs={{0,4},{2,6},{4,0},{6,2},{8,12},{10,14},{12,8},{14,10},{16,20},{18,... | collective-permute-start | bytes 294920 | tf_op jit(solution)/shard_map/kv_line/ppermute | solution.py:24
  94.6 3.4 %queries.2.refs_3_ = bf16[3,4,128,128]{3,2,1,0:T(8,128)(2,1)S(1)} custom-call(s32[16]{0:T(128)S(1)} %pad_add_fusion.1.refs_0_, s32[16]{0:T(128)S(1)} %stack.117.refs_1_, bf16[8,136,256]{2,1,0:T(8,128)(2,1)S(1)} %norm.1.refs_2_, bf16[8,136,256]{2,1,0:T(8,128)(2,1)S(1)} %collective-permute-done.1.refs_3_, ...), custom_call_target="tpu_custom_call" | custom-call | flops 1811939328 | bytes 7733248 | tf_op jit(solution)/shard_map/queries/pallas_call | solution.py:245
  98.0 2.0 %queries.3.refs_3_ = bf16[1,4,128,128]{3,2,1,0:T(8,128)(2,1)S(1)} custom-call(s32[16]{0:T(128)S(1)} %pad_add_fusion.1.refs_0_, s32[16]{0:T(128)S(1)} %stack.117.refs_1_, bf16[8,136,256]{2,1,0:T(8,128)(2,1)S(1)} %collective-permute-done.7.value.refs_2_, bf16[4,136,256]{2,1,0:T(8,128)(2,1)S(1)} %collective-permute-done.14.refs_3_, ...), custom_call_target="tpu_custom_call" | custom-call | flops 603979776 | bytes 5373952 | tf_op jit(solution)/shard_map/queries/pallas_call | solution.py:245
  100.0 0.6 collective-permute-start.21
  100.7 0.4 collective-permute-start.23
  101.1 0.8 collective-permute-done.22.refs_10_
  101.9 0.1 collective-permute-done.23.refs_11_
  102.1 5.5 %attend.4 = bf16[128,512]{1,0:T(8,128)(2,1)S(1)} custom-call(s32[1]{0:T(128)} %copy.8.refs_0_, s32[4]{0:T(128)S(1)} %get-tuple-element.69.refs_1_, s32[16]{0:T(128)S(1)} %stack.122.refs_2_, bf16[1,4,128,128]{3,2,1,0:T(8,128)(2,1)S(1)} %queries.3.refs_3_, bf16[3,192,256]{2,1,0:T(8,128)(2,1)S(1)} %keys_values.3.refs_4_, ...), custom_call_target="tpu_custom_call" | custom-call | flops 805306368 | bytes 1572864 | tf_op jit(solution)/shard_map/attend/pallas_call | solution.py:380
  107.6 0.2 collective-permute-start.24
  107.7 4.6 %attend.5 = bf16[128,512]{1,0:T(8,128)(2,1)S(1)} custom-call(s32[1]{0:T(128)} %copy.8.refs_0_, s32[4]{0:T(128)S(1)} %get-tuple-element.69.refs_1_, s32[16]{0:T(128)S(1)} %stack.122.refs_2_, bf16[3,4,128,128]{3,2,1,0:T(8,128)(2,1)S(1)} %queries.2.refs_3_, bf16[3,192,256]{2,1,0:T(8,128)(2,1)S(1)} %keys_values.3.refs_4_, ...), custom_call_target="tpu_custom_call" | custom-call | flops 805306368 | bytes 1572864 | tf_op jit(solution)/shard_map/attend/pallas_call | solution.py:380
  112.4 4.0 %attend.6 = bf16[128,512]{1,0:T(8,128)(2,1)S(1)} custom-call(s32[1]{0:T(128)} %copy.8.refs_0_, s32[4]{0:T(128)S(1)} %get-tuple-element.69.refs_1_, s32[16]{0:T(128)S(1)} %stack.122.refs_2_, bf16[3,4,128,128]{3,2,1,0:T(8,128)(2,1)S(1)} %queries.2.refs_3_, bf16[3,192,256]{2,1,0:T(8,128)(2,1)S(1)} %keys_values.3.refs_4_, ...), custom_call_target="tpu_custom_call" | custom-call | flops 805306368 | bytes 1572864 | tf_op jit(solution)/shard_map/attend/pallas_call | solution.py:380
  116.4 0.6 collective-permute-start.25
  117.1 3.8 %collective-permute-start.26 = (bf16[128,512]{1,0:T(8,128)(2,1)S(1)}, bf16[128,512]{1,0:T(8,128)(2,1)S(1)}, u32[]{:S(2)}, u32[]{:S(2)}) collective-permute-start(bf16[128,512]{1,0:T(8,128)(2,1)S(1)} %attend.5), channel_id=1, source_target_pairs={{0,16},{2,18},{4,20},{6,22},{8,24},{10,26},{12,28},{14,30},{16,0},... | collective-permute-start | bytes 393224 | tf_op jit(solution)/shard_map/mixed_2/ppermute | solution.py:24
  120.9 1.0 copy-done.5
  121.8 3.6 %attend.7 = bf16[128,512]{1,0:T(8,128)(2,1)S(1)} custom-call(s32[1]{0:T(128)} %copy.8.refs_0_, s32[4]{0:T(128)S(1)} %get-tuple-element.69.refs_1_, s32[16]{0:T(128)S(1)} %stack.122.refs_2_, bf16[3,4,128,128]{3,2,1,0:T(8,128)(2,1)S(1)} %queries.2.refs_3_, bf16[3,192,256]{2,1,0:T(8,128)(2,1)S(1)} %keys_values.3.refs_4_, ...), custom_call_target="tpu_custom_call" | custom-call | flops 805306368 | bytes 1572864 | tf_op jit(solution)/shard_map/attend/pallas_call | solution.py:380
  125.5 1.7 %collective-permute-done.26 = bf16[128,512]{1,0:T(8,128)(2,1)S(1)} collective-permute-done((bf16[128,512]{1,0:T(8,128)(2,1)S(1)}, bf16[128,512]{1,0:T(8,128)(2,1)S(1)}, u32[]{:S(2)}, u32[]{:S(2)}) %collective-permute-start.26) | collective-permute-done | bytes 131104 | tf_op jit(solution)/shard_map/mixed_2/ppermute | solution.py:24
  127.3 0.8 pad_maximum_fusion.3
  (52 shorter events, 0.8 us)
Async XLA Ops:
  0.0 1.6 %copy-start = (bf16[128,2048]{1,0:T(8,128)(2,1)S(1)}, bf16[128,2048]{1,0:T(8,128)(2,1)}, u32[]{:S(2)}) copy-start(bf16[128,2048]{1,0:T(8,128)(2,1)} %stream.1) | copy-start | bytes 1572868
  0.0 1.6 %copy-start.1 = (bf16[8,2048]{1,0:T(8,128)(2,1)S(1)}, bf16[8,2048]{1,0:T(8,128)(2,1)}, u32[]{:S(2)}) copy-start(bf16[8,2048]{1,0:T(8,128)(2,1)} %hidden.3) | copy-start | bytes 98308
  0.0 4.8 %copy-start.9 = (s32[8]{0:T(128)S(1)}, s32[8]{0:T(128)}, u32[]{:S(2)}) copy-start(s32[8]{0:T(128)} %param.12) | copy-start | bytes 100
  0.0 4.8 %copy-start.7 = (bf16[2,64,512]{2,1,0:T(8,128)(2,1)S(1)}, bf16[2,64,512]{2,1,0:T(8,128)(2,1)}, u32[]{:S(2)}) copy-start(bf16[2,64,512]{2,1,0:T(8,128)(2,1)} %param.10) | copy-start | bytes 393220
  1.5 9.1 %copy-start.8 = (f32[4096]{0:T(1024)S(1)}, f32[4096]{0:T(1024)}, u32[]{:S(2)}) copy-start(f32[4096]{0:T(1024)} %param.8) | copy-start | bytes 49156
  1.8 9.6 %collective-permute-start = (f32[136,128]{1,0:T(8,128)S(1)}, f32[136,128]{1,0:T(8,128)S(1)}, u32[]{:S(2)}, u32[]{:S(2)}) collective-permute-start(f32[136,128]{1,0:T(8,128)S(1)} %squares.1.refs_0_), channel_id=1, source_target_pairs={{0,1},{1,0},{2,3},{3,2},{4,5},{5,4},{6,7},{7,6},{8,9},{9,8},{10,11... | collective-permute-start | bytes 208904 | tf_op jit(solution)/shard_map/side_sums/ppermute | solution.py:24
  5.8 30.2 %collective-permute-start.5 = (bf16[288,768]{1,0:T(8,128)(2,1)}, bf16[288,768]{1,0:T(8,128)(2,1)}, u32[]{:S(2)}, u32[]{:S(2)}) collective-permute-start(bf16[288,768]{1,0:T(8,128)(2,1)} %get-tuple-element.130), channel_id=1, source_target_pairs={{0,8},{2,10},{4,12},{6,14},{8,0},{10,2},{12,4},{14,6},{16,24},{18,... | collective-permute-start | bytes 1327112 | tf_op jit(solution)/shard_map/w_1/ppermute | solution.py:24
  7.4 20.7 %collective-permute-start.3 = (bf16[288,768]{1,0:T(8,128)(2,1)}, bf16[288,768]{1,0:T(8,128)(2,1)S(1)}, u32[]{:S(2)}, u32[]{:S(2)}) collective-permute-start(bf16[288,768]{1,0:T(8,128)(2,1)} %get-tuple-element.131), channel_id=1, source_target_pairs={{0,16},{2,18},{4,20},{6,22},{8,24},{10,26},{12,28},{14,30},{16,0},... | collective-permute-start | bytes 1327112 | tf_op jit(solution)/shard_map/w_2/ppermute | solution.py:24
  11.6 38.3 %collective-permute-start.2 = (bf16[8,136,256]{2,1,0:T(8,128)(2,1)S(1)}, bf16[8,136,256]{2,1,0:T(8,128)(2,1)S(1)}, u32[]{:S(2)}, u32[]{:S(2)}) collective-permute-start(bf16[8,136,256]{2,1,0:T(8,128)(2,1)S(1)} %norm.1.refs_2_), channel_id=1, source_target_pairs={{0,8},{2,10},{4,12},{6,14},{8,0},{10,2},{12,4},{14,6},{16,24},{18,... | collective-permute-start | bytes 1671176 | tf_op jit(solution)/shard_map/x_next_1/ppermute | solution.py:24
  12.1 37.8 %collective-permute-start.1 = (bf16[8,136,256]{2,1,0:T(8,128)(2,1)S(1)}, bf16[8,136,256]{2,1,0:T(8,128)(2,1)S(1)}, u32[]{:S(2)}, u32[]{:S(2)}) collective-permute-start(bf16[8,136,256]{2,1,0:T(8,128)(2,1)S(1)} %norm.1.refs_2_), channel_id=1, source_target_pairs={{0,1},{1,0},{2,3},{3,2},{4,5},{5,4},{6,7},{7,6},{8,9},{9,8},{10,11... | collective-permute-start | bytes 1671176 | tf_op jit(solution)/shard_map/side_own/ppermute | solution.py:24
  28.1 0.8 copy-start.2
  29.0 31.1 %collective-permute-start.4 = (bf16[8,136,256]{2,1,0:T(8,128)(2,1)S(1)}, bf16[8,136,256]{2,1,0:T(8,128)(2,1)S(1)}, u32[]{:S(2)}, u32[]{:S(2)}) collective-permute-start(bf16[8,136,256]{2,1,0:T(8,128)(2,1)S(1)} %norm.1.refs_2_), channel_id=1, source_target_pairs={{0,16},{2,18},{4,20},{6,22},{8,24},{10,26},{12,28},{14,30},{16,0},... | collective-permute-start | bytes 1671176 | tf_op jit(solution)/shard_map/x_far_2/ppermute | solution.py:24
  32.1 1.0 copy-start.3
  34.2 25.9 %collective-permute-start.6 = (bf16[2,256,768]{2,1,0:T(8,128)(2,1)}, bf16[2,256,768]{2,1,0:T(8,128)(2,1)S(1)}, u32[]{:S(2)}, u32[]{:S(2)}) collective-permute-start(bf16[2,256,768]{2,1,0:T(8,128)(2,1)} %get-tuple-element.60.refs_0_), channel_id=1, source_target_pairs={{0,4},{2,6},{4,0},{6,2},{8,12},{10,14},{12,8},{14,10},{16,20},{18,... | collective-permute-start | bytes 2359304 | tf_op jit(solution)/shard_map/line_w02/ppermute | solution.py:24
  37.4 1.8 %copy-start.6 = (bf16[96,256]{1,0:T(8,128)(2,1)S(1)}, bf16[96,256]{1,0:T(8,128)(2,1)}, u32[]{:S(2)}) copy-start(bf16[96,256]{1,0:T(8,128)(2,1)} %get-tuple-element.67) | copy-start | bytes 147460
  60.1 10.3 %collective-permute-start.10 = (bf16[288,768]{1,0:T(8,128)(2,1)S(1)}, bf16[288,768]{1,0:T(8,128)(2,1)S(1)}, u32[]{:S(2)}, u32[]{:S(2)}) collective-permute-start(bf16[288,768]{1,0:T(8,128)(2,1)S(1)} %maximum_maximum_fusion), channel_id=1, source_target_pairs={{0,24},{2,26},{4,28},{6,30},{8,16},{10,18},{12,20},{14,22},{16,8},... | collective-permute-start | bytes 1327112 | tf_op jit(solution)/shard_map/w_3/ppermute | solution.py:24
  62.0 7.8 %collective-permute-start.12 = (bf16[1,256,768]{2,1,0:T(8,128)(2,1)S(1)}, bf16[1,256,768]{2,1,0:T(8,128)(2,1)S(1)}, u32[]{:S(2)}, u32[]{:S(2)}) collective-permute-start(bf16[1,256,768]{2,1,0:T(8,128)(2,1)S(1)} %get-tuple-element.80), channel_id=1, source_target_pairs={{0,4},{2,6},{4,0},{6,2},{8,12},{10,14},{12,8},{14,10},{16,20},{18,... | collective-permute-start | bytes 1179656 | tf_op jit(solution)/shard_map/line_w1/ppermute | solution.py:24
  63.5 9.6 %collective-permute-start.9 = (bf16[8,136,256]{2,1,0:T(8,128)(2,1)S(1)}, bf16[8,136,256]{2,1,0:T(8,128)(2,1)S(1)}, u32[]{:S(2)}, u32[]{:S(2)}) collective-permute-start(bf16[8,136,256]{2,1,0:T(8,128)(2,1)S(1)} %collective-permute-done.4.refs_6_), channel_id=1, source_target_pairs={{0,1},{1,0},{2,3},{3,2},{4,5},{5,4},{6,7},{7,6},{8,9},{9,8},{10,11... | collective-permute-start | bytes 1671176 | tf_op jit(solution)/shard_map/side_far/ppermute | solution.py:24
  64.0 12.3 %collective-permute-start.7 = (bf16[8,136,256]{2,1,0:T(8,128)(2,1)S(1)}, bf16[8,136,256]{2,1,0:T(8,128)(2,1)S(1)}, u32[]{:S(2)}, u32[]{:S(2)}) collective-permute-start(bf16[8,136,256]{2,1,0:T(8,128)(2,1)S(1)} %collective-permute-done.4.refs_6_), channel_id=1, source_target_pairs={{0,8},{2,10},{4,12},{6,14},{8,0},{10,2},{12,4},{14,6},{16,24},{18,... | collective-permute-start | bytes 1671176 | tf_op jit(solution)/shard_map/x_last_1/ppermute | solution.py:24
  64.0 15.1 %collective-permute-start.8 = (bf16[8,136,256]{2,1,0:T(8,128)(2,1)S(1)}, bf16[8,136,256]{2,1,0:T(8,128)(2,1)S(1)}, u32[]{:S(2)}, u32[]{:S(2)}) collective-permute-start(bf16[8,136,256]{2,1,0:T(8,128)(2,1)S(1)} %collective-permute-done.2.refs_4_), channel_id=1, source_target_pairs={{0,1},{1,0},{2,3},{3,2},{4,5},{5,4},{6,7},{7,6},{8,9},{9,8},{10,11... | collective-permute-start | bytes 1671176 | tf_op jit(solution)/shard_map/side_next/ppermute | solution.py:24
  69.9 12.4 %collective-permute-start.13 = (bf16[6,256,768]{2,1,0:T(8,128)(2,1)S(1)}, bf16[6,256,768]{2,1,0:T(8,128)(2,1)S(1)}, u32[]{:S(2)}, u32[]{:S(2)}) collective-permute-start(bf16[6,256,768]{2,1,0:T(8,128)(2,1)S(1)} %join.1.refs_5_.refs_8_), channel_id=1, source_target_pairs={{0,2},{2,0},{4,6},{6,4},{8,10},{10,8},{12,14},{14,12},{16,18},{18,... | collective-permute-start | bytes 7077896 | tf_op jit(solution)/shard_map/core_w/ppermute | solution.py:24
  71.2 11.1 %collective-permute-start.11 = (bf16[1,256,768]{2,1,0:T(8,128)(2,1)S(1)}, bf16[1,256,768]{2,1,0:T(8,128)(2,1)S(1)}, u32[]{:S(2)}, u32[]{:S(2)}) collective-permute-start(bf16[1,256,768]{2,1,0:T(8,128)(2,1)S(1)} %get-tuple-element.85.refs_6_.refs_9_), channel_id=1, source_target_pairs={{0,4},{2,6},{4,0},{6,2},{8,12},{10,14},{12,8},{14,10},{16,20},{18,... | collective-permute-start | bytes 1179656 | tf_op jit(solution)/shard_map/line_w3/ppermute | solution.py:24
  82.3 1.7 %collective-permute-start.16 = (bf16[1,256,768]{2,1,0:T(8,128)(2,1)S(1)}, bf16[1,256,768]{2,1,0:T(8,128)(2,1)S(1)}, u32[]{:S(2)}, u32[]{:S(2)}) collective-permute-start(bf16[1,256,768]{2,1,0:T(8,128)(2,1)S(1)} %get-tuple-element.85.refs_6_.refs_9_), channel_id=1, source_target_pairs={{0,2},{2,0},{4,6},{6,4},{8,10},{10,8},{12,14},{14,12},{16,18},{18,... | collective-permute-start | bytes 1179656 | tf_op jit(solution)/shard_map/core_w3/ppermute | solution.py:24
  82.3 2.3 %collective-permute-start.17 = (bf16[1,256,768]{2,1,0:T(8,128)(2,1)S(1)}, bf16[1,256,768]{2,1,0:T(8,128)(2,1)S(1)}, u32[]{:S(2)}, u32[]{:S(2)}) collective-permute-start(bf16[1,256,768]{2,1,0:T(8,128)(2,1)S(1)} %collective-permute-done.11.refs_7_.refs_10_), channel_id=1, source_target_pairs={{0,2},{2,0},{4,6},{6,4},{8,10},{10,8},{12,14},{14,12},{16,18},{18,... | collective-permute-start | bytes 1179656 | tf_op jit(solution)/shard_map/core_w3_line/ppermute | solution.py:24
  82.8 8.6 %collective-permute-start.14 = (bf16[4,136,256]{2,1,0:T(8,128)(2,1)S(1)}, bf16[4,136,256]{2,1,0:T(8,128)(2,1)S(1)}, u32[]{:S(2)}, u32[]{:S(2)}) collective-permute-start(bf16[4,136,256]{2,1,0:T(8,128)(2,1)S(1)} %half.2), channel_id=1, source_target_pairs={{0,1},{1,0},{2,3},{3,2},{4,5},{5,4},{6,7},{7,6},{8,9},{9,8},{10,11... | collective-permute-start | bytes 835592 | tf_op jit(solution)/shard_map/side_last/ppermute | solution.py:24
  83.3 8.3 %collective-permute-start.15 = (bf16[4,136,256]{2,1,0:T(8,128)(2,1)S(1)}, bf16[4,136,256]{2,1,0:T(8,128)(2,1)S(1)}, u32[]{:S(2)}, u32[]{:S(2)}) collective-permute-start(bf16[4,136,256]{2,1,0:T(8,128)(2,1)S(1)} %half.3), channel_id=1, source_target_pairs={{0,8},{2,10},{4,12},{6,14},{8,0},{10,2},{12,4},{14,6},{16,24},{18,... | collective-permute-start | bytes 835592 | tf_op jit(solution)/shard_map/x_last_side_1/ppermute | solution.py:24
  87.0 13.0 %collective-permute-start.18 = (bf16[3,192,256]{2,1,0:T(8,128)(2,1)S(1)}, bf16[3,192,256]{2,1,0:T(8,128)(2,1)S(1)}, u32[]{:S(2)}, u32[]{:S(2)}) collective-permute-start(bf16[3,192,256]{2,1,0:T(8,128)(2,1)S(1)} %keys_values.3.refs_4_), channel_id=1, source_target_pairs={{0,4},{2,6},{4,0},{6,2},{8,12},{10,14},{12,8},{14,10},{16,20},{18,... | collective-permute-start | bytes 884744 | tf_op jit(solution)/shard_map/kv_line/ppermute | solution.py:24
  93.0 7.0 %collective-permute-start.19 = (bf16[1,192,256]{2,1,0:T(8,128)(2,1)S(1)}, bf16[1,192,256]{2,1,0:T(8,128)(2,1)S(1)}, u32[]{:S(2)}, u32[]{:S(2)}) collective-permute-start(bf16[1,192,256]{2,1,0:T(8,128)(2,1)S(1)} %keys_values.2.refs_8_), channel_id=1, source_target_pairs={{0,4},{2,6},{4,0},{6,2},{8,12},{10,14},{12,8},{14,10},{16,20},{18,... | collective-permute-start | bytes 294920 | tf_op jit(solution)/shard_map/kv_line/ppermute | solution.py:24
  94.6 7.3 %collective-permute-start.20 = (bf16[3,192,256]{2,1,0:T(8,128)(2,1)S(1)}, bf16[3,192,256]{2,1,0:T(8,128)(2,1)S(1)}, u32[]{:S(2)}, u32[]{:S(2)}) collective-permute-start(bf16[3,192,256]{2,1,0:T(8,128)(2,1)S(1)} %keys_values.3.refs_4_), channel_id=1, source_target_pairs={{0,2},{2,0},{4,6},{6,4},{8,10},{10,8},{12,14},{14,12},{16,18},{18,... | collective-permute-start | bytes 884744 | tf_op jit(solution)/shard_map/core_kv/ppermute | solution.py:24
  100.0 2.1 %collective-permute-start.21 = (bf16[3,192,256]{2,1,0:T(8,128)(2,1)S(1)}, bf16[3,192,256]{2,1,0:T(8,128)(2,1)S(1)}, u32[]{:S(2)}, u32[]{:S(2)}) collective-permute-start(bf16[3,192,256]{2,1,0:T(8,128)(2,1)S(1)} %collective-permute-done.18.refs_5_), channel_id=1, source_target_pairs={{0,2},{2,0},{4,6},{6,4},{8,10},{10,8},{12,14},{14,12},{16,18},{18,... | collective-permute-start | bytes 884744 | tf_op jit(solution)/shard_map/core_kv_line/ppermute | solution.py:24
  100.6 1.3 %collective-permute-start.22 = (bf16[1,192,256]{2,1,0:T(8,128)(2,1)S(1)}, bf16[1,192,256]{2,1,0:T(8,128)(2,1)S(1)}, u32[]{:S(2)}, u32[]{:S(2)}) collective-permute-start(bf16[1,192,256]{2,1,0:T(8,128)(2,1)S(1)} %keys_values.2.refs_8_), channel_id=1, source_target_pairs={{0,2},{2,0},{4,6},{6,4},{8,10},{10,8},{12,14},{14,12},{16,18},{18,... | collective-permute-start | bytes 294920 | tf_op jit(solution)/shard_map/core_kv/ppermute | solution.py:24
  100.7 1.4 %collective-permute-start.23 = (bf16[1,192,256]{2,1,0:T(8,128)(2,1)S(1)}, bf16[1,192,256]{2,1,0:T(8,128)(2,1)S(1)}, u32[]{:S(2)}, u32[]{:S(2)}) collective-permute-start(bf16[1,192,256]{2,1,0:T(8,128)(2,1)S(1)} %collective-permute-done.19.refs_9_), channel_id=1, source_target_pairs={{0,2},{2,0},{4,6},{6,4},{8,10},{10,8},{12,14},{14,12},{16,18},{18,... | collective-permute-start | bytes 294920 | tf_op jit(solution)/shard_map/core_kv_line/ppermute | solution.py:24
  101.9 10.5 %copy-start.4 = (bf16[3,192,256]{2,1,0:T(8,128)(2,1)}, bf16[3,192,256]{2,1,0:T(8,128)(2,1)S(1)}, u32[]{:S(2)}) copy-start(bf16[3,192,256]{2,1,0:T(8,128)(2,1)S(1)} %collective-permute-done.20.refs_6_) | copy-start | bytes 884740
  107.6 13.3 %collective-permute-start.24 = (bf16[128,512]{1,0:T(8,128)(2,1)S(1)}, bf16[128,512]{1,0:T(8,128)(2,1)S(1)}, u32[]{:S(2)}, u32[]{:S(2)}) collective-permute-start(bf16[128,512]{1,0:T(8,128)(2,1)S(1)} %attend.4), channel_id=1, source_target_pairs={{0,24},{2,26},{4,28},{6,30},{8,16},{10,18},{12,20},{14,22},{16,8},... | collective-permute-start | bytes 393224 | tf_op jit(solution)/shard_map/mixed_3/ppermute | solution.py:24
  116.4 9.0 %collective-permute-start.25 = (bf16[128,512]{1,0:T(8,128)(2,1)S(1)}, bf16[128,512]{1,0:T(8,128)(2,1)S(1)}, u32[]{:S(2)}, u32[]{:S(2)}) collective-permute-start(bf16[128,512]{1,0:T(8,128)(2,1)S(1)} %attend.6), channel_id=1, source_target_pairs={{0,8},{2,10},{4,12},{6,14},{8,0},{10,2},{12,4},{14,6},{16,24},{18,... | collective-permute-start | bytes 393224 | tf_op jit(solution)/shard_map/mixed_1/ppermute | solution.py:24
  117.1 10.1 %collective-permute-start.26 = (bf16[128,512]{1,0:T(8,128)(2,1)S(1)}, bf16[128,512]{1,0:T(8,128)(2,1)S(1)}, u32[]{:S(2)}, u32[]{:S(2)}) collective-permute-start(bf16[128,512]{1,0:T(8,128)(2,1)S(1)} %attend.5), channel_id=1, source_target_pairs={{0,16},{2,18},{4,20},{6,22},{8,24},{10,26},{12,28},{14,30},{16,0},... | collective-permute-start | bytes 393224 | tf_op jit(solution)/shard_map/mixed_2/ppermute | solution.py:24
  120.9 1.0 copy-start.5

commit v7 on v6

--- a/solution.py
+++ b/solution.py
@@ -43,6 +43,7 @@
         in_specs=[VMEM] * 2,
         out_specs=VMEM,
         compiler_params=pltpu.CompilerParams(vmem_limit_bytes=8 * 2**20),
+        cost_estimate=pl.CostEstimate(flops=1, bytes_accessed=1, transcendentals=0),
         name="squares",
     )(stream, hidden)
 
@@ -69,6 +70,7 @@
         in_specs=[VMEM] * (3 + len(sums)),
         out_specs=VMEM,
         compiler_params=pltpu.CompilerParams(vmem_limit_bytes=12 * 2**20),
+        cost_estimate=pl.CostEstimate(flops=1, bytes_accessed=1, transcendentals=0),
         name="norm",
     )(stream, hidden, gain.reshape(1, -1), *sums)
 
@@ -465,13 +467,14 @@
         w_sent = [jnp.concatenate([w, folded(c)], 0) for w, c in zip(w_cut[:3], caches)]
         w_own = w_cut[0][None]
         w_1, w_2 = across(w_sent[1], 1, "w"), across(w_sent[2], 2, "w")
-        far, next_x = across(after(own, w_2), 2, "x_far"), across(own, 1, "x_next")
-        own_side = sides(own, "own")
-        w_some, _, cache_2 = unpack([w_own], [w_2], depth, fold)
-        w_line = line(w_some, "w02")
+        far, next_x = across(own, 2, "x_far"), across(own, 1, "x_next")
+        own_line = line(w_own, "w0")
+        own_side = sides(after(own, own_line), "own")
+        w_some, w_line, cache_2 = unpack([w_own], [w_2], depth, fold)
+        w_line = line(w_line, "w2")
         w_some, w_mid, cache_1 = unpack([w_some], [w_1], depth, fold)
         cache_mid = (cache_1, cache_2)
-        late, late_cache, _ = lax.optimization_barrier((plane, caches[3], w_2))
+        late, late_cache, _ = lax.optimization_barrier((plane, caches[3], own))
         w_sent_3 = jnp.concatenate([w_cut[3], folded(late_cache)], 0)
         q_ids, cosine, sine = tables(late)
         ids = jnp.arange(count, dtype=jnp.int32)
@@ -482,9 +485,10 @@
         kv_ids = [(late ^ k) * crew + (inner ^ turn) for k in range(heads) for turn in (0, 2, 1, 3)]
         kv_ids = jnp.stack(kv_ids).astype(jnp.int32)
         numbers = (q_ids, cosine, sine, x_ids, w_ids, kv_ids)
-        own, own_side, next_x, far, w_some, w_mid, cache_mid, w_3, w_line, numbers = (
+        lines = (own_line, w_line)
+        own, own_side, next_x, far, w_some, w_mid, cache_mid, w_3, lines, numbers = (
             lax.optimization_barrier(
-                (own, own_side, next_x, far, w_some, w_mid, cache_mid, w_sent_3, w_line, numbers)
+                (own, own_side, next_x, far, w_some, w_mid, cache_mid, w_sent_3, lines, numbers)
             )
         )
         q_ids, cosine, sine, x_ids, w_ids, kv_ids = numbers
@@ -494,7 +498,7 @@
         w_mid_line = line(w_mid, "w1")
         w_last, _, cache_last = unpack([], [w_3], depth, fold)
         w_last_line = line(w_last, "w3")
-        w_some = join([w_some, w_line, w_mid_line])
+        w_some = join([w_some, *lines, w_mid_line])
         w_some_core = core(w_some, "w")
         last_low, far_high = half(last, 0), half(far_side, 1)
         moved = (last, next_side, far_side, w_last, w_last_line, w_some)
@@ -539,6 +543,7 @@
         for chunk in x_chunks:
             chunk[0] = after(chunk[0], kv_new[1])
         queries = [*projected(False, True, (0, 1, 2)), *projected(False, True, (3,))]
+        first_queries = queries[0]
         queries = list(lax.optimization_barrier(tuple(queries)))
     else:
         kv_new, queries = [[value] for value in projected(True, True, tuple(range(heads)))]
@@ -546,7 +551,7 @@
     if squared:
         kv_parts, places = [], []
         fars = [swap(mine, "seq", seq, 2, "kv_line") for mine in kv_new]
-        fars = lax.optimization_barrier((*fars, queries[1]))
+        fars = lax.optimization_barrier((*fars, first_queries))
         for mine, far in zip(kv_new, fars):
             places += [(len(kv_parts) + n, i) for i in range(mine.shape[0]) for n in range(4)]
             kv_parts += [mine, far, core(mine, "kv"), core(far, "kv_line")]

time: 128 us -> 127 us (level)
  waiting for transfers between devices: 57.4 us -> 63.2 us
  local copies, waits for them, and re-layouts: 4.6 us -> 1.85 us
  Pallas kernels: 30.9 us -> 28.5 us
  starting transfers between devices: 29.6 us -> 27.3 us
    ppermute x27 -> x28, waiting for transfers between devices: 57.4 us -> 63.2 us  [swap(): return lax.ppermute(value, axis, [(i, i ^ mask) for i in range(size)])]
    unnamed x20 -> x12, local copies, waits for them, and re-layouts: 2.77 us -> 0.02 us
    ppermute x27 -> x28, starting transfers between devices: 29.6 us -> 27.3 us  [swap(): return lax.ppermute(value, axis, [(i, i ^ mask) for i in range(size)])]
    pallas_call x3, Pallas kernels: 3.3 us -> 0.99 us  [unpack(): pl.pallas_call(functools.partial(unpack_kernel, len(plain), fold, len(pla...]
  transfers between devices with their start and end apart: 27 -> 28, of which waited for: 16 -> 11; matrix products, arithmetic and copies ran while one was open for 3% -> 3% of each run, Pallas kernels for 20% -> 18%
where the time goes in v7:
time: 127 us
  waiting for transfers between devices  63.2 us (50%)
  Pallas kernels  28.5 us (22%)
  starting transfers between devices  27.3 us (21%)
  other arithmetic  4.76 us (4%)
  local copies, waits for them, and re-layouts  1.85 us (1%)
    ppermute x28, waiting for transfers between devices, swap(): return lax.ppermute(value, axis, [(i, i ^ mask) for i in range(size)])  63.2 us
    ppermute x28, starting transfers between devices, swap(): return lax.ppermute(value, axis, [(i, i ^ mask) for i in range(size)])  27.3 us
    pallas_call x4, Pallas kernels, attend(): pl.pallas_call(functools.partial(attend_kernel, slots, tok, places), grid...  17.8 us
    pallas_call x4, Pallas kernels, project(): pl.pallas_call(functools.partial(project_kernel, kv, tiles, first_slot, t...  9.17 us
  transfers between devices with their start and end apart: 28, of which 11 were waited for; matrix products, arithmetic and copies ran while one was open for 3% of the time, Pallas kernels for 18%

profile of v7, /device:TPU:0, one launch (start us, length us, event | category | flops | bytes accessed | tf_op | source)
XLA Modules:
  0.0 126.5 jit_solution(12786050511864591903)
XLA Ops:
  0.0 1.5 %constant_dynamic-slice_fusion = (bf16[256,768]{1,0:T(8,128)(2,1)S(1)}, bf16[256,768]{1,0:T(8,128)(2,1)S(1)}, bf16[256,768]{1,0:T(8,128)(2,1)S(1)}, bf16[256,768]{1,0:T(8,128)(2,1)S(1)}) fusion(bf16[256,3072]{1,0:T(8,128)(2,1)} %param.9, s32[]{:T(128)S(6)} %select_n.55, s32[]{:T(128)S(6)} %select_n.53, s32[]{:T(128)S(6)} %select_n.52, s32[]{:T(128)S(6)} %select_n.54), kind=kLoop, calls=%fused_computation.50 | loop fusion | bytes 3145744 | tf_op jit(solution)/shard_map/dynamic_slice | solution.py:419
  1.5 0.0 copy-start.4
  1.6 0.2 squares.1.refs_0_
  1.8 3.0 %collective-permute-start = (f32[136,128]{1,0:T(8,128)S(1)}, f32[136,128]{1,0:T(8,128)S(1)}, u32[]{:S(2)}, u32[]{:S(2)}) collective-permute-start(f32[136,128]{1,0:T(8,128)S(1)} %squares.1.refs_0_), channel_id=1, source_target_pairs={{0,1},{1,0},{2,3},{3,2},{4,5},{5,4},{6,7},{7,6},{8,9},{9,8},{10,11... | collective-permute-start | bytes 208904 | tf_op jit(solution)/shard_map/side_sums/ppermute | solution.py:24
  4.8 1.5 %collective-permute-start.1 = (bf16[1,256,768]{2,1,0:T(8,128)(2,1)S(1)}, bf16[1,256,768]{2,1,0:T(8,128)(2,1)S(1)}, u32[]{:S(2)}, u32[]{:S(2)}) collective-permute-start(bf16[1,256,768]{2,1,0:T(8,128)(2,1)S(1)} %bitcast.54), channel_id=1, source_target_pairs={{0,4},{2,6},{4,0},{6,2},{8,12},{10,14},{12,8},{14,10},{16,20},{18,... | collective-permute-start | bytes 1179656 | tf_op jit(solution)/shard_map/line_w0/ppermute | solution.py:24
  6.3 1.0 fusion.7
  7.3 1.6 %collective-permute-start.6 = (bf16[288,768]{1,0:T(8,128)(2,1)}, bf16[288,768]{1,0:T(8,128)(2,1)S(1)}, u32[]{:S(2)}, u32[]{:S(2)}) collective-permute-start(bf16[288,768]{1,0:T(8,128)(2,1)} %get-tuple-element.134), channel_id=1, source_target_pairs={{0,8},{2,10},{4,12},{6,14},{8,0},{10,2},{12,4},{14,6},{16,24},{18,... | collective-permute-start | bytes 1327112 | tf_op jit(solution)/shard_map/w_1/ppermute | solution.py:24
  8.9 2.6 %collective-permute-start.5 = (bf16[288,768]{1,0:T(8,128)(2,1)}, bf16[288,768]{1,0:T(8,128)(2,1)S(1)}, u32[]{:S(2)}, u32[]{:S(2)}) collective-permute-start(bf16[288,768]{1,0:T(8,128)(2,1)} %get-tuple-element.135), channel_id=1, source_target_pairs={{0,16},{2,18},{4,20},{6,22},{8,24},{10,26},{12,28},{14,30},{16,0},... | collective-permute-start | bytes 1327112 | tf_op jit(solution)/shard_map/w_2/ppermute | solution.py:24
  12.2 0.1 pad_add_fusion.1.refs_0_
  12.3 0.2 norm.1.refs_2_
  12.5 0.1 broadcast_multiply_fusion.1
  12.6 0.1 iota_add_fusion
  12.7 0.1 add_add_fusion
  12.8 0.8 maximum_maximum_fusion
  13.6 0.3 collective-permute-start.4
  13.9 0.4 collective-permute-start.3
  14.4 0.1 stack.122.refs_2_
  14.5 0.1 stack.117.refs_1_
  14.6 1.4 %fusion.16 = (f32[4,192,64]{2,1,0:T(8,128)S(1)}, f32[4,192,64]{2,1,0:T(8,128)S(1)}, f32[4,192,64]{2,1,0:T(8,128)S(1)}) fusion(f32[64]{0:T(128)S(1)} %multiply_exponential_fusion, f32[4,192]{1,0:T(4,128)S(1)} %add_convert_fusion), kind=kLoop, calls=%fused_computation.32 | loop fusion | flops 98304 | bytes 593152 | tf_op jit(solution)/shard_map/neg | solution.py:451
  16.0 0.3 pad_maximum_fusion.4
  16.3 0.6 collective-permute-start.2
  16.9 27.6 %collective-permute-done.5.refs_1_ = bf16[288,768]{1,0:T(8,128)(2,1)S(1)} collective-permute-done((bf16[288,768]{1,0:T(8,128)(2,1)}, bf16[288,768]{1,0:T(8,128)(2,1)S(1)}, u32[]{:S(2)}, u32[]{:S(2)}) %collective-permute-start.5) | collective-permute-done | bytes 442400 | tf_op jit(solution)/shard_map/w_2/ppermute | solution.py:24
  44.5 0.1 unpack.3
  44.6 0.6 collective-permute-start.7
  45.2 0.1 unpack.4
  45.3 9.2 %collective-permute-done.4.refs_6_ = bf16[8,136,256]{2,1,0:T(8,128)(2,1)S(1)} collective-permute-done((bf16[8,136,256]{2,1,0:T(8,128)(2,1)S(1)}, bf16[8,136,256]{2,1,0:T(8,128)(2,1)S(1)}, u32[]{:S(2)}, u32[]{:S(2)}) %collective-permute-start.4) | collective-permute-done | bytes 557088 | tf_op jit(solution)/shard_map/x_far_2/ppermute | solution.py:24
  54.5 2.6 %collective-permute-start.11 = (bf16[288,768]{1,0:T(8,128)(2,1)S(1)}, bf16[288,768]{1,0:T(8,128)(2,1)S(1)}, u32[]{:S(2)}, u32[]{:S(2)}) collective-permute-start(bf16[288,768]{1,0:T(8,128)(2,1)S(1)} %copy-done.2), channel_id=1, source_target_pairs={{0,24},{2,26},{4,28},{6,30},{8,16},{10,18},{12,20},{14,22},{16,8},... | collective-permute-start | bytes 1327112 | tf_op jit(solution)/shard_map/w_3/ppermute | solution.py:24
  57.1 0.5 collective-permute-start.13
  57.7 0.5 collective-permute-start.10
  58.2 1.5 %collective-permute-start.9 = (bf16[8,136,256]{2,1,0:T(8,128)(2,1)S(1)}, bf16[8,136,256]{2,1,0:T(8,128)(2,1)S(1)}, u32[]{:S(2)}, u32[]{:S(2)}) collective-permute-start(bf16[8,136,256]{2,1,0:T(8,128)(2,1)S(1)} %collective-permute-done.3.refs_4_), channel_id=1, source_target_pairs={{0,1},{1,0},{2,3},{3,2},{4,5},{5,4},{6,7},{7,6},{8,9},{9,8},{10,11... | collective-permute-start | bytes 1671176 | tf_op jit(solution)/shard_map/side_next/ppermute | solution.py:24
  59.7 6.2 %collective-permute-done.13.refs_3_ = bf16[1,256,768]{2,1,0:T(8,128)(2,1)S(1)} collective-permute-done((bf16[1,256,768]{2,1,0:T(8,128)(2,1)S(1)}, bf16[1,256,768]{2,1,0:T(8,128)(2,1)S(1)}, u32[]{:S(2)}, u32[]{:S(2)}) %collective-permute-start.13) | collective-permute-done | bytes 393248 | tf_op jit(solution)/shard_map/line_w1/ppermute | solution.py:24
  65.9 0.2 join.1.refs_5_.refs_8_
  66.0 0.1 collective-permute-start.14
  66.1 3.4 %collective-permute-done.11.refs_0_ = bf16[288,768]{1,0:T(8,128)(2,1)S(1)} collective-permute-done((bf16[288,768]{1,0:T(8,128)(2,1)S(1)}, bf16[288,768]{1,0:T(8,128)(2,1)S(1)}, u32[]{:S(2)}, u32[]{:S(2)}) %collective-permute-start.11) | collective-permute-done | bytes 442400 | tf_op jit(solution)/shard_map/w_3/ppermute | solution.py:24
  69.5 0.8 unpack.5
  70.3 0.5 collective-permute-start.12
  70.9 2.3 %collective-permute-done.10.value.refs_7_ = bf16[8,136,256]{2,1,0:T(8,128)(2,1)S(1)} collective-permute-done((bf16[8,136,256]{2,1,0:T(8,128)(2,1)S(1)}, bf16[8,136,256]{2,1,0:T(8,128)(2,1)S(1)}, u32[]{:S(2)}, u32[]{:S(2)}) %collective-permute-start.10) | collective-permute-done | bytes 557088 | tf_op jit(solution)/shard_map/side_far/ppermute | solution.py:24
  73.2 5.3 %collective-permute-done.8.value.refs_2_ = bf16[8,136,256]{2,1,0:T(8,128)(2,1)S(1)} collective-permute-done((bf16[8,136,256]{2,1,0:T(8,128)(2,1)S(1)}, bf16[8,136,256]{2,1,0:T(8,128)(2,1)S(1)}, u32[]{:S(2)}, u32[]{:S(2)}) %collective-permute-start.8) | collective-permute-done | bytes 557088 | tf_op jit(solution)/shard_map/x_last_1/ppermute | solution.py:24
  78.6 3.0 %collective-permute-done.9.refs_5_ = bf16[8,136,256]{2,1,0:T(8,128)(2,1)S(1)} collective-permute-done((bf16[8,136,256]{2,1,0:T(8,128)(2,1)S(1)}, bf16[8,136,256]{2,1,0:T(8,128)(2,1)S(1)}, u32[]{:S(2)}, u32[]{:S(2)}) %collective-permute-start.9) | collective-permute-done | bytes 557088 | tf_op jit(solution)/shard_map/side_next/ppermute | solution.py:24
  81.6 0.5 collective-permute-start.18
  82.1 0.5 collective-permute-start.15
  82.6 1.6 %collective-permute-start.16 = (bf16[4,136,256]{2,1,0:T(8,128)(2,1)S(1)}, bf16[4,136,256]{2,1,0:T(8,128)(2,1)S(1)}, u32[]{:S(2)}, u32[]{:S(2)}) collective-permute-start(bf16[4,136,256]{2,1,0:T(8,128)(2,1)S(1)} %half.3), channel_id=1, source_target_pairs={{0,8},{2,10},{4,12},{6,14},{8,0},{10,2},{12,4},{14,6},{16,24},{18,... | collective-permute-start | bytes 835592 | tf_op jit(solution)/shard_map/x_last_side_1/ppermute | solution.py:24
  84.2 2.4 %keys_values.3.refs_4_ = bf16[3,192,256]{2,1,0:T(8,128)(2,1)S(1)} custom-call(s32[16]{0:T(128)S(1)} %pad_add_fusion.1.refs_0_, s32[16]{0:T(128)S(1)} %stack.117.refs_1_, bf16[8,136,256]{2,1,0:T(8,128)(2,1)S(1)} %norm.1.refs_2_, bf16[8,136,256]{2,1,0:T(8,128)(2,1)S(1)} %collective-permute-done.2.refs_3_, ...), custom_call_target="tpu_custom_call" | custom-call | flops 905969664 | bytes 5636096 | tf_op jit(solution)/shard_map/keys_values/pallas_call | solution.py:247
  86.6 1.2 collective-permute-start.19
  87.9 2.9 %collective-permute-done.15.refs_3_ = bf16[4,136,256]{2,1,0:T(8,128)(2,1)S(1)} collective-permute-done((bf16[4,136,256]{2,1,0:T(8,128)(2,1)S(1)}, bf16[4,136,256]{2,1,0:T(8,128)(2,1)S(1)}, u32[]{:S(2)}, u32[]{:S(2)}) %collective-permute-start.15) | collective-permute-done | bytes 278560 | tf_op jit(solution)/shard_map/side_last/ppermute | solution.py:24
  90.7 0.2 collective-permute-done.16.refs_4_
  91.0 1.4 %keys_values.2.refs_8_ = bf16[1,192,256]{2,1,0:T(8,128)(2,1)S(1)} custom-call(s32[16]{0:T(128)S(1)} %pad_add_fusion.1.refs_0_, s32[16]{0:T(128)S(1)} %stack.117.refs_1_, bf16[8,136,256]{2,1,0:T(8,128)(2,1)S(1)} %collective-permute-done.8.value.refs_2_, bf16[4,136,256]{2,1,0:T(8,128)(2,1)S(1)} %collective-permute-done.15.refs_3_, ...), custom_call_target="tpu_custom_call" | custom-call | flops 301989888 | bytes 3276800 | tf_op jit(solution)/shard_map/keys_values/pallas_call | solution.py:247
  92.4 1.6 %collective-permute-start.20 = (bf16[1,192,256]{2,1,0:T(8,128)(2,1)S(1)}, bf16[1,192,256]{2,1,0:T(8,128)(2,1)S(1)}, u32[]{:S(2)}, u32[]{:S(2)}) collective-permute-start(bf16[1,192,256]{2,1,0:T(8,128)(2,1)S(1)} %keys_values.2.refs_8_), channel_id=1, source_target_pairs={{0,4},{2,6},{4,0},{6,2},{8,12},{10,14},{12,8},{14,10},{16,20},{18,... | collective-permute-start | bytes 294920 | tf_op jit(solution)/shard_map/kv_line/ppermute | solution.py:24
  93.9 3.4 %queries.2.refs_3_ = bf16[3,4,128,128]{3,2,1,0:T(8,128)(2,1)S(1)} custom-call(s32[16]{0:T(128)S(1)} %pad_add_fusion.1.refs_0_, s32[16]{0:T(128)S(1)} %stack.117.refs_1_, bf16[8,136,256]{2,1,0:T(8,128)(2,1)S(1)} %norm.1.refs_2_, bf16[8,136,256]{2,1,0:T(8,128)(2,1)S(1)} %collective-permute-done.2.refs_3_, ...), custom_call_target="tpu_custom_call" | custom-call | flops 1811939328 | bytes 7733248 | tf_op jit(solution)/shard_map/queries/pallas_call | solution.py:247
  97.3 0.2 collective-permute-done.20.refs_9_
  97.5 0.4 collective-permute-start.22
  97.9 0.1 collective-permute-start.23
  98.0 0.4 collective-permute-start.24
  98.4 2.0 %queries.3.refs_3_ = bf16[1,4,128,128]{3,2,1,0:T(8,128)(2,1)S(1)} custom-call(s32[16]{0:T(128)S(1)} %pad_add_fusion.1.refs_0_, s32[16]{0:T(128)S(1)} %stack.117.refs_1_, bf16[8,136,256]{2,1,0:T(8,128)(2,1)S(1)} %collective-permute-done.8.value.refs_2_, bf16[4,136,256]{2,1,0:T(8,128)(2,1)S(1)} %collective-permute-done.15.refs_3_, ...), custom_call_target="tpu_custom_call" | custom-call | flops 603979776 | bytes 5373952 | tf_op jit(solution)/shard_map/queries/pallas_call | solution.py:247
  100.4 5.5 %attend.4 = bf16[128,512]{1,0:T(8,128)(2,1)S(1)} custom-call(s32[1]{0:T(128)} %copy.8.refs_0_, s32[4]{0:T(128)S(1)} %get-tuple-element.72.refs_1_, s32[16]{0:T(128)S(1)} %stack.122.refs_2_, bf16[1,4,128,128]{3,2,1,0:T(8,128)(2,1)S(1)} %queries.3.refs_3_, bf16[3,192,256]{2,1,0:T(8,128)(2,1)S(1)} %keys_values.3.refs_4_, ...), custom_call_target="tpu_custom_call" | custom-call | flops 805306368 | bytes 1572864 | tf_op jit(solution)/shard_map/attend/pallas_call | solution.py:382
  105.9 0.2 collective-permute-start.25
  106.1 4.6 %attend.5 = bf16[128,512]{1,0:T(8,128)(2,1)S(1)} custom-call(s32[1]{0:T(128)} %copy.8.refs_0_, s32[4]{0:T(128)S(1)} %get-tuple-element.72.refs_1_, s32[16]{0:T(128)S(1)} %stack.122.refs_2_, bf16[3,4,128,128]{3,2,1,0:T(8,128)(2,1)S(1)} %queries.2.refs_3_, bf16[3,192,256]{2,1,0:T(8,128)(2,1)S(1)} %keys_values.3.refs_4_, ...), custom_call_target="tpu_custom_call" | custom-call | flops 805306368 | bytes 1572864 | tf_op jit(solution)/shard_map/attend/pallas_call | solution.py:382
  110.7 4.0 %attend.6 = bf16[128,512]{1,0:T(8,128)(2,1)S(1)} custom-call(s32[1]{0:T(128)} %copy.8.refs_0_, s32[4]{0:T(128)S(1)} %get-tuple-element.72.refs_1_, s32[16]{0:T(128)S(1)} %stack.122.refs_2_, bf16[3,4,128,128]{3,2,1,0:T(8,128)(2,1)S(1)} %queries.2.refs_3_, bf16[3,192,256]{2,1,0:T(8,128)(2,1)S(1)} %keys_values.3.refs_4_, ...), custom_call_target="tpu_custom_call" | custom-call | flops 805306368 | bytes 1572864 | tf_op jit(solution)/shard_map/attend/pallas_call | solution.py:382
  114.8 1.7 %collective-permute-start.26 = (bf16[128,512]{1,0:T(8,128)(2,1)S(1)}, bf16[128,512]{1,0:T(8,128)(2,1)S(1)}, u32[]{:S(2)}, u32[]{:S(2)}) collective-permute-start(bf16[128,512]{1,0:T(8,128)(2,1)S(1)} %attend.6), channel_id=1, source_target_pairs={{0,8},{2,10},{4,12},{6,14},{8,0},{10,2},{12,4},{14,6},{16,24},{18,... | collective-permute-start | bytes 393224 | tf_op jit(solution)/shard_map/mixed_1/ppermute | solution.py:24
  116.5 2.7 %collective-permute-start.27 = (bf16[128,512]{1,0:T(8,128)(2,1)S(1)}, bf16[128,512]{1,0:T(8,128)(2,1)S(1)}, u32[]{:S(2)}, u32[]{:S(2)}) collective-permute-start(bf16[128,512]{1,0:T(8,128)(2,1)S(1)} %attend.5), channel_id=1, source_target_pairs={{0,16},{2,18},{4,20},{6,22},{8,24},{10,26},{12,28},{14,30},{16,0},... | collective-permute-start | bytes 393224 | tf_op jit(solution)/shard_map/mixed_2/ppermute | solution.py:24
  119.2 3.6 %attend.7 = bf16[128,512]{1,0:T(8,128)(2,1)S(1)} custom-call(s32[1]{0:T(128)} %copy.8.refs_0_, s32[4]{0:T(128)S(1)} %get-tuple-element.72.refs_1_, s32[16]{0:T(128)S(1)} %stack.122.refs_2_, bf16[3,4,128,128]{3,2,1,0:T(8,128)(2,1)S(1)} %queries.2.refs_3_, bf16[3,192,256]{2,1,0:T(8,128)(2,1)S(1)} %keys_values.3.refs_4_, ...), custom_call_target="tpu_custom_call" | custom-call | flops 805306368 | bytes 1572864 | tf_op jit(solution)/shard_map/attend/pallas_call | solution.py:382
  122.8 2.7 %collective-permute-done.27 = bf16[128,512]{1,0:T(8,128)(2,1)S(1)} collective-permute-done((bf16[128,512]{1,0:T(8,128)(2,1)S(1)}, bf16[128,512]{1,0:T(8,128)(2,1)S(1)}, u32[]{:S(2)}, u32[]{:S(2)}) %collective-permute-start.27) | collective-permute-done | bytes 131104 | tf_op jit(solution)/shard_map/mixed_2/ppermute | solution.py:24
  125.6 0.1 pad_maximum_fusion.2
  125.7 0.8 pad_maximum_fusion.3
  (45 shorter events, 0.3 us)
Async XLA Ops:
  0.0 1.6 %copy-start = (bf16[128,2048]{1,0:T(8,128)(2,1)S(1)}, bf16[128,2048]{1,0:T(8,128)(2,1)}, u32[]{:S(2)}) copy-start(bf16[128,2048]{1,0:T(8,128)(2,1)} %stream.1) | copy-start | bytes 1572868
  0.0 1.6 %copy-start.1 = (bf16[8,2048]{1,0:T(8,128)(2,1)S(1)}, bf16[8,2048]{1,0:T(8,128)(2,1)}, u32[]{:S(2)}) copy-start(bf16[8,2048]{1,0:T(8,128)(2,1)} %hidden.3) | copy-start | bytes 98308
  0.0 6.3 %copy-start.5 = (s32[8]{0:T(128)S(1)}, s32[8]{0:T(128)}, u32[]{:S(2)}) copy-start(s32[8]{0:T(128)} %param.12) | copy-start | bytes 100
  0.0 6.3 %copy-start.3 = (bf16[2,64,512]{2,1,0:T(8,128)(2,1)S(1)}, bf16[2,64,512]{2,1,0:T(8,128)(2,1)}, u32[]{:S(2)}) copy-start(bf16[2,64,512]{2,1,0:T(8,128)(2,1)} %param.10) | copy-start | bytes 393220
  1.5 10.6 %copy-start.4 = (f32[4096]{0:T(1024)S(1)}, f32[4096]{0:T(1024)}, u32[]{:S(2)}) copy-start(f32[4096]{0:T(1024)} %param.8) | copy-start | bytes 49156
  1.8 10.5 %collective-permute-start = (f32[136,128]{1,0:T(8,128)S(1)}, f32[136,128]{1,0:T(8,128)S(1)}, u32[]{:S(2)}, u32[]{:S(2)}) collective-permute-start(f32[136,128]{1,0:T(8,128)S(1)} %squares.1.refs_0_), channel_id=1, source_target_pairs={{0,1},{1,0},{2,3},{3,2},{4,5},{5,4},{6,7},{7,6},{8,9},{9,8},{10,11... | collective-permute-start | bytes 208904 | tf_op jit(solution)/shard_map/side_sums/ppermute | solution.py:24
  4.8 11.5 %collective-permute-start.1 = (bf16[1,256,768]{2,1,0:T(8,128)(2,1)S(1)}, bf16[1,256,768]{2,1,0:T(8,128)(2,1)S(1)}, u32[]{:S(2)}, u32[]{:S(2)}) collective-permute-start(bf16[1,256,768]{2,1,0:T(8,128)(2,1)S(1)} %bitcast.54), channel_id=1, source_target_pairs={{0,4},{2,6},{4,0},{6,2},{8,12},{10,14},{12,8},{14,10},{16,20},{18,... | collective-permute-start | bytes 1179656 | tf_op jit(solution)/shard_map/line_w0/ppermute | solution.py:24
  7.3 37.9 %collective-permute-start.6 = (bf16[288,768]{1,0:T(8,128)(2,1)}, bf16[288,768]{1,0:T(8,128)(2,1)S(1)}, u32[]{:S(2)}, u32[]{:S(2)}) collective-permute-start(bf16[288,768]{1,0:T(8,128)(2,1)} %get-tuple-element.134), channel_id=1, source_target_pairs={{0,8},{2,10},{4,12},{6,14},{8,0},{10,2},{12,4},{14,6},{16,24},{18,... | collective-permute-start | bytes 1327112 | tf_op jit(solution)/shard_map/w_1/ppermute | solution.py:24
  8.9 35.6 %collective-permute-start.5 = (bf16[288,768]{1,0:T(8,128)(2,1)}, bf16[288,768]{1,0:T(8,128)(2,1)S(1)}, u32[]{:S(2)}, u32[]{:S(2)}) collective-permute-start(bf16[288,768]{1,0:T(8,128)(2,1)} %get-tuple-element.135), channel_id=1, source_target_pairs={{0,16},{2,18},{4,20},{6,22},{8,24},{10,26},{12,28},{14,30},{16,0},... | collective-permute-start | bytes 1327112 | tf_op jit(solution)/shard_map/w_2/ppermute | solution.py:24
  13.6 40.9 %collective-permute-start.4 = (bf16[8,136,256]{2,1,0:T(8,128)(2,1)S(1)}, bf16[8,136,256]{2,1,0:T(8,128)(2,1)S(1)}, u32[]{:S(2)}, u32[]{:S(2)}) collective-permute-start(bf16[8,136,256]{2,1,0:T(8,128)(2,1)S(1)} %norm.1.refs_2_), channel_id=1, source_target_pairs={{0,16},{2,18},{4,20},{6,22},{8,24},{10,26},{12,28},{14,30},{16,0},... | collective-permute-start | bytes 1671176 | tf_op jit(solution)/shard_map/x_far_2/ppermute | solution.py:24
  13.9 40.6 %collective-permute-start.3 = (bf16[8,136,256]{2,1,0:T(8,128)(2,1)S(1)}, bf16[8,136,256]{2,1,0:T(8,128)(2,1)S(1)}, u32[]{:S(2)}, u32[]{:S(2)}) collective-permute-start(bf16[8,136,256]{2,1,0:T(8,128)(2,1)S(1)} %norm.1.refs_2_), channel_id=1, source_target_pairs={{0,8},{2,10},{4,12},{6,14},{8,0},{10,2},{12,4},{14,6},{16,24},{18,... | collective-permute-start | bytes 1671176 | tf_op jit(solution)/shard_map/x_next_1/ppermute | solution.py:24
  16.3 38.2 %collective-permute-start.2 = (bf16[8,136,256]{2,1,0:T(8,128)(2,1)S(1)}, bf16[8,136,256]{2,1,0:T(8,128)(2,1)S(1)}, u32[]{:S(2)}, u32[]{:S(2)}) collective-permute-start(bf16[8,136,256]{2,1,0:T(8,128)(2,1)S(1)} %norm.1.refs_2_), channel_id=1, source_target_pairs={{0,1},{1,0},{2,3},{3,2},{4,5},{5,4},{6,7},{7,6},{8,9},{9,8},{10,11... | collective-permute-start | bytes 1671176 | tf_op jit(solution)/shard_map/side_own/ppermute | solution.py:24
  44.6 9.9 %collective-permute-start.7 = (bf16[1,256,768]{2,1,0:T(8,128)(2,1)S(1)}, bf16[1,256,768]{2,1,0:T(8,128)(2,1)S(1)}, u32[]{:S(2)}, u32[]{:S(2)}) collective-permute-start(bf16[1,256,768]{2,1,0:T(8,128)(2,1)S(1)} %get-tuple-element.70), channel_id=1, source_target_pairs={{0,4},{2,6},{4,0},{6,2},{8,12},{10,14},{12,8},{14,10},{16,20},{18,... | collective-permute-start | bytes 1179656 | tf_op jit(solution)/shard_map/line_w2/ppermute | solution.py:24
  45.2 9.3 %copy-start.2 = (bf16[288,768]{1,0:T(8,128)(2,1)S(1)}, bf16[288,768]{1,0:T(8,128)(2,1)}, u32[]{:S(2)}) copy-start(bf16[288,768]{1,0:T(8,128)(2,1)} %maximum_maximum_fusion) | copy-start | bytes 1327108
  54.5 15.0 %collective-permute-start.11 = (bf16[288,768]{1,0:T(8,128)(2,1)S(1)}, bf16[288,768]{1,0:T(8,128)(2,1)S(1)}, u32[]{:S(2)}, u32[]{:S(2)}) collective-permute-start(bf16[288,768]{1,0:T(8,128)(2,1)S(1)} %copy-done.2), channel_id=1, source_target_pairs={{0,24},{2,26},{4,28},{6,30},{8,16},{10,18},{12,20},{14,22},{16,8},... | collective-permute-start | bytes 1327112 | tf_op jit(solution)/shard_map/w_3/ppermute | solution.py:24
  57.1 8.8 %collective-permute-start.13 = (bf16[1,256,768]{2,1,0:T(8,128)(2,1)S(1)}, bf16[1,256,768]{2,1,0:T(8,128)(2,1)S(1)}, u32[]{:S(2)}, u32[]{:S(2)}) collective-permute-start(bf16[1,256,768]{2,1,0:T(8,128)(2,1)S(1)} %get-tuple-element.84), channel_id=1, source_target_pairs={{0,4},{2,6},{4,0},{6,2},{8,12},{10,14},{12,8},{14,10},{16,20},{18,... | collective-permute-start | bytes 1179656 | tf_op jit(solution)/shard_map/line_w1/ppermute | solution.py:24
  57.7 15.6 %collective-permute-start.10 = (bf16[8,136,256]{2,1,0:T(8,128)(2,1)S(1)}, bf16[8,136,256]{2,1,0:T(8,128)(2,1)S(1)}, u32[]{:S(2)}, u32[]{:S(2)}) collective-permute-start(bf16[8,136,256]{2,1,0:T(8,128)(2,1)S(1)} %collective-permute-done.4.refs_6_), channel_id=1, source_target_pairs={{0,1},{1,0},{2,3},{3,2},{4,5},{5,4},{6,7},{7,6},{8,9},{9,8},{10,11... | collective-permute-start | bytes 1671176 | tf_op jit(solution)/shard_map/side_far/ppermute | solution.py:24
  58.2 20.4 %collective-permute-start.8 = (bf16[8,136,256]{2,1,0:T(8,128)(2,1)S(1)}, bf16[8,136,256]{2,1,0:T(8,128)(2,1)S(1)}, u32[]{:S(2)}, u32[]{:S(2)}) collective-permute-start(bf16[8,136,256]{2,1,0:T(8,128)(2,1)S(1)} %collective-permute-done.4.refs_6_), channel_id=1, source_target_pairs={{0,8},{2,10},{4,12},{6,14},{8,0},{10,2},{12,4},{14,6},{16,24},{18,... | collective-permute-start | bytes 1671176 | tf_op jit(solution)/shard_map/x_last_1/ppermute | solution.py:24
  58.2 23.4 %collective-permute-start.9 = (bf16[8,136,256]{2,1,0:T(8,128)(2,1)S(1)}, bf16[8,136,256]{2,1,0:T(8,128)(2,1)S(1)}, u32[]{:S(2)}, u32[]{:S(2)}) collective-permute-start(bf16[8,136,256]{2,1,0:T(8,128)(2,1)S(1)} %collective-permute-done.3.refs_4_), channel_id=1, source_target_pairs={{0,1},{1,0},{2,3},{3,2},{4,5},{5,4},{6,7},{7,6},{8,9},{9,8},{10,11... | collective-permute-start | bytes 1671176 | tf_op jit(solution)/shard_map/side_next/ppermute | solution.py:24
  66.0 15.6 %collective-permute-start.14 = (bf16[6,256,768]{2,1,0:T(8,128)(2,1)S(1)}, bf16[6,256,768]{2,1,0:T(8,128)(2,1)S(1)}, u32[]{:S(2)}, u32[]{:S(2)}) collective-permute-start(bf16[6,256,768]{2,1,0:T(8,128)(2,1)S(1)} %join.1.refs_5_.refs_8_), channel_id=1, source_target_pairs={{0,2},{2,0},{4,6},{6,4},{8,10},{10,8},{12,14},{14,12},{16,18},{18,... | collective-permute-start | bytes 7077896 | tf_op jit(solution)/shard_map/core_w/ppermute | solution.py:24
  70.3 11.2 %collective-permute-start.12 = (bf16[1,256,768]{2,1,0:T(8,128)(2,1)S(1)}, bf16[1,256,768]{2,1,0:T(8,128)(2,1)S(1)}, u32[]{:S(2)}, u32[]{:S(2)}) collective-permute-start(bf16[1,256,768]{2,1,0:T(8,128)(2,1)S(1)} %get-tuple-element.89.refs_6_.refs_9_), channel_id=1, source_target_pairs={{0,4},{2,6},{4,0},{6,2},{8,12},{10,14},{12,8},{14,10},{16,20},{18,... | collective-permute-start | bytes 1179656 | tf_op jit(solution)/shard_map/line_w3/ppermute | solution.py:24
  81.6 2.6 %collective-permute-start.17 = (bf16[1,256,768]{2,1,0:T(8,128)(2,1)S(1)}, bf16[1,256,768]{2,1,0:T(8,128)(2,1)S(1)}, u32[]{:S(2)}, u32[]{:S(2)}) collective-permute-start(bf16[1,256,768]{2,1,0:T(8,128)(2,1)S(1)} %get-tuple-element.89.refs_6_.refs_9_), channel_id=1, source_target_pairs={{0,2},{2,0},{4,6},{6,4},{8,10},{10,8},{12,14},{14,12},{16,18},{18,... | collective-permute-start | bytes 1179656 | tf_op jit(solution)/shard_map/core_w3/ppermute | solution.py:24
  81.6 2.6 %collective-permute-start.18 = (bf16[1,256,768]{2,1,0:T(8,128)(2,1)S(1)}, bf16[1,256,768]{2,1,0:T(8,128)(2,1)S(1)}, u32[]{:S(2)}, u32[]{:S(2)}) collective-permute-start(bf16[1,256,768]{2,1,0:T(8,128)(2,1)S(1)} %collective-permute-done.12.refs_7_.refs_10_), channel_id=1, source_target_pairs={{0,2},{2,0},{4,6},{6,4},{8,10},{10,8},{12,14},{14,12},{16,18},{18,... | collective-permute-start | bytes 1179656 | tf_op jit(solution)/shard_map/core_w3_line/ppermute | solution.py:24
  82.1 8.6 %collective-permute-start.15 = (bf16[4,136,256]{2,1,0:T(8,128)(2,1)S(1)}, bf16[4,136,256]{2,1,0:T(8,128)(2,1)S(1)}, u32[]{:S(2)}, u32[]{:S(2)}) collective-permute-start(bf16[4,136,256]{2,1,0:T(8,128)(2,1)S(1)} %half.2), channel_id=1, source_target_pairs={{0,1},{1,0},{2,3},{3,2},{4,5},{5,4},{6,7},{7,6},{8,9},{9,8},{10,11... | collective-permute-start | bytes 835592 | tf_op jit(solution)/shard_map/side_last/ppermute | solution.py:24
  82.6 8.4 %collective-permute-start.16 = (bf16[4,136,256]{2,1,0:T(8,128)(2,1)S(1)}, bf16[4,136,256]{2,1,0:T(8,128)(2,1)S(1)}, u32[]{:S(2)}, u32[]{:S(2)}) collective-permute-start(bf16[4,136,256]{2,1,0:T(8,128)(2,1)S(1)} %half.3), channel_id=1, source_target_pairs={{0,8},{2,10},{4,12},{6,14},{8,0},{10,2},{12,4},{14,6},{16,24},{18,... | collective-permute-start | bytes 835592 | tf_op jit(solution)/shard_map/x_last_side_1/ppermute | solution.py:24
  86.6 10.9 %collective-permute-start.19 = (bf16[3,192,256]{2,1,0:T(8,128)(2,1)S(1)}, bf16[3,192,256]{2,1,0:T(8,128)(2,1)S(1)}, u32[]{:S(2)}, u32[]{:S(2)}) collective-permute-start(bf16[3,192,256]{2,1,0:T(8,128)(2,1)S(1)} %keys_values.3.refs_4_), channel_id=1, source_target_pairs={{0,4},{2,6},{4,0},{6,2},{8,12},{10,14},{12,8},{14,10},{16,20},{18,... | collective-permute-start | bytes 884744 | tf_op jit(solution)/shard_map/kv_line/ppermute | solution.py:24
  92.4 5.1 %collective-permute-start.20 = (bf16[1,192,256]{2,1,0:T(8,128)(2,1)S(1)}, bf16[1,192,256]{2,1,0:T(8,128)(2,1)S(1)}, u32[]{:S(2)}, u32[]{:S(2)}) collective-permute-start(bf16[1,192,256]{2,1,0:T(8,128)(2,1)S(1)} %keys_values.2.refs_8_), channel_id=1, source_target_pairs={{0,4},{2,6},{4,0},{6,2},{8,12},{10,14},{12,8},{14,10},{16,20},{18,... | collective-permute-start | bytes 294920 | tf_op jit(solution)/shard_map/kv_line/ppermute | solution.py:24
  93.9 6.5 %collective-permute-start.21 = (bf16[3,192,256]{2,1,0:T(8,128)(2,1)S(1)}, bf16[3,192,256]{2,1,0:T(8,128)(2,1)S(1)}, u32[]{:S(2)}, u32[]{:S(2)}) collective-permute-start(bf16[3,192,256]{2,1,0:T(8,128)(2,1)S(1)} %keys_values.3.refs_4_), channel_id=1, source_target_pairs={{0,2},{2,0},{4,6},{6,4},{8,10},{10,8},{12,14},{14,12},{16,18},{18,... | collective-permute-start | bytes 884744 | tf_op jit(solution)/shard_map/core_kv/ppermute | solution.py:24
  97.5 2.9 %collective-permute-start.22 = (bf16[3,192,256]{2,1,0:T(8,128)(2,1)S(1)}, bf16[3,192,256]{2,1,0:T(8,128)(2,1)S(1)}, u32[]{:S(2)}, u32[]{:S(2)}) collective-permute-start(bf16[3,192,256]{2,1,0:T(8,128)(2,1)S(1)} %collective-permute-done.19.refs_5_), channel_id=1, source_target_pairs={{0,2},{2,0},{4,6},{6,4},{8,10},{10,8},{12,14},{14,12},{16,18},{18,... | collective-permute-start | bytes 884744 | tf_op jit(solution)/shard_map/core_kv_line/ppermute | solution.py:24
  97.9 2.5 %collective-permute-start.23 = (bf16[1,192,256]{2,1,0:T(8,128)(2,1)S(1)}, bf16[1,192,256]{2,1,0:T(8,128)(2,1)S(1)}, u32[]{:S(2)}, u32[]{:S(2)}) collective-permute-start(bf16[1,192,256]{2,1,0:T(8,128)(2,1)S(1)} %keys_values.2.refs_8_), channel_id=1, source_target_pairs={{0,2},{2,0},{4,6},{6,4},{8,10},{10,8},{12,14},{14,12},{16,18},{18,... | collective-permute-start | bytes 294920 | tf_op jit(solution)/shard_map/core_kv/ppermute | solution.py:24
  98.0 2.4 %collective-permute-start.24 = (bf16[1,192,256]{2,1,0:T(8,128)(2,1)S(1)}, bf16[1,192,256]{2,1,0:T(8,128)(2,1)S(1)}, u32[]{:S(2)}, u32[]{:S(2)}) collective-permute-start(bf16[1,192,256]{2,1,0:T(8,128)(2,1)S(1)} %collective-permute-done.20.refs_9_), channel_id=1, source_target_pairs={{0,2},{2,0},{4,6},{6,4},{8,10},{10,8},{12,14},{14,12},{16,18},{18,... | collective-permute-start | bytes 294920 | tf_op jit(solution)/shard_map/core_kv_line/ppermute | solution.py:24
  105.9 13.3 %collective-permute-start.25 = (bf16[128,512]{1,0:T(8,128)(2,1)S(1)}, bf16[128,512]{1,0:T(8,128)(2,1)S(1)}, u32[]{:S(2)}, u32[]{:S(2)}) collective-permute-start(bf16[128,512]{1,0:T(8,128)(2,1)S(1)} %attend.4), channel_id=1, source_target_pairs={{0,24},{2,26},{4,28},{6,30},{8,16},{10,18},{12,20},{14,22},{16,8},... | collective-permute-start | bytes 393224 | tf_op jit(solution)/shard_map/mixed_3/ppermute | solution.py:24
  114.8 8.1 %collective-permute-start.26 = (bf16[128,512]{1,0:T(8,128)(2,1)S(1)}, bf16[128,512]{1,0:T(8,128)(2,1)S(1)}, u32[]{:S(2)}, u32[]{:S(2)}) collective-permute-start(bf16[128,512]{1,0:T(8,128)(2,1)S(1)} %attend.6), channel_id=1, source_target_pairs={{0,8},{2,10},{4,12},{6,14},{8,0},{10,2},{12,4},{14,6},{16,24},{18,... | collective-permute-start | bytes 393224 | tf_op jit(solution)/shard_map/mixed_1/ppermute | solution.py:24
  116.5 9.1 %collective-permute-start.27 = (bf16[128,512]{1,0:T(8,128)(2,1)S(1)}, bf16[128,512]{1,0:T(8,128)(2,1)S(1)}, u32[]{:S(2)}, u32[]{:S(2)}) collective-permute-start(bf16[128,512]{1,0:T(8,128)(2,1)S(1)} %attend.5), channel_id=1, source_target_pairs={{0,16},{2,18},{4,20},{6,22},{8,24},{10,26},{12,28},{14,30},{16,0},... | collective-permute-start | bytes 393224 | tf_op jit(solution)/shard_map/mixed_2/ppermute | solution.py:24

commit v8 on v7

--- a/solution.py
+++ b/solution.py
@@ -566,9 +566,9 @@
         )
 
     back = [None] * heads
-    for slots in tuple((k,) for k in reversed(range(heads))):
+    for slots in ((3, 2), (1,), (0,)) if squared else tuple((k,) for k in range(heads)):
         some = [(queries[k // 3], k % 3) if squared else (queries[0], k) for k in slots]
-        if squared and slots != (3,):
+        if squared and slots[0] < 3:
             earlier = back[3:] if slots == (0,) else []
             some = [(after(some[0][0], *mixed, *earlier), some[0][1])]
         mixed = attend(slots, prefix_len, some, q_ids, kv_parts, places, kv_ids, tok)

time: 127 us -> 125 us (0.984)
  waiting for transfers between devices: 63.2 us -> 60.7 us
    ppermute x28, waiting for transfers between devices: 63.2 us -> 60.7 us  [swap(): return lax.ppermute(value, axis, [(i, i ^ mask) for i in range(size)])]
    pallas_call x4 -> x3, Pallas kernels: 17.8 us -> 17.2 us  [attend(): pl.pallas_call(functools.partial(attend_kernel, slots, tok, places), grid...]
  transfers between devices with their start and end apart: 28 -> 28, of which waited for: 11 -> 11; matrix products, arithmetic and copies ran while one was open for 3% -> 3% of each run, Pallas kernels for 18% -> 15%
where the time goes in v8:
time: 125 us; the launch traced here: 124 us
  waiting for transfers between devices  60.7 us (49%)
  Pallas kernels  27.9 us (22%)
  starting transfers between devices  27.8 us (22%)
  other arithmetic  4.76 us (4%)
  local copies, waits for them, and re-layouts  1.85 us (1%)
    ppermute x28, waiting for transfers between devices, swap(): return lax.ppermute(value, axis, [(i, i ^ mask) for i in range(size)])  60.7 us
    ppermute x28, starting transfers between devices, swap(): return lax.ppermute(value, axis, [(i, i ^ mask) for i in range(size)])  27.8 us
    pallas_call x3, Pallas kernels, attend(): pl.pallas_call(functools.partial(attend_kernel, slots, tok, places), grid...  17.2 us
    pallas_call x4, Pallas kernels, project(): pl.pallas_call(functools.partial(project_kernel, kv, tiles, first_slot, t...  9.17 us
  transfers between devices with their start and end apart: 28, of which 11 were waited for; matrix products, arithmetic and copies ran while one was open for 3% of the time, Pallas kernels for 15%

profile of v8, /device:TPU:0, one launch (start us, length us, event | category | flops | bytes accessed | tf_op | source)
XLA Modules:
  0.0 124.1 jit_solution(855227915501213284)
XLA Ops:
  0.0 1.5 %constant_dynamic-slice_fusion = (bf16[256,768]{1,0:T(8,128)(2,1)S(1)}, bf16[256,768]{1,0:T(8,128)(2,1)S(1)}, bf16[256,768]{1,0:T(8,128)(2,1)S(1)}, bf16[256,768]{1,0:T(8,128)(2,1)S(1)}) fusion(bf16[256,3072]{1,0:T(8,128)(2,1)} %param.9, s32[]{:T(128)S(6)} %select_n.55, s32[]{:T(128)S(6)} %select_n.53, s32[]{:T(128)S(6)} %select_n.52, s32[]{:T(128)S(6)} %select_n.54), kind=kLoop, calls=%fused_computation.50 | loop fusion | bytes 3145744 | tf_op jit(solution)/shard_map/dynamic_slice | solution.py:419
  1.5 0.0 copy-start.4
  1.6 0.2 squares.1.refs_0_
  1.8 3.0 %collective-permute-start = (f32[136,128]{1,0:T(8,128)S(1)}, f32[136,128]{1,0:T(8,128)S(1)}, u32[]{:S(2)}, u32[]{:S(2)}) collective-permute-start(f32[136,128]{1,0:T(8,128)S(1)} %squares.1.refs_0_), channel_id=1, source_target_pairs={{0,1},{1,0},{2,3},{3,2},{4,5},{5,4},{6,7},{7,6},{8,9},{9,8},{10,11... | collective-permute-start | bytes 208904 | tf_op jit(solution)/shard_map/side_sums/ppermute | solution.py:24
  4.8 1.5 %collective-permute-start.1 = (bf16[1,256,768]{2,1,0:T(8,128)(2,1)S(1)}, bf16[1,256,768]{2,1,0:T(8,128)(2,1)S(1)}, u32[]{:S(2)}, u32[]{:S(2)}) collective-permute-start(bf16[1,256,768]{2,1,0:T(8,128)(2,1)S(1)} %bitcast.54), channel_id=1, source_target_pairs={{0,4},{2,6},{4,0},{6,2},{8,12},{10,14},{12,8},{14,10},{16,20},{18,... | collective-permute-start | bytes 1179656 | tf_op jit(solution)/shard_map/line_w0/ppermute | solution.py:24
  6.3 1.0 fusion.7
  7.3 1.6 %collective-permute-start.6 = (bf16[288,768]{1,0:T(8,128)(2,1)}, bf16[288,768]{1,0:T(8,128)(2,1)S(1)}, u32[]{:S(2)}, u32[]{:S(2)}) collective-permute-start(bf16[288,768]{1,0:T(8,128)(2,1)} %get-tuple-element.136), channel_id=1, source_target_pairs={{0,8},{2,10},{4,12},{6,14},{8,0},{10,2},{12,4},{14,6},{16,24},{18,... | collective-permute-start | bytes 1327112 | tf_op jit(solution)/shard_map/w_1/ppermute | solution.py:24
  8.9 2.6 %collective-permute-start.5 = (bf16[288,768]{1,0:T(8,128)(2,1)}, bf16[288,768]{1,0:T(8,128)(2,1)S(1)}, u32[]{:S(2)}, u32[]{:S(2)}) collective-permute-start(bf16[288,768]{1,0:T(8,128)(2,1)} %get-tuple-element.137), channel_id=1, source_target_pairs={{0,16},{2,18},{4,20},{6,22},{8,24},{10,26},{12,28},{14,30},{16,0},... | collective-permute-start | bytes 1327112 | tf_op jit(solution)/shard_map/w_2/ppermute | solution.py:24
  12.2 0.1 pad_add_fusion.1.refs_0_
  12.3 0.2 norm.1.refs_2_
  12.5 0.1 broadcast_multiply_fusion.1
  12.6 0.1 iota_add_fusion
  12.7 0.1 add_add_fusion
  12.8 0.8 maximum_maximum_fusion
  13.6 0.3 collective-permute-start.4
  13.9 0.4 collective-permute-start.3
  14.4 0.1 stack.122.refs_2_
  14.5 0.1 stack.117.refs_1_
  14.6 1.4 %fusion.16 = (f32[4,192,64]{2,1,0:T(8,128)S(1)}, f32[4,192,64]{2,1,0:T(8,128)S(1)}, f32[4,192,64]{2,1,0:T(8,128)S(1)}) fusion(f32[64]{0:T(128)S(1)} %multiply_exponential_fusion, f32[4,192]{1,0:T(4,128)S(1)} %add_convert_fusion), kind=kLoop, calls=%fused_computation.32 | loop fusion | flops 98304 | bytes 593152 | tf_op jit(solution)/shard_map/neg | solution.py:451
  16.0 0.3 pad_maximum_fusion.4
  16.3 0.0 collective-permute-done.1.refs_1_
  16.3 0.6 collective-permute-start.2
  16.9 27.7 %collective-permute-done.5.refs_1_ = bf16[288,768]{1,0:T(8,128)(2,1)S(1)} collective-permute-done((bf16[288,768]{1,0:T(8,128)(2,1)}, bf16[288,768]{1,0:T(8,128)(2,1)S(1)}, u32[]{:S(2)}, u32[]{:S(2)}) %collective-permute-start.5) | collective-permute-done | bytes 442400 | tf_op jit(solution)/shard_map/w_2/ppermute | solution.py:24
  44.5 0.1 unpack.3
  44.6 0.6 collective-permute-start.7
  45.2 0.1 unpack.4
  45.3 9.2 %collective-permute-done.4.refs_6_ = bf16[8,136,256]{2,1,0:T(8,128)(2,1)S(1)} collective-permute-done((bf16[8,136,256]{2,1,0:T(8,128)(2,1)S(1)}, bf16[8,136,256]{2,1,0:T(8,128)(2,1)S(1)}, u32[]{:S(2)}, u32[]{:S(2)}) %collective-permute-start.4) | collective-permute-done | bytes 557088 | tf_op jit(solution)/shard_map/x_far_2/ppermute | solution.py:24
  54.5 2.6 %collective-permute-start.11 = (bf16[288,768]{1,0:T(8,128)(2,1)S(1)}, bf16[288,768]{1,0:T(8,128)(2,1)S(1)}, u32[]{:S(2)}, u32[]{:S(2)}) collective-permute-start(bf16[288,768]{1,0:T(8,128)(2,1)S(1)} %copy-done.2), channel_id=1, source_target_pairs={{0,24},{2,26},{4,28},{6,30},{8,16},{10,18},{12,20},{14,22},{16,8},... | collective-permute-start | bytes 1327112 | tf_op jit(solution)/shard_map/w_3/ppermute | solution.py:24
  57.1 0.5 collective-permute-start.13
  57.7 0.5 collective-permute-start.10
  58.2 1.5 %collective-permute-start.9 = (bf16[8,136,256]{2,1,0:T(8,128)(2,1)S(1)}, bf16[8,136,256]{2,1,0:T(8,128)(2,1)S(1)}, u32[]{:S(2)}, u32[]{:S(2)}) collective-permute-start(bf16[8,136,256]{2,1,0:T(8,128)(2,1)S(1)} %collective-permute-done.3.refs_4_), channel_id=1, source_target_pairs={{0,1},{1,0},{2,3},{3,2},{4,5},{5,4},{6,7},{7,6},{8,9},{9,8},{10,11... | collective-permute-start | bytes 1671176 | tf_op jit(solution)/shard_map/side_next/ppermute | solution.py:24
  59.7 6.2 %collective-permute-done.13.refs_3_ = bf16[1,256,768]{2,1,0:T(8,128)(2,1)S(1)} collective-permute-done((bf16[1,256,768]{2,1,0:T(8,128)(2,1)S(1)}, bf16[1,256,768]{2,1,0:T(8,128)(2,1)S(1)}, u32[]{:S(2)}, u32[]{:S(2)}) %collective-permute-start.13) | collective-permute-done | bytes 393248 | tf_op jit(solution)/shard_map/line_w1/ppermute | solution.py:24
  65.9 0.2 join.1.refs_5_.refs_8_
  66.0 0.1 collective-permute-start.14
  66.1 3.4 %collective-permute-done.11.refs_0_ = bf16[288,768]{1,0:T(8,128)(2,1)S(1)} collective-permute-done((bf16[288,768]{1,0:T(8,128)(2,1)S(1)}, bf16[288,768]{1,0:T(8,128)(2,1)S(1)}, u32[]{:S(2)}, u32[]{:S(2)}) %collective-permute-start.11) | collective-permute-done | bytes 442400 | tf_op jit(solution)/shard_map/w_3/ppermute | solution.py:24
  69.6 0.8 unpack.5
  70.4 0.5 collective-permute-start.12
  70.9 2.3 %collective-permute-done.10.value.refs_7_ = bf16[8,136,256]{2,1,0:T(8,128)(2,1)S(1)} collective-permute-done((bf16[8,136,256]{2,1,0:T(8,128)(2,1)S(1)}, bf16[8,136,256]{2,1,0:T(8,128)(2,1)S(1)}, u32[]{:S(2)}, u32[]{:S(2)}) %collective-permute-start.10) | collective-permute-done | bytes 557088 | tf_op jit(solution)/shard_map/side_far/ppermute | solution.py:24
  73.2 5.3 %collective-permute-done.8.value.refs_2_ = bf16[8,136,256]{2,1,0:T(8,128)(2,1)S(1)} collective-permute-done((bf16[8,136,256]{2,1,0:T(8,128)(2,1)S(1)}, bf16[8,136,256]{2,1,0:T(8,128)(2,1)S(1)}, u32[]{:S(2)}, u32[]{:S(2)}) %collective-permute-start.8) | collective-permute-done | bytes 557088 | tf_op jit(solution)/shard_map/x_last_1/ppermute | solution.py:24
  78.6 3.0 %collective-permute-done.9.refs_5_ = bf16[8,136,256]{2,1,0:T(8,128)(2,1)S(1)} collective-permute-done((bf16[8,136,256]{2,1,0:T(8,128)(2,1)S(1)}, bf16[8,136,256]{2,1,0:T(8,128)(2,1)S(1)}, u32[]{:S(2)}, u32[]{:S(2)}) %collective-permute-start.9) | collective-permute-done | bytes 557088 | tf_op jit(solution)/shard_map/side_next/ppermute | solution.py:24
  81.6 0.5 collective-permute-start.18
  82.1 0.5 collective-permute-start.15
  82.6 1.6 %collective-permute-start.16 = (bf16[4,136,256]{2,1,0:T(8,128)(2,1)S(1)}, bf16[4,136,256]{2,1,0:T(8,128)(2,1)S(1)}, u32[]{:S(2)}, u32[]{:S(2)}) collective-permute-start(bf16[4,136,256]{2,1,0:T(8,128)(2,1)S(1)} %half.3), channel_id=1, source_target_pairs={{0,8},{2,10},{4,12},{6,14},{8,0},{10,2},{12,4},{14,6},{16,24},{18,... | collective-permute-start | bytes 835592 | tf_op jit(solution)/shard_map/x_last_side_1/ppermute | solution.py:24
  84.2 2.4 %keys_values.3.refs_5_.refs_4_ = bf16[3,192,256]{2,1,0:T(8,128)(2,1)S(1)} custom-call(s32[16]{0:T(128)S(1)} %pad_add_fusion.1.refs_0_, s32[16]{0:T(128)S(1)} %stack.117.refs_1_, bf16[8,136,256]{2,1,0:T(8,128)(2,1)S(1)} %norm.1.refs_2_, bf16[8,136,256]{2,1,0:T(8,128)(2,1)S(1)} %collective-permute-done.2.refs_3_, ...), custom_call_target="tpu_custom_call" | custom-call | flops 905969664 | bytes 5636096 | tf_op jit(solution)/shard_map/keys_values/pallas_call | solution.py:247
  86.6 1.2 %collective-permute-start.19 = (bf16[3,192,256]{2,1,0:T(8,128)(2,1)S(1)}, bf16[3,192,256]{2,1,0:T(8,128)(2,1)S(1)}, u32[]{:S(2)}, u32[]{:S(2)}) collective-permute-start(bf16[3,192,256]{2,1,0:T(8,128)(2,1)S(1)} %keys_values.3.refs_5_.refs_4_), channel_id=1, source_target_pairs={{0,4},{2,6},{4,0},{6,2},{8,12},{10,14},{12,8},{14,10},{16,20},{18,... | collective-permute-start | bytes 884744 | tf_op jit(solution)/shard_map/kv_line/ppermute | solution.py:24
  87.9 2.9 %collective-permute-done.15.refs_3_ = bf16[4,136,256]{2,1,0:T(8,128)(2,1)S(1)} collective-permute-done((bf16[4,136,256]{2,1,0:T(8,128)(2,1)S(1)}, bf16[4,136,256]{2,1,0:T(8,128)(2,1)S(1)}, u32[]{:S(2)}, u32[]{:S(2)}) %collective-permute-start.15) | collective-permute-done | bytes 278560 | tf_op jit(solution)/shard_map/side_last/ppermute | solution.py:24
  90.7 0.2 collective-permute-done.16.refs_4_
  91.0 1.4 %keys_values.2.refs_9_.refs_8_ = bf16[1,192,256]{2,1,0:T(8,128)(2,1)S(1)} custom-call(s32[16]{0:T(128)S(1)} %pad_add_fusion.1.refs_0_, s32[16]{0:T(128)S(1)} %stack.117.refs_1_, bf16[8,136,256]{2,1,0:T(8,128)(2,1)S(1)} %collective-permute-done.8.value.refs_2_, bf16[4,136,256]{2,1,0:T(8,128)(2,1)S(1)} %collective-permute-done.15.refs_3_, ...), custom_call_target="tpu_custom_call" | custom-call | flops 301989888 | bytes 3276800 | tf_op jit(solution)/shard_map/keys_values/pallas_call | solution.py:247
  92.4 1.6 %collective-permute-start.20 = (bf16[1,192,256]{2,1,0:T(8,128)(2,1)S(1)}, bf16[1,192,256]{2,1,0:T(8,128)(2,1)S(1)}, u32[]{:S(2)}, u32[]{:S(2)}) collective-permute-start(bf16[1,192,256]{2,1,0:T(8,128)(2,1)S(1)} %keys_values.2.refs_9_.refs_8_), channel_id=1, source_target_pairs={{0,4},{2,6},{4,0},{6,2},{8,12},{10,14},{12,8},{14,10},{16,20},{18,... | collective-permute-start | bytes 294920 | tf_op jit(solution)/shard_map/kv_line/ppermute | solution.py:24
  93.9 3.4 %queries.2.refs_4_.refs_3_ = bf16[3,4,128,128]{3,2,1,0:T(8,128)(2,1)S(1)} custom-call(s32[16]{0:T(128)S(1)} %pad_add_fusion.1.refs_0_, s32[16]{0:T(128)S(1)} %stack.117.refs_1_, bf16[8,136,256]{2,1,0:T(8,128)(2,1)S(1)} %norm.1.refs_2_, bf16[8,136,256]{2,1,0:T(8,128)(2,1)S(1)} %collective-permute-done.2.refs_3_, ...), custom_call_target="tpu_custom_call" | custom-call | flops 1811939328 | bytes 7733248 | tf_op jit(solution)/shard_map/queries/pallas_call | solution.py:247
  97.3 0.2 collective-permute-done.20.refs_10_.refs_9_
  97.5 0.4 collective-permute-start.22
  97.9 0.1 collective-permute-start.23
  98.0 0.4 collective-permute-start.24
  98.5 2.0 %queries.3.refs_3_ = bf16[1,4,128,128]{3,2,1,0:T(8,128)(2,1)S(1)} custom-call(s32[16]{0:T(128)S(1)} %pad_add_fusion.1.refs_0_, s32[16]{0:T(128)S(1)} %stack.117.refs_1_, bf16[8,136,256]{2,1,0:T(8,128)(2,1)S(1)} %collective-permute-done.8.value.refs_2_, bf16[4,136,256]{2,1,0:T(8,128)(2,1)S(1)} %collective-permute-done.15.refs_3_, ...), custom_call_target="tpu_custom_call" | custom-call | flops 603979776 | bytes 5373952 | tf_op jit(solution)/shard_map/queries/pallas_call | solution.py:247
  100.5 9.5 %attend.3 = (bf16[128,512]{1,0:T(8,128)(2,1)S(1)}, bf16[128,512]{1,0:T(8,128)(2,1)S(1)}) custom-call(s32[1]{0:T(128)} %copy.8.refs_0_, s32[4]{0:T(128)S(1)} %get-tuple-element.73.refs_1_, s32[16]{0:T(128)S(1)} %stack.122.refs_2_, bf16[1,4,128,128]{3,2,1,0:T(8,128)(2,1)S(1)} %queries.3.refs_3_, bf16[3,4,128,128]{3,2,1,0:T(8,128)(2,1)S(1)} %queries.2.refs_4_.refs_3_, ...), custom_call_target="tpu_custom_call" | custom-call | flops 1610612736 | bytes 1572864 | tf_op jit(solution)/shard_map/attend/pallas_call | solution.py:382
  110.0 0.1 collective-permute-start.25
  110.1 4.0 %attend.4 = bf16[128,512]{1,0:T(8,128)(2,1)S(1)} custom-call(s32[1]{0:T(128)} %copy.8.refs_0_, s32[4]{0:T(128)S(1)} %get-tuple-element.73.refs_1_, s32[16]{0:T(128)S(1)} %stack.122.refs_2_, bf16[3,4,128,128]{3,2,1,0:T(8,128)(2,1)S(1)} %queries.2.refs_4_.refs_3_, bf16[3,192,256]{2,1,0:T(8,128)(2,1)S(1)} %keys_values.3.refs_5_.refs_4_, ...), custom_call_target="tpu_custom_call" | custom-call | flops 805306368 | bytes 1572864 | tf_op jit(solution)/shard_map/attend/pallas_call | solution.py:382
  114.1 0.6 collective-permute-start.26
  114.7 4.5 %collective-permute-start.27 = (bf16[128,512]{1,0:T(8,128)(2,1)S(1)}, bf16[128,512]{1,0:T(8,128)(2,1)S(1)}, u32[]{:S(2)}, u32[]{:S(2)}) collective-permute-start(bf16[128,512]{1,0:T(8,128)(2,1)S(1)} %get-tuple-element.110), channel_id=1, source_target_pairs={{0,16},{2,18},{4,20},{6,22},{8,24},{10,26},{12,28},{14,30},{16,0},... | collective-permute-start | bytes 393224 | tf_op jit(solution)/shard_map/mixed_2/ppermute | solution.py:24
  119.2 3.6 %attend.5 = bf16[128,512]{1,0:T(8,128)(2,1)S(1)} custom-call(s32[1]{0:T(128)} %copy.8.refs_0_, s32[4]{0:T(128)S(1)} %get-tuple-element.73.refs_1_, s32[16]{0:T(128)S(1)} %stack.122.refs_2_, bf16[3,4,128,128]{3,2,1,0:T(8,128)(2,1)S(1)} %queries.2.refs_4_.refs_3_, bf16[3,192,256]{2,1,0:T(8,128)(2,1)S(1)} %keys_values.3.refs_5_.refs_4_, ...), custom_call_target="tpu_custom_call" | custom-call | flops 805306368 | bytes 1572864 | tf_op jit(solution)/shard_map/attend/pallas_call | solution.py:382
  122.8 0.2 collective-permute-done.26
  123.1 0.1 pad_maximum_fusion.2
  123.2 0.8 pad_maximum_fusion.3
  (44 shorter events, 0.3 us)
Async XLA Ops:
  0.0 1.6 %copy-start = (bf16[128,2048]{1,0:T(8,128)(2,1)S(1)}, bf16[128,2048]{1,0:T(8,128)(2,1)}, u32[]{:S(2)}) copy-start(bf16[128,2048]{1,0:T(8,128)(2,1)} %stream.1) | copy-start | bytes 1572868
  0.0 1.6 %copy-start.1 = (bf16[8,2048]{1,0:T(8,128)(2,1)S(1)}, bf16[8,2048]{1,0:T(8,128)(2,1)}, u32[]{:S(2)}) copy-start(bf16[8,2048]{1,0:T(8,128)(2,1)} %hidden.3) | copy-start | bytes 98308
  0.0 6.3 %copy-start.5 = (s32[8]{0:T(128)S(1)}, s32[8]{0:T(128)}, u32[]{:S(2)}) copy-start(s32[8]{0:T(128)} %param.12) | copy-start | bytes 100
  0.0 6.3 %copy-start.3 = (bf16[2,64,512]{2,1,0:T(8,128)(2,1)S(1)}, bf16[2,64,512]{2,1,0:T(8,128)(2,1)}, u32[]{:S(2)}) copy-start(bf16[2,64,512]{2,1,0:T(8,128)(2,1)} %param.10) | copy-start | bytes 393220
  1.5 10.6 %copy-start.4 = (f32[4096]{0:T(1024)S(1)}, f32[4096]{0:T(1024)}, u32[]{:S(2)}) copy-start(f32[4096]{0:T(1024)} %param.8) | copy-start | bytes 49156
  1.8 10.5 %collective-permute-start = (f32[136,128]{1,0:T(8,128)S(1)}, f32[136,128]{1,0:T(8,128)S(1)}, u32[]{:S(2)}, u32[]{:S(2)}) collective-permute-start(f32[136,128]{1,0:T(8,128)S(1)} %squares.1.refs_0_), channel_id=1, source_target_pairs={{0,1},{1,0},{2,3},{3,2},{4,5},{5,4},{6,7},{7,6},{8,9},{9,8},{10,11... | collective-permute-start | bytes 208904 | tf_op jit(solution)/shard_map/side_sums/ppermute | solution.py:24
  4.8 11.5 %collective-permute-start.1 = (bf16[1,256,768]{2,1,0:T(8,128)(2,1)S(1)}, bf16[1,256,768]{2,1,0:T(8,128)(2,1)S(1)}, u32[]{:S(2)}, u32[]{:S(2)}) collective-permute-start(bf16[1,256,768]{2,1,0:T(8,128)(2,1)S(1)} %bitcast.54), channel_id=1, source_target_pairs={{0,4},{2,6},{4,0},{6,2},{8,12},{10,14},{12,8},{14,10},{16,20},{18,... | collective-permute-start | bytes 1179656 | tf_op jit(solution)/shard_map/line_w0/ppermute | solution.py:24
  7.3 37.9 %collective-permute-start.6 = (bf16[288,768]{1,0:T(8,128)(2,1)}, bf16[288,768]{1,0:T(8,128)(2,1)S(1)}, u32[]{:S(2)}, u32[]{:S(2)}) collective-permute-start(bf16[288,768]{1,0:T(8,128)(2,1)} %get-tuple-element.136), channel_id=1, source_target_pairs={{0,8},{2,10},{4,12},{6,14},{8,0},{10,2},{12,4},{14,6},{16,24},{18,... | collective-permute-start | bytes 1327112 | tf_op jit(solution)/shard_map/w_1/ppermute | solution.py:24
  8.9 35.6 %collective-permute-start.5 = (bf16[288,768]{1,0:T(8,128)(2,1)}, bf16[288,768]{1,0:T(8,128)(2,1)S(1)}, u32[]{:S(2)}, u32[]{:S(2)}) collective-permute-start(bf16[288,768]{1,0:T(8,128)(2,1)} %get-tuple-element.137), channel_id=1, source_target_pairs={{0,16},{2,18},{4,20},{6,22},{8,24},{10,26},{12,28},{14,30},{16,0},... | collective-permute-start | bytes 1327112 | tf_op jit(solution)/shard_map/w_2/ppermute | solution.py:24
  13.6 40.9 %collective-permute-start.4 = (bf16[8,136,256]{2,1,0:T(8,128)(2,1)S(1)}, bf16[8,136,256]{2,1,0:T(8,128)(2,1)S(1)}, u32[]{:S(2)}, u32[]{:S(2)}) collective-permute-start(bf16[8,136,256]{2,1,0:T(8,128)(2,1)S(1)} %norm.1.refs_2_), channel_id=1, source_target_pairs={{0,16},{2,18},{4,20},{6,22},{8,24},{10,26},{12,28},{14,30},{16,0},... | collective-permute-start | bytes 1671176 | tf_op jit(solution)/shard_map/x_far_2/ppermute | solution.py:24
  13.9 40.6 %collective-permute-start.3 = (bf16[8,136,256]{2,1,0:T(8,128)(2,1)S(1)}, bf16[8,136,256]{2,1,0:T(8,128)(2,1)S(1)}, u32[]{:S(2)}, u32[]{:S(2)}) collective-permute-start(bf16[8,136,256]{2,1,0:T(8,128)(2,1)S(1)} %norm.1.refs_2_), channel_id=1, source_target_pairs={{0,8},{2,10},{4,12},{6,14},{8,0},{10,2},{12,4},{14,6},{16,24},{18,... | collective-permute-start | bytes 1671176 | tf_op jit(solution)/shard_map/x_next_1/ppermute | solution.py:24
  16.3 38.2 %collective-permute-start.2 = (bf16[8,136,256]{2,1,0:T(8,128)(2,1)S(1)}, bf16[8,136,256]{2,1,0:T(8,128)(2,1)S(1)}, u32[]{:S(2)}, u32[]{:S(2)}) collective-permute-start(bf16[8,136,256]{2,1,0:T(8,128)(2,1)S(1)} %norm.1.refs_2_), channel_id=1, source_target_pairs={{0,1},{1,0},{2,3},{3,2},{4,5},{5,4},{6,7},{7,6},{8,9},{9,8},{10,11... | collective-permute-start | bytes 1671176 | tf_op jit(solution)/shard_map/side_own/ppermute | solution.py:24
  44.6 9.9 %collective-permute-start.7 = (bf16[1,256,768]{2,1,0:T(8,128)(2,1)S(1)}, bf16[1,256,768]{2,1,0:T(8,128)(2,1)S(1)}, u32[]{:S(2)}, u32[]{:S(2)}) collective-permute-start(bf16[1,256,768]{2,1,0:T(8,128)(2,1)S(1)} %get-tuple-element.71), channel_id=1, source_target_pairs={{0,4},{2,6},{4,0},{6,2},{8,12},{10,14},{12,8},{14,10},{16,20},{18,... | collective-permute-start | bytes 1179656 | tf_op jit(solution)/shard_map/line_w2/ppermute | solution.py:24
  45.2 9.3 %copy-start.2 = (bf16[288,768]{1,0:T(8,128)(2,1)S(1)}, bf16[288,768]{1,0:T(8,128)(2,1)}, u32[]{:S(2)}) copy-start(bf16[288,768]{1,0:T(8,128)(2,1)} %maximum_maximum_fusion) | copy-start | bytes 1327108
  54.5 15.0 %collective-permute-start.11 = (bf16[288,768]{1,0:T(8,128)(2,1)S(1)}, bf16[288,768]{1,0:T(8,128)(2,1)S(1)}, u32[]{:S(2)}, u32[]{:S(2)}) collective-permute-start(bf16[288,768]{1,0:T(8,128)(2,1)S(1)} %copy-done.2), channel_id=1, source_target_pairs={{0,24},{2,26},{4,28},{6,30},{8,16},{10,18},{12,20},{14,22},{16,8},... | collective-permute-start | bytes 1327112 | tf_op jit(solution)/shard_map/w_3/ppermute | solution.py:24
  57.1 8.8 %collective-permute-start.13 = (bf16[1,256,768]{2,1,0:T(8,128)(2,1)S(1)}, bf16[1,256,768]{2,1,0:T(8,128)(2,1)S(1)}, u32[]{:S(2)}, u32[]{:S(2)}) collective-permute-start(bf16[1,256,768]{2,1,0:T(8,128)(2,1)S(1)} %get-tuple-element.85), channel_id=1, source_target_pairs={{0,4},{2,6},{4,0},{6,2},{8,12},{10,14},{12,8},{14,10},{16,20},{18,... | collective-permute-start | bytes 1179656 | tf_op jit(solution)/shard_map/line_w1/ppermute | solution.py:24
  57.7 15.6 %collective-permute-start.10 = (bf16[8,136,256]{2,1,0:T(8,128)(2,1)S(1)}, bf16[8,136,256]{2,1,0:T(8,128)(2,1)S(1)}, u32[]{:S(2)}, u32[]{:S(2)}) collective-permute-start(bf16[8,136,256]{2,1,0:T(8,128)(2,1)S(1)} %collective-permute-done.4.refs_6_), channel_id=1, source_target_pairs={{0,1},{1,0},{2,3},{3,2},{4,5},{5,4},{6,7},{7,6},{8,9},{9,8},{10,11... | collective-permute-start | bytes 1671176 | tf_op jit(solution)/shard_map/side_far/ppermute | solution.py:24
  58.2 20.4 %collective-permute-start.8 = (bf16[8,136,256]{2,1,0:T(8,128)(2,1)S(1)}, bf16[8,136,256]{2,1,0:T(8,128)(2,1)S(1)}, u32[]{:S(2)}, u32[]{:S(2)}) collective-permute-start(bf16[8,136,256]{2,1,0:T(8,128)(2,1)S(1)} %collective-permute-done.4.refs_6_), channel_id=1, source_target_pairs={{0,8},{2,10},{4,12},{6,14},{8,0},{10,2},{12,4},{14,6},{16,24},{18,... | collective-permute-start | bytes 1671176 | tf_op jit(solution)/shard_map/x_last_1/ppermute | solution.py:24
  58.2 23.4 %collective-permute-start.9 = (bf16[8,136,256]{2,1,0:T(8,128)(2,1)S(1)}, bf16[8,136,256]{2,1,0:T(8,128)(2,1)S(1)}, u32[]{:S(2)}, u32[]{:S(2)}) collective-permute-start(bf16[8,136,256]{2,1,0:T(8,128)(2,1)S(1)} %collective-permute-done.3.refs_4_), channel_id=1, source_target_pairs={{0,1},{1,0},{2,3},{3,2},{4,5},{5,4},{6,7},{7,6},{8,9},{9,8},{10,11... | collective-permute-start | bytes 1671176 | tf_op jit(solution)/shard_map/side_next/ppermute | solution.py:24
  66.0 15.6 %collective-permute-start.14 = (bf16[6,256,768]{2,1,0:T(8,128)(2,1)S(1)}, bf16[6,256,768]{2,1,0:T(8,128)(2,1)S(1)}, u32[]{:S(2)}, u32[]{:S(2)}) collective-permute-start(bf16[6,256,768]{2,1,0:T(8,128)(2,1)S(1)} %join.1.refs_5_.refs_8_), channel_id=1, source_target_pairs={{0,2},{2,0},{4,6},{6,4},{8,10},{10,8},{12,14},{14,12},{16,18},{18,... | collective-permute-start | bytes 7077896 | tf_op jit(solution)/shard_map/core_w/ppermute | solution.py:24
  70.4 11.2 %collective-permute-start.12 = (bf16[1,256,768]{2,1,0:T(8,128)(2,1)S(1)}, bf16[1,256,768]{2,1,0:T(8,128)(2,1)S(1)}, u32[]{:S(2)}, u32[]{:S(2)}) collective-permute-start(bf16[1,256,768]{2,1,0:T(8,128)(2,1)S(1)} %get-tuple-element.90.refs_6_.refs_9_), channel_id=1, source_target_pairs={{0,4},{2,6},{4,0},{6,2},{8,12},{10,14},{12,8},{14,10},{16,20},{18,... | collective-permute-start | bytes 1179656 | tf_op jit(solution)/shard_map/line_w3/ppermute | solution.py:24
  81.6 2.6 %collective-permute-start.17 = (bf16[1,256,768]{2,1,0:T(8,128)(2,1)S(1)}, bf16[1,256,768]{2,1,0:T(8,128)(2,1)S(1)}, u32[]{:S(2)}, u32[]{:S(2)}) collective-permute-start(bf16[1,256,768]{2,1,0:T(8,128)(2,1)S(1)} %get-tuple-element.90.refs_6_.refs_9_), channel_id=1, source_target_pairs={{0,2},{2,0},{4,6},{6,4},{8,10},{10,8},{12,14},{14,12},{16,18},{18,... | collective-permute-start | bytes 1179656 | tf_op jit(solution)/shard_map/core_w3/ppermute | solution.py:24
  81.6 2.6 %collective-permute-start.18 = (bf16[1,256,768]{2,1,0:T(8,128)(2,1)S(1)}, bf16[1,256,768]{2,1,0:T(8,128)(2,1)S(1)}, u32[]{:S(2)}, u32[]{:S(2)}) collective-permute-start(bf16[1,256,768]{2,1,0:T(8,128)(2,1)S(1)} %collective-permute-done.12.refs_7_.refs_10_), channel_id=1, source_target_pairs={{0,2},{2,0},{4,6},{6,4},{8,10},{10,8},{12,14},{14,12},{16,18},{18,... | collective-permute-start | bytes 1179656 | tf_op jit(solution)/shard_map/core_w3_line/ppermute | solution.py:24
  82.1 8.6 %collective-permute-start.15 = (bf16[4,136,256]{2,1,0:T(8,128)(2,1)S(1)}, bf16[4,136,256]{2,1,0:T(8,128)(2,1)S(1)}, u32[]{:S(2)}, u32[]{:S(2)}) collective-permute-start(bf16[4,136,256]{2,1,0:T(8,128)(2,1)S(1)} %half.2), channel_id=1, source_target_pairs={{0,1},{1,0},{2,3},{3,2},{4,5},{5,4},{6,7},{7,6},{8,9},{9,8},{10,11... | collective-permute-start | bytes 835592 | tf_op jit(solution)/shard_map/side_last/ppermute | solution.py:24
  82.6 8.4 %collective-permute-start.16 = (bf16[4,136,256]{2,1,0:T(8,128)(2,1)S(1)}, bf16[4,136,256]{2,1,0:T(8,128)(2,1)S(1)}, u32[]{:S(2)}, u32[]{:S(2)}) collective-permute-start(bf16[4,136,256]{2,1,0:T(8,128)(2,1)S(1)} %half.3), channel_id=1, source_target_pairs={{0,8},{2,10},{4,12},{6,14},{8,0},{10,2},{12,4},{14,6},{16,24},{18,... | collective-permute-start | bytes 835592 | tf_op jit(solution)/shard_map/x_last_side_1/ppermute | solution.py:24
  86.6 10.9 %collective-permute-start.19 = (bf16[3,192,256]{2,1,0:T(8,128)(2,1)S(1)}, bf16[3,192,256]{2,1,0:T(8,128)(2,1)S(1)}, u32[]{:S(2)}, u32[]{:S(2)}) collective-permute-start(bf16[3,192,256]{2,1,0:T(8,128)(2,1)S(1)} %keys_values.3.refs_5_.refs_4_), channel_id=1, source_target_pairs={{0,4},{2,6},{4,0},{6,2},{8,12},{10,14},{12,8},{14,10},{16,20},{18,... | collective-permute-start | bytes 884744 | tf_op jit(solution)/shard_map/kv_line/ppermute | solution.py:24
  92.4 5.1 %collective-permute-start.20 = (bf16[1,192,256]{2,1,0:T(8,128)(2,1)S(1)}, bf16[1,192,256]{2,1,0:T(8,128)(2,1)S(1)}, u32[]{:S(2)}, u32[]{:S(2)}) collective-permute-start(bf16[1,192,256]{2,1,0:T(8,128)(2,1)S(1)} %keys_values.2.refs_9_.refs_8_), channel_id=1, source_target_pairs={{0,4},{2,6},{4,0},{6,2},{8,12},{10,14},{12,8},{14,10},{16,20},{18,... | collective-permute-start | bytes 294920 | tf_op jit(solution)/shard_map/kv_line/ppermute | solution.py:24
  93.9 6.5 %collective-permute-start.21 = (bf16[3,192,256]{2,1,0:T(8,128)(2,1)S(1)}, bf16[3,192,256]{2,1,0:T(8,128)(2,1)S(1)}, u32[]{:S(2)}, u32[]{:S(2)}) collective-permute-start(bf16[3,192,256]{2,1,0:T(8,128)(2,1)S(1)} %keys_values.3.refs_5_.refs_4_), channel_id=1, source_target_pairs={{0,2},{2,0},{4,6},{6,4},{8,10},{10,8},{12,14},{14,12},{16,18},{18,... | collective-permute-start | bytes 884744 | tf_op jit(solution)/shard_map/core_kv/ppermute | solution.py:24
  97.5 2.9 %collective-permute-start.22 = (bf16[3,192,256]{2,1,0:T(8,128)(2,1)S(1)}, bf16[3,192,256]{2,1,0:T(8,128)(2,1)S(1)}, u32[]{:S(2)}, u32[]{:S(2)}) collective-permute-start(bf16[3,192,256]{2,1,0:T(8,128)(2,1)S(1)} %collective-permute-done.19.refs_6_.refs_5_), channel_id=1, source_target_pairs={{0,2},{2,0},{4,6},{6,4},{8,10},{10,8},{12,14},{14,12},{16,18},{18,... | collective-permute-start | bytes 884744 | tf_op jit(solution)/shard_map/core_kv_line/ppermute | solution.py:24
  97.9 2.5 %collective-permute-start.23 = (bf16[1,192,256]{2,1,0:T(8,128)(2,1)S(1)}, bf16[1,192,256]{2,1,0:T(8,128)(2,1)S(1)}, u32[]{:S(2)}, u32[]{:S(2)}) collective-permute-start(bf16[1,192,256]{2,1,0:T(8,128)(2,1)S(1)} %keys_values.2.refs_9_.refs_8_), channel_id=1, source_target_pairs={{0,2},{2,0},{4,6},{6,4},{8,10},{10,8},{12,14},{14,12},{16,18},{18,... | collective-permute-start | bytes 294920 | tf_op jit(solution)/shard_map/core_kv/ppermute | solution.py:24
  98.0 2.4 %collective-permute-start.24 = (bf16[1,192,256]{2,1,0:T(8,128)(2,1)S(1)}, bf16[1,192,256]{2,1,0:T(8,128)(2,1)S(1)}, u32[]{:S(2)}, u32[]{:S(2)}) collective-permute-start(bf16[1,192,256]{2,1,0:T(8,128)(2,1)S(1)} %collective-permute-done.20.refs_10_.refs_9_), channel_id=1, source_target_pairs={{0,2},{2,0},{4,6},{6,4},{8,10},{10,8},{12,14},{14,12},{16,18},{18,... | collective-permute-start | bytes 294920 | tf_op jit(solution)/shard_map/core_kv_line/ppermute | solution.py:24
  110.0 9.2 %collective-permute-start.25 = (bf16[128,512]{1,0:T(8,128)(2,1)S(1)}, bf16[128,512]{1,0:T(8,128)(2,1)S(1)}, u32[]{:S(2)}, u32[]{:S(2)}) collective-permute-start(bf16[128,512]{1,0:T(8,128)(2,1)S(1)} %get-tuple-element.109), channel_id=1, source_target_pairs={{0,24},{2,26},{4,28},{6,30},{8,16},{10,18},{12,20},{14,22},{16,8},... | collective-permute-start | bytes 393224 | tf_op jit(solution)/shard_map/mixed_3/ppermute | solution.py:24
  114.1 9.0 %collective-permute-start.26 = (bf16[128,512]{1,0:T(8,128)(2,1)S(1)}, bf16[128,512]{1,0:T(8,128)(2,1)S(1)}, u32[]{:S(2)}, u32[]{:S(2)}) collective-permute-start(bf16[128,512]{1,0:T(8,128)(2,1)S(1)} %attend.4), channel_id=1, source_target_pairs={{0,8},{2,10},{4,12},{6,14},{8,0},{10,2},{12,4},{14,6},{16,24},{18,... | collective-permute-start | bytes 393224 | tf_op jit(solution)/shard_map/mixed_1/ppermute | solution.py:24
  114.7 8.4 %collective-permute-start.27 = (bf16[128,512]{1,0:T(8,128)(2,1)S(1)}, bf16[128,512]{1,0:T(8,128)(2,1)S(1)}, u32[]{:S(2)}, u32[]{:S(2)}) collective-permute-start(bf16[128,512]{1,0:T(8,128)(2,1)S(1)} %get-tuple-element.110), channel_id=1, source_target_pairs={{0,16},{2,18},{4,20},{6,22},{8,24},{10,26},{12,28},{14,30},{16,0},... | collective-permute-start | bytes 393224 | tf_op jit(solution)/shard_map/mixed_2/ppermute | solution.py:24

commit v9 on v8

--- a/solution.py
+++ b/solution.py
@@ -539,11 +539,14 @@
         return project(kv, q, slots[0], chunks, x_ids, w_parts, w_ids, cosine, sine, some, tok, redo)
 
     if squared:
-        kv_new = [*projected(True, False, (0, 1, 2)), *projected(True, False, (3,))]
-        for chunk in x_chunks:
-            chunk[0] = after(chunk[0], kv_new[1])
-        queries = [*projected(False, True, (0, 1, 2)), *projected(False, True, (3,))]
-        first_queries = queries[0]
+        kv_new = projected(True, False, (0, 1, 2))
+        x_chunks[0][0] = after(own, kv_new[0])
+        queries = projected(False, True, (0, 1, 2))
+        x_chunks[3][0] = after(last, queries[0])
+        kv_new = [*kv_new, *projected(True, False, (3,))]
+        x_chunks[3][0] = after(x_chunks[3][0], kv_new[1])
+        queries = [*queries, *projected(False, True, (3,))]
+        first_queries = queries[1]
         queries = list(lax.optimization_barrier(tuple(queries)))
     else:
         kv_new, queries = [[value] for value in projected(True, True, tuple(range(heads)))]

time: 125 us -> 123 us (0.984)
  no operation moved by 1% of the time
where the time goes in v9:
time: 123 us
  waiting for transfers between devices  60.4 us (49%)
  Pallas kernels  28.1 us (23%)
  starting transfers between devices  27.1 us (22%)
  other arithmetic  4.76 us (4%)
  local copies, waits for them, and re-layouts  1.85 us (2%)
    ppermute x28, waiting for transfers between devices, swap(): return lax.ppermute(value, axis, [(i, i ^ mask) for i in range(size)])  60.4 us
    ppermute x28, starting transfers between devices, swap(): return lax.ppermute(value, axis, [(i, i ^ mask) for i in range(size)])  27.1 us
    pallas_call x3, Pallas kernels, attend(): pl.pallas_call(functools.partial(attend_kernel, slots, tok, places), grid...  17.3 us
    pallas_call x4, Pallas kernels, project(): pl.pallas_call(functools.partial(project_kernel, kv, tiles, first_slot, t...  9.17 us
  transfers between devices with their start and end apart: 28, of which 11 were waited for; matrix products, arithmetic and copies ran while one was open for 3% of the time, Pallas kernels for 15%

profile of v9, /device:TPU:0, one launch (start us, length us, event | category | flops | bytes accessed | tf_op | source)
XLA Modules:
  0.0 123.1 jit_solution(8288871873466282506)
XLA Ops:
  0.0 1.5 %constant_dynamic-slice_fusion = (bf16[256,768]{1,0:T(8,128)(2,1)S(1)}, bf16[256,768]{1,0:T(8,128)(2,1)S(1)}, bf16[256,768]{1,0:T(8,128)(2,1)S(1)}, bf16[256,768]{1,0:T(8,128)(2,1)S(1)}) fusion(bf16[256,3072]{1,0:T(8,128)(2,1)} %param.9, s32[]{:T(128)S(6)} %select_n.55, s32[]{:T(128)S(6)} %select_n.53, s32[]{:T(128)S(6)} %select_n.52, s32[]{:T(128)S(6)} %select_n.54), kind=kLoop, calls=%fused_computation.50 | loop fusion | bytes 3145744 | tf_op jit(solution)/shard_map/dynamic_slice | solution.py:419
  1.5 0.0 copy-start.4
  1.6 0.2 squares.1.refs_0_
  1.8 3.0 %collective-permute-start = (f32[136,128]{1,0:T(8,128)S(1)}, f32[136,128]{1,0:T(8,128)S(1)}, u32[]{:S(2)}, u32[]{:S(2)}) collective-permute-start(f32[136,128]{1,0:T(8,128)S(1)} %squares.1.refs_0_), channel_id=1, source_target_pairs={{0,1},{1,0},{2,3},{3,2},{4,5},{5,4},{6,7},{7,6},{8,9},{9,8},{10,11... | collective-permute-start | bytes 208904 | tf_op jit(solution)/shard_map/side_sums/ppermute | solution.py:24
  4.8 1.5 %collective-permute-start.1 = (bf16[1,256,768]{2,1,0:T(8,128)(2,1)S(1)}, bf16[1,256,768]{2,1,0:T(8,128)(2,1)S(1)}, u32[]{:S(2)}, u32[]{:S(2)}) collective-permute-start(bf16[1,256,768]{2,1,0:T(8,128)(2,1)S(1)} %bitcast.54), channel_id=1, source_target_pairs={{0,4},{2,6},{4,0},{6,2},{8,12},{10,14},{12,8},{14,10},{16,20},{18,... | collective-permute-start | bytes 1179656 | tf_op jit(solution)/shard_map/line_w0/ppermute | solution.py:24
  6.3 1.0 fusion.7
  7.3 1.6 %collective-permute-start.6 = (bf16[288,768]{1,0:T(8,128)(2,1)}, bf16[288,768]{1,0:T(8,128)(2,1)S(1)}, u32[]{:S(2)}, u32[]{:S(2)}) collective-permute-start(bf16[288,768]{1,0:T(8,128)(2,1)} %get-tuple-element.134), channel_id=1, source_target_pairs={{0,8},{2,10},{4,12},{6,14},{8,0},{10,2},{12,4},{14,6},{16,24},{18,... | collective-permute-start | bytes 1327112 | tf_op jit(solution)/shard_map/w_1/ppermute | solution.py:24
  8.9 2.6 %collective-permute-start.5 = (bf16[288,768]{1,0:T(8,128)(2,1)}, bf16[288,768]{1,0:T(8,128)(2,1)S(1)}, u32[]{:S(2)}, u32[]{:S(2)}) collective-permute-start(bf16[288,768]{1,0:T(8,128)(2,1)} %get-tuple-element.135), channel_id=1, source_target_pairs={{0,16},{2,18},{4,20},{6,22},{8,24},{10,26},{12,28},{14,30},{16,0},... | collective-permute-start | bytes 1327112 | tf_op jit(solution)/shard_map/w_2/ppermute | solution.py:24
  12.2 0.1 pad_add_fusion.1.refs_0_
  12.3 0.0 collective-permute-done.refs_1_
  12.3 0.2 norm.1.refs_2_
  12.5 0.1 broadcast_multiply_fusion.1
  12.6 0.1 iota_add_fusion
  12.7 0.1 add_add_fusion
  12.8 0.8 maximum_maximum_fusion
  13.6 0.3 collective-permute-start.4
  13.9 0.4 collective-permute-start.3
  14.4 0.1 stack.122.refs_2_
  14.5 0.1 stack.117.refs_1_
  14.6 1.4 %fusion.16 = (f32[4,192,64]{2,1,0:T(8,128)S(1)}, f32[4,192,64]{2,1,0:T(8,128)S(1)}, f32[4,192,64]{2,1,0:T(8,128)S(1)}) fusion(f32[64]{0:T(128)S(1)} %multiply_exponential_fusion, f32[4,192]{1,0:T(4,128)S(1)} %add_convert_fusion), kind=kLoop, calls=%fused_computation.32 | loop fusion | flops 98304 | bytes 593152 | tf_op jit(solution)/shard_map/neg | solution.py:451
  16.0 0.3 pad_maximum_fusion.4
  16.3 0.0 collective-permute-done.1.refs_1_
  16.3 0.6 collective-permute-start.2
  16.9 27.7 %collective-permute-done.5.refs_1_ = bf16[288,768]{1,0:T(8,128)(2,1)S(1)} collective-permute-done((bf16[288,768]{1,0:T(8,128)(2,1)}, bf16[288,768]{1,0:T(8,128)(2,1)S(1)}, u32[]{:S(2)}, u32[]{:S(2)}) %collective-permute-start.5) | collective-permute-done | bytes 442400 | tf_op jit(solution)/shard_map/w_2/ppermute | solution.py:24
  44.5 0.1 unpack.3
  44.6 0.6 collective-permute-start.7
  45.2 0.1 unpack.4
  45.3 9.2 %collective-permute-done.4.refs_6_ = bf16[8,136,256]{2,1,0:T(8,128)(2,1)S(1)} collective-permute-done((bf16[8,136,256]{2,1,0:T(8,128)(2,1)S(1)}, bf16[8,136,256]{2,1,0:T(8,128)(2,1)S(1)}, u32[]{:S(2)}, u32[]{:S(2)}) %collective-permute-start.4) | collective-permute-done | bytes 557088 | tf_op jit(solution)/shard_map/x_far_2/ppermute | solution.py:24
  54.5 2.6 %collective-permute-start.11 = (bf16[288,768]{1,0:T(8,128)(2,1)S(1)}, bf16[288,768]{1,0:T(8,128)(2,1)S(1)}, u32[]{:S(2)}, u32[]{:S(2)}) collective-permute-start(bf16[288,768]{1,0:T(8,128)(2,1)S(1)} %copy-done.2), channel_id=1, source_target_pairs={{0,24},{2,26},{4,28},{6,30},{8,16},{10,18},{12,20},{14,22},{16,8},... | collective-permute-start | bytes 1327112 | tf_op jit(solution)/shard_map/w_3/ppermute | solution.py:24
  57.1 0.5 collective-permute-start.13
  57.7 0.5 collective-permute-start.10
  58.2 1.5 %collective-permute-start.9 = (bf16[8,136,256]{2,1,0:T(8,128)(2,1)S(1)}, bf16[8,136,256]{2,1,0:T(8,128)(2,1)S(1)}, u32[]{:S(2)}, u32[]{:S(2)}) collective-permute-start(bf16[8,136,256]{2,1,0:T(8,128)(2,1)S(1)} %collective-permute-done.3.refs_4_), channel_id=1, source_target_pairs={{0,1},{1,0},{2,3},{3,2},{4,5},{5,4},{6,7},{7,6},{8,9},{9,8},{10,11... | collective-permute-start | bytes 1671176 | tf_op jit(solution)/shard_map/side_next/ppermute | solution.py:24
  59.7 6.2 %collective-permute-done.13.refs_3_ = bf16[1,256,768]{2,1,0:T(8,128)(2,1)S(1)} collective-permute-done((bf16[1,256,768]{2,1,0:T(8,128)(2,1)S(1)}, bf16[1,256,768]{2,1,0:T(8,128)(2,1)S(1)}, u32[]{:S(2)}, u32[]{:S(2)}) %collective-permute-start.13) | collective-permute-done | bytes 393248 | tf_op jit(solution)/shard_map/line_w1/ppermute | solution.py:24
  65.9 0.2 join.1.refs_8_.refs_5_
  66.0 0.1 collective-permute-start.14
  66.1 3.4 %collective-permute-done.11.refs_0_ = bf16[288,768]{1,0:T(8,128)(2,1)S(1)} collective-permute-done((bf16[288,768]{1,0:T(8,128)(2,1)S(1)}, bf16[288,768]{1,0:T(8,128)(2,1)S(1)}, u32[]{:S(2)}, u32[]{:S(2)}) %collective-permute-start.11) | collective-permute-done | bytes 442400 | tf_op jit(solution)/shard_map/w_3/ppermute | solution.py:24
  69.6 0.8 unpack.5
  70.4 0.5 collective-permute-start.12
  70.9 2.3 %collective-permute-done.10.value.refs_7_ = bf16[8,136,256]{2,1,0:T(8,128)(2,1)S(1)} collective-permute-done((bf16[8,136,256]{2,1,0:T(8,128)(2,1)S(1)}, bf16[8,136,256]{2,1,0:T(8,128)(2,1)S(1)}, u32[]{:S(2)}, u32[]{:S(2)}) %collective-permute-start.10) | collective-permute-done | bytes 557088 | tf_op jit(solution)/shard_map/side_far/ppermute | solution.py:24
  73.2 5.3 %collective-permute-done.8.value.refs_2_ = bf16[8,136,256]{2,1,0:T(8,128)(2,1)S(1)} collective-permute-done((bf16[8,136,256]{2,1,0:T(8,128)(2,1)S(1)}, bf16[8,136,256]{2,1,0:T(8,128)(2,1)S(1)}, u32[]{:S(2)}, u32[]{:S(2)}) %collective-permute-start.8) | collective-permute-done | bytes 557088 | tf_op jit(solution)/shard_map/x_last_1/ppermute | solution.py:24
  78.6 3.0 %collective-permute-done.9.refs_5_ = bf16[8,136,256]{2,1,0:T(8,128)(2,1)S(1)} collective-permute-done((bf16[8,136,256]{2,1,0:T(8,128)(2,1)S(1)}, bf16[8,136,256]{2,1,0:T(8,128)(2,1)S(1)}, u32[]{:S(2)}, u32[]{:S(2)}) %collective-permute-start.9) | collective-permute-done | bytes 557088 | tf_op jit(solution)/shard_map/side_next/ppermute | solution.py:24
  81.6 0.5 collective-permute-start.16
  82.1 0.5 collective-permute-start.17
  82.6 1.6 %collective-permute-start.18 = (bf16[4,136,256]{2,1,0:T(8,128)(2,1)S(1)}, bf16[4,136,256]{2,1,0:T(8,128)(2,1)S(1)}, u32[]{:S(2)}, u32[]{:S(2)}) collective-permute-start(bf16[4,136,256]{2,1,0:T(8,128)(2,1)S(1)} %half.3), channel_id=1, source_target_pairs={{0,8},{2,10},{4,12},{6,14},{8,0},{10,2},{12,4},{14,6},{16,24},{18,... | collective-permute-start | bytes 835592 | tf_op jit(solution)/shard_map/x_last_side_1/ppermute | solution.py:24
  84.2 2.4 %keys_values.2.refs_5_.refs_4_ = bf16[3,192,256]{2,1,0:T(8,128)(2,1)S(1)} custom-call(s32[16]{0:T(128)S(1)} %pad_add_fusion.1.refs_0_, s32[16]{0:T(128)S(1)} %stack.117.refs_1_, bf16[8,136,256]{2,1,0:T(8,128)(2,1)S(1)} %norm.1.refs_2_, bf16[8,136,256]{2,1,0:T(8,128)(2,1)S(1)} %collective-permute-done.2.refs_3_, ...), custom_call_target="tpu_custom_call" | custom-call | flops 905969664 | bytes 5636096 | tf_op jit(solution)/shard_map/keys_values/pallas_call | solution.py:247
  86.6 1.2 %collective-permute-start.19 = (bf16[3,192,256]{2,1,0:T(8,128)(2,1)S(1)}, bf16[3,192,256]{2,1,0:T(8,128)(2,1)S(1)}, u32[]{:S(2)}, u32[]{:S(2)}) collective-permute-start(bf16[3,192,256]{2,1,0:T(8,128)(2,1)S(1)} %keys_values.2.refs_5_.refs_4_), channel_id=1, source_target_pairs={{0,4},{2,6},{4,0},{6,2},{8,12},{10,14},{12,8},{14,10},{16,20},{18,... | collective-permute-start | bytes 884744 | tf_op jit(solution)/shard_map/kv_line/ppermute | solution.py:24
  87.9 3.4 %queries.2.refs_4_.refs_3_ = bf16[3,4,128,128]{3,2,1,0:T(8,128)(2,1)S(1)} custom-call(s32[16]{0:T(128)S(1)} %pad_add_fusion.1.refs_0_, s32[16]{0:T(128)S(1)} %stack.117.refs_1_, bf16[8,136,256]{2,1,0:T(8,128)(2,1)S(1)} %norm.1.refs_2_, bf16[8,136,256]{2,1,0:T(8,128)(2,1)S(1)} %collective-permute-done.2.refs_3_, ...), custom_call_target="tpu_custom_call" | custom-call | flops 1811939328 | bytes 7733248 | tf_op jit(solution)/shard_map/queries/pallas_call | solution.py:247
  91.3 1.4 %keys_values.3.refs_9_.refs_8_ = bf16[1,192,256]{2,1,0:T(8,128)(2,1)S(1)} custom-call(s32[16]{0:T(128)S(1)} %pad_add_fusion.1.refs_0_, s32[16]{0:T(128)S(1)} %stack.117.refs_1_, bf16[8,136,256]{2,1,0:T(8,128)(2,1)S(1)} %collective-permute-done.8.value.refs_2_, bf16[4,136,256]{2,1,0:T(8,128)(2,1)S(1)} %collective-permute-done.17.refs_3_, ...), custom_call_target="tpu_custom_call" | custom-call | flops 301989888 | bytes 3276800 | tf_op jit(solution)/shard_map/keys_values/pallas_call | solution.py:247
  92.7 1.2 %collective-permute-start.20 = (bf16[1,192,256]{2,1,0:T(8,128)(2,1)S(1)}, bf16[1,192,256]{2,1,0:T(8,128)(2,1)S(1)}, u32[]{:S(2)}, u32[]{:S(2)}) collective-permute-start(bf16[1,192,256]{2,1,0:T(8,128)(2,1)S(1)} %keys_values.3.refs_9_.refs_8_), channel_id=1, source_target_pairs={{0,4},{2,6},{4,0},{6,2},{8,12},{10,14},{12,8},{14,10},{16,20},{18,... | collective-permute-start | bytes 294920 | tf_op jit(solution)/shard_map/kv_line/ppermute | solution.py:24
  93.9 2.0 %queries.3.refs_3_ = bf16[1,4,128,128]{3,2,1,0:T(8,128)(2,1)S(1)} custom-call(s32[16]{0:T(128)S(1)} %pad_add_fusion.1.refs_0_, s32[16]{0:T(128)S(1)} %stack.117.refs_1_, bf16[8,136,256]{2,1,0:T(8,128)(2,1)S(1)} %collective-permute-done.8.value.refs_2_, bf16[4,136,256]{2,1,0:T(8,128)(2,1)S(1)} %collective-permute-done.17.refs_3_, ...), custom_call_target="tpu_custom_call" | custom-call | flops 603979776 | bytes 5373952 | tf_op jit(solution)/shard_map/queries/pallas_call | solution.py:247
  95.9 1.6 %collective-permute-done.20.refs_10_.refs_9_ = bf16[1,192,256]{2,1,0:T(8,128)(2,1)S(1)} collective-permute-done((bf16[1,192,256]{2,1,0:T(8,128)(2,1)S(1)}, bf16[1,192,256]{2,1,0:T(8,128)(2,1)S(1)}, u32[]{:S(2)}, u32[]{:S(2)}) %collective-permute-start.20) | collective-permute-done | bytes 98336 | tf_op jit(solution)/shard_map/kv_line/ppermute | solution.py:24
  97.5 0.5 collective-permute-start.23
  98.0 0.0 collective-permute-start.24
  98.0 1.2 collective-permute-done.23.refs_11_.refs_10_
  99.3 0.1 collective-permute-done.24.refs_12_.refs_11_
  99.4 9.6 %attend.3 = (bf16[128,512]{1,0:T(8,128)(2,1)S(1)}, bf16[128,512]{1,0:T(8,128)(2,1)S(1)}) custom-call(s32[1]{0:T(128)} %copy.8.refs_0_, s32[4]{0:T(128)S(1)} %get-tuple-element.72.refs_1_, s32[16]{0:T(128)S(1)} %stack.122.refs_2_, bf16[1,4,128,128]{3,2,1,0:T(8,128)(2,1)S(1)} %queries.3.refs_3_, bf16[3,4,128,128]{3,2,1,0:T(8,128)(2,1)S(1)} %queries.2.refs_4_.refs_3_, ...), custom_call_target="tpu_custom_call" | custom-call | flops 1610612736 | bytes 1572864 | tf_op jit(solution)/shard_map/attend/pallas_call | solution.py:382
  109.0 0.1 collective-permute-start.25
  109.1 4.1 %attend.4 = bf16[128,512]{1,0:T(8,128)(2,1)S(1)} custom-call(s32[1]{0:T(128)} %copy.8.refs_0_, s32[4]{0:T(128)S(1)} %get-tuple-element.72.refs_1_, s32[16]{0:T(128)S(1)} %stack.122.refs_2_, bf16[3,4,128,128]{3,2,1,0:T(8,128)(2,1)S(1)} %queries.2.refs_4_.refs_3_, bf16[3,192,256]{2,1,0:T(8,128)(2,1)S(1)} %keys_values.2.refs_5_.refs_4_, ...), custom_call_target="tpu_custom_call" | custom-call | flops 805306368 | bytes 1572864 | tf_op jit(solution)/shard_map/attend/pallas_call | solution.py:382
  113.1 1.0 collective-permute-start.26
  114.2 4.1 %collective-permute-start.27 = (bf16[128,512]{1,0:T(8,128)(2,1)S(1)}, bf16[128,512]{1,0:T(8,128)(2,1)S(1)}, u32[]{:S(2)}, u32[]{:S(2)}) collective-permute-start(bf16[128,512]{1,0:T(8,128)(2,1)S(1)} %get-tuple-element.108), channel_id=1, source_target_pairs={{0,16},{2,18},{4,20},{6,22},{8,24},{10,26},{12,28},{14,30},{16,0},... | collective-permute-start | bytes 393224 | tf_op jit(solution)/shard_map/mixed_2/ppermute | solution.py:24
  118.2 3.7 %attend.5 = bf16[128,512]{1,0:T(8,128)(2,1)S(1)} custom-call(s32[1]{0:T(128)} %copy.8.refs_0_, s32[4]{0:T(128)S(1)} %get-tuple-element.72.refs_1_, s32[16]{0:T(128)S(1)} %stack.122.refs_2_, bf16[3,4,128,128]{3,2,1,0:T(8,128)(2,1)S(1)} %queries.2.refs_4_.refs_3_, bf16[3,192,256]{2,1,0:T(8,128)(2,1)S(1)} %keys_values.2.refs_5_.refs_4_, ...), custom_call_target="tpu_custom_call" | custom-call | flops 805306368 | bytes 1572864 | tf_op jit(solution)/shard_map/attend/pallas_call | solution.py:382
  121.9 0.2 collective-permute-done.26
  122.1 0.1 pad_maximum_fusion.2
  122.3 0.8 pad_maximum_fusion.3
  (44 shorter events, 0.3 us)
Async XLA Ops:
  0.0 1.6 %copy-start = (bf16[128,2048]{1,0:T(8,128)(2,1)S(1)}, bf16[128,2048]{1,0:T(8,128)(2,1)}, u32[]{:S(2)}) copy-start(bf16[128,2048]{1,0:T(8,128)(2,1)} %stream.1) | copy-start | bytes 1572868
  0.0 1.6 %copy-start.1 = (bf16[8,2048]{1,0:T(8,128)(2,1)S(1)}, bf16[8,2048]{1,0:T(8,128)(2,1)}, u32[]{:S(2)}) copy-start(bf16[8,2048]{1,0:T(8,128)(2,1)} %hidden.3) | copy-start | bytes 98308
  0.0 6.3 %copy-start.5 = (s32[8]{0:T(128)S(1)}, s32[8]{0:T(128)}, u32[]{:S(2)}) copy-start(s32[8]{0:T(128)} %param.12) | copy-start | bytes 100
  0.0 6.3 %copy-start.3 = (bf16[2,64,512]{2,1,0:T(8,128)(2,1)S(1)}, bf16[2,64,512]{2,1,0:T(8,128)(2,1)}, u32[]{:S(2)}) copy-start(bf16[2,64,512]{2,1,0:T(8,128)(2,1)} %param.10) | copy-start | bytes 393220
  1.5 10.6 %copy-start.4 = (f32[4096]{0:T(1024)S(1)}, f32[4096]{0:T(1024)}, u32[]{:S(2)}) copy-start(f32[4096]{0:T(1024)} %param.8) | copy-start | bytes 49156
  1.8 10.5 %collective-permute-start = (f32[136,128]{1,0:T(8,128)S(1)}, f32[136,128]{1,0:T(8,128)S(1)}, u32[]{:S(2)}, u32[]{:S(2)}) collective-permute-start(f32[136,128]{1,0:T(8,128)S(1)} %squares.1.refs_0_), channel_id=1, source_target_pairs={{0,1},{1,0},{2,3},{3,2},{4,5},{5,4},{6,7},{7,6},{8,9},{9,8},{10,11... | collective-permute-start | bytes 208904 | tf_op jit(solution)/shard_map/side_sums/ppermute | solution.py:24
  4.8 11.5 %collective-permute-start.1 = (bf16[1,256,768]{2,1,0:T(8,128)(2,1)S(1)}, bf16[1,256,768]{2,1,0:T(8,128)(2,1)S(1)}, u32[]{:S(2)}, u32[]{:S(2)}) collective-permute-start(bf16[1,256,768]{2,1,0:T(8,128)(2,1)S(1)} %bitcast.54), channel_id=1, source_target_pairs={{0,4},{2,6},{4,0},{6,2},{8,12},{10,14},{12,8},{14,10},{16,20},{18,... | collective-permute-start | bytes 1179656 | tf_op jit(solution)/shard_map/line_w0/ppermute | solution.py:24
  7.3 37.9 %collective-permute-start.6 = (bf16[288,768]{1,0:T(8,128)(2,1)}, bf16[288,768]{1,0:T(8,128)(2,1)S(1)}, u32[]{:S(2)}, u32[]{:S(2)}) collective-permute-start(bf16[288,768]{1,0:T(8,128)(2,1)} %get-tuple-element.134), channel_id=1, source_target_pairs={{0,8},{2,10},{4,12},{6,14},{8,0},{10,2},{12,4},{14,6},{16,24},{18,... | collective-permute-start | bytes 1327112 | tf_op jit(solution)/shard_map/w_1/ppermute | solution.py:24
  8.9 35.6 %collective-permute-start.5 = (bf16[288,768]{1,0:T(8,128)(2,1)}, bf16[288,768]{1,0:T(8,128)(2,1)S(1)}, u32[]{:S(2)}, u32[]{:S(2)}) collective-permute-start(bf16[288,768]{1,0:T(8,128)(2,1)} %get-tuple-element.135), channel_id=1, source_target_pairs={{0,16},{2,18},{4,20},{6,22},{8,24},{10,26},{12,28},{14,30},{16,0},... | collective-permute-start | bytes 1327112 | tf_op jit(solution)/shard_map/w_2/ppermute | solution.py:24
  13.6 40.9 %collective-permute-start.4 = (bf16[8,136,256]{2,1,0:T(8,128)(2,1)S(1)}, bf16[8,136,256]{2,1,0:T(8,128)(2,1)S(1)}, u32[]{:S(2)}, u32[]{:S(2)}) collective-permute-start(bf16[8,136,256]{2,1,0:T(8,128)(2,1)S(1)} %norm.1.refs_2_), channel_id=1, source_target_pairs={{0,16},{2,18},{4,20},{6,22},{8,24},{10,26},{12,28},{14,30},{16,0},... | collective-permute-start | bytes 1671176 | tf_op jit(solution)/shard_map/x_far_2/ppermute | solution.py:24
  13.9 40.6 %collective-permute-start.3 = (bf16[8,136,256]{2,1,0:T(8,128)(2,1)S(1)}, bf16[8,136,256]{2,1,0:T(8,128)(2,1)S(1)}, u32[]{:S(2)}, u32[]{:S(2)}) collective-permute-start(bf16[8,136,256]{2,1,0:T(8,128)(2,1)S(1)} %norm.1.refs_2_), channel_id=1, source_target_pairs={{0,8},{2,10},{4,12},{6,14},{8,0},{10,2},{12,4},{14,6},{16,24},{18,... | collective-permute-start | bytes 1671176 | tf_op jit(solution)/shard_map/x_next_1/ppermute | solution.py:24
  16.3 38.2 %collective-permute-start.2 = (bf16[8,136,256]{2,1,0:T(8,128)(2,1)S(1)}, bf16[8,136,256]{2,1,0:T(8,128)(2,1)S(1)}, u32[]{:S(2)}, u32[]{:S(2)}) collective-permute-start(bf16[8,136,256]{2,1,0:T(8,128)(2,1)S(1)} %norm.1.refs_2_), channel_id=1, source_target_pairs={{0,1},{1,0},{2,3},{3,2},{4,5},{5,4},{6,7},{7,6},{8,9},{9,8},{10,11... | collective-permute-start | bytes 1671176 | tf_op jit(solution)/shard_map/side_own/ppermute | solution.py:24
  44.6 9.9 %collective-permute-start.7 = (bf16[1,256,768]{2,1,0:T(8,128)(2,1)S(1)}, bf16[1,256,768]{2,1,0:T(8,128)(2,1)S(1)}, u32[]{:S(2)}, u32[]{:S(2)}) collective-permute-start(bf16[1,256,768]{2,1,0:T(8,128)(2,1)S(1)} %get-tuple-element.70), channel_id=1, source_target_pairs={{0,4},{2,6},{4,0},{6,2},{8,12},{10,14},{12,8},{14,10},{16,20},{18,... | collective-permute-start | bytes 1179656 | tf_op jit(solution)/shard_map/line_w2/ppermute | solution.py:24
  45.2 9.3 %copy-start.2 = (bf16[288,768]{1,0:T(8,128)(2,1)S(1)}, bf16[288,768]{1,0:T(8,128)(2,1)}, u32[]{:S(2)}) copy-start(bf16[288,768]{1,0:T(8,128)(2,1)} %maximum_maximum_fusion) | copy-start | bytes 1327108
  54.5 15.0 %collective-permute-start.11 = (bf16[288,768]{1,0:T(8,128)(2,1)S(1)}, bf16[288,768]{1,0:T(8,128)(2,1)S(1)}, u32[]{:S(2)}, u32[]{:S(2)}) collective-permute-start(bf16[288,768]{1,0:T(8,128)(2,1)S(1)} %copy-done.2), channel_id=1, source_target_pairs={{0,24},{2,26},{4,28},{6,30},{8,16},{10,18},{12,20},{14,22},{16,8},... | collective-permute-start | bytes 1327112 | tf_op jit(solution)/shard_map/w_3/ppermute | solution.py:24
  57.1 8.8 %collective-permute-start.13 = (bf16[1,256,768]{2,1,0:T(8,128)(2,1)S(1)}, bf16[1,256,768]{2,1,0:T(8,128)(2,1)S(1)}, u32[]{:S(2)}, u32[]{:S(2)}) collective-permute-start(bf16[1,256,768]{2,1,0:T(8,128)(2,1)S(1)} %get-tuple-element.85), channel_id=1, source_target_pairs={{0,4},{2,6},{4,0},{6,2},{8,12},{10,14},{12,8},{14,10},{16,20},{18,... | collective-permute-start | bytes 1179656 | tf_op jit(solution)/shard_map/line_w1/ppermute | solution.py:24
  57.7 15.6 %collective-permute-start.10 = (bf16[8,136,256]{2,1,0:T(8,128)(2,1)S(1)}, bf16[8,136,256]{2,1,0:T(8,128)(2,1)S(1)}, u32[]{:S(2)}, u32[]{:S(2)}) collective-permute-start(bf16[8,136,256]{2,1,0:T(8,128)(2,1)S(1)} %collective-permute-done.4.refs_6_), channel_id=1, source_target_pairs={{0,1},{1,0},{2,3},{3,2},{4,5},{5,4},{6,7},{7,6},{8,9},{9,8},{10,11... | collective-permute-start | bytes 1671176 | tf_op jit(solution)/shard_map/side_far/ppermute | solution.py:24
  58.2 20.4 %collective-permute-start.8 = (bf16[8,136,256]{2,1,0:T(8,128)(2,1)S(1)}, bf16[8,136,256]{2,1,0:T(8,128)(2,1)S(1)}, u32[]{:S(2)}, u32[]{:S(2)}) collective-permute-start(bf16[8,136,256]{2,1,0:T(8,128)(2,1)S(1)} %collective-permute-done.4.refs_6_), channel_id=1, source_target_pairs={{0,8},{2,10},{4,12},{6,14},{8,0},{10,2},{12,4},{14,6},{16,24},{18,... | collective-permute-start | bytes 1671176 | tf_op jit(solution)/shard_map/x_last_1/ppermute | solution.py:24
  58.2 23.4 %collective-permute-start.9 = (bf16[8,136,256]{2,1,0:T(8,128)(2,1)S(1)}, bf16[8,136,256]{2,1,0:T(8,128)(2,1)S(1)}, u32[]{:S(2)}, u32[]{:S(2)}) collective-permute-start(bf16[8,136,256]{2,1,0:T(8,128)(2,1)S(1)} %collective-permute-done.3.refs_4_), channel_id=1, source_target_pairs={{0,1},{1,0},{2,3},{3,2},{4,5},{5,4},{6,7},{7,6},{8,9},{9,8},{10,11... | collective-permute-start | bytes 1671176 | tf_op jit(solution)/shard_map/side_next/ppermute | solution.py:24
  66.0 15.6 %collective-permute-start.14 = (bf16[6,256,768]{2,1,0:T(8,128)(2,1)S(1)}, bf16[6,256,768]{2,1,0:T(8,128)(2,1)S(1)}, u32[]{:S(2)}, u32[]{:S(2)}) collective-permute-start(bf16[6,256,768]{2,1,0:T(8,128)(2,1)S(1)} %join.1.refs_8_.refs_5_), channel_id=1, source_target_pairs={{0,2},{2,0},{4,6},{6,4},{8,10},{10,8},{12,14},{14,12},{16,18},{18,... | collective-permute-start | bytes 7077896 | tf_op jit(solution)/shard_map/core_w/ppermute | solution.py:24
  70.4 11.2 %collective-permute-start.12 = (bf16[1,256,768]{2,1,0:T(8,128)(2,1)S(1)}, bf16[1,256,768]{2,1,0:T(8,128)(2,1)S(1)}, u32[]{:S(2)}, u32[]{:S(2)}) collective-permute-start(bf16[1,256,768]{2,1,0:T(8,128)(2,1)S(1)} %get-tuple-element.89.refs_9_.refs_6_), channel_id=1, source_target_pairs={{0,4},{2,6},{4,0},{6,2},{8,12},{10,14},{12,8},{14,10},{16,20},{18,... | collective-permute-start | bytes 1179656 | tf_op jit(solution)/shard_map/line_w3/ppermute | solution.py:24
  81.6 2.6 %collective-permute-start.15 = (bf16[1,256,768]{2,1,0:T(8,128)(2,1)S(1)}, bf16[1,256,768]{2,1,0:T(8,128)(2,1)S(1)}, u32[]{:S(2)}, u32[]{:S(2)}) collective-permute-start(bf16[1,256,768]{2,1,0:T(8,128)(2,1)S(1)} %get-tuple-element.89.refs_9_.refs_6_), channel_id=1, source_target_pairs={{0,2},{2,0},{4,6},{6,4},{8,10},{10,8},{12,14},{14,12},{16,18},{18,... | collective-permute-start | bytes 1179656 | tf_op jit(solution)/shard_map/core_w3/ppermute | solution.py:24
  81.6 2.6 %collective-permute-start.16 = (bf16[1,256,768]{2,1,0:T(8,128)(2,1)S(1)}, bf16[1,256,768]{2,1,0:T(8,128)(2,1)S(1)}, u32[]{:S(2)}, u32[]{:S(2)}) collective-permute-start(bf16[1,256,768]{2,1,0:T(8,128)(2,1)S(1)} %collective-permute-done.12.refs_10_.refs_7_), channel_id=1, source_target_pairs={{0,2},{2,0},{4,6},{6,4},{8,10},{10,8},{12,14},{14,12},{16,18},{18,... | collective-permute-start | bytes 1179656 | tf_op jit(solution)/shard_map/core_w3_line/ppermute | solution.py:24
  82.1 9.2 %collective-permute-start.17 = (bf16[4,136,256]{2,1,0:T(8,128)(2,1)S(1)}, bf16[4,136,256]{2,1,0:T(8,128)(2,1)S(1)}, u32[]{:S(2)}, u32[]{:S(2)}) collective-permute-start(bf16[4,136,256]{2,1,0:T(8,128)(2,1)S(1)} %half.2), channel_id=1, source_target_pairs={{0,1},{1,0},{2,3},{3,2},{4,5},{5,4},{6,7},{7,6},{8,9},{9,8},{10,11... | collective-permute-start | bytes 835592 | tf_op jit(solution)/shard_map/side_last/ppermute | solution.py:24
  82.6 8.7 %collective-permute-start.18 = (bf16[4,136,256]{2,1,0:T(8,128)(2,1)S(1)}, bf16[4,136,256]{2,1,0:T(8,128)(2,1)S(1)}, u32[]{:S(2)}, u32[]{:S(2)}) collective-permute-start(bf16[4,136,256]{2,1,0:T(8,128)(2,1)S(1)} %half.3), channel_id=1, source_target_pairs={{0,8},{2,10},{4,12},{6,14},{8,0},{10,2},{12,4},{14,6},{16,24},{18,... | collective-permute-start | bytes 835592 | tf_op jit(solution)/shard_map/x_last_side_1/ppermute | solution.py:24
  86.6 10.9 %collective-permute-start.19 = (bf16[3,192,256]{2,1,0:T(8,128)(2,1)S(1)}, bf16[3,192,256]{2,1,0:T(8,128)(2,1)S(1)}, u32[]{:S(2)}, u32[]{:S(2)}) collective-permute-start(bf16[3,192,256]{2,1,0:T(8,128)(2,1)S(1)} %keys_values.2.refs_5_.refs_4_), channel_id=1, source_target_pairs={{0,4},{2,6},{4,0},{6,2},{8,12},{10,14},{12,8},{14,10},{16,20},{18,... | collective-permute-start | bytes 884744 | tf_op jit(solution)/shard_map/kv_line/ppermute | solution.py:24
  92.7 4.8 %collective-permute-start.20 = (bf16[1,192,256]{2,1,0:T(8,128)(2,1)S(1)}, bf16[1,192,256]{2,1,0:T(8,128)(2,1)S(1)}, u32[]{:S(2)}, u32[]{:S(2)}) collective-permute-start(bf16[1,192,256]{2,1,0:T(8,128)(2,1)S(1)} %keys_values.3.refs_9_.refs_8_), channel_id=1, source_target_pairs={{0,4},{2,6},{4,0},{6,2},{8,12},{10,14},{12,8},{14,10},{16,20},{18,... | collective-permute-start | bytes 294920 | tf_op jit(solution)/shard_map/kv_line/ppermute | solution.py:24
  93.9 5.3 %collective-permute-start.21 = (bf16[3,192,256]{2,1,0:T(8,128)(2,1)S(1)}, bf16[3,192,256]{2,1,0:T(8,128)(2,1)S(1)}, u32[]{:S(2)}, u32[]{:S(2)}) collective-permute-start(bf16[3,192,256]{2,1,0:T(8,128)(2,1)S(1)} %keys_values.2.refs_5_.refs_4_), channel_id=1, source_target_pairs={{0,2},{2,0},{4,6},{6,4},{8,10},{10,8},{12,14},{14,12},{16,18},{18,... | collective-permute-start | bytes 884744 | tf_op jit(solution)/shard_map/core_kv/ppermute | solution.py:24
  97.5 1.9 %collective-permute-start.22 = (bf16[3,192,256]{2,1,0:T(8,128)(2,1)S(1)}, bf16[3,192,256]{2,1,0:T(8,128)(2,1)S(1)}, u32[]{:S(2)}, u32[]{:S(2)}) collective-permute-start(bf16[3,192,256]{2,1,0:T(8,128)(2,1)S(1)} %collective-permute-done.19.refs_6_.refs_5_), channel_id=1, source_target_pairs={{0,2},{2,0},{4,6},{6,4},{8,10},{10,8},{12,14},{14,12},{16,18},{18,... | collective-permute-start | bytes 884744 | tf_op jit(solution)/shard_map/core_kv_line/ppermute | solution.py:24
  97.5 1.7 %collective-permute-start.23 = (bf16[1,192,256]{2,1,0:T(8,128)(2,1)S(1)}, bf16[1,192,256]{2,1,0:T(8,128)(2,1)S(1)}, u32[]{:S(2)}, u32[]{:S(2)}) collective-permute-start(bf16[1,192,256]{2,1,0:T(8,128)(2,1)S(1)} %keys_values.3.refs_9_.refs_8_), channel_id=1, source_target_pairs={{0,2},{2,0},{4,6},{6,4},{8,10},{10,8},{12,14},{14,12},{16,18},{18,... | collective-permute-start | bytes 294920 | tf_op jit(solution)/shard_map/core_kv/ppermute | solution.py:24
  98.0 1.4 %collective-permute-start.24 = (bf16[1,192,256]{2,1,0:T(8,128)(2,1)S(1)}, bf16[1,192,256]{2,1,0:T(8,128)(2,1)S(1)}, u32[]{:S(2)}, u32[]{:S(2)}) collective-permute-start(bf16[1,192,256]{2,1,0:T(8,128)(2,1)S(1)} %collective-permute-done.20.refs_10_.refs_9_), channel_id=1, source_target_pairs={{0,2},{2,0},{4,6},{6,4},{8,10},{10,8},{12,14},{14,12},{16,18},{18,... | collective-permute-start | bytes 294920 | tf_op jit(solution)/shard_map/core_kv_line/ppermute | solution.py:24
  109.0 9.2 %collective-permute-start.25 = (bf16[128,512]{1,0:T(8,128)(2,1)S(1)}, bf16[128,512]{1,0:T(8,128)(2,1)S(1)}, u32[]{:S(2)}, u32[]{:S(2)}) collective-permute-start(bf16[128,512]{1,0:T(8,128)(2,1)S(1)} %get-tuple-element.107), channel_id=1, source_target_pairs={{0,24},{2,26},{4,28},{6,30},{8,16},{10,18},{12,20},{14,22},{16,8},... | collective-permute-start | bytes 393224 | tf_op jit(solution)/shard_map/mixed_3/ppermute | solution.py:24
  113.1 9.0 %collective-permute-start.26 = (bf16[128,512]{1,0:T(8,128)(2,1)S(1)}, bf16[128,512]{1,0:T(8,128)(2,1)S(1)}, u32[]{:S(2)}, u32[]{:S(2)}) collective-permute-start(bf16[128,512]{1,0:T(8,128)(2,1)S(1)} %attend.4), channel_id=1, source_target_pairs={{0,8},{2,10},{4,12},{6,14},{8,0},{10,2},{12,4},{14,6},{16,24},{18,... | collective-permute-start | bytes 393224 | tf_op jit(solution)/shard_map/mixed_1/ppermute | solution.py:24
  114.2 8.0 %collective-permute-start.27 = (bf16[128,512]{1,0:T(8,128)(2,1)S(1)}, bf16[128,512]{1,0:T(8,128)(2,1)S(1)}, u32[]{:S(2)}, u32[]{:S(2)}) collective-permute-start(bf16[128,512]{1,0:T(8,128)(2,1)S(1)} %get-tuple-element.108), channel_id=1, source_target_pairs={{0,16},{2,18},{4,20},{6,22},{8,24},{10,26},{12,28},{14,30},{16,0},... | collective-permute-start | bytes 393224 | tf_op jit(solution)/shard_map/mixed_2/ppermute | solution.py:24
